TPU v7x, 32 devices: a whole 2x2x4 slice. The times are simulated.
32 devices in a mesh: dp: 8 (over z, core), expert: 4 (over y, x).
Axes of the slice: x: 2, y: 2, z: 4, core: 2. Of those that a mesh axis runs over, the one named last changes fastest.
Arguments:
- gen_rows: bfloat16 [4096, 2048], P(('dp', 'expert')), may hold values from -6 to 6
- gen_lengths: int32 [8, 4, 8], P('dp', 'expert'), may hold values from 1 to 16, as said below
- gen_adv: bfloat16 [8, 4, 8], P('dp', 'expert'), may hold values from -4 to 4
- destination: int32 [8, 4, 8], P('dp', 'expert'), may hold values from 0 to 7, as said below
- expert_ids: int32 [4096, 2], P(('dp', 'expert')), may hold values from 0 to 3, all different within a row; in each aligned block of 128 rows (0 to 127, 128 to 255, ...) at most 128 rows name the same one
- gate_values: float32 [4096, 2], P(('dp', 'expert')), may hold values from 0.1 to 1
- cotangent: bfloat16 [4096, 2048], P(('dp', 'expert')), may hold values from -6 to 6
- w_gate: bfloat16 [4, 2048, 768], P('expert'), may hold values from -0.125 to 0.125
- w_up: bfloat16 [4, 2048, 768], P('expert'), may hold values from -0.125 to 0.125
- w_down: bfloat16 [4, 768, 2048], P('expert'), may hold values from -0.21875 to 0.21875
Outputs:
- layer_out: bfloat16 [4096, 2048], P(('dp', 'expert'))
- input_grad: bfloat16 [4096, 2048], P(('dp', 'expert'))
- grad_gate: bfloat16 [4, 2048, 768], P('expert', 'dp')
- grad_up: bfloat16 [4, 2048, 768], P('expert', 'dp')
- grad_down: bfloat16 [4, 768, 2048], P('expert', 'dp')
Inputs may be any that keep to these rules, and one draw needn't show every extreme that they name: `gen_lengths`: every device holds a sequence of exactly 16 tokens. `destination`: the sequences of one generation device go to distinct trainer ranks, and each trainer device receives exactly 8 sequences. `expert_ids`: within the rows of one device, no expert is named more than 128 times, a bound that some block reaches.
All inputs are finite; a program needn't handle non-finite values.
Results may differ from a plain program's by a relative error of at most 0.017.
Values may be sent and summed in bfloat16 or wider, within the bound.
No kernel may reach another device: no remote copies, remote signals or barrier semaphores. Data moves between devices by JAX's collectives and lax.ppermute only.
A program may use at most 128 MiB of HBM per device.

v0:
```python
import functools

import jax
import jax.numpy as jnp
from jax import lax
from jax.experimental import pallas as pl
from jax.experimental.pallas import tpu as pltpu
from jax.sharding import PartitionSpec as P

CORES = 2
LANES = 128
F32 = jnp.float32
BF16 = jnp.bfloat16
MIB = 1 << 20


def contract(left, right, left_dim, right_dim):
    return lax.dot_general(left, right, (((left_dim,), (right_dim,)), ((), ())), preferred_element_type=F32)


def params(mib, **more):
    return pltpu.CompilerParams(vmem_limit_bytes=mib * MIB, **more)


def vmem():
    return pl.BlockSpec(memory_space=pltpu.VMEM)


def smem():
    return pl.BlockSpec(memory_space=pltpu.SMEM)


def hbm():
    return pl.BlockSpec(memory_space=pl.ANY)


def pick_kernel(me_ref, dest_ref, len_ref, adv_ref, rows_ref, *outs):
    seqs, slot, width = rows_ref.shape
    lane = lax.broadcasted_iota(jnp.int32, (slot, LANES), 1)
    for i, out in enumerate(outs):
        target = me_ref[0] ^ i
        seq = jnp.int32(0)
        live = jnp.int32(0)
        for s in range(seqs):
            hit = dest_ref[s] == target
            seq = jnp.where(hit, s, seq)
            live = jnp.where(hit, 1, live)
        rows = rows_ref[pl.ds(seq, 1)][0]
        length = jnp.where(live == 1, len_ref[seq], 0.0)
        notes = jnp.where(lane == 0, length, jnp.where(lane == 1, adv_ref[seq], 0.0))
        out[:, :width] = rows
        out[:, width:] = notes.astype(BF16)


def pick(me, dest, lengths, adv, rows, n_dp):
    seqs, slot, width = rows.shape
    return pl.pallas_call(
        pick_kernel,
        out_shape=[jax.ShapeDtypeStruct((slot, width + LANES), BF16)] * n_dp,
        in_specs=[smem(), smem(), smem(), smem(), vmem()],
        out_specs=[vmem()] * n_dp,
        compiler_params=params(16),
        name="pick",
    )(me, dest, lengths, adv, rows)


def assemble_kernel(me_ref, *refs):
    pieces, (x_ref, scale_ref) = refs[:-2], refs[-2:]
    slot = pieces[0].shape[0]
    width = x_ref.shape[1]
    position = lax.broadcasted_iota(jnp.int32, (slot, 1), 0).astype(F32)
    for i, piece in enumerate(pieces):
        at = pl.multiple_of((me_ref[0] ^ i) * slot, slot)
        x_ref[pl.ds(at, slot), :] = piece[:, :width]
        notes = piece[:, width:].astype(F32)
        length, adv = notes[:, 0:1], notes[:, 1:2]
        scale_ref[pl.ds(at, slot), :] = jnp.where(position < length, adv / length, 0.0)


def assemble(me, pieces, width):
    slot = pieces[0].shape[0]
    rows = slot * len(pieces)
    return pl.pallas_call(
        assemble_kernel,
        out_shape=[jax.ShapeDtypeStruct((rows, width), BF16), jax.ShapeDtypeStruct((rows, 1), F32)],
        in_specs=[smem()] + [vmem()] * len(pieces),
        out_specs=[vmem()] * 2,
        compiler_params=params(16),
        name="assemble",
    )(me, *pieces)


def reassign(gen_rows, gen_lengths, gen_adv, destination, n_dp):
    seq_dev = destination.shape[2]
    width = gen_rows.shape[1]
    slot = gen_rows.shape[0] // seq_dev
    g = lax.axis_index("dp")
    me = g.reshape(1).astype(jnp.int32)
    pieces = pick(
        me,
        destination[0, 0],
        gen_lengths[0, 0].astype(F32),
        gen_adv[0, 0].astype(F32),
        gen_rows.reshape(seq_dev, slot, width),
        n_dp,
    )
    got = [pieces[0]]
    for i in range(1, n_dp):
        got.append(lax.ppermute(pieces[i], "dp", [(d, d ^ i) for d in range(n_dp)]))
    if n_dp == seq_dev:
        return assemble(me, got, width)
    stack = jnp.stack(got)[jnp.arange(n_dp, dtype=jnp.int32) ^ g]
    lengths = stack[:, 0, width].astype(F32)
    adv = stack[:, 0, width + 1].astype(F32)
    arrived = lengths > 0
    arrival = jnp.cumsum(arrived.astype(jnp.int32)) - 1
    chosen = arrived[None, :] & (arrival[None, :] == jnp.arange(seq_dev, dtype=jnp.int32)[:, None])
    from_peer = jnp.sum(jnp.where(chosen, jnp.arange(n_dp, dtype=jnp.int32)[None, :], 0), axis=1)
    x = stack[from_peer][:, :, :width].reshape(seq_dev * slot, width)
    position = jnp.arange(slot, dtype=jnp.int32).astype(F32)
    length = lengths[from_peer][:, None]
    scale = jnp.where(position[None, :] < length, adv[from_peer][:, None] / length, 0.0)
    return x, scale.reshape(seq_dev * slot, 1)


def swap(value, i, n_ex):
    return lax.ppermute(value, "expert", [(d, d ^ i) for d in range(n_ex)])


def gather_rows(rows, n_ex):
    if n_ex != 4:
        return [rows] + [swap(rows, i, n_ex) for i in range(1, n_ex)]
    half = rows.shape[0] // 2
    first = swap(rows, 1, n_ex)
    second = swap(rows, 2, n_ex)
    return [rows, first, second, swap(first[:half], 2, n_ex), swap(second[half:], 1, n_ex)]


def load_pieces(pieces, whole, sems):
    at, copies = 0, []
    for i, piece in enumerate(pieces):
        size = piece.shape[0]
        copies.append(pltpu.make_async_copy(piece, whole.at[pl.ds(at, size)], sems.at[i]))
        at += size
    for copy in copies:
        copy.start()
    for copy in copies:
        copy.wait()


def hidden_grad_kernel(count, w_ref, *refs):
    pieces, (out, whole_out, whole, sems, out_sem) = refs[:count], refs[count:]
    step = pl.program_id(0)

    @pl.when(step == 0)
    def _():
        load_pieces(pieces, whole, sems)
        pltpu.make_async_copy(whole, whole_out, out_sem).start()

    out[...] = contract(whole[...], w_ref[...], 1, 1)

    @pl.when(step == pl.num_programs(0) - 1)
    def _():
        pltpu.make_async_copy(whole, whole_out, out_sem).wait()


def hidden_grad(pieces, w_down):
    rows = sum(p.shape[0] for p in pieces)
    units, width = w_down.shape
    tile = 256
    return pl.pallas_call(
        functools.partial(hidden_grad_kernel, len(pieces)),
        grid=(units // tile,),
        out_shape=[jax.ShapeDtypeStruct((rows, units), F32), jax.ShapeDtypeStruct((rows, width), BF16)],
        in_specs=[pl.BlockSpec((tile, width), lambda j: (j, 0))] + [hbm()] * len(pieces),
        out_specs=[pl.BlockSpec((rows, tile), lambda j: (0, j)), hbm()],
        scratch_shapes=[
            pltpu.VMEM((rows, width), BF16),
            pltpu.SemaphoreType.DMA((len(pieces),)),
            pltpu.SemaphoreType.DMA,
        ],
        compiler_params=params(32),
        cost_estimate=pl.CostEstimate(
            flops=2 * rows * units * width, bytes_accessed=2 * units * width + 4 * rows * width, transcendentals=0
        ),
        name="hidden_grad",
    )(w_down, *pieces)


def units_kernel(count, wg_ref, wu_ref, hg_ref, gs_ref, *refs):
    pieces, (gate_out, up_out, hid_out, hs_out, whole_out, whole, sems, out_sem) = refs[:count], refs[count:]
    step = pl.program_id(0)

    @pl.when(step == 0)
    def _():
        load_pieces(pieces, whole, sems)
        pltpu.make_async_copy(whole, whole_out, out_sem).start()

    x = whole[...]
    gate = jnp.dot(x, wg_ref[...], preferred_element_type=F32)
    up = jnp.dot(x, wu_ref[...], preferred_element_type=F32)
    gs = gs_ref[...]
    sig = jax.nn.sigmoid(gate)
    act = gate * sig
    hid = (act * up).astype(BF16)
    hid_out[...] = hid
    hs_out[...] = (hid.astype(F32) * gs).astype(BF16)
    hg = hg_ref[...] * gs
    gate_out[...] = (hg * up * sig * (1.0 + gate * (1.0 - sig))).astype(BF16)
    up_out[...] = (hg * act).astype(BF16)

    @pl.when(step == pl.num_programs(0) - 1)
    def _():
        pltpu.make_async_copy(whole, whole_out, out_sem).wait()


def hidden_units(pieces, w_gate, w_up, hg, gs):
    rows, units = hg.shape
    width = w_gate.shape[0]
    tile = 256
    columns = pl.BlockSpec((rows, tile), lambda j: (0, j))
    weights = pl.BlockSpec((width, tile), lambda j: (0, j))
    return pl.pallas_call(
        functools.partial(units_kernel, len(pieces)),
        grid=(units // tile,),
        out_shape=[jax.ShapeDtypeStruct((rows, units), BF16)] * 4 + [jax.ShapeDtypeStruct((rows, width), BF16)],
        in_specs=[weights, weights, columns, pl.BlockSpec((rows, 1), lambda j: (0, 0))] + [hbm()] * len(pieces),
        out_specs=[columns] * 4 + [hbm()],
        scratch_shapes=[
            pltpu.VMEM((rows, width), BF16),
            pltpu.SemaphoreType.DMA((len(pieces),)),
            pltpu.SemaphoreType.DMA,
        ],
        compiler_params=params(44),
        cost_estimate=pl.CostEstimate(
            flops=4 * rows * units * width, bytes_accessed=4 * units * width + 4 * rows * width, transcendentals=rows * units
        ),
        name="hidden_units",
    )(w_gate, w_up, hg, gs, *pieces)


def column_grad_kernel(core_ref, x_ref, grad_ref, other, mine):
    value = contract(x_ref[...], grad_ref[...], 0, 0).astype(BF16)

    @pl.when(pl.program_id(0) == 0)
    def _():
        other[0] = value

    @pl.when(pl.program_id(0) == 1)
    def _():
        mine[0] = value


def column_grad(core, x, grad, n_dp):
    rows, width = x.shape
    units = grad.shape[1]
    n_z, shard = n_dp // CORES, width // n_dp
    out = jax.ShapeDtypeStruct((n_z, shard, units), BF16)
    return pl.pallas_call(
        column_grad_kernel,
        grid_spec=pltpu.PrefetchScalarGridSpec(
            num_scalar_prefetch=1,
            grid=(CORES, n_z),
            in_specs=[
                pl.BlockSpec((rows, shard), lambda k, z, core: (0, CORES * z + jnp.where(k == 0, 1 - core[0], core[0]))),
                pl.BlockSpec((rows, units), lambda k, z, core: (0, 0)),
            ],
            out_specs=[
                pl.BlockSpec((1, shard, units), lambda k, z, core: (jnp.where(k == 0, z, n_z - 1), 0, 0)),
                pl.BlockSpec((1, shard, units), lambda k, z, core: (jnp.where(k == 0, 0, z), 0, 0)),
            ],
        ),
        out_shape=[out, out],
        compiler_params=params(24),
        cost_estimate=pl.CostEstimate(
            flops=2 * rows * units * width, bytes_accessed=2 * units * width + 2 * rows * width, transcendentals=0
        ),
        name="column_grad",
    )(core, x, grad)


def row_grad_kernel(core_ref, hid_ref, dy_ref, other, mine):
    value = contract(hid_ref[...], dy_ref[...], 0, 0).astype(BF16)
    n_z, shard, _ = mine.shape

    for z in range(n_z):
        low = value[CORES * z * shard : (CORES * z + 1) * shard]
        high = value[(CORES * z + 1) * shard : (CORES * z + 2) * shard]

        @pl.when(core_ref[0] == 0)
        def _(low=low, high=high, z=z):
            mine[z] = low
            other[z] = high

        @pl.when(core_ref[0] == 1)
        def _(low=low, high=high, z=z):
            mine[z] = high
            other[z] = low


def row_grad(core, hid, dy, n_dp):
    rows, units = hid.shape
    width = dy.shape[1]
    n_z, shard = n_dp // CORES, units // n_dp
    tile = 512
    out = jax.ShapeDtypeStruct((n_z, shard, width), BF16)
    block = pl.BlockSpec((n_z, shard, tile), lambda j, core: (0, 0, j))
    return pl.pallas_call(
        row_grad_kernel,
        grid_spec=pltpu.PrefetchScalarGridSpec(
            num_scalar_prefetch=1,
            grid=(width // tile,),
            in_specs=[
                pl.BlockSpec((rows, units), lambda j, core: (0, 0)),
                pl.BlockSpec((rows, tile), lambda j, core: (0, j)),
            ],
            out_specs=[block, block],
        ),
        out_shape=[out, out],
        compiler_params=params(32),
        cost_estimate=pl.CostEstimate(
            flops=2 * rows * units * width, bytes_accessed=2 * units * width + 2 * rows * width, transcendentals=0
        ),
        name="row_grad",
    )(core, hid, dy)


def outputs_kernel(n_ex, hid_ref, w_ref, *outs):
    value = jnp.dot(hid_ref[...], w_ref[...], preferred_element_type=F32).astype(BF16)
    size = outs[0].shape[0]
    for i in range(n_ex):
        outs[i][...] = value[i * size : (i + 1) * size]


def layer_outputs(hid, w_down, n_ex):
    rows, units = hid.shape
    width = w_down.shape[1]
    tile = 512
    size = rows // n_ex
    return pl.pallas_call(
        functools.partial(outputs_kernel, n_ex),
        grid=(width // tile,),
        out_shape=[jax.ShapeDtypeStruct((size, width), BF16)] * n_ex,
        in_specs=[pl.BlockSpec((rows, units), lambda j: (0, 0)), pl.BlockSpec((units, tile), lambda j: (0, j))],
        out_specs=[pl.BlockSpec((size, tile), lambda j: (0, j))] * n_ex,
        compiler_params=params(32),
        cost_estimate=pl.CostEstimate(
            flops=2 * rows * units * width, bytes_accessed=2 * units * width + 2 * rows * width, transcendentals=0
        ),
        name="layer_outputs",
    )(hid, w_down)


def input_grads_kernel(n_ex, gate_ref, up_ref, wg_ref, wu_ref, *outs):
    value = contract(gate_ref[...], wg_ref[...], 1, 1) + contract(up_ref[...], wu_ref[...], 1, 1)
    value = value.astype(BF16)
    size = outs[0].shape[0]
    for i in range(n_ex):
        outs[i][...] = value[i * size : (i + 1) * size]


def input_grads(gate_grad, up_grad, w_gate, w_up, n_ex):
    rows, units = gate_grad.shape
    width = w_gate.shape[0]
    tile = 512
    size = rows // n_ex
    whole = pl.BlockSpec((rows, units), lambda j: (0, 0))
    weights = pl.BlockSpec((tile, units), lambda j: (j, 0))
    return pl.pallas_call(
        functools.partial(input_grads_kernel, n_ex),
        grid=(width // tile,),
        out_shape=[jax.ShapeDtypeStruct((size, width), BF16)] * n_ex,
        in_specs=[whole, whole, weights, weights],
        out_specs=[pl.BlockSpec((size, tile), lambda j: (0, j))] * n_ex,
        compiler_params=params(40),
        cost_estimate=pl.CostEstimate(
            flops=4 * rows * units * width, bytes_accessed=4 * units * width + 2 * rows * width, transcendentals=0
        ),
        name="input_grads",
    )(gate_grad, up_grad, w_gate, w_up)


def take(parts, at):
    total = None
    for part in parts:
        value = lax.dynamic_index_in_dim(part, at, 0, keepdims=False).astype(F32)
        total = value if total is None else total + value
    return total


def line_steps(all_parts, n_dp):
    n_z = n_dp // CORES
    z = lax.axis_index("dp") // CORES
    right = [None] * len(all_parts)
    left = [None] * len(all_parts)
    for s in range(1, n_z):
        to_right = [(CORES * k + c, CORES * (k + 1) + c) for k in range(s) for c in range(CORES)]
        to_left = [(CORES * (n_z - 1 - k) + c, CORES * (n_z - 2 - k) + c) for k in range(s) for c in range(CORES)]
        for p, parts in enumerate(all_parts):
            up = take(parts, jnp.minimum(n_z - s + z, n_z - 1))
            down = take(parts, jnp.maximum(s + z - n_z, 0))
            if s > 1:
                up = up + right[p].astype(F32)
                down = down + left[p].astype(F32)
            right[p] = lax.ppermute(up.astype(BF16), "dp", to_right)
            left[p] = lax.ppermute(down.astype(BF16), "dp", to_left)
    out = []
    for p, parts in enumerate(all_parts):
        total = take(parts, z)
        if n_z > 1:
            total = total + right[p].astype(F32) + left[p].astype(F32)
        out.append(total.astype(BF16))
    return out


def on_device(
    gen_rows, gen_lengths, gen_adv, destination, expert_ids, gate_values, cotangent, w_gate, w_up, w_down
):
    n_dp = lax.axis_size("dp")
    n_ex = lax.axis_size("expert")
    weight_gate, weight_up, weight_down = w_gate[0], w_up[0], w_down[0]
    g, e = lax.axis_index("dp"), lax.axis_index("expert")
    core = (g % CORES).reshape(1).astype(jnp.int32)
    other_core = [(d, d ^ 1) for d in range(n_dp)]

    cot_pieces = gather_rows(cotangent, n_ex)
    x, scale = reassign(gen_rows, gen_lengths, gen_adv, destination, n_dp)
    x_pieces = gather_rows(x, n_ex)

    gates = [
        jnp.sum(jnp.where(expert_ids == (e ^ i), gate_values, 0.0), axis=1, keepdims=True) for i in range(n_ex)
    ]
    gs = [gates[0] * scale] + [swap(gates[i] * scale, i, n_ex) for i in range(1, n_ex)]
    gs = jnp.concatenate(gs, axis=0)

    hg, dy_all = hidden_grad(cot_pieces, weight_down)
    gate_grad, up_grad, hid, hid_scaled, x_all = hidden_units(x_pieces, weight_gate, weight_up, hg, gs)

    gate_other, gate_mine = column_grad(core, x_all, gate_grad, n_dp)
    gate_got = lax.ppermute(gate_other, "dp", other_core)
    up_other, up_mine = column_grad(core, x_all, up_grad, n_dp)
    up_got = lax.ppermute(up_other, "dp", other_core)
    down_other, down_mine = row_grad(core, hid_scaled, dy_all, n_dp)
    down_got = lax.ppermute(down_other, "dp", other_core)

    outs = layer_outputs(hid, weight_down, n_ex)
    outs = [outs[0]] + [swap(outs[i], i, n_ex) for i in range(1, n_ex)]
    grads = input_grads(gate_grad, up_grad, weight_gate, weight_up, n_ex)
    grads = [grads[0]] + [swap(grads[i], i, n_ex) for i in range(1, n_ex)]

    sums = line_steps([(gate_mine, gate_got), (up_mine, up_got), (down_mine, down_got)], n_dp)
    layer_out = sum(gates[i] * outs[i].astype(F32) for i in range(n_ex)).astype(BF16)
    input_grad = sum(part.astype(F32) for part in grads).astype(BF16)
    return layer_out, input_grad, sums[0][None], sums[1][None], sums[2][None]


def solution(mesh):
    rows = P(("dp", "expert"), None)
    seqs = P("dp", "expert", None)
    weights = P("expert", None, None)
    shards = P("expert", "dp", None)
    return jax.shard_map(
        on_device,
        mesh=mesh,
        in_specs=(rows, seqs, seqs, seqs, rows, rows, rows, weights, weights, weights),
        out_specs=(rows, rows, shards, shards, shards),
        check_vma=False,
    )
```

profile of v0, /device:TPU:12, one launch (start us, length us, event | category | flops | bytes accessed | tf_op | source)
XLA Modules:
  0.0 209.5 jit_solution(5407564876612929849)
XLA Ops:
  8.1 2.5 %collective-permute-start.5 = (bf16[16,2176]{1,0:T(8,128)(2,1)S(1)}, bf16[16,2176]{1,0:T(8,128)(2,1)S(1)}, u32[]{:S(2)}, u32[]{:S(2)}) collective-permute-start(bf16[16,2176]{1,0:T(8,128)(2,1)S(1)} %get-tuple-element.39), channel_id=1, source_target_pairs={{0,8},{4,12},{8,0},{12,4},{16,24},{20,28},{24,16},{28,20},{1,9},{5... | collective-permute-start | bytes 208904 | tf_op jit(solution)/shard_map/ppermute | solution.py:109
  12.9 2.2 %collective-permute-start.7 = (bf16[16,2176]{1,0:T(8,128)(2,1)S(1)}, bf16[16,2176]{1,0:T(8,128)(2,1)S(1)}, u32[]{:S(2)}, u32[]{:S(2)}) collective-permute-start(bf16[16,2176]{1,0:T(8,128)(2,1)S(1)} %get-tuple-element.41), channel_id=1, source_target_pairs={{0,16},{4,20},{8,24},{12,28},{16,0},{20,4},{24,8},{28,12},{1,17},{... | collective-permute-start | bytes 208904 | tf_op jit(solution)/shard_map/ppermute | solution.py:109
  18.0 2.4 %collective-permute-done.7.refs_4_ = bf16[16,2176]{1,0:T(8,128)(2,1)S(1)} collective-permute-done((bf16[16,2176]{1,0:T(8,128)(2,1)S(1)}, bf16[16,2176]{1,0:T(8,128)(2,1)S(1)}, u32[]{:S(2)}, u32[]{:S(2)}) %collective-permute-start.7) | collective-permute-done | bytes 69664 | tf_op jit(solution)/shard_map/ppermute | solution.py:109
  20.4 2.1 %collective-permute-done.8.refs_5_ = bf16[16,2176]{1,0:T(8,128)(2,1)S(1)} collective-permute-done((bf16[16,2176]{1,0:T(8,128)(2,1)S(1)}, bf16[16,2176]{1,0:T(8,128)(2,1)S(1)}, u32[]{:S(2)}, u32[]{:S(2)}) %collective-permute-start.8) | collective-permute-done | bytes 69664 | tf_op jit(solution)/shard_map/ppermute | solution.py:109
  22.5 3.0 %collective-permute-done.9.refs_6_ = bf16[16,2176]{1,0:T(8,128)(2,1)S(1)} collective-permute-done((bf16[16,2176]{1,0:T(8,128)(2,1)S(1)}, bf16[16,2176]{1,0:T(8,128)(2,1)S(1)}, u32[]{:S(2)}, u32[]{:S(2)}) %collective-permute-start.9) | collective-permute-done | bytes 69664 | tf_op jit(solution)/shard_map/ppermute | solution.py:109
  25.8 2.0 collective-permute-start.15
  32.4 1.9 collective-permute-start.3
  36.0 4.6 %collective-permute-done.14.refs_1_ = bf16[128,2048]{1,0:T(8,128)(2,1)S(1)} collective-permute-done((bf16[128,2048]{1,0:T(8,128)(2,1)S(1)}, bf16[128,2048]{1,0:T(8,128)(2,1)S(1)}, u32[]{:S(2)}, u32[]{:S(2)}) %collective-permute-start.14) | collective-permute-done | bytes 524320 | tf_op jit(solution)/shard_map/ppermute | solution.py:127
  43.6 3.5 %collective-permute-done.11 = f32[128,1]{1,0:T(8,128)S(1)} collective-permute-done((f32[128,1]{1,0:T(8,128)}, f32[128,1]{1,0:T(8,128)S(1)}, u32[]{:S(2)}, u32[]{:S(2)}) %collective-permute-start.11) | collective-permute-done | bytes 544 | tf_op jit(solution)/shard_map/ppermute | solution.py:127
  52.5 3.6 %hidden_grad.1 = (f32[512,768]{1,0:T(8,128)S(1)}, bf16[512,2048]{1,0:T(8,128)(2,1)S(1)}) custom-call(bf16[768,2048]{1,0:T(8,128)(2,1)S(1)} %bitcast.108, bf16[128,2048]{1,0:T(8,128)(2,1)S(1)} %copy-done.8, bf16[128,2048]{1,0:T(8,128)(2,1)S(1)} %collective-permute-done.refs_1_, bf16[128,2048]{1,0:T(8,128)(2,1)S(1)} %collective-permute-done.1.refs_2_, ...), custom_call_target="tpu_custom_call" | custom-call | flops 1610612736 | bytes 7340032 | tf_op jit(solution)/shard_map/hidden_grad/pallas_call | solution.py:171
  56.2 6.5 %hidden_units.1 = (bf16[512,768]{1,0:T(8,128)(2,1)S(1)}, bf16[512,768]{1,0:T(8,128)(2,1)S(1)}, bf16[512,768]{1,0:T(8,128)(2,1)S(1)}, bf16[512,768]{1,0:T(8,128)(2,1)S(1)}, bf16[512,2048]{1,0:T(8,128)(2,1)S(1)}) custom-call(bf16[2048,768]{1,0:T(8,128)(2,1)} %bitcast.110, bf16[2048,768]{1,0:T(8,128)(2,1)} %bitcast.112, ...), custom_call_target="tpu_custom_call" | custom-call | flops 3221225472 | bytes 10485760 | tf_op jit(solution)/shard_map/hidden_units/pallas_call | solution.py:223
  62.8 4.0 %row_grad.1 = (bf16[4,96,2048]{2,1,0:T(8,128)(2,1)}, bf16[4,96,2048]{2,1,0:T(8,128)(2,1)S(1)}) custom-call(s32[1]{0:T(128)} %bitcast.12.core_ref, bf16[512,768]{1,0:T(8,128)(2,1)S(1)} %get-tuple-element.63.hid_ref, bf16[512,2048]{1,0:T(8,128)(2,1)S(1)} %get-tuple-element.64.dy_ref), custom_call_target="tpu_custom_call" | custom-call | flops 1610612736 | bytes 5242880 | tf_op jit(solution)/shard_map/row_grad/pallas_call | solution.py:308
  66.8 3.5 %layer_outputs.1 = (bf16[128,2048]{1,0:T(8,128)(2,1)S(1)}, bf16[128,2048]{1,0:T(8,128)(2,1)}, bf16[128,2048]{1,0:T(8,128)(2,1)}, bf16[128,2048]{1,0:T(8,128)(2,1)}) custom-call(bf16[512,768]{1,0:T(8,128)(2,1)S(1)} %get-tuple-element.47.hid_ref, bf16[768,2048]{1,0:T(8,128)(2,1)S(1)} %bitcast.109), custom_call_target="tpu_custom_call" | custom-call | flops 1610612736 | bytes 5242880 | tf_op jit(solution)/shard_map/layer_outputs/pallas_call | solution.py:340
  71.2 5.3 %column_grad.3 = (bf16[4,256,768]{2,1,0:T(8,128)(2,1)}, bf16[4,256,768]{2,1,0:T(8,128)(2,1)S(1)}) custom-call(s32[1]{0:T(128)} %bitcast.12.core_ref, bf16[512,2048]{1,0:T(8,128)(2,1)S(1)} %get-tuple-element.58.x_ref, bf16[512,768]{1,0:T(8,128)(2,1)S(1)} %get-tuple-element.53.up_ref.grad_ref), custom_call_target="tpu_custom_call" | custom-call | flops 1610612736 | bytes 5242880 | tf_op jit(solution)/shard_map/column_grad/pallas_call | solution.py:259
  82.3 4.0 %column_grad.2 = (bf16[4,256,768]{2,1,0:T(8,128)(2,1)S(1)}, bf16[4,256,768]{2,1,0:T(8,128)(2,1)S(1)}) custom-call(s32[1]{0:T(128)} %bitcast.12.core_ref, bf16[512,2048]{1,0:T(8,128)(2,1)S(1)} %copy-done.10, bf16[512,768]{1,0:T(8,128)(2,1)S(1)} %copy-done.12), custom_call_target="tpu_custom_call" | custom-call | flops 1610612736 | bytes 5242880 | tf_op jit(solution)/shard_map/column_grad/pallas_call | solution.py:259
  88.4 4.2 %input_grads.1 = (bf16[128,2048]{1,0:T(8,128)(2,1)S(1)}, bf16[128,2048]{1,0:T(8,128)(2,1)S(1)}, bf16[128,2048]{1,0:T(8,128)(2,1)S(1)}, bf16[128,2048]{1,0:T(8,128)(2,1)S(1)}) custom-call(bf16[512,768]{1,0:T(8,128)(2,1)S(1)} %copy-done.13, bf16[512,768]{1,0:T(8,128)(2,1)S(1)} %copy-done.15, bf16[2048,768]{1,0:T(8,128)(2,1)S(1)} %bitcast.111, ...), custom_call_target="tpu_custom_call" | custom-call | flops 3221225472 | bytes 8388608 | tf_op jit(solution)/shard_map/input_grads/pallas_call | solution.py:369
  92.6 9.9 %collective-permute-done.19 = bf16[128,2048]{1,0:T(8,128)(2,1)} collective-permute-done((bf16[128,2048]{1,0:T(8,128)(2,1)}, bf16[128,2048]{1,0:T(8,128)(2,1)}, u32[]{:S(2)}, u32[]{:S(2)}) %collective-permute-start.19) | collective-permute-done | bytes 524320 | tf_op jit(solution)/shard_map/ppermute | solution.py:127
  105.9 2.6 %add_convert_fusion.1 = bf16[128,2048]{1,0:T(8,128)(2,1)} fusion(bf16[128,2048]{1,0:T(8,128)(2,1)} %collective-permute-done.20, bf16[128,2048]{1,0:T(8,128)(2,1)} %collective-permute-done.19, bf16[128,2048]{1,0:T(8,128)(2,1)} %collective-permute-done.18, bf16[128,2048]{1,0:T(8,128)(2,1)S(1)} %copy-done.2, f32[128]{0:T(128)S(1)} %get-tuple-element.69, ...), kind=kLoop, calls=%fused_computation.1 | loop fusion | flops 3145728 | bytes 2623488 | tf_op jit(solution)/shard_map/convert_element_type | solution.py:452
  112.6 4.7 %collective-permute-done.21 = bf16[128,2048]{1,0:T(8,128)(2,1)S(1)} collective-permute-done((bf16[128,2048]{1,0:T(8,128)(2,1)S(1)}, bf16[128,2048]{1,0:T(8,128)(2,1)S(1)}, u32[]{:S(2)}, u32[]{:S(2)}) %collective-permute-start.21) | collective-permute-done | bytes 524320 | tf_op jit(solution)/shard_map/ppermute | solution.py:127
  118.6 10.1 %collective-permute-done.22 = bf16[128,2048]{1,0:T(8,128)(2,1)S(1)} collective-permute-done((bf16[128,2048]{1,0:T(8,128)(2,1)S(1)}, bf16[128,2048]{1,0:T(8,128)(2,1)S(1)}, u32[]{:S(2)}, u32[]{:S(2)}) %collective-permute-start.22) | collective-permute-done | bytes 524320 | tf_op jit(solution)/shard_map/ppermute | solution.py:127
  134.5 4.4 %collective-permute-start.33 = (bf16[256,768]{1,0:T(8,128)(2,1)S(1)}, bf16[256,768]{1,0:T(8,128)(2,1)S(1)}, u32[]{:S(2)}, u32[]{:S(2)}) collective-permute-start(bf16[256,768]{1,0:T(8,128)(2,1)S(1)} %fusion.8), channel_id=1, source_target_pairs={{0,8},{4,12},{8,16},{12,20},{1,9},{5,13},{9,17},{13,21},{2,10},{6,... | collective-permute-start | bytes 1179656 | tf_op jit(solution)/shard_map/ppermute | solution.py:405
  140.1 5.3 %collective-permute-done.25 = bf16[256,768]{1,0:T(8,128)(2,1)S(1)} collective-permute-done((bf16[256,768]{1,0:T(8,128)(2,1)S(1)}, bf16[256,768]{1,0:T(8,128)(2,1)S(1)}, u32[]{:S(2)}, u32[]{:S(2)}) %collective-permute-start.25) | collective-permute-done | bytes 393248 | tf_op jit(solution)/shard_map/ppermute | solution.py:405
  147.4 7.9 %collective-permute-start.26 = (bf16[256,768]{1,0:T(8,128)(2,1)S(1)}, bf16[256,768]{1,0:T(8,128)(2,1)S(1)}, u32[]{:S(2)}, u32[]{:S(2)}) collective-permute-start(bf16[256,768]{1,0:T(8,128)(2,1)S(1)} %fusion.14), channel_id=1, source_target_pairs={{0,8},{4,12},{8,16},{12,20},{1,9},{5,13},{9,17},{13,21},{2,10},{6,... | collective-permute-start | bytes 1179656 | tf_op jit(solution)/shard_map/ppermute | solution.py:405
  158.0 4.1 %collective-permute-done.40 = bf16[96,2048]{1,0:T(8,128)(2,1)S(1)} collective-permute-done((bf16[96,2048]{1,0:T(8,128)(2,1)S(1)}, bf16[96,2048]{1,0:T(8,128)(2,1)S(1)}, u32[]{:S(2)}, u32[]{:S(2)}) %collective-permute-start.40) | collective-permute-done | bytes 393248 | tf_op jit(solution)/shard_map/ppermute | solution.py:405
  165.0 4.6 %collective-permute-start.41 = (bf16[96,2048]{1,0:T(8,128)(2,1)S(1)}, bf16[96,2048]{1,0:T(8,128)(2,1)S(1)}, u32[]{:S(2)}, u32[]{:S(2)}) collective-permute-start(bf16[96,2048]{1,0:T(8,128)(2,1)S(1)} %get-tuple-element.71), channel_id=1, source_target_pairs={{0,8},{4,12},{8,16},{12,20},{16,24},{20,28},{1,9},{5,13},{9,17},{1... | collective-permute-start | bytes 1179656 | tf_op jit(solution)/shard_map/ppermute | solution.py:405
  173.1 4.6 %collective-permute-start.27 = (bf16[256,768]{1,0:T(8,128)(2,1)S(1)}, bf16[256,768]{1,0:T(8,128)(2,1)S(1)}, u32[]{:S(2)}, u32[]{:S(2)}) collective-permute-start(bf16[256,768]{1,0:T(8,128)(2,1)S(1)} %get-tuple-element.79), channel_id=1, source_target_pairs={{0,8},{4,12},{8,16},{12,20},{16,24},{20,28},{1,9},{5,13},{9,17},{1... | collective-permute-start | bytes 1179656 | tf_op jit(solution)/shard_map/ppermute | solution.py:405
  181.9 5.0 %collective-permute-done.29 = bf16[256,768]{1,0:T(8,128)(2,1)S(1)} collective-permute-done((bf16[256,768]{1,0:T(8,128)(2,1)S(1)}, bf16[256,768]{1,0:T(8,128)(2,1)S(1)}, u32[]{:S(2)}, u32[]{:S(2)}) %collective-permute-start.29) | collective-permute-done | bytes 393248 | tf_op jit(solution)/shard_map/ppermute | solution.py:406
  190.9 4.4 %collective-permute-done.37 = bf16[256,768]{1,0:T(8,128)(2,1)S(1)} collective-permute-done((bf16[256,768]{1,0:T(8,128)(2,1)S(1)}, bf16[256,768]{1,0:T(8,128)(2,1)S(1)}, u32[]{:S(2)}, u32[]{:S(2)}) %collective-permute-start.37) | collective-permute-done | bytes 393248 | tf_op jit(solution)/shard_map/ppermute | solution.py:406
  195.3 1.9 fusion.25
  197.2 6.5 %collective-permute-done.44 = bf16[96,2048]{1,0:T(8,128)(2,1)S(1)} collective-permute-done((bf16[96,2048]{1,0:T(8,128)(2,1)S(1)}, bf16[96,2048]{1,0:T(8,128)(2,1)S(1)}, u32[]{:S(2)}, u32[]{:S(2)}) %collective-permute-start.44) | collective-permute-done | bytes 393248 | tf_op jit(solution)/shard_map/ppermute | solution.py:406
  203.7 2.0 fusion.26
  205.7 2.8 %collective-permute-done.30 = bf16[256,768]{1,0:T(8,128)(2,1)S(1)} collective-permute-done((bf16[256,768]{1,0:T(8,128)(2,1)S(1)}, bf16[256,768]{1,0:T(8,128)(2,1)S(1)}, u32[]{:S(2)}, u32[]{:S(2)}) %collective-permute-start.30) | collective-permute-done | bytes 393248 | tf_op jit(solution)/shard_map/ppermute | solution.py:406
  (129 shorter events, 72.3 us)
Async XLA Ops:
  0.6 30.2 %collective-permute-start = (bf16[128,2048]{1,0:T(8,128)(2,1)}, bf16[128,2048]{1,0:T(8,128)(2,1)S(1)}, u32[]{:S(2)}, u32[]{:S(2)}) collective-permute-start(bf16[128,2048]{1,0:T(8,128)(2,1)} %refs_0_.1), channel_id=1, source_target_pairs={{0,1},{1,0},{2,3},{3,2},{4,5},{5,4},{6,7},{7,6},{8,9},{9,8},{10,11... | collective-permute-start | bytes 1572872 | tf_op jit(solution)/shard_map/ppermute | solution.py:127
  2.2 29.5 %collective-permute-start.1 = (bf16[128,2048]{1,0:T(8,128)(2,1)}, bf16[128,2048]{1,0:T(8,128)(2,1)S(1)}, u32[]{:S(2)}, u32[]{:S(2)}) collective-permute-start(bf16[128,2048]{1,0:T(8,128)(2,1)} %refs_0_.1), channel_id=1, source_target_pairs={{0,2},{1,3},{2,0},{3,1},{4,6},{5,7},{6,4},{7,5},{8,10},{9,11},{10,... | collective-permute-start | bytes 1572872 | tf_op jit(solution)/shard_map/ppermute | solution.py:127
  25.7 14.9 %collective-permute-start.14 = (bf16[128,2048]{1,0:T(8,128)(2,1)S(1)}, bf16[128,2048]{1,0:T(8,128)(2,1)S(1)}, u32[]{:S(2)}, u32[]{:S(2)}) collective-permute-start(bf16[128,2048]{1,0:T(8,128)(2,1)S(1)} %get-tuple-element.46.refs_0_), channel_id=1, source_target_pairs={{0,1},{1,0},{2,3},{3,2},{4,5},{5,4},{6,7},{7,6},{8,9},{9,8},{10,11... | collective-permute-start | bytes 1572872 | tf_op jit(solution)/shard_map/ppermute | solution.py:127
  25.8 16.3 %collective-permute-start.15 = (bf16[128,2048]{1,0:T(8,128)(2,1)S(1)}, bf16[128,2048]{1,0:T(8,128)(2,1)S(1)}, u32[]{:S(2)}, u32[]{:S(2)}) collective-permute-start(bf16[128,2048]{1,0:T(8,128)(2,1)S(1)} %get-tuple-element.46.refs_0_), channel_id=1, source_target_pairs={{0,2},{1,3},{2,0},{3,1},{4,6},{5,7},{6,4},{7,5},{8,10},{9,11},{10,... | collective-permute-start | bytes 1572872 | tf_op jit(solution)/shard_map/ppermute | solution.py:127
  31.6 19.0 %collective-permute-start.2 = (bf16[64,2048]{1,0:T(8,128)(2,1)}, bf16[64,2048]{1,0:T(8,128)(2,1)S(1)}, u32[]{:S(2)}, u32[]{:S(2)}) collective-permute-start(bf16[64,2048]{1,0:T(8,128)(2,1)} %slice.16), channel_id=1, source_target_pairs={{0,2},{1,3},{2,0},{3,1},{4,6},{5,7},{6,4},{7,5},{8,10},{9,11},{10,... | collective-permute-start | bytes 786440 | tf_op jit(solution)/shard_map/ppermute | solution.py:127
  32.4 18.3 %collective-permute-start.3 = (bf16[64,2048]{1,0:T(8,128)(2,1)}, bf16[64,2048]{1,0:T(8,128)(2,1)}, u32[]{:S(2)}, u32[]{:S(2)}) collective-permute-start(bf16[64,2048]{1,0:T(8,128)(2,1)} %slice.17), channel_id=1, source_target_pairs={{0,1},{1,0},{2,3},{3,2},{4,5},{5,4},{6,7},{7,6},{8,9},{9,8},{10,11... | collective-permute-start | bytes 786440 | tf_op jit(solution)/shard_map/ppermute | solution.py:127
  66.8 39.0 %collective-permute-start.38 = (bf16[4,96,2048]{2,1,0:T(8,128)(2,1)}, bf16[4,96,2048]{2,1,0:T(8,128)(2,1)}, u32[]{:S(2)}, u32[]{:S(2)}) collective-permute-start(bf16[4,96,2048]{2,1,0:T(8,128)(2,1)} %get-tuple-element.66), channel_id=1, source_target_pairs={{0,4},{4,0},{8,12},{12,8},{16,20},{20,16},{24,28},{28,24},{1,5},{5... | collective-permute-start | bytes 4718600 | tf_op jit(solution)/shard_map/ppermute | solution.py:444
  70.3 16.0 %collective-permute-start.18 = (bf16[128,2048]{1,0:T(8,128)(2,1)}, bf16[128,2048]{1,0:T(8,128)(2,1)}, u32[]{:S(2)}, u32[]{:S(2)}) collective-permute-start(bf16[128,2048]{1,0:T(8,128)(2,1)} %get-tuple-element.49), channel_id=1, source_target_pairs={{0,1},{1,0},{2,3},{3,2},{4,5},{5,4},{6,7},{7,6},{8,9},{9,8},{10,11... | collective-permute-start | bytes 1572872 | tf_op jit(solution)/shard_map/ppermute | solution.py:127
  76.6 33.4 %collective-permute-start.31 = (bf16[4,256,768]{2,1,0:T(8,128)(2,1)}, bf16[4,256,768]{2,1,0:T(8,128)(2,1)}, u32[]{:S(2)}, u32[]{:S(2)}) collective-permute-start(bf16[4,256,768]{2,1,0:T(8,128)(2,1)} %get-tuple-element.62), channel_id=1, source_target_pairs={{0,4},{4,0},{8,12},{12,8},{16,20},{20,16},{24,28},{28,24},{1,5},{5... | collective-permute-start | bytes 4718600 | tf_op jit(solution)/shard_map/ppermute | solution.py:442
  76.8 25.7 %collective-permute-start.19 = (bf16[128,2048]{1,0:T(8,128)(2,1)}, bf16[128,2048]{1,0:T(8,128)(2,1)}, u32[]{:S(2)}, u32[]{:S(2)}) collective-permute-start(bf16[128,2048]{1,0:T(8,128)(2,1)} %get-tuple-element.50), channel_id=1, source_target_pairs={{0,2},{1,3},{2,0},{3,1},{4,6},{5,7},{6,4},{7,5},{8,10},{9,11},{10,... | collective-permute-start | bytes 1572872 | tf_op jit(solution)/shard_map/ppermute | solution.py:127
  78.4 25.7 %collective-permute-start.20 = (bf16[128,2048]{1,0:T(8,128)(2,1)}, bf16[128,2048]{1,0:T(8,128)(2,1)}, u32[]{:S(2)}, u32[]{:S(2)}) collective-permute-start(bf16[128,2048]{1,0:T(8,128)(2,1)} %get-tuple-element.51), channel_id=1, source_target_pairs={{0,3},{1,2},{2,1},{3,0},{4,7},{5,6},{6,5},{7,4},{8,11},{9,10},{10,... | collective-permute-start | bytes 1572872 | tf_op jit(solution)/shard_map/ppermute | solution.py:127
  86.3 44.8 %collective-permute-start.24 = (bf16[4,256,768]{2,1,0:T(8,128)(2,1)S(1)}, bf16[4,256,768]{2,1,0:T(8,128)(2,1)S(1)}, u32[]{:S(2)}, u32[]{:S(2)}) collective-permute-start(bf16[4,256,768]{2,1,0:T(8,128)(2,1)S(1)} %get-tuple-element.60), channel_id=1, source_target_pairs={{0,4},{4,0},{8,12},{12,8},{16,20},{20,16},{24,28},{28,24},{1,5},{5... | collective-permute-start | bytes 4718600 | tf_op jit(solution)/shard_map/ppermute | solution.py:440
  102.4 14.8 %collective-permute-start.21 = (bf16[128,2048]{1,0:T(8,128)(2,1)S(1)}, bf16[128,2048]{1,0:T(8,128)(2,1)S(1)}, u32[]{:S(2)}, u32[]{:S(2)}) collective-permute-start(bf16[128,2048]{1,0:T(8,128)(2,1)S(1)} %get-tuple-element.55), channel_id=1, source_target_pairs={{0,1},{1,0},{2,3},{3,2},{4,5},{5,4},{6,7},{7,6},{8,9},{9,8},{10,11... | collective-permute-start | bytes 1572872 | tf_op jit(solution)/shard_map/ppermute | solution.py:127
  104.0 24.6 %collective-permute-start.22 = (bf16[128,2048]{1,0:T(8,128)(2,1)S(1)}, bf16[128,2048]{1,0:T(8,128)(2,1)S(1)}, u32[]{:S(2)}, u32[]{:S(2)}) collective-permute-start(bf16[128,2048]{1,0:T(8,128)(2,1)S(1)} %get-tuple-element.56), channel_id=1, source_target_pairs={{0,2},{1,3},{2,0},{3,1},{4,6},{5,7},{6,4},{7,5},{8,10},{9,11},{10,... | collective-permute-start | bytes 1572872 | tf_op jit(solution)/shard_map/ppermute | solution.py:127
  105.8 22.9 %collective-permute-start.23 = (bf16[128,2048]{1,0:T(8,128)(2,1)S(1)}, bf16[128,2048]{1,0:T(8,128)(2,1)S(1)}, u32[]{:S(2)}, u32[]{:S(2)}) collective-permute-start(bf16[128,2048]{1,0:T(8,128)(2,1)S(1)} %get-tuple-element.57), channel_id=1, source_target_pairs={{0,3},{1,2},{2,1},{3,0},{4,7},{5,6},{6,5},{7,4},{8,11},{9,10},{10,... | collective-permute-start | bytes 1572872 | tf_op jit(solution)/shard_map/ppermute | solution.py:127
  110.0 24.5 %collective-permute-start.39 = (bf16[96,2048]{1,0:T(8,128)(2,1)S(1)}, bf16[96,2048]{1,0:T(8,128)(2,1)S(1)}, u32[]{:S(2)}, u32[]{:S(2)}) collective-permute-start(bf16[96,2048]{1,0:T(8,128)(2,1)S(1)} %get-tuple-element.73), channel_id=1, source_target_pairs={{0,8},{4,12},{1,9},{5,13},{2,10},{6,14},{3,11},{7,15}} | collective-permute-start | bytes 1179656 | tf_op jit(solution)/shard_map/ppermute | solution.py:405
  117.3 15.4 %collective-permute-start.32 = (bf16[256,768]{1,0:T(8,128)(2,1)S(1)}, bf16[256,768]{1,0:T(8,128)(2,1)S(1)}, u32[]{:S(2)}, u32[]{:S(2)}) collective-permute-start(bf16[256,768]{1,0:T(8,128)(2,1)S(1)} %get-tuple-element.77), channel_id=1, source_target_pairs={{0,8},{4,12},{1,9},{5,13},{2,10},{6,14},{3,11},{7,15}} | collective-permute-start | bytes 1179656 | tf_op jit(solution)/shard_map/ppermute | solution.py:405
  129.8 28.2 %collective-permute-start.42 = (bf16[96,2048]{1,0:T(8,128)(2,1)S(1)}, bf16[96,2048]{1,0:T(8,128)(2,1)S(1)}, u32[]{:S(2)}, u32[]{:S(2)}) collective-permute-start(bf16[96,2048]{1,0:T(8,128)(2,1)S(1)} %get-tuple-element.74), channel_id=1, source_target_pairs={{24,16},{28,20},{25,17},{29,21},{26,18},{30,22},{27,19},{31,23}} | collective-permute-start | bytes 1179656 | tf_op jit(solution)/shard_map/ppermute | solution.py:406
  130.5 16.9 %collective-permute-start.35 = (bf16[256,768]{1,0:T(8,128)(2,1)S(1)}, bf16[256,768]{1,0:T(8,128)(2,1)S(1)}, u32[]{:S(2)}, u32[]{:S(2)}) collective-permute-start(bf16[256,768]{1,0:T(8,128)(2,1)S(1)} %get-tuple-element.78), channel_id=1, source_target_pairs={{24,16},{28,20},{25,17},{29,21},{26,18},{30,22},{27,19},{31,23}} | collective-permute-start | bytes 1179656 | tf_op jit(solution)/shard_map/ppermute | solution.py:406
  132.7 36.9 %collective-permute-start.28 = (bf16[256,768]{1,0:T(8,128)(2,1)S(1)}, bf16[256,768]{1,0:T(8,128)(2,1)S(1)}, u32[]{:S(2)}, u32[]{:S(2)}) collective-permute-start(bf16[256,768]{1,0:T(8,128)(2,1)S(1)} %get-tuple-element.82), channel_id=1, source_target_pairs={{24,16},{28,20},{25,17},{29,21},{26,18},{30,22},{27,19},{31,23}} | collective-permute-start | bytes 1179656 | tf_op jit(solution)/shard_map/ppermute | solution.py:406
  134.5 20.8 %collective-permute-start.33 = (bf16[256,768]{1,0:T(8,128)(2,1)S(1)}, bf16[256,768]{1,0:T(8,128)(2,1)S(1)}, u32[]{:S(2)}, u32[]{:S(2)}) collective-permute-start(bf16[256,768]{1,0:T(8,128)(2,1)S(1)} %fusion.8), channel_id=1, source_target_pairs={{0,8},{4,12},{8,16},{12,20},{1,9},{5,13},{9,17},{13,21},{2,10},{6,... | collective-permute-start | bytes 1179656 | tf_op jit(solution)/shard_map/ppermute | solution.py:405
  145.3 16.9 %collective-permute-start.40 = (bf16[96,2048]{1,0:T(8,128)(2,1)S(1)}, bf16[96,2048]{1,0:T(8,128)(2,1)S(1)}, u32[]{:S(2)}, u32[]{:S(2)}) collective-permute-start(bf16[96,2048]{1,0:T(8,128)(2,1)S(1)} %fusion.2), channel_id=1, source_target_pairs={{0,8},{4,12},{8,16},{12,20},{1,9},{5,13},{9,17},{13,21},{2,10},{6,... | collective-permute-start | bytes 1179656 | tf_op jit(solution)/shard_map/ppermute | solution.py:405
  147.4 24.1 %collective-permute-start.26 = (bf16[256,768]{1,0:T(8,128)(2,1)S(1)}, bf16[256,768]{1,0:T(8,128)(2,1)S(1)}, u32[]{:S(2)}, u32[]{:S(2)}) collective-permute-start(bf16[256,768]{1,0:T(8,128)(2,1)S(1)} %fusion.14), channel_id=1, source_target_pairs={{0,8},{4,12},{8,16},{12,20},{1,9},{5,13},{9,17},{13,21},{2,10},{6,... | collective-permute-start | bytes 1179656 | tf_op jit(solution)/shard_map/ppermute | solution.py:405
  156.7 16.4 %collective-permute-start.36 = (bf16[256,768]{1,0:T(8,128)(2,1)S(1)}, bf16[256,768]{1,0:T(8,128)(2,1)S(1)}, u32[]{:S(2)}, u32[]{:S(2)}) collective-permute-start(bf16[256,768]{1,0:T(8,128)(2,1)S(1)} %get-tuple-element.76), channel_id=1, source_target_pairs={{24,16},{28,20},{16,8},{20,12},{25,17},{29,21},{17,9},{21,13},{26,... | collective-permute-start | bytes 1179656 | tf_op jit(solution)/shard_map/ppermute | solution.py:406
  163.7 15.1 %collective-permute-start.43 = (bf16[96,2048]{1,0:T(8,128)(2,1)S(1)}, bf16[96,2048]{1,0:T(8,128)(2,1)S(1)}, u32[]{:S(2)}, u32[]{:S(2)}) collective-permute-start(bf16[96,2048]{1,0:T(8,128)(2,1)S(1)} %get-tuple-element.72), channel_id=1, source_target_pairs={{24,16},{28,20},{16,8},{20,12},{25,17},{29,21},{17,9},{21,13},{26,... | collective-permute-start | bytes 1179656 | tf_op jit(solution)/shard_map/ppermute | solution.py:406
  165.0 32.3 %collective-permute-start.41 = (bf16[96,2048]{1,0:T(8,128)(2,1)S(1)}, bf16[96,2048]{1,0:T(8,128)(2,1)S(1)}, u32[]{:S(2)}, u32[]{:S(2)}) collective-permute-start(bf16[96,2048]{1,0:T(8,128)(2,1)S(1)} %get-tuple-element.71), channel_id=1, source_target_pairs={{0,8},{4,12},{8,16},{12,20},{16,24},{20,28},{1,9},{5,13},{9,17},{1... | collective-permute-start | bytes 1179656 | tf_op jit(solution)/shard_map/ppermute | solution.py:405
  169.5 19.4 %collective-permute-start.34 = (bf16[256,768]{1,0:T(8,128)(2,1)S(1)}, bf16[256,768]{1,0:T(8,128)(2,1)S(1)}, u32[]{:S(2)}, u32[]{:S(2)}) collective-permute-start(bf16[256,768]{1,0:T(8,128)(2,1)S(1)} %get-tuple-element.75), channel_id=1, source_target_pairs={{0,8},{4,12},{8,16},{12,20},{16,24},{20,28},{1,9},{5,13},{9,17},{1... | collective-permute-start | bytes 1179656 | tf_op jit(solution)/shard_map/ppermute | solution.py:405
  171.8 15.1 %collective-permute-start.29 = (bf16[256,768]{1,0:T(8,128)(2,1)S(1)}, bf16[256,768]{1,0:T(8,128)(2,1)S(1)}, u32[]{:S(2)}, u32[]{:S(2)}) collective-permute-start(bf16[256,768]{1,0:T(8,128)(2,1)S(1)} %get-tuple-element.80), channel_id=1, source_target_pairs={{24,16},{28,20},{16,8},{20,12},{25,17},{29,21},{17,9},{21,13},{26,... | collective-permute-start | bytes 1179656 | tf_op jit(solution)/shard_map/ppermute | solution.py:406
  173.1 32.6 %collective-permute-start.27 = (bf16[256,768]{1,0:T(8,128)(2,1)S(1)}, bf16[256,768]{1,0:T(8,128)(2,1)S(1)}, u32[]{:S(2)}, u32[]{:S(2)}) collective-permute-start(bf16[256,768]{1,0:T(8,128)(2,1)S(1)} %get-tuple-element.79), channel_id=1, source_target_pairs={{0,8},{4,12},{8,16},{12,20},{16,24},{20,28},{1,9},{5,13},{9,17},{1... | collective-permute-start | bytes 1179656 | tf_op jit(solution)/shard_map/ppermute | solution.py:405
  178.8 16.5 %collective-permute-start.37 = (bf16[256,768]{1,0:T(8,128)(2,1)S(1)}, bf16[256,768]{1,0:T(8,128)(2,1)S(1)}, u32[]{:S(2)}, u32[]{:S(2)}) collective-permute-start(bf16[256,768]{1,0:T(8,128)(2,1)S(1)} %fusion.7), channel_id=1, source_target_pairs={{24,16},{28,20},{16,8},{20,12},{8,0},{12,4},{25,17},{29,21},{17,9}... | collective-permute-start | bytes 1179656 | tf_op jit(solution)/shard_map/ppermute | solution.py:406
  186.9 16.9 %collective-permute-start.44 = (bf16[96,2048]{1,0:T(8,128)(2,1)S(1)}, bf16[96,2048]{1,0:T(8,128)(2,1)S(1)}, u32[]{:S(2)}, u32[]{:S(2)}) collective-permute-start(bf16[96,2048]{1,0:T(8,128)(2,1)S(1)} %fusion.1), channel_id=1, source_target_pairs={{24,16},{28,20},{16,8},{20,12},{8,0},{12,4},{25,17},{29,21},{17,9}... | collective-permute-start | bytes 1179656 | tf_op jit(solution)/shard_map/ppermute | solution.py:406
  189.0 19.5 %collective-permute-start.30 = (bf16[256,768]{1,0:T(8,128)(2,1)S(1)}, bf16[256,768]{1,0:T(8,128)(2,1)S(1)}, u32[]{:S(2)}, u32[]{:S(2)}) collective-permute-start(bf16[256,768]{1,0:T(8,128)(2,1)S(1)} %fusion.13), channel_id=1, source_target_pairs={{24,16},{28,20},{16,8},{20,12},{8,0},{12,4},{25,17},{29,21},{17,9}... | collective-permute-start | bytes 1179656 | tf_op jit(solution)/shard_map/ppermute | solution.py:406
  (29 other events, 196.0 us)
where the time goes:
time: 211 us; the launch traced here: 209 us
  waiting for transfers between devices  71.1 us (34%)
  starting transfers between devices  69 us (33%)
  Pallas kernels  32 us (15%)
  other arithmetic  24.1 us (11%)
  local copies, waits for them, and re-layouts  12.1 us (6%)
    ppermute x17, waiting for transfers between devices, swap(): return lax.ppermute(value, 'expert', [(d, d ^ i) for d in range(n_ex)])  32.7 us
    ppermute x9, starting transfers between devices, line_steps(): right[p] = lax.ppermute(up.astype(BF16), 'dp', to_right)  29.1 us
    ppermute x17, starting transfers between devices, swap(): return lax.ppermute(value, 'expert', [(d, d ^ i) for d in range(n_ex)])  19.1 us
    ppermute x9, waiting for transfers between devices, line_steps(): left[p] = lax.ppermute(down.astype(BF16), 'dp', to_left)  18.7 us
    ppermute x9, starting transfers between devices, line_steps(): left[p] = lax.ppermute(down.astype(BF16), 'dp', to_left)  11.7 us
    ppermute x7, waiting for transfers between devices, reassign(): got.append(lax.ppermute(pieces[i], 'dp', [(d, d ^ i) for d in range(n_dp)]))  10.3 us
    ppermute x9, waiting for transfers between devices, line_steps(): right[p] = lax.ppermute(up.astype(BF16), 'dp', to_right)  9.41 us
    pallas_call x2, Pallas kernels, column_grad(): pl.pallas_call(column_grad_kernel, grid_spec=pltpu.PrefetchScalarGridSpec...  9.33 us
  transfers between devices with their start and end apart: 45, of which 16 were waited for; matrix products, arithmetic and copies ran while one was open for 13% of the time, Pallas kernels for 10%

commit v1 on v0

v1 whole, which is shorter than its diff:
```python
import functools

import jax
import jax.numpy as jnp
from jax import lax
from jax.experimental import pallas as pl
from jax.experimental.pallas import tpu as pltpu
from jax.sharding import PartitionSpec as P

CORES = 2
LANES = 128
F32 = jnp.float32
BF16 = jnp.bfloat16
MIB = 1 << 20


def contract(left, right, left_dim, right_dim):
    return lax.dot_general(left, right, (((left_dim,), (right_dim,)), ((), ())), preferred_element_type=F32)


def params(mib, **more):
    return pltpu.CompilerParams(vmem_limit_bytes=mib * MIB, **more)


def vmem():
    return pl.BlockSpec(memory_space=pltpu.VMEM)


def hbm():
    return pl.BlockSpec(memory_space=pl.ANY)


LENGTH, ADV, GATES = 0, 1, 2
PARTS = 3


def pick_kernel(n_dp, dest_hbm, len_ref, adv_ref, rows_ref, *refs):
    outs, (dest_ref, sem) = refs[:n_dp], refs[n_dp:]
    copy = pltpu.make_async_copy(dest_hbm, dest_ref, sem)
    copy.start()
    seqs, slot, width = rows_ref.shape
    lane = lax.broadcasted_iota(jnp.int32, (slot, LANES), 1)
    which = lax.broadcasted_iota(jnp.int32, (1, seqs), 1)
    lengths = len_ref[0].astype(F32)
    advs = adv_ref[0].astype(F32)
    me = lax.axis_index("dp")
    copy.wait()
    for i, out in enumerate(outs):
        seq = jnp.int32(0)
        live = jnp.int32(0)
        for s in range(seqs):
            hit = dest_ref[0, 0, s] == (me ^ i)
            seq = jnp.where(hit, s, seq)
            live = jnp.where(hit, 1, live)
        mine = (which == seq) & (live == 1)
        length = jnp.sum(jnp.where(mine, lengths, 0.0), axis=1, keepdims=True)
        adv = jnp.sum(jnp.where(mine, advs, 0.0), axis=1, keepdims=True)
        out[:, :width] = rows_ref[pl.ds(seq, 1)][0]
        out[:, width:] = jnp.where(lane == LENGTH, length, jnp.where(lane == ADV, adv, 0.0)).astype(BF16)


def pick(dest, lengths, adv, rows, n_dp):
    seqs, slot, width = rows.shape
    return pl.pallas_call(
        functools.partial(pick_kernel, n_dp),
        out_shape=[jax.ShapeDtypeStruct((slot, width + LANES), BF16)] * n_dp,
        in_specs=[hbm(), vmem(), vmem(), vmem()],
        out_specs=[vmem()] * n_dp,
        scratch_shapes=[pltpu.SMEM(dest.shape, jnp.int32), pltpu.SemaphoreType.DMA],
        compiler_params=params(16),
        name="pick",
    )(dest, lengths, adv, rows)


def gate_notes(ids, gates):
    lane = lax.broadcasted_iota(jnp.int32, (ids.shape[0], LANES), 1) - GATES
    expert = lane // PARTS
    value = jnp.zeros(lane.shape, F32)
    for k in range(ids.shape[1]):
        value = value + jnp.where(ids[:, k : k + 1] == expert, gates[:, k : k + 1], 0.0)
    value = jnp.where(lane < 0, 0.0, value)
    high = value.astype(BF16).astype(F32)
    middle = (value - high).astype(BF16).astype(F32)
    low = value - high - middle
    part = lane % PARTS
    return jnp.where(part == 0, high, jnp.where(part == 1, middle, low))


def assemble_kernel(n_dp, ids_ref, gates_ref, *refs):
    pieces, x_ref = refs[:n_dp], refs[-1]
    slot, wide = pieces[0].shape
    width = wide - LANES
    me = lax.axis_index("dp")
    for i, piece in enumerate(pieces):
        at = pl.multiple_of((me ^ i) * slot, slot)
        x_ref[pl.ds(at, slot), :] = piece[...]
    notes = gate_notes(ids_ref[...], gates_ref[...])
    x_ref[:, width:] = (x_ref[:, width:].astype(F32) + notes).astype(BF16)


def assemble(pieces, ids, gates, after):
    slot, wide = pieces[0].shape
    n_dp = len(pieces)
    return pl.pallas_call(
        functools.partial(assemble_kernel, n_dp),
        out_shape=jax.ShapeDtypeStruct((slot * n_dp, wide), BF16),
        in_specs=[vmem()] * (2 + n_dp) + [hbm()] * len(after),
        out_specs=vmem(),
        compiler_params=params(16),
        name="assemble",
    )(ids, gates, *pieces, *after)


def reassign(gen_rows, gen_lengths, gen_adv, destination, ids, gates, after, n_dp):
    seq_dev = destination.shape[2]
    width = gen_rows.shape[1]
    slot = gen_rows.shape[0] // seq_dev
    g = lax.axis_index("dp")
    pieces = pick(destination, gen_lengths, gen_adv, gen_rows.reshape(seq_dev, slot, width), n_dp)
    got = [None] * n_dp
    got[0] = pieces[0]
    for i in reversed(range(1, n_dp)):
        got[i] = lax.ppermute(pieces[i], "dp", [(d, d ^ i) for d in range(n_dp)])
    if n_dp == seq_dev:
        return assemble(got, ids, gates, after)
    stack = jnp.stack(got)[jnp.arange(n_dp, dtype=jnp.int32) ^ g]
    arrived = stack[:, 0, width + LENGTH] > 0
    arrival = jnp.cumsum(arrived.astype(jnp.int32)) - 1
    chosen = arrived[None, :] & (arrival[None, :] == jnp.arange(seq_dev, dtype=jnp.int32)[:, None])
    from_peer = jnp.sum(jnp.where(chosen, jnp.arange(n_dp, dtype=jnp.int32)[None, :], 0), axis=1)
    x = stack[from_peer].reshape(seq_dev * slot, width + LANES)
    notes = (x[:, width:].astype(F32) + gate_notes(ids, gates)).astype(BF16)
    return jnp.concatenate([x[:, :width], notes], axis=1)


def swap(value, i, n_ex):
    return lax.ppermute(value, "expert", [(d, d ^ i) for d in range(n_ex)])


def gather_rows(rows, n_ex):
    if n_ex != 4:
        return [rows] + [swap(rows, i, n_ex) for i in range(1, n_ex)]
    half = rows.shape[0] // 2
    first = swap(rows, 1, n_ex)
    second = swap(rows, 2, n_ex)
    return [rows, first, second, swap(first[:half], 2, n_ex), swap(second[half:], 1, n_ex)]


def with_last(pieces, size):
    at, cut = 0, sum(p.shape[0] for p in pieces) - size
    for i, piece in enumerate(pieces):
        if at == cut:
            return pieces[:i], pieces[i:]
        at += piece.shape[0]


def tie(value, *others):
    return lax.optimization_barrier((value,) + others)[0]


def load_pieces(pieces, whole, sems):
    at, copies = 0, []
    for i, piece in enumerate(pieces):
        size = piece.shape[0]
        copies.append(pltpu.make_async_copy(piece, whole.at[pl.ds(at, size)], sems.at[i]))
        at += size
    for copy in copies:
        copy.start()
    for copy in copies:
        copy.wait()


def hidden_grad_kernel(count, w_ref, *refs):
    pieces, (out, whole_out, whole, sems, out_sem) = refs[:count], refs[count:]
    step = pl.program_id(0)

    @pl.when(step == 0)
    def _():
        load_pieces(pieces, whole, sems)
        pltpu.make_async_copy(whole, whole_out, out_sem).start()

    out[...] = contract(whole[...], w_ref[...], 1, 1)

    @pl.when(step == pl.num_programs(0) - 1)
    def _():
        pltpu.make_async_copy(whole, whole_out, out_sem).wait()


def hidden_grad(pieces, w_down):
    rows = sum(p.shape[0] for p in pieces)
    units, width = w_down.shape
    tile = 256
    return pl.pallas_call(
        functools.partial(hidden_grad_kernel, len(pieces)),
        grid=(units // tile,),
        out_shape=[jax.ShapeDtypeStruct((rows, units), F32), jax.ShapeDtypeStruct((rows, width), BF16)],
        in_specs=[pl.BlockSpec((tile, width), lambda j: (j, 0))] + [hbm()] * len(pieces),
        out_specs=[pl.BlockSpec((rows, tile), lambda j: (0, j)), hbm()],
        scratch_shapes=[
            pltpu.VMEM((rows, width), BF16),
            pltpu.SemaphoreType.DMA((len(pieces),)),
            pltpu.SemaphoreType.DMA,
        ],
        compiler_params=params(32),
        cost_estimate=pl.CostEstimate(
            flops=2 * rows * units * width, bytes_accessed=2 * units * width + 4 * rows * width, transcendentals=0
        ),
        name="hidden_grad",
    )(w_down, *pieces)


def units_kernel(count, slot, first, wg_ref, wu_ref, hg_ref, *refs):
    if not first:
        refs = refs[5:]
    pieces, (gate_out, up_out, hid_out, hs_out, whole_out, whole, gs_ref, sems, out_sem) = refs[:count], refs[count:]
    step = pl.program_id(0)
    rows, wide = whole.shape
    width = wide - LANES
    start = 0 if first else whole_out.shape[0] - rows

    @pl.when(step == 0)
    def _():
        load_pieces(pieces, whole, sems)
        pltpu.make_async_copy(whole, whole_out.at[pl.ds(start, rows)], out_sem).start()
        notes = whole[:, width:].astype(F32)
        lane = lax.broadcasted_iota(jnp.int32, notes.shape, 1) - GATES - PARTS * lax.axis_index("expert")
        gate = jnp.sum(jnp.where((lane >= 0) & (lane < PARTS), notes, 0.0), axis=1, keepdims=True)
        length, adv = notes[:, LENGTH : LENGTH + 1], notes[:, ADV : ADV + 1]
        position = lax.broadcasted_iota(jnp.int32, (rows, 1), 0) % slot
        gs_ref[...] = jnp.where(position.astype(F32) < length, gate * (adv / length), 0.0)

    x = whole[:, :width]
    gate = jnp.dot(x, wg_ref[...], preferred_element_type=F32)
    up = jnp.dot(x, wu_ref[...], preferred_element_type=F32)
    gs = gs_ref[...]
    sig = jax.nn.sigmoid(gate)
    act = gate * sig
    hid = (act * up).astype(BF16)
    hid_out[...] = hid
    hs_out[...] = (hid.astype(F32) * gs).astype(BF16)
    hg = hg_ref[...] * gs
    gate_out[...] = (hg * up * sig * (1.0 + gate * (1.0 - sig))).astype(BF16)
    up_out[...] = (hg * act).astype(BF16)

    @pl.when(step == pl.num_programs(0) - 1)
    def _():
        pltpu.make_async_copy(whole, whole_out.at[pl.ds(start, rows)], out_sem).wait()


def hidden_units(pieces, w_gate, w_up, hg, slot, before=None):
    total, units = hg.shape
    width = w_gate.shape[0]
    rows = sum(p.shape[0] for p in pieces)
    tile = 256
    at = 0 if before is None else total // rows - 1
    columns = pl.BlockSpec((rows, tile), lambda j: (at, j))
    weights = pl.BlockSpec((width, tile), lambda j: (0, j))
    before = before or []
    return pl.pallas_call(
        functools.partial(units_kernel, len(pieces), slot, not before),
        grid=(units // tile,),
        out_shape=[jax.ShapeDtypeStruct((total, units), BF16)] * 4 + [jax.ShapeDtypeStruct((total, width + LANES), BF16)],
        in_specs=[weights, weights, columns] + [hbm()] * (len(before) + len(pieces)),
        out_specs=[columns] * 4 + [hbm()],
        scratch_shapes=[
            pltpu.VMEM((rows, width + LANES), BF16),
            pltpu.VMEM((rows, 1), F32),
            pltpu.SemaphoreType.DMA((len(pieces),)),
            pltpu.SemaphoreType.DMA,
        ],
        input_output_aliases={3 + i: i for i in range(len(before))},
        compiler_params=params(48),
        cost_estimate=pl.CostEstimate(
            flops=4 * rows * units * width, bytes_accessed=4 * units * width + 4 * rows * width, transcendentals=rows * units
        ),
        name="hidden_units",
    )(w_gate, w_up, hg, *before, *pieces)


def column_grads_kernel(place_ref, x_ref, gate_ref, up_ref, other, mine):
    turned = x_ref[...].T
    gate = jnp.dot(turned, gate_ref[...], preferred_element_type=F32).astype(BF16)
    up = jnp.dot(turned, up_ref[...], preferred_element_type=F32).astype(BF16)

    @pl.when(pl.program_id(0) == 0)
    def _():
        other[0, 0] = gate
        other[0, 1] = up

    @pl.when(pl.program_id(0) == 1)
    def _():
        mine[0, 0] = gate
        mine[0, 1] = up


def column_grads(place, x, gate_grad, up_grad, n_dp, blocks):
    rows, units = gate_grad.shape
    width = x.shape[1] - LANES
    n_z, shard = n_dp // CORES, width // n_dp
    count, last = len(blocks), blocks[0]
    out = jax.ShapeDtypeStruct((count, 2, shard, units), BF16)

    def column(k, b, place):
        chip = jnp.where(place[1] == 0, last - b, n_z - 1 - (last - b))
        return 0, CORES * chip + jnp.where(k == 0, 1 - place[0], place[0])

    whole = pl.BlockSpec((rows, units), lambda k, b, place: (0, 0))
    return pl.pallas_call(
        column_grads_kernel,
        grid_spec=pltpu.PrefetchScalarGridSpec(
            num_scalar_prefetch=1,
            grid=(CORES, count),
            in_specs=[pl.BlockSpec((rows, shard), column), whole, whole],
            out_specs=[
                pl.BlockSpec((1, 2, shard, units), lambda k, b, place: (jnp.where(k == 0, b, count - 1), 0, 0, 0)),
                pl.BlockSpec((1, 2, shard, units), lambda k, b, place: (jnp.where(k == 0, 0, b), 0, 0, 0)),
            ],
        ),
        out_shape=[out, out],
        compiler_params=params(40),
        cost_estimate=pl.CostEstimate(
            flops=8 * rows * units * shard * count,
            bytes_accessed=16 * units * shard * count + 4 * rows * shard * count + 4 * rows * units,
            transcendentals=0,
        ),
        name="column_grads",
    )(place, x, gate_grad, up_grad)


def row_grad_kernel(place_ref, hid_ref, dy_ref, other, mine):
    value = contract(hid_ref[...], dy_ref[...], 0, 0).astype(BF16)
    n_z, shard, _ = mine.shape

    for z in range(n_z):
        low = value[CORES * z * shard : (CORES * z + 1) * shard]
        high = value[(CORES * z + 1) * shard : (CORES * z + 2) * shard]
        chip = jnp.where(place_ref[1] == 0, z, n_z - 1 - z)
        at = n_z - 1 - chip

        @pl.when(place_ref[0] == 0)
        def _(low=low, high=high, at=at):
            mine[at] = low
            other[at] = high

        @pl.when(place_ref[0] == 1)
        def _(low=low, high=high, at=at):
            mine[at] = high
            other[at] = low


def row_grad(place, hid, dy, n_dp):
    rows, units = hid.shape
    width = dy.shape[1]
    n_z, shard = n_dp // CORES, units // n_dp
    tile = 512
    out = jax.ShapeDtypeStruct((n_z, shard, width), BF16)
    block = pl.BlockSpec((n_z, shard, tile), lambda j, place: (0, 0, j))
    return pl.pallas_call(
        row_grad_kernel,
        grid_spec=pltpu.PrefetchScalarGridSpec(
            num_scalar_prefetch=1,
            grid=(width // tile,),
            in_specs=[
                pl.BlockSpec((rows, units), lambda j, place: (0, 0)),
                pl.BlockSpec((rows, tile), lambda j, place: (0, j)),
            ],
            out_specs=[block, block],
        ),
        out_shape=[out, out],
        compiler_params=params(32),
        cost_estimate=pl.CostEstimate(
            flops=2 * rows * units * width, bytes_accessed=2 * units * width + 2 * rows * width, transcendentals=0
        ),
        name="row_grad",
    )(place, hid, dy)


def outputs_kernel(n_ex, hid_ref, w_ref, *outs):
    value = jnp.dot(hid_ref[...], w_ref[...], preferred_element_type=F32).astype(BF16)
    size = outs[0].shape[0]
    for i in range(n_ex):
        outs[i][...] = value[i * size : (i + 1) * size]


def layer_outputs(hid, w_down, n_ex):
    rows, units = hid.shape
    width = w_down.shape[1]
    tile = 512
    size = rows // n_ex
    return pl.pallas_call(
        functools.partial(outputs_kernel, n_ex),
        grid=(width // tile,),
        out_shape=[jax.ShapeDtypeStruct((size, width), BF16)] * n_ex,
        in_specs=[pl.BlockSpec((rows, units), lambda j: (0, 0)), pl.BlockSpec((units, tile), lambda j: (0, j))],
        out_specs=[pl.BlockSpec((size, tile), lambda j: (0, j))] * n_ex,
        compiler_params=params(32),
        cost_estimate=pl.CostEstimate(
            flops=2 * rows * units * width, bytes_accessed=2 * units * width + 2 * rows * width, transcendentals=0
        ),
        name="layer_outputs",
    )(hid, w_down)


def input_grads_kernel(n_ex, gate_ref, up_ref, wg_ref, wu_ref, *outs):
    value = contract(gate_ref[...], wg_ref[...], 1, 1) + contract(up_ref[...], wu_ref[...], 1, 1)
    value = value.astype(BF16)
    size = outs[0].shape[0]
    for i in range(n_ex):
        outs[i][...] = value[i * size : (i + 1) * size]


def input_grads(gate_grad, up_grad, w_gate, w_up, n_ex):
    rows, units = gate_grad.shape
    width = w_gate.shape[0]
    tile = 512
    size = rows // n_ex
    whole = pl.BlockSpec((rows, units), lambda j: (0, 0))
    weights = pl.BlockSpec((tile, units), lambda j: (j, 0))
    return pl.pallas_call(
        functools.partial(input_grads_kernel, n_ex),
        grid=(width // tile,),
        out_shape=[jax.ShapeDtypeStruct((size, width), BF16)] * n_ex,
        in_specs=[whole, whole, weights, weights],
        out_specs=[pl.BlockSpec((size, tile), lambda j: (0, j))] * n_ex,
        compiler_params=params(40),
        cost_estimate=pl.CostEstimate(
            flops=4 * rows * units * width, bytes_accessed=4 * units * width + 2 * rows * width, transcendentals=0
        ),
        name="input_grads",
    )(gate_grad, up_grad, w_gate, w_up)


def add(*parts):
    return sum(part.astype(F32) for part in parts).astype(BF16)


def line_permute(value, link, n_dp):
    n_z = n_dp // CORES
    pairs = [(link, link + 1), (n_z - 1 - link, n_z - 2 - link)]
    return lax.ppermute(value, "dp", [(CORES * a + c, CORES * b + c) for a, b in pairs for c in range(CORES)])


def on_device(
    gen_rows, gen_lengths, gen_adv, destination, expert_ids, gate_values, cotangent, w_gate, w_up, w_down
):
    n_dp = lax.axis_size("dp")
    n_ex = lax.axis_size("expert")
    n_z = n_dp // CORES
    size = cotangent.shape[0]
    slot = gen_rows.shape[0] // destination.shape[2]
    weight_gate, weight_up, weight_down = w_gate[0], w_up[0], w_down[0]
    g, e = lax.axis_index("dp"), lax.axis_index("expert")
    z = g // CORES
    flipped = z >= n_z // 2
    place = jnp.stack([g % CORES, flipped.astype(jnp.int32)]).astype(jnp.int32)
    near = jnp.where(flipped, n_z - 1 - z, z)
    other_core = [(d, d ^ 1) for d in range(n_dp)]

    def swap_core(value):
        return lax.ppermute(value, "dp", other_core)

    cot_pieces = gather_rows(cotangent, n_ex)
    x = reassign(
        gen_rows, gen_lengths, gen_adv, destination, expert_ids, gate_values, cot_pieces[1:3], n_dp
    )
    x_pieces = gather_rows(x, n_ex)
    hg, dy_all = hidden_grad(cot_pieces, weight_down)
    early, late = with_last(x_pieces, size)
    before = hidden_units(early, weight_gate, weight_up, hg, slot)
    gate_grad, up_grad, hid, hid_scaled, x_all = hidden_units(late, weight_gate, weight_up, hg, slot, before)

    far = n_z - 1
    sums = [[None, None] for _ in range(n_z)]
    other, mine = column_grads(place, x_all, gate_grad, up_grad, n_dp, [far])
    sums[far][0] = add(mine[0], swap_core(other)[0])
    other, mine = row_grad(place, tie(hid_scaled, other), dy_all, n_dp)
    got = swap_core(other)
    for k in range(n_z):
        sums[k][1] = add(mine[far - k], got[far - k])
    rest = list(range(far - 1, -1, -1))
    other, mine = column_grads(place, tie(x_all, other), gate_grad, up_grad, n_dp, rest)
    got = swap_core(other)
    for i, k in enumerate(rest):
        sums[k][0] = add(mine[i], got[i])

    hid, gate_grad, up_grad, _, _ = lax.optimization_barrier((hid, gate_grad, up_grad, other, sums[far][0]))
    outs = layer_outputs(hid, weight_down, n_ex)
    grads = input_grads(gate_grad, up_grad, weight_gate, weight_up, n_ex)
    outs = [outs[0]] + [swap(outs[i], i, n_ex) for i in range(1, n_ex)]
    grads = [grads[0]] + [swap(tie(grads[i], outs[i]), i, n_ex) for i in range(1, n_ex)]

    passed = {}
    ends = [[], []]
    for link in range(n_z - 1):
        issued = []
        for d in range(far, link, -1):
            for p in range(2):
                value = sums[d if link < n_z // 2 else far - d][p]
                if link > 0:
                    value = add(value, passed[link - 1, d, p])
                if len(issued) >= 2:
                    value = tie(value, issued[-2])
                got = line_permute(value, link, n_dp)
                issued.append(got)
                passed[link, d, p] = got
                if d == link + 1:
                    ends[p].append(got)
    totals = []
    for p in range(2):
        own = sum(jnp.where(near == k, sums[k][p].astype(F32), 0.0) for k in range((n_z + 1) // 2))
        totals.append(add(own, *ends[p]))

    gates = [
        jnp.sum(jnp.where(expert_ids == (e ^ i), gate_values, 0.0), axis=1, keepdims=True) for i in range(n_ex)
    ]
    layer_out = sum(gates[i] * outs[i].astype(F32) for i in range(n_ex)).astype(BF16)
    input_grad = add(*grads)
    return layer_out, input_grad, totals[0][0:1], totals[0][1:2], totals[1][None]


def solution(mesh):
    rows = P(("dp", "expert"), None)
    seqs = P("dp", "expert", None)
    weights = P("expert", None, None)
    shards = P("expert", "dp", None)
    return jax.shard_map(
        on_device,
        mesh=mesh,
        in_specs=(rows, seqs, seqs, seqs, rows, rows, rows, weights, weights, weights),
        out_specs=(rows, rows, shards, shards, shards),
        check_vma=False,
    )
```

time: 211 us -> 200 us (0.948)
  starting transfers between devices: 69 us -> 46.2 us
  waiting for transfers between devices: 71.1 us -> 82.8 us
  other arithmetic: 24.1 us -> 15.8 us
  local copies, waits for them, and re-layouts: 12.1 us -> 17.2 us
  Pallas kernels: 32 us -> 35.6 us
    ppermute x28 -> x22, starting transfers between devices: 49.9 us -> 29.6 us  [the longest x12 22.2 us: line_permute(): lax.ppermute(value, 'dp', [(CORES * a + c, CORES * b + c) for a, b in pai...]
    ppermute x28 -> x22, waiting for transfers between devices: 38.4 us -> 55.6 us  [the longest x12 46.5 us: line_permute(): lax.ppermute(value, 'dp', [(CORES * a + c, CORES * b + c) for a, b in pai...]
    unnamed x32 -> x52, local copies, waits for them, and re-layouts: 8.27 us -> 14.8 us
    ppermute x17 -> x14, waiting for transfers between devices: 32.7 us -> 27.2 us  [swap(): return lax.ppermute(value, 'expert', [(d, d ^ i) for d in range(n_ex)])]
    pallas_call x5 -> x6, Pallas kernels: 16.7 us -> 19.8 us  [the longest x2 10.9 us: hidden_units(): pl.pallas_call(functools.partial(units_kernel, len(pieces), slot, not bef...]
    broadcast_in_dim x3 -> x1, other arithmetic: 4.85 us -> 2.14 us  [on_device(): totals[1][None]]
    ppermute x17 -> x14, starting transfers between devices: 19.1 us -> 16.6 us  [swap(): return lax.ppermute(value, 'expert', [(d, d ^ i) for d in range(n_ex)])]
    convert_element_type x15 -> x11, other arithmetic: 13.4 us -> 11 us  [add(): return sum((part.astype(F32) for part in parts)).astype(BF16)]
  transfers between devices with their start and end apart: 45 -> 36, of which waited for: 16 -> 18; matrix products, arithmetic and copies ran while one was open for 13% -> 9% of each run, Pallas kernels for 10% -> 15%
where the time goes in v1:
time: 200 us; the launch traced here: 199 us
  waiting for transfers between devices  82.8 us (41%)
  starting transfers between devices  46.2 us (23%)
  Pallas kernels  35.6 us (18%)
  local copies, waits for them, and re-layouts  17.2 us (9%)
  other arithmetic  15.8 us (8%)
    ppermute x12, waiting for transfers between devices, line_permute(): lax.ppermute(value, 'dp', [(CORES * a + c, CORES * b + c) for a, b in pai...  46.5 us
    ppermute x14, waiting for transfers between devices, swap(): return lax.ppermute(value, 'expert', [(d, d ^ i) for d in range(n_ex)])  27.2 us
    ppermute x12, starting transfers between devices, line_permute(): lax.ppermute(value, 'dp', [(CORES * a + c, CORES * b + c) for a, b in pai...  22.2 us
    ppermute x14, starting transfers between devices, swap(): return lax.ppermute(value, 'expert', [(d, d ^ i) for d in range(n_ex)])  16.6 us
    unnamed x52, local copies, waits for them, and re-layouts  14.8 us
    convert_element_type x11, other arithmetic, add(): return sum((part.astype(F32) for part in parts)).astype(BF16)  11 us
    pallas_call x2, Pallas kernels, hidden_units(): pl.pallas_call(functools.partial(units_kernel, len(pieces), slot, not bef...  10.9 us
    ppermute x7, waiting for transfers between devices, reassign(): got[i] = lax.ppermute(pieces[i], 'dp', [(d, d ^ i) for d in range(n_dp)])  9.14 us
  transfers between devices with their start and end apart: 36, of which 18 were waited for; matrix products, arithmetic and copies ran while one was open for 9% of the time, Pallas kernels for 15%

profile of v1, /device:TPU:12, one launch (start us, length us, event | category | flops | bytes accessed | tf_op | source)
XLA Modules:
  0.0 198.8 jit_solution(5209173324606195338)
XLA Ops:
  8.4 2.6 %collective-permute-start.7 = (bf16[16,2176]{1,0:T(8,128)(2,1)S(1)}, bf16[16,2176]{1,0:T(8,128)(2,1)S(1)}, u32[]{:S(2)}, u32[]{:S(2)}) collective-permute-start(bf16[16,2176]{1,0:T(8,128)(2,1)S(1)} %get-tuple-element.58), channel_id=1, source_target_pairs={{0,16},{4,20},{8,24},{12,28},{16,0},{20,4},{24,8},{28,12},{1,17},{... | collective-permute-start | bytes 208904 | tf_op jit(solution)/shard_map/ppermute | solution.py:123
  13.9 2.1 %collective-permute-done.7.refs_4_ = bf16[16,2176]{1,0:T(8,128)(2,1)S(1)} collective-permute-done((bf16[16,2176]{1,0:T(8,128)(2,1)S(1)}, bf16[16,2176]{1,0:T(8,128)(2,1)S(1)}, u32[]{:S(2)}, u32[]{:S(2)}) %collective-permute-start.7) | collective-permute-done | bytes 69664 | tf_op jit(solution)/shard_map/ppermute | solution.py:123
  19.1 3.6 %collective-permute-done.9.refs_6_ = bf16[16,2176]{1,0:T(8,128)(2,1)S(1)} collective-permute-done((bf16[16,2176]{1,0:T(8,128)(2,1)S(1)}, bf16[16,2176]{1,0:T(8,128)(2,1)S(1)}, u32[]{:S(2)}, u32[]{:S(2)}) %collective-permute-start.9) | collective-permute-done | bytes 69664 | tf_op jit(solution)/shard_map/ppermute | solution.py:123
  29.8 9.9 %collective-permute-done.11.refs_1_ = bf16[128,2176]{1,0:T(8,128)(2,1)S(1)} collective-permute-done((bf16[128,2176]{1,0:T(8,128)(2,1)S(1)}, bf16[128,2176]{1,0:T(8,128)(2,1)S(1)}, u32[]{:S(2)}, u32[]{:S(2)}) %collective-permute-start.11) | collective-permute-done | bytes 557088 | tf_op jit(solution)/shard_map/ppermute | solution.py:137
  41.9 3.8 %collective-permute-done.2.refs_3_ = bf16[64,2048]{1,0:T(8,128)(2,1)S(1)} collective-permute-done((bf16[64,2048]{1,0:T(8,128)(2,1)}, bf16[64,2048]{1,0:T(8,128)(2,1)S(1)}, u32[]{:S(2)}, u32[]{:S(2)}) %collective-permute-start.2) | collective-permute-done | bytes 262176 | tf_op jit(solution)/shard_map/ppermute | solution.py:137
  47.7 3.6 %hidden_grad.1 = (f32[512,768]{1,0:T(8,128)S(1)}, bf16[512,2048]{1,0:T(8,128)(2,1)S(1)}) custom-call(bf16[768,2048]{1,0:T(8,128)(2,1)S(1)} %bitcast.41, bf16[128,2048]{1,0:T(8,128)(2,1)S(1)} %copy-done.21, bf16[128,2048]{1,0:T(8,128)(2,1)S(1)} %collective-permute-done.refs_1_.refs_8_, bf16[128,2048]{1,0:T(8,128)(2,1)S(1)} %collective-permute-done.1.refs_2_.refs_9_, ...), custom_call_target="tpu_custom_call" | custom-call | flops 1610612736 | bytes 7340032 | tf_op jit(solution)/shard_map/hidden_grad/pallas_call | solution.py:193
  52.5 6.3 %hidden_units.2 = (bf16[512,768]{1,0:T(8,128)(2,1)S(1)}, bf16[512,768]{1,0:T(8,128)(2,1)S(1)}, bf16[512,768]{1,0:T(8,128)(2,1)S(1)}, bf16[512,768]{1,0:T(8,128)(2,1)S(1)}, bf16[512,2176]{1,0:T(8,128)(2,1)}) custom-call(bf16[2048,768]{1,0:T(8,128)(2,1)} %bitcast.34, bf16[2048,768]{1,0:T(8,128)(2,1)} %bitcast.37, f32[512,768]{1,0:T(8,128)} %copy-done.3, ...), custom_call_target="tpu_custom_call" | custom-call | flops 2415919104 | bytes 9437184 | tf_op jit(solution)/shard_map/hidden_units/pallas_call | solution.py:259
  58.8 4.5 %hidden_units.3 = (bf16[512,768]{1,0:T(8,128)(2,1)S(1)}, bf16[512,768]{1,0:T(8,128)(2,1)S(1)}, bf16[512,768]{1,0:T(8,128)(2,1)S(1)}, bf16[512,768]{1,0:T(8,128)(2,1)S(1)}, bf16[512,2176]{1,0:T(8,128)(2,1)}) custom-call(bf16[2048,768]{1,0:T(8,128)(2,1)} %bitcast.35, ...), custom_call_target="tpu_custom_call", output_to_operand_aliasing={{0}: (3, {}), {1}: (4, {}), {2}: (5, {}), {3}: (6, {}), {4}... | custom-call | flops 805306368 | bytes 7340032 | tf_op jit(solution)/shard_map/hidden_units/pallas_call | solution.py:259
  63.4 2.2 %copy-done.2 = bf16[512,2176]{1,0:T(8,128)(2,1)S(1)} copy-done((bf16[512,2176]{1,0:T(8,128)(2,1)S(1)}, bf16[512,2176]{1,0:T(8,128)(2,1)}, u32[]{:S(2)}) %copy-start.2) | copy-done | bytes 2228248
  65.6 2.0 %column_grads.2 = (bf16[1,2,256,768]{3,2,1,0:T(8,128)(2,1)S(1)}, bf16[1,2,256,768]{3,2,1,0:T(8,128)(2,1)S(1)}) custom-call(s32[2]{0:T(128)S(1)} %pad_add_fusion.place_ref, bf16[512,2176]{1,0:T(8,128)(2,1)S(1)} %copy-done.2, bf16[512,768]{1,0:T(8,128)(2,1)S(1)} %get-tuple-element.84.gate_ref, bf16[512,768]{1,0:T(8,128)(2,1)S(1)} %get-tuple-element.85.up_ref), custom_call_target="tpu_custom_call" | custom-call | flops 805306368 | bytes 5242880 | tf_op jit(solution)/shard_map/column_grads/pallas_call | solution.py:308
  67.7 4.6 %row_grad.1 = (bf16[4,96,2048]{2,1,0:T(8,128)(2,1)}, bf16[4,96,2048]{2,1,0:T(8,128)(2,1)S(1)}) custom-call(s32[2]{0:T(128)S(1)} %pad_add_fusion.place_ref, bf16[512,768]{1,0:T(8,128)(2,1)S(1)} %get-tuple-element.73.hid_ref, bf16[512,2048]{1,0:T(8,128)(2,1)S(1)} %get-tuple-element.74.dy_ref), custom_call_target="tpu_custom_call" | custom-call | flops 1610612736 | bytes 5242880 | tf_op jit(solution)/shard_map/row_grad/pallas_call | solution.py:358
  72.7 6.0 %column_grads.3 = (bf16[3,2,256,768]{3,2,1,0:T(8,128)(2,1)}, bf16[3,2,256,768]{3,2,1,0:T(8,128)(2,1)S(1)}) custom-call(s32[2]{0:T(128)S(1)} %pad_add_fusion.place_ref, bf16[512,2176]{1,0:T(8,128)(2,1)S(1)} %copy-done.2, bf16[512,768]{1,0:T(8,128)(2,1)S(1)} %get-tuple-element.84.gate_ref, bf16[512,768]{1,0:T(8,128)(2,1)S(1)} %get-tuple-element.85.up_ref), custom_call_target="tpu_custom_call" | custom-call | flops 2415919104 | bytes 12582912 | tf_op jit(solution)/shard_map/column_grads/pallas_call | solution.py:308
  80.1 3.5 %layer_outputs.1 = (bf16[128,2048]{1,0:T(8,128)(2,1)S(1)}, bf16[128,2048]{1,0:T(8,128)(2,1)}, bf16[128,2048]{1,0:T(8,128)(2,1)}, bf16[128,2048]{1,0:T(8,128)(2,1)}) custom-call(bf16[512,768]{1,0:T(8,128)(2,1)S(1)} %get-tuple-element.79.hid_ref, bf16[768,2048]{1,0:T(8,128)(2,1)S(1)} %bitcast.42), custom_call_target="tpu_custom_call" | custom-call | flops 1610612736 | bytes 5242880 | tf_op jit(solution)/shard_map/layer_outputs/pallas_call | solution.py:390
  84.4 2.6 %collective-permute-start.18 = (bf16[128,2048]{1,0:T(8,128)(2,1)}, bf16[128,2048]{1,0:T(8,128)(2,1)}, u32[]{:S(2)}, u32[]{:S(2)}) collective-permute-start(bf16[128,2048]{1,0:T(8,128)(2,1)} %get-tuple-element.83), channel_id=1, source_target_pairs={{0,3},{1,2},{2,1},{3,0},{4,7},{5,6},{6,5},{7,4},{8,11},{9,10},{10,... | collective-permute-start | bytes 1572872 | tf_op jit(solution)/shard_map/ppermute | solution.py:137
  92.1 4.2 %input_grads.1 = (bf16[128,2048]{1,0:T(8,128)(2,1)S(1)}, bf16[128,2048]{1,0:T(8,128)(2,1)S(1)}, bf16[128,2048]{1,0:T(8,128)(2,1)S(1)}, bf16[128,2048]{1,0:T(8,128)(2,1)S(1)}) custom-call(bf16[512,768]{1,0:T(8,128)(2,1)S(1)} %copy-done.8, bf16[512,768]{1,0:T(8,128)(2,1)S(1)} %copy-done.10, bf16[2048,768]{1,0:T(8,128)(2,1)S(1)} %bitcast.36, ...), custom_call_target="tpu_custom_call" | custom-call | flops 3221225472 | bytes 8388608 | tf_op jit(solution)/shard_map/input_grads/pallas_call | solution.py:419
  96.3 4.1 %collective-permute-done.18 = bf16[128,2048]{1,0:T(8,128)(2,1)} collective-permute-done((bf16[128,2048]{1,0:T(8,128)(2,1)}, bf16[128,2048]{1,0:T(8,128)(2,1)}, u32[]{:S(2)}, u32[]{:S(2)}) %collective-permute-start.18) | collective-permute-done | bytes 524320 | tf_op jit(solution)/shard_map/ppermute | solution.py:137
  101.7 9.3 %collective-permute-done.17 = bf16[128,2048]{1,0:T(8,128)(2,1)} collective-permute-done((bf16[128,2048]{1,0:T(8,128)(2,1)}, bf16[128,2048]{1,0:T(8,128)(2,1)}, u32[]{:S(2)}, u32[]{:S(2)}) %collective-permute-start.17) | collective-permute-done | bytes 524320 | tf_op jit(solution)/shard_map/ppermute | solution.py:137
  117.1 2.6 %add_convert_fusion.7 = bf16[128,2048]{1,0:T(8,128)(2,1)} fusion(bf16[128,2048]{1,0:T(8,128)(2,1)} %collective-permute-done.18, bf16[128,2048]{1,0:T(8,128)(2,1)} %collective-permute-done.17, bf16[128,2048]{1,0:T(8,128)(2,1)} %collective-permute-done.16, bf16[128,2048]{1,0:T(8,128)(2,1)S(1)} %copy-done.15, f32[128]{0:T(128)S(1)} %get-tuple-element.103, ...), kind=kLoop, calls=%fused_computation.15 | loop fusion | flops 3145728 | bytes 2623488 | tf_op jit(solution)/shard_map/convert_element_type | solution.py:516
  119.8 9.3 %collective-permute-done.30 = bf16[96,2048]{1,0:T(8,128)(2,1)S(1)} collective-permute-done((bf16[96,2048]{1,0:T(8,128)(2,1)S(1)}, bf16[96,2048]{1,0:T(8,128)(2,1)S(1)}, u32[]{:S(2)}, u32[]{:S(2)}) %collective-permute-start.30) | collective-permute-done | bytes 393248 | tf_op jit(solution)/shard_map/ppermute | solution.py:440
  129.2 3.6 %collective-permute-start.33 = (bf16[96,2048]{1,0:T(8,128)(2,1)S(1)}, bf16[96,2048]{1,0:T(8,128)(2,1)S(1)}, u32[]{:S(2)}, u32[]{:S(2)}) collective-permute-start(bf16[96,2048]{1,0:T(8,128)(2,1)S(1)} %add_convert_fusion.8), channel_id=1, source_target_pairs={{8,16},{12,20},{16,8},{20,12},{9,17},{13,21},{17,9},{21,13},{10,18... | collective-permute-start | bytes 1179656 | tf_op jit(solution)/shard_map/ppermute | solution.py:440
  133.1 2.2 %collective-permute-start.26 = (bf16[2,256,768]{2,1,0:T(8,128)(2,1)S(1)}, bf16[2,256,768]{2,1,0:T(8,128)(2,1)S(1)}, u32[]{:S(2)}, u32[]{:S(2)}) collective-permute-start(bf16[2,256,768]{2,1,0:T(8,128)(2,1)S(1)} %add_convert_fusion), channel_id=1, source_target_pairs={{8,16},{12,20},{16,8},{20,12},{9,17},{13,21},{17,9},{21,13},{10,18... | collective-permute-start | bytes 2359304 | tf_op jit(solution)/shard_map/ppermute | solution.py:440
  138.4 4.7 %collective-permute-done.33 = bf16[96,2048]{1,0:T(8,128)(2,1)S(1)} collective-permute-done((bf16[96,2048]{1,0:T(8,128)(2,1)S(1)}, bf16[96,2048]{1,0:T(8,128)(2,1)S(1)}, u32[]{:S(2)}, u32[]{:S(2)}) %collective-permute-start.33) | collective-permute-done | bytes 393248 | tf_op jit(solution)/shard_map/ppermute | solution.py:440
  145.6 3.7 %collective-permute-done.31 = bf16[96,2048]{1,0:T(8,128)(2,1)S(1)} collective-permute-done((bf16[96,2048]{1,0:T(8,128)(2,1)S(1)}, bf16[96,2048]{1,0:T(8,128)(2,1)S(1)}, u32[]{:S(2)}, u32[]{:S(2)}) %collective-permute-start.31) | collective-permute-done | bytes 393248 | tf_op jit(solution)/shard_map/ppermute | solution.py:440
  151.0 7.3 %collective-permute-done.26 = bf16[2,256,768]{2,1,0:T(8,128)(2,1)S(1)} collective-permute-done((bf16[2,256,768]{2,1,0:T(8,128)(2,1)S(1)}, bf16[2,256,768]{2,1,0:T(8,128)(2,1)S(1)}, u32[]{:S(2)}, u32[]{:S(2)}) %collective-permute-start.26) | collective-permute-done | bytes 786464 | tf_op jit(solution)/shard_map/ppermute | solution.py:440
  161.0 2.8 %collective-permute-done.24 = bf16[2,256,768]{2,1,0:T(8,128)(2,1)S(1)} collective-permute-done((bf16[2,256,768]{2,1,0:T(8,128)(2,1)S(1)}, bf16[2,256,768]{2,1,0:T(8,128)(2,1)S(1)}, u32[]{:S(2)}, u32[]{:S(2)}) %collective-permute-start.24) | collective-permute-done | bytes 786464 | tf_op jit(solution)/shard_map/ppermute | solution.py:440
  165.5 3.5 %collective-permute-start.34 = (bf16[96,2048]{1,0:T(8,128)(2,1)S(1)}, bf16[96,2048]{1,0:T(8,128)(2,1)S(1)}, u32[]{:S(2)}, u32[]{:S(2)}) collective-permute-start(bf16[96,2048]{1,0:T(8,128)(2,1)S(1)} %add_convert_fusion.9), channel_id=1, source_target_pairs={{8,16},{12,20},{16,8},{20,12},{9,17},{13,21},{17,9},{21,13},{10,18... | collective-permute-start | bytes 1179656 | tf_op jit(solution)/shard_map/ppermute | solution.py:440
  170.3 2.4 %collective-permute-start.27 = (bf16[2,256,768]{2,1,0:T(8,128)(2,1)S(1)}, bf16[2,256,768]{2,1,0:T(8,128)(2,1)S(1)}, u32[]{:S(2)}, u32[]{:S(2)}) collective-permute-start(bf16[2,256,768]{2,1,0:T(8,128)(2,1)S(1)} %add_convert_fusion.1), channel_id=1, source_target_pairs={{8,16},{12,20},{16,8},{20,12},{9,17},{13,21},{17,9},{21,13},{10,18... | collective-permute-start | bytes 2359304 | tf_op jit(solution)/shard_map/ppermute | solution.py:440
  175.1 4.3 %collective-permute-done.34 = bf16[96,2048]{1,0:T(8,128)(2,1)S(1)} collective-permute-done((bf16[96,2048]{1,0:T(8,128)(2,1)S(1)}, bf16[96,2048]{1,0:T(8,128)(2,1)S(1)}, u32[]{:S(2)}, u32[]{:S(2)}) %collective-permute-start.34) | collective-permute-done | bytes 393248 | tf_op jit(solution)/shard_map/ppermute | solution.py:440
  179.5 3.5 %collective-permute-done.32 = bf16[96,2048]{1,0:T(8,128)(2,1)S(1)} collective-permute-done((bf16[96,2048]{1,0:T(8,128)(2,1)S(1)}, bf16[96,2048]{1,0:T(8,128)(2,1)S(1)}, u32[]{:S(2)}, u32[]{:S(2)}) %collective-permute-start.32) | collective-permute-done | bytes 393248 | tf_op jit(solution)/shard_map/ppermute | solution.py:440
  182.9 2.1 %fusion.20 = bf16[1,96,2048]{2,1,0:T(8,128)(2,1)} fusion(bf16[96,2048]{1,0:T(8,128)(2,1)S(1)} %collective-permute-done.35, bf16[96,2048]{1,0:T(8,128)(2,1)S(1)} %collective-permute-done.34, bf16[96,2048]{1,0:T(8,128)(2,1)S(1)} %collective-permute-done.32, bf16[96,2048]{1,0:T(8,128)(2,1)S(1)} %get-tuple-element.99, pred[]{:T(512)S(6)} %eq.43, pred[]{:T(512)S(6)} %eq.42, ...), kind=kLoop, calls=%fused_computation.38 | loop fusion | flops 3145728 | bytes 2752514 | tf_op jit(solution)/shard_map/broadcast_in_dim | solution.py:518
  185.1 7.8 %collective-permute-done.27 = bf16[2,256,768]{2,1,0:T(8,128)(2,1)S(1)} collective-permute-done((bf16[2,256,768]{2,1,0:T(8,128)(2,1)S(1)}, bf16[2,256,768]{2,1,0:T(8,128)(2,1)S(1)}, u32[]{:S(2)}, u32[]{:S(2)}) %collective-permute-start.27) | collective-permute-done | bytes 786464 | tf_op jit(solution)/shard_map/ppermute | solution.py:440
  192.9 3.1 %collective-permute-done.25 = bf16[2,256,768]{2,1,0:T(8,128)(2,1)S(1)} collective-permute-done((bf16[2,256,768]{2,1,0:T(8,128)(2,1)S(1)}, bf16[2,256,768]{2,1,0:T(8,128)(2,1)S(1)}, u32[]{:S(2)}, u32[]{:S(2)}) %collective-permute-start.25) | collective-permute-done | bytes 786464 | tf_op jit(solution)/shard_map/ppermute | solution.py:440
  (122 shorter events, 59.8 us)
Async XLA Ops:
  0.6 23.3 %collective-permute-start = (bf16[128,2048]{1,0:T(8,128)(2,1)}, bf16[128,2048]{1,0:T(8,128)(2,1)S(1)}, u32[]{:S(2)}, u32[]{:S(2)}) collective-permute-start(bf16[128,2048]{1,0:T(8,128)(2,1)} %refs_0_.1), channel_id=1, source_target_pairs={{0,1},{1,0},{2,3},{3,2},{4,5},{5,4},{6,7},{7,6},{8,9},{9,8},{10,11... | collective-permute-start | bytes 1572872 | tf_op jit(solution)/shard_map/ppermute | solution.py:137
  2.2 21.8 %collective-permute-start.1 = (bf16[128,2048]{1,0:T(8,128)(2,1)}, bf16[128,2048]{1,0:T(8,128)(2,1)S(1)}, u32[]{:S(2)}, u32[]{:S(2)}) collective-permute-start(bf16[128,2048]{1,0:T(8,128)(2,1)} %refs_0_.1), channel_id=1, source_target_pairs={{0,2},{1,3},{2,0},{3,1},{4,6},{5,7},{6,4},{7,5},{8,10},{9,11},{10,... | collective-permute-start | bytes 1572872 | tf_op jit(solution)/shard_map/ppermute | solution.py:137
  8.4 7.6 %collective-permute-start.7 = (bf16[16,2176]{1,0:T(8,128)(2,1)S(1)}, bf16[16,2176]{1,0:T(8,128)(2,1)S(1)}, u32[]{:S(2)}, u32[]{:S(2)}) collective-permute-start(bf16[16,2176]{1,0:T(8,128)(2,1)S(1)} %get-tuple-element.58), channel_id=1, source_target_pairs={{0,16},{4,20},{8,24},{12,28},{16,0},{20,4},{24,8},{28,12},{1,17},{... | collective-permute-start | bytes 208904 | tf_op jit(solution)/shard_map/ppermute | solution.py:123
  13.0 9.7 %collective-permute-start.9 = (bf16[16,2176]{1,0:T(8,128)(2,1)S(1)}, bf16[16,2176]{1,0:T(8,128)(2,1)S(1)}, u32[]{:S(2)}, u32[]{:S(2)}) collective-permute-start(bf16[16,2176]{1,0:T(8,128)(2,1)S(1)} %get-tuple-element.60), channel_id=1, source_target_pairs={{0,24},{4,28},{8,16},{12,20},{16,8},{20,12},{24,0},{28,4},{1,25},{... | collective-permute-start | bytes 208904 | tf_op jit(solution)/shard_map/ppermute | solution.py:123
  16.0 8.0 %collective-permute-start.10 = (bf16[16,2176]{1,0:T(8,128)(2,1)S(1)}, bf16[16,2176]{1,0:T(8,128)(2,1)S(1)}, u32[]{:S(2)}, u32[]{:S(2)}) collective-permute-start(bf16[16,2176]{1,0:T(8,128)(2,1)S(1)} %get-tuple-element.61), channel_id=1, source_target_pairs={{0,28},{4,24},{8,20},{12,16},{16,12},{20,8},{24,4},{28,0},{1,29},{... | collective-permute-start | bytes 208904 | tf_op jit(solution)/shard_map/ppermute | solution.py:123
  24.2 15.5 %collective-permute-start.11 = (bf16[128,2176]{1,0:T(8,128)(2,1)S(1)}, bf16[128,2176]{1,0:T(8,128)(2,1)S(1)}, u32[]{:S(2)}, u32[]{:S(2)}) collective-permute-start(bf16[128,2176]{1,0:T(8,128)(2,1)S(1)} %assemble.1.refs_0_), channel_id=1, source_target_pairs={{0,1},{1,0},{2,3},{3,2},{4,5},{5,4},{6,7},{7,6},{8,9},{9,8},{10,11... | collective-permute-start | bytes 1671176 | tf_op jit(solution)/shard_map/ppermute | solution.py:137
  24.6 16.7 %collective-permute-start.12 = (bf16[128,2176]{1,0:T(8,128)(2,1)S(1)}, bf16[128,2176]{1,0:T(8,128)(2,1)S(1)}, u32[]{:S(2)}, u32[]{:S(2)}) collective-permute-start(bf16[128,2176]{1,0:T(8,128)(2,1)S(1)} %assemble.1.refs_0_), channel_id=1, source_target_pairs={{0,2},{1,3},{2,0},{3,1},{4,6},{5,7},{6,4},{7,5},{8,10},{9,11},{10,... | collective-permute-start | bytes 1671176 | tf_op jit(solution)/shard_map/ppermute | solution.py:137
  27.0 18.8 %collective-permute-start.2 = (bf16[64,2048]{1,0:T(8,128)(2,1)}, bf16[64,2048]{1,0:T(8,128)(2,1)S(1)}, u32[]{:S(2)}, u32[]{:S(2)}) collective-permute-start(bf16[64,2048]{1,0:T(8,128)(2,1)} %slice.80), channel_id=1, source_target_pairs={{0,2},{1,3},{2,0},{3,1},{4,6},{5,7},{6,4},{7,5},{8,10},{9,11},{10,... | collective-permute-start | bytes 786440 | tf_op jit(solution)/shard_map/ppermute | solution.py:137
  28.1 17.7 %collective-permute-start.3 = (bf16[64,2048]{1,0:T(8,128)(2,1)}, bf16[64,2048]{1,0:T(8,128)(2,1)}, u32[]{:S(2)}, u32[]{:S(2)}) collective-permute-start(bf16[64,2048]{1,0:T(8,128)(2,1)} %slice.81), channel_id=1, source_target_pairs={{0,1},{1,0},{2,3},{3,2},{4,5},{5,4},{6,7},{7,6},{8,9},{9,8},{10,11... | collective-permute-start | bytes 786440 | tf_op jit(solution)/shard_map/ppermute | solution.py:137
  39.7 19.1 %collective-permute-start.13 = (bf16[64,2176]{1,0:T(8,128)(2,1)S(1)}, bf16[64,2176]{1,0:T(8,128)(2,1)S(1)}, u32[]{:S(2)}, u32[]{:S(2)}) collective-permute-start(bf16[64,2176]{1,0:T(8,128)(2,1)S(1)} %slice.82), channel_id=1, source_target_pairs={{0,2},{1,3},{2,0},{3,1},{4,6},{5,7},{6,4},{7,5},{8,10},{9,11},{10,... | collective-permute-start | bytes 835592 | tf_op jit(solution)/shard_map/ppermute | solution.py:137
  41.3 17.5 %collective-permute-start.14 = (bf16[64,2176]{1,0:T(8,128)(2,1)S(1)}, bf16[64,2176]{1,0:T(8,128)(2,1)S(1)}, u32[]{:S(2)}, u32[]{:S(2)}) collective-permute-start(bf16[64,2176]{1,0:T(8,128)(2,1)S(1)} %slice.83), channel_id=1, source_target_pairs={{0,1},{1,0},{2,3},{3,2},{4,5},{5,4},{6,7},{7,6},{8,9},{9,8},{10,11... | collective-permute-start | bytes 835592 | tf_op jit(solution)/shard_map/ppermute | solution.py:137
  67.6 11.2 %collective-permute-start.15 = (bf16[1,2,256,768]{3,2,1,0:T(8,128)(2,1)S(1)}, bf16[1,2,256,768]{3,2,1,0:T(8,128)(2,1)S(1)}, u32[]{:S(2)}, u32[]{:S(2)}) collective-permute-start(bf16[1,2,256,768]{3,2,1,0:T(8,128)(2,1)S(1)} %get-tuple-element.72), channel_id=1, source_target_pairs={{0,4},{4,0},{8,12},{12,8},{16,20},{20,16},{24,28},{28,24},{1,5},{5... | collective-permute-start | bytes 2359304 | tf_op jit(solution)/shard_map/ppermute | solution.py:460
  72.3 41.9 %collective-permute-start.29 = (bf16[4,96,2048]{2,1,0:T(8,128)(2,1)}, bf16[4,96,2048]{2,1,0:T(8,128)(2,1)}, u32[]{:S(2)}, u32[]{:S(2)}) collective-permute-start(bf16[4,96,2048]{2,1,0:T(8,128)(2,1)} %get-tuple-element.75), channel_id=1, source_target_pairs={{0,4},{4,0},{8,12},{12,8},{16,20},{20,16},{24,28},{28,24},{1,5},{5... | collective-permute-start | bytes 4718600 | tf_op jit(solution)/shard_map/ppermute | solution.py:460
  78.8 56.6 %collective-permute-start.22 = (bf16[3,2,256,768]{3,2,1,0:T(8,128)(2,1)}, bf16[3,2,256,768]{3,2,1,0:T(8,128)(2,1)}, u32[]{:S(2)}, u32[]{:S(2)}) collective-permute-start(bf16[3,2,256,768]{3,2,1,0:T(8,128)(2,1)} %get-tuple-element.77), channel_id=1, source_target_pairs={{0,4},{4,0},{8,12},{12,8},{16,20},{20,16},{24,28},{28,24},{1,5},{5... | collective-permute-start | bytes 7077896 | tf_op jit(solution)/shard_map/ppermute | solution.py:460
  84.4 16.0 %collective-permute-start.18 = (bf16[128,2048]{1,0:T(8,128)(2,1)}, bf16[128,2048]{1,0:T(8,128)(2,1)}, u32[]{:S(2)}, u32[]{:S(2)}) collective-permute-start(bf16[128,2048]{1,0:T(8,128)(2,1)} %get-tuple-element.83), channel_id=1, source_target_pairs={{0,3},{1,2},{2,1},{3,0},{4,7},{5,6},{6,5},{7,4},{8,11},{9,10},{10,... | collective-permute-start | bytes 1572872 | tf_op jit(solution)/shard_map/ppermute | solution.py:137
  87.0 24.0 %collective-permute-start.17 = (bf16[128,2048]{1,0:T(8,128)(2,1)}, bf16[128,2048]{1,0:T(8,128)(2,1)}, u32[]{:S(2)}, u32[]{:S(2)}) collective-permute-start(bf16[128,2048]{1,0:T(8,128)(2,1)} %get-tuple-element.82), channel_id=1, source_target_pairs={{0,2},{1,3},{2,0},{3,1},{4,6},{5,7},{6,4},{7,5},{8,10},{9,11},{10,... | collective-permute-start | bytes 1572872 | tf_op jit(solution)/shard_map/ppermute | solution.py:137
  87.5 25.3 %collective-permute-start.16 = (bf16[128,2048]{1,0:T(8,128)(2,1)}, bf16[128,2048]{1,0:T(8,128)(2,1)}, u32[]{:S(2)}, u32[]{:S(2)}) collective-permute-start(bf16[128,2048]{1,0:T(8,128)(2,1)} %get-tuple-element.81), channel_id=1, source_target_pairs={{0,1},{1,0},{2,3},{3,2},{4,5},{5,4},{6,7},{7,6},{8,9},{9,8},{10,11... | collective-permute-start | bytes 1572872 | tf_op jit(solution)/shard_map/ppermute | solution.py:137
  100.4 32.5 %collective-permute-start.23 = (bf16[2,256,768]{2,1,0:T(8,128)(2,1)S(1)}, bf16[2,256,768]{2,1,0:T(8,128)(2,1)S(1)}, u32[]{:S(2)}, u32[]{:S(2)}) collective-permute-start(bf16[2,256,768]{2,1,0:T(8,128)(2,1)S(1)} %copy-done.22), channel_id=1, source_target_pairs={{0,8},{4,12},{24,16},{28,20},{1,9},{5,13},{25,17},{29,21},{2,10},{... | collective-permute-start | bytes 2359304 | tf_op jit(solution)/shard_map/ppermute | solution.py:440
  111.0 54.5 %collective-permute-start.21 = (bf16[128,2048]{1,0:T(8,128)(2,1)S(1)}, bf16[128,2048]{1,0:T(8,128)(2,1)S(1)}, u32[]{:S(2)}, u32[]{:S(2)}) collective-permute-start(bf16[128,2048]{1,0:T(8,128)(2,1)S(1)} %get-tuple-element.92), channel_id=1, source_target_pairs={{0,3},{1,2},{2,1},{3,0},{4,7},{5,6},{6,5},{7,4},{8,11},{9,10},{10,... | collective-permute-start | bytes 1572872 | tf_op jit(solution)/shard_map/ppermute | solution.py:137
  112.8 56.2 %collective-permute-start.20 = (bf16[128,2048]{1,0:T(8,128)(2,1)S(1)}, bf16[128,2048]{1,0:T(8,128)(2,1)S(1)}, u32[]{:S(2)}, u32[]{:S(2)}) collective-permute-start(bf16[128,2048]{1,0:T(8,128)(2,1)S(1)} %get-tuple-element.90), channel_id=1, source_target_pairs={{0,2},{1,3},{2,0},{3,1},{4,6},{5,7},{6,4},{7,5},{8,10},{9,11},{10,... | collective-permute-start | bytes 1572872 | tf_op jit(solution)/shard_map/ppermute | solution.py:137
  115.8 13.3 %collective-permute-start.30 = (bf16[96,2048]{1,0:T(8,128)(2,1)S(1)}, bf16[96,2048]{1,0:T(8,128)(2,1)S(1)}, u32[]{:S(2)}, u32[]{:S(2)}) collective-permute-start(bf16[96,2048]{1,0:T(8,128)(2,1)S(1)} %get-tuple-element.108), channel_id=1, source_target_pairs={{0,8},{4,12},{24,16},{28,20},{1,9},{5,13},{25,17},{29,21},{2,10},{... | collective-permute-start | bytes 1179656 | tf_op jit(solution)/shard_map/ppermute | solution.py:440
  129.2 13.9 %collective-permute-start.33 = (bf16[96,2048]{1,0:T(8,128)(2,1)S(1)}, bf16[96,2048]{1,0:T(8,128)(2,1)S(1)}, u32[]{:S(2)}, u32[]{:S(2)}) collective-permute-start(bf16[96,2048]{1,0:T(8,128)(2,1)S(1)} %add_convert_fusion.8), channel_id=1, source_target_pairs={{8,16},{12,20},{16,8},{20,12},{9,17},{13,21},{17,9},{21,13},{10,18... | collective-permute-start | bytes 1179656 | tf_op jit(solution)/shard_map/ppermute | solution.py:440
  133.1 25.2 %collective-permute-start.26 = (bf16[2,256,768]{2,1,0:T(8,128)(2,1)S(1)}, bf16[2,256,768]{2,1,0:T(8,128)(2,1)S(1)}, u32[]{:S(2)}, u32[]{:S(2)}) collective-permute-start(bf16[2,256,768]{2,1,0:T(8,128)(2,1)S(1)} %add_convert_fusion), channel_id=1, source_target_pairs={{8,16},{12,20},{16,8},{20,12},{9,17},{13,21},{17,9},{21,13},{10,18... | collective-permute-start | bytes 2359304 | tf_op jit(solution)/shard_map/ppermute | solution.py:440
  135.3 13.9 %collective-permute-start.31 = (bf16[96,2048]{1,0:T(8,128)(2,1)S(1)}, bf16[96,2048]{1,0:T(8,128)(2,1)S(1)}, u32[]{:S(2)}, u32[]{:S(2)}) collective-permute-start(bf16[96,2048]{1,0:T(8,128)(2,1)S(1)} %get-tuple-element.98), channel_id=1, source_target_pairs={{0,8},{4,12},{24,16},{28,20},{1,9},{5,13},{25,17},{29,21},{2,10},{... | collective-permute-start | bytes 1179656 | tf_op jit(solution)/shard_map/ppermute | solution.py:440
  143.2 20.6 %collective-permute-start.24 = (bf16[2,256,768]{2,1,0:T(8,128)(2,1)S(1)}, bf16[2,256,768]{2,1,0:T(8,128)(2,1)S(1)}, u32[]{:S(2)}, u32[]{:S(2)}) collective-permute-start(bf16[2,256,768]{2,1,0:T(8,128)(2,1)S(1)} %get-tuple-element.94), channel_id=1, source_target_pairs={{0,8},{4,12},{24,16},{28,20},{1,9},{5,13},{25,17},{29,21},{2,10},{... | collective-permute-start | bytes 2359304 | tf_op jit(solution)/shard_map/ppermute | solution.py:440
  149.3 21.0 %collective-permute-start.19 = (bf16[128,2048]{1,0:T(8,128)(2,1)S(1)}, bf16[128,2048]{1,0:T(8,128)(2,1)S(1)}, u32[]{:S(2)}, u32[]{:S(2)}) collective-permute-start(bf16[128,2048]{1,0:T(8,128)(2,1)S(1)} %get-tuple-element.88), channel_id=1, source_target_pairs={{0,1},{1,0},{2,3},{3,2},{4,5},{5,4},{6,7},{7,6},{8,9},{9,8},{10,11... | collective-permute-start | bytes 1572872 | tf_op jit(solution)/shard_map/ppermute | solution.py:137
  158.3 14.4 %collective-permute-start.35 = (bf16[96,2048]{1,0:T(8,128)(2,1)S(1)}, bf16[96,2048]{1,0:T(8,128)(2,1)S(1)}, u32[]{:S(2)}, u32[]{:S(2)}) collective-permute-start(bf16[96,2048]{1,0:T(8,128)(2,1)S(1)} %fusion.11), channel_id=1, source_target_pairs={{16,24},{20,28},{8,0},{12,4},{17,25},{21,29},{9,1},{13,5},{18,26},... | collective-permute-start | bytes 1179656 | tf_op jit(solution)/shard_map/ppermute | solution.py:440
  163.8 21.3 %collective-permute-start.28 = (bf16[2,256,768]{2,1,0:T(8,128)(2,1)S(1)}, bf16[2,256,768]{2,1,0:T(8,128)(2,1)S(1)}, u32[]{:S(2)}, u32[]{:S(2)}) collective-permute-start(bf16[2,256,768]{2,1,0:T(8,128)(2,1)S(1)} %fusion.5), channel_id=1, source_target_pairs={{16,24},{20,28},{8,0},{12,4},{17,25},{21,29},{9,1},{13,5},{18,26},... | collective-permute-start | bytes 2359304 | tf_op jit(solution)/shard_map/ppermute | solution.py:440
  165.5 13.9 %collective-permute-start.34 = (bf16[96,2048]{1,0:T(8,128)(2,1)S(1)}, bf16[96,2048]{1,0:T(8,128)(2,1)S(1)}, u32[]{:S(2)}, u32[]{:S(2)}) collective-permute-start(bf16[96,2048]{1,0:T(8,128)(2,1)S(1)} %add_convert_fusion.9), channel_id=1, source_target_pairs={{8,16},{12,20},{16,8},{20,12},{9,17},{13,21},{17,9},{21,13},{10,18... | collective-permute-start | bytes 1179656 | tf_op jit(solution)/shard_map/ppermute | solution.py:440
  169.0 13.9 %collective-permute-start.32 = (bf16[96,2048]{1,0:T(8,128)(2,1)S(1)}, bf16[96,2048]{1,0:T(8,128)(2,1)S(1)}, u32[]{:S(2)}, u32[]{:S(2)}) collective-permute-start(bf16[96,2048]{1,0:T(8,128)(2,1)S(1)} %get-tuple-element.99), channel_id=1, source_target_pairs={{0,8},{4,12},{24,16},{28,20},{1,9},{5,13},{25,17},{29,21},{2,10},{... | collective-permute-start | bytes 1179656 | tf_op jit(solution)/shard_map/ppermute | solution.py:440
  170.3 22.6 %collective-permute-start.27 = (bf16[2,256,768]{2,1,0:T(8,128)(2,1)S(1)}, bf16[2,256,768]{2,1,0:T(8,128)(2,1)S(1)}, u32[]{:S(2)}, u32[]{:S(2)}) collective-permute-start(bf16[2,256,768]{2,1,0:T(8,128)(2,1)S(1)} %add_convert_fusion.1), channel_id=1, source_target_pairs={{8,16},{12,20},{16,8},{20,12},{9,17},{13,21},{17,9},{21,13},{10,18... | collective-permute-start | bytes 2359304 | tf_op jit(solution)/shard_map/ppermute | solution.py:440
  172.7 23.3 %collective-permute-start.25 = (bf16[2,256,768]{2,1,0:T(8,128)(2,1)S(1)}, bf16[2,256,768]{2,1,0:T(8,128)(2,1)S(1)}, u32[]{:S(2)}, u32[]{:S(2)}) collective-permute-start(bf16[2,256,768]{2,1,0:T(8,128)(2,1)S(1)} %get-tuple-element.95), channel_id=1, source_target_pairs={{0,8},{4,12},{24,16},{28,20},{1,9},{5,13},{25,17},{29,21},{2,10},{... | collective-permute-start | bytes 2359304 | tf_op jit(solution)/shard_map/ppermute | solution.py:440
  (29 other events, 172.8 us)

commit v2 on v1

v2 whole, which is shorter than its diff:
```python
import functools
import math

import jax
import jax.numpy as jnp
from jax import lax
from jax.experimental import pallas as pl
from jax.experimental.pallas import tpu as pltpu
from jax.sharding import PartitionSpec as P

CORES = 2
LANES = 128
F32 = jnp.float32
BF16 = jnp.bfloat16
MIB = 1 << 20
BIG = 24
EARLY = (1, 2, 7)


def contract(left, right, left_dim, right_dim):
    return lax.dot_general(left, right, (((left_dim,), (right_dim,)), ((), ())), preferred_element_type=F32)


def params(mib, **more):
    return pltpu.CompilerParams(vmem_limit_bytes=mib * MIB, **more)


def room(rows, width):
    return 16 + rows * width * 10 // MIB


def cost(flops, bytes_accessed):
    return pl.CostEstimate(flops=flops, bytes_accessed=bytes_accessed, transcendentals=0)


def vmem():
    return pl.BlockSpec(memory_space=pltpu.VMEM)


def in_hbm(value):
    return pltpu.with_memory_space_constraint(value, pltpu.HBM)


def hbm():
    return pl.BlockSpec(memory_space=pl.ANY)


LENGTH, ADV, GATES = 0, 1, 2
PARTS = 3


def pick_kernel(n_dp, dest_hbm, len_hbm, adv_hbm, rows_hbm, *refs):
    outs, (dest_ref, len_ref, adv_ref, sems, row_sems) = refs[:n_dp], refs[n_dp:]
    small = [
        pltpu.make_async_copy(source, target, sems.at[i])
        for i, (source, target) in enumerate(((dest_hbm, dest_ref), (len_hbm, len_ref), (adv_hbm, adv_ref)))
    ]
    for copy in small:
        copy.start()
    seqs, slot, width = rows_hbm.shape
    lane = lax.broadcasted_iota(jnp.int32, (slot, LANES), 1)
    which = lax.broadcasted_iota(jnp.int32, (1, seqs), 1)
    me = lax.axis_index("dp")
    small[0].wait()
    found, copies = [], []
    for i, out in enumerate(outs):
        seq = jnp.int32(0)
        live = jnp.int32(0)
        for s in range(seqs):
            hit = dest_ref[0, 0, s] == (me ^ i)
            seq = jnp.where(hit, s, seq)
            live = jnp.where(hit, 1, live)
        found.append((seq, live))
        copies.append(pltpu.make_async_copy(rows_hbm.at[seq], out.at[:, pl.ds(0, width)], row_sems.at[i]))
        copies[-1].start()
    small[1].wait()
    small[2].wait()
    lengths = len_ref[0].astype(F32)
    advs = adv_ref[0].astype(F32)
    for (seq, live), out in zip(found, outs):
        mine = (which == seq) & (live == 1)
        length = jnp.sum(jnp.where(mine, lengths, 0.0), axis=1, keepdims=True)
        adv = jnp.sum(jnp.where(mine, advs, 0.0), axis=1, keepdims=True)
        out[:, width:] = jnp.where(lane == LENGTH, length, jnp.where(lane == ADV, adv, 0.0)).astype(BF16)
    for copy in copies:
        copy.wait()


def pick(dest, lengths, adv, rows, n_dp):
    seqs, slot, width = rows.shape
    return pl.pallas_call(
        functools.partial(pick_kernel, n_dp),
        out_shape=[jax.ShapeDtypeStruct((slot, width + LANES), BF16)] * n_dp,
        in_specs=[hbm()] * 4,
        out_specs=[vmem()] * n_dp,
        scratch_shapes=[
            pltpu.SMEM(dest.shape, jnp.int32),
            pltpu.VMEM(lengths.shape, lengths.dtype),
            pltpu.VMEM(adv.shape, adv.dtype),
            pltpu.SemaphoreType.DMA((3,)),
            pltpu.SemaphoreType.DMA((n_dp,)),
        ],
        compiler_params=params(16),
        name="pick",
    )(*[in_hbm(value) for value in (dest, lengths, adv, rows)])


def gate_notes(ids, gates):
    note = lax.broadcasted_iota(jnp.int32, (LANES, ids.shape[1]), 0) - GATES
    expert, part = note // PARTS, note % PARTS
    value = jnp.zeros(note.shape, F32)
    for k in range(ids.shape[0]):
        value = value + jnp.where(ids[k : k + 1] == expert, gates[k : k + 1], 0.0)
    value = jnp.where(note < 0, 0.0, value)
    high = value.astype(BF16).astype(F32)
    middle = (value - high).astype(BF16).astype(F32)
    low = value - high - middle
    return jnp.where(part == 0, high, jnp.where(part == 1, middle, low))


def assemble_kernel(n_dp, ids_ref, gates_ref, *refs):
    pieces, x_ref = refs[:n_dp], refs[-1]
    slot, wide = pieces[0].shape
    width = wide - LANES
    me = lax.axis_index("dp")
    for i, piece in enumerate(pieces):
        at = pl.multiple_of((me ^ i) * slot, slot)
        x_ref[pl.ds(at, slot), :] = piece[...]
    notes = gate_notes(ids_ref[...], gates_ref[...]).T
    x_ref[:, width:] = (x_ref[:, width:].astype(F32) + notes).astype(BF16)


def assemble(pieces, ids, gates, after):
    slot, wide = pieces[0].shape
    n_dp = len(pieces)
    return pl.pallas_call(
        functools.partial(assemble_kernel, n_dp),
        out_shape=jax.ShapeDtypeStruct((slot * n_dp, wide), BF16),
        in_specs=[vmem()] * (2 + n_dp) + [hbm()] * len(after),
        out_specs=vmem(),
        compiler_params=params(16),
        name="assemble",
    )(ids, gates, *pieces, *after)


def send_sequences(gen_rows, gen_lengths, gen_adv, destination, n_dp):
    seq_dev = destination.shape[2]
    slot = gen_rows.shape[0] // seq_dev
    pieces = pick(destination, gen_lengths, gen_adv, gen_rows.reshape(seq_dev, slot, gen_rows.shape[1]), n_dp)
    return [pieces[0]] + [
        lax.ppermute(pieces[i], "dp", [(d, d ^ i) for d in range(n_dp)]) for i in range(1, n_dp)
    ]


def place_sequences(got, seq_dev, ids, gates, after):
    n_dp = len(got)
    if n_dp == seq_dev:
        return assemble(got, ids.T, gates.T, after)
    slot, wide = got[0].shape
    width = wide - LANES
    g = lax.axis_index("dp")
    stack = jnp.stack(got)[jnp.arange(n_dp, dtype=jnp.int32) ^ g]
    arrived = stack[:, 0, width + LENGTH] > 0
    arrival = jnp.cumsum(arrived.astype(jnp.int32)) - 1
    chosen = arrived[None, :] & (arrival[None, :] == jnp.arange(seq_dev, dtype=jnp.int32)[:, None])
    from_peer = jnp.sum(jnp.where(chosen, jnp.arange(n_dp, dtype=jnp.int32)[None, :], 0), axis=1)
    x = stack[from_peer].reshape(seq_dev * slot, wide)
    notes = (x[:, width:].astype(F32) + gate_notes(ids.T, gates.T).T).astype(BF16)
    return jnp.concatenate([x[:, :width], notes], axis=1)


def swap(value, i, n_ex):
    return lax.ppermute(value, "expert", [(d, d ^ i) for d in range(n_ex)])


def gather_rows(rows, n_ex, between=None):
    if n_ex != 4:
        return [rows] + [swap(rows, i, n_ex) for i in range(1, n_ex)]
    half = rows.shape[0] // 2
    first = swap(rows, 1, n_ex)
    second = swap(rows, 2, n_ex)
    low, high = first[:half], second[half:]
    if between:
        low, high, *_ = lax.optimization_barrier((low, high, *between))
    return [rows, first, second, swap(low, 2, n_ex), swap(high, 1, n_ex)]


def with_last(pieces, size):
    at, cut = 0, sum(p.shape[0] for p in pieces) - size
    for i, piece in enumerate(pieces):
        if at == cut:
            return pieces[:i], pieces[i:]
        at += piece.shape[0]


def tie(value, *others):
    return lax.optimization_barrier((value,) + others)[0]


def load_pieces(pieces, whole, sems):
    at, copies = 0, []
    for i, piece in enumerate(pieces):
        size = piece.shape[0]
        copies.append(pltpu.make_async_copy(piece, whole.at[pl.ds(at, size)], sems.at[i]))
        at += size
    for copy in copies:
        copy.start()
    for copy in copies:
        copy.wait()


def hidden_grad_kernel(count, w_ref, *refs):
    pieces, (out, whole_out, whole, sems, out_sem) = refs[:count], refs[count:]
    step = pl.program_id(0)

    @pl.when(step == 0)
    def _():
        load_pieces(pieces, whole, sems)
        pltpu.make_async_copy(whole, whole_out, out_sem).start()

    out[...] = contract(whole[...], w_ref[...], 1, 1)

    @pl.when(step == pl.num_programs(0) - 1)
    def _():
        pltpu.make_async_copy(whole, whole_out, out_sem).wait()


def hidden_grad(pieces, w_down):
    rows = sum(p.shape[0] for p in pieces)
    units, width = w_down.shape
    tile = 256
    return pl.pallas_call(
        functools.partial(hidden_grad_kernel, len(pieces)),
        grid=(units // tile,),
        out_shape=[jax.ShapeDtypeStruct((rows, units), F32), jax.ShapeDtypeStruct((rows, width), BF16)],
        in_specs=[pl.BlockSpec((tile, width), lambda j: (j, 0))] + [hbm()] * len(pieces),
        out_specs=[pl.BlockSpec((rows, tile), lambda j: (0, j)), hbm()],
        scratch_shapes=[
            pltpu.VMEM((rows, width), BF16),
            pltpu.SemaphoreType.DMA((len(pieces),)),
            pltpu.SemaphoreType.DMA,
        ],
        compiler_params=params(BIG),
        cost_estimate=cost(2 * rows * units * width, 2 * units * width + 4 * rows * width),
        name="hidden_grad",
    )(w_down, *pieces)


def shard_place(shard, n_dp):
    me = lax.axis_index("dp")
    n_z = n_dp // CORES
    chip, core = shard // CORES, shard % CORES
    at = jnp.where(me // CORES >= n_z // 2, chip, n_z - 1 - chip)
    return jnp.where(core == me % CORES, n_z, 0) + at


def units_kernel(count, slot, first, n_dp, wg_ref, wu_ref, hg_ref, *refs):
    if not first:
        refs = refs[6:]
    pieces, refs = refs[:count], refs[count:]
    gate_out, up_out, hid_out, turned_hs, turned_x, gates_out, whole, gs_ref, sems = refs
    step = pl.program_id(0)
    rows, wide = whole.shape
    width = wide - LANES

    @pl.when(step == 0)
    def _():
        load_pieces(pieces, whole, sems)
        notes = whole[:, width:].astype(F32)
        lane = lax.broadcasted_iota(jnp.int32, notes.shape, 1) - GATES - PARTS * lax.axis_index("expert")
        gates = jnp.sum(jnp.where((lane >= 0) & (lane < PARTS), notes, 0.0), axis=1, keepdims=True)
        length, adv = notes[:, LENGTH : LENGTH + 1], notes[:, ADV : ADV + 1]
        position = lax.broadcasted_iota(jnp.int32, (rows, 1), 0) % slot
        gates_out[...] = gates
        gs_ref[...] = jnp.where(position.astype(F32) < length, gates * (adv / length), 0.0)
        strip = width // n_dp
        for i in range(n_dp):
            at = pl.multiple_of(shard_place(i, n_dp) * strip, strip)
            turned_x[pl.ds(at, strip), :] = whole[:, i * strip : (i + 1) * strip].T

    x = whole[:, :width]
    gate = jnp.dot(x, wg_ref[...], preferred_element_type=F32)
    up = jnp.dot(x, wu_ref[...], preferred_element_type=F32)
    gs = gs_ref[...]
    sig = jax.nn.sigmoid(gate)
    act = gate * sig
    hid = (act * up).astype(BF16)
    hid_out[...] = hid
    turned = (hid.astype(F32) * gs).astype(BF16).T
    tile, shard = turned.shape[0], turned_hs.shape[0] // n_dp
    chunk = math.gcd(tile, shard)
    for i in range(tile // chunk):
        row = step * tile + i * chunk
        at = shard_place(row // shard, n_dp) * shard + row % shard
        turned_hs[pl.ds(pl.multiple_of(at, chunk), chunk), :] = turned[i * chunk : (i + 1) * chunk]
    hg = hg_ref[...] * gs
    gate_out[...] = (hg * up * sig * (1.0 + gate * (1.0 - sig))).astype(BF16)
    up_out[...] = (hg * act).astype(BF16)


def hidden_units(pieces, w_gate, w_up, hg, slot, n_dp, before=None):
    total, units = hg.shape
    width = w_gate.shape[0]
    rows = sum(p.shape[0] for p in pieces)
    tile = 256
    at = 0 if before is None else total // rows - 1
    columns = pl.BlockSpec((rows, tile), lambda j: (at, j))
    weights = pl.BlockSpec((width, tile), lambda j: (0, j))
    before = before or []
    return pl.pallas_call(
        functools.partial(units_kernel, len(pieces), slot, not before, n_dp),
        grid=(units // tile,),
        out_shape=[jax.ShapeDtypeStruct((total, units), BF16)] * 3
        + [
            jax.ShapeDtypeStruct((units, total), BF16),
            jax.ShapeDtypeStruct((width, total), BF16),
            jax.ShapeDtypeStruct((total, 1), F32),
        ],
        in_specs=[weights, weights, columns] + [hbm()] * (len(before) + len(pieces)),
        out_specs=[columns] * 3
        + [
            pl.BlockSpec((units, rows), lambda j: (0, at)),
            pl.BlockSpec((width, rows), lambda j: (0, at)),
            pl.BlockSpec((rows, 1), lambda j: (at, 0)),
        ],
        scratch_shapes=[
            pltpu.VMEM((rows, width + LANES), BF16),
            pltpu.VMEM((rows, 1), F32),
            pltpu.SemaphoreType.DMA((len(pieces),)),
        ],
        input_output_aliases={3 + i: i for i in range(len(before))},
        compiler_params=params(room(rows, width)),
        cost_estimate=cost(4 * rows * units * width, 4 * units * width + 4 * rows * width),
        name="hidden_units",
    )(w_gate, w_up, hg, *before, *pieces)


def far_grads_kernel(x_ref, gate_ref, up_ref, other, mine):
    gate = jnp.dot(x_ref[...], gate_ref[...], preferred_element_type=F32).astype(BF16)
    up = jnp.dot(x_ref[...], up_ref[...], preferred_element_type=F32).astype(BF16)

    @pl.when(pl.program_id(0) == 0)
    def _():
        other[0] = gate
        other[1] = up

    @pl.when(pl.program_id(0) == 1)
    def _():
        mine[0] = gate
        mine[1] = up


def far_grads(turned_x, gate_grad, up_grad, n_dp):
    rows, units = gate_grad.shape
    width = turned_x.shape[0]
    n_z, shard = n_dp // CORES, width // n_dp
    out = pl.BlockSpec((2, shard, units), lambda k: (0, 0, 0))
    whole = pl.BlockSpec((rows, units), lambda k: (0, 0))
    return pl.pallas_call(
        far_grads_kernel,
        grid=(CORES,),
        in_specs=[pl.BlockSpec((shard, rows), lambda k: (k * n_z, 0)), whole, whole],
        out_specs=[out, out],
        out_shape=[pltpu.HBM((2, shard, units), BF16)] * 2,
        compiler_params=params(BIG),
        cost_estimate=cost(8 * rows * units * shard, 16 * units * shard + 4 * rows * units),
        name="far_grads",
    )(turned_x, gate_grad, up_grad)


def rest_grads_kernel(shard, x_ref, gate_ref, up_ref, other, mine):
    count = other.shape[0]
    for k, out in enumerate((other, mine)):
        x = x_ref[pl.ds((k * (count + 1) + 1) * shard, count * shard), :]
        for p, grad in enumerate((gate_ref, up_ref)):
            value = jnp.dot(x, grad[...], preferred_element_type=F32).astype(BF16)
            for b in range(count):
                out[b, p] = value[b * shard : (b + 1) * shard]


def rest_grads(turned_x, gate_grad, up_grad, n_dp):
    rows, units = gate_grad.shape
    width = turned_x.shape[0]
    n_z, shard = n_dp // CORES, width // n_dp
    tile = 256
    columns = pl.BlockSpec((rows, tile), lambda j: (0, j))
    out = pl.BlockSpec((n_z - 1, 2, shard, tile), lambda j: (0, 0, 0, j))
    return pl.pallas_call(
        functools.partial(rest_grads_kernel, shard),
        grid=(units // tile,),
        in_specs=[pl.BlockSpec((width, rows), lambda j: (0, 0)), columns, columns],
        out_specs=[out, out],
        out_shape=[pltpu.HBM((n_z - 1, 2, shard, units), BF16)] * 2,
        compiler_params=params(room(rows, width)),
        cost_estimate=cost(4 * rows * units * width, 4 * units * width + 4 * rows * units),
        name="rest_grads",
    )(turned_x, gate_grad, up_grad)


def row_grad_kernel(hid_ref, dy_ref, other, mine):
    n_z, shard, tile = mine.shape
    value = jnp.dot(hid_ref[...], dy_ref[...], preferred_element_type=F32).astype(BF16)
    for k, out in enumerate((other, mine)):
        for b in range(n_z):
            at = (k * n_z + b) * shard
            out[b] = value[at : at + shard]


def row_grad(turned_hid, dy, n_dp):
    units, rows = turned_hid.shape
    width = dy.shape[1]
    n_z, shard = n_dp // CORES, units // n_dp
    tile = 512
    block = pl.BlockSpec((n_z, shard, tile), lambda j: (0, 0, j))
    return pl.pallas_call(
        row_grad_kernel,
        grid=(width // tile,),
        in_specs=[pl.BlockSpec((units, rows), lambda j: (0, 0)), pl.BlockSpec((rows, tile), lambda j: (0, j))],
        out_specs=[block, block],
        out_shape=[pltpu.HBM((n_z, shard, width), BF16)] * 2,
        compiler_params=params(BIG),
        cost_estimate=cost(2 * rows * units * width, 2 * units * width + 2 * rows * width),
        name="row_grad",
    )(turned_hid, dy)


def outputs_kernel(layer_groups, grad_groups, hid_ref, gates_ref, gate_ref, up_ref, wd_ref, wg_ref, wu_ref, *outs):
    layer = jnp.dot(hid_ref[...], wd_ref[...], preferred_element_type=F32) * gates_ref[...]
    value = contract(gate_ref[...], wg_ref[...], 1, 1) + contract(up_ref[...], wu_ref[...], 1, 1)
    size = outs[0].shape[1]
    for result, groups, refs in (
        (layer.astype(BF16), layer_groups, outs[: len(layer_groups)]),
        (value.astype(BF16), grad_groups, outs[len(layer_groups) :]),
    ):
        for group, out in zip(groups, refs):
            for n, i in enumerate(group):
                out[n] = result[i * size : (i + 1) * size]


def outputs(hid, gates, gate_grad, up_grad, w_down, w_gate, w_up, n_ex, layer_groups, grad_groups):
    rows, units = hid.shape
    width = w_down.shape[1]
    tile = 512
    size = rows // n_ex
    whole = pl.BlockSpec((rows, units), lambda j: (0, 0))
    columns = pl.BlockSpec((units, tile), lambda j: (0, j))
    weights = pl.BlockSpec((tile, units), lambda j: (j, 0))
    counts = [len(group) for group in layer_groups + grad_groups]
    return pl.pallas_call(
        functools.partial(outputs_kernel, layer_groups, grad_groups),
        grid=(width // tile,),
        out_shape=[jax.ShapeDtypeStruct((n, size, width), BF16) for n in counts],
        in_specs=[whole, pl.BlockSpec((rows, 1), lambda j: (0, 0)), whole, whole, columns, weights, weights],
        out_specs=[pl.BlockSpec((n, size, tile), lambda j: (0, 0, j)) for n in counts],
        compiler_params=params(room(rows, width)),
        cost_estimate=cost(6 * rows * units * width, 6 * units * width + 4 * rows * width),
        name="outputs",
    )(hid, gates, gate_grad, up_grad, w_down, w_gate, w_up)


def add(*parts):
    return sum(part.astype(F32) for part in parts).astype(BF16)


def outputs_home(hid, gates, gate_grad, up_grad, w_down, w_gate, w_up, n_ex):
    weights = (hid, gates, gate_grad, up_grad, w_down, w_gate, w_up, n_ex)
    if n_ex != 4:
        single = [[i] for i in range(n_ex)]
        parts = outputs(*weights, single, single)
        layer, grad = [], []
        for i in range(n_ex):
            layer.append(swap(parts[i][0], i, n_ex) if i else parts[i][0])
            grad.append(swap(parts[n_ex + i][0], i, n_ex) if i else parts[n_ex + i][0])
        return add(*layer), add(*grad)
    layer0, layer2, layer13, grad0, grad1, grad23 = outputs(*weights, [[0], [2], [1, 3]], [[0], [1], [2, 3]])
    layer_got = swap(layer13, 1, n_ex)
    grad_got = swap(grad23, 2, n_ex)
    layer_last = swap(add(layer2[0], layer_got[1]), 2, n_ex)
    grad_last = swap(add(grad1[0], grad_got[1]), 1, n_ex)
    return add(layer0[0], layer_got[0], layer_last), add(grad0[0], grad_got[0], grad_last)


def line_permute(value, links, n_dp):
    n_z = n_dp // CORES
    pairs = [pair for k in links for pair in ((k, k + 1), (n_z - 1 - k, n_z - 2 - k))]
    return lax.ppermute(value, "dp", [(CORES * a + c, CORES * b + c) for a, b in pairs for c in range(CORES)])


def on_device(
    gen_rows, gen_lengths, gen_adv, destination, expert_ids, gate_values, cotangent, w_gate, w_up, w_down
):
    n_dp = lax.axis_size("dp")
    n_ex = lax.axis_size("expert")
    n_z = n_dp // CORES
    size = cotangent.shape[0]
    slot = gen_rows.shape[0] // destination.shape[2]
    weight_gate, weight_up, weight_down = w_gate[0], w_up[0], w_down[0]
    g = lax.axis_index("dp")
    z = g // CORES
    near = jnp.minimum(z, n_z - 1 - z)
    other_core = [(d, d ^ 1) for d in range(n_dp)]

    def swap_core(value):
        return lax.ppermute(value, "dp", other_core)

    got = send_sequences(gen_rows, gen_lengths, gen_adv, destination, n_dp)
    cot_pieces = gather_rows(cotangent, n_ex, [got[i] for i in EARLY if i < n_dp])
    x = place_sequences(got, destination.shape[2], expert_ids, gate_values, cot_pieces[3:5])
    hg, dy_all = hidden_grad(cot_pieces, weight_down)
    x_pieces = gather_rows(x, n_ex, [hg])
    early, late = with_last(x_pieces, size)
    before = hidden_units(early, weight_gate, weight_up, hg, slot, n_dp)
    gate_grad, up_grad, hid, turned_hs, turned_x, gates = hidden_units(
        late, weight_gate, weight_up, hg, slot, n_dp, before
    )

    far = n_z - 1
    rest = list(range(far - 1, -1, -1))
    far_other, far_mine = far_grads(turned_x, gate_grad, up_grad, n_dp)
    row_other, row_mine = row_grad(tie(turned_hs, far_other), dy_all, n_dp)
    rest_other, rest_mine = rest_grads(tie(turned_x, row_other), gate_grad, up_grad, n_dp)
    far_got, row_got, rest_got = swap_core(far_other), swap_core(row_other), swap_core(rest_other)
    sums = [[None, None] for _ in range(n_z)]
    sums[far][0] = add(tie(far_mine, rest_other), far_got)
    for k in range(n_z):
        sums[k][1] = add(row_mine[far - k], row_got[far - k])
    for i, k in enumerate(rest):
        sums[k][0] = add(rest_mine[i], rest_got[i])

    passed = {}
    ends = [[], []]
    joined = n_z > 3
    at_end = near == 0

    def own(link, d, p):
        return sums[d if link < n_z // 2 else far - d][p]

    for link in range(n_z - 1 - joined):
        issued = []
        for d in range(far, link + (joined and link == 0), -1):
            for p in range(2):
                value = own(link, d, p)
                if link > 0:
                    value = add(value, passed[link - 1, d, p])
                ahead = 2 if link == 0 else 1
                if len(issued) >= ahead:
                    value = tie(value, issued[-ahead])
                got = line_permute(value, [link], n_dp)
                issued.append(got)
                passed[link, d, p] = got
                if d == link + 1:
                    ends[p].append(got)
        if link == 0:
            firsts = issued
    if joined:
        for p in range(2):
            value = jnp.where(at_end, own(0, 1, p), add(own(n_z - 2, far, p), passed[n_z - 3, far, p]))
            got = line_permute(tie(value, firsts[-2]), [0, n_z - 2], n_dp)
            firsts.append(got)
            ends[p].append(got)
    totals = []
    for p in range(2):
        mine = sum(jnp.where(near == k, sums[k][p].astype(F32), 0.0) for k in range((n_z + 1) // 2))
        mine = lax.optimization_barrier(add(mine, *ends[p][:-1]))
        totals.append(add(mine, ends[p][-1]))

    hid, gate_grad, up_grad, _ = lax.optimization_barrier((hid, gate_grad, up_grad, firsts[0]))
    layer_out, input_grad = outputs_home(
        hid, gates, gate_grad, up_grad, weight_down, weight_gate, weight_up, n_ex
    )
    return layer_out, input_grad, totals[0][0:1], totals[0][1:2], totals[1][None]


def solution(mesh):
    rows = P(("dp", "expert"), None)
    seqs = P("dp", "expert", None)
    weights = P("expert", None, None)
    shards = P("expert", "dp", None)
    return jax.shard_map(
        on_device,
        mesh=mesh,
        in_specs=(rows, seqs, seqs, seqs, rows, rows, rows, weights, weights, weights),
        out_specs=(rows, rows, shards, shards, shards),
        check_vma=False,
    )
```

time: 200 us -> 169 us (0.84)
  local copies, waits for them, and re-layouts: 17.2 us -> 5.12 us
  waiting for transfers between devices: 82.8 us -> 74 us
  Pallas kernels: 35.6 us -> 29.5 us
  starting transfers between devices: 46.2 us -> 41 us
    ppermute x12 -> x10, waiting for transfers between devices: 46.5 us -> 35.7 us  [line_permute(): lax.ppermute(value, 'dp', [(CORES * a + c, CORES * b + c) for a, b in pai...]
    unnamed x52 -> x34, local copies, waits for them, and re-layouts: 14.8 us -> 4.11 us
    ppermute x14 -> x12, waiting for transfers between devices: 27.2 us -> 32.9 us  [swap(): return lax.ppermute(value, 'expert', [(d, d ^ i) for d in range(n_ex)])]
    ppermute x14 -> x12, starting transfers between devices: 16.6 us -> 11.3 us  [swap(): return lax.ppermute(value, 'expert', [(d, d ^ i) for d in range(n_ex)])]
    pallas_call x5 -> x4, Pallas kernels: 20.3 us -> 16.2 us  [the longest x1 6.12 us: outputs(): pl.pallas_call(functools.partial(outputs_kernel, layer_groups, grad_group...]
    ppermute x7, waiting for transfers between devices: 9.14 us -> 5.3 us  [send_sequences(): lax.ppermute(pieces[i], 'dp', [(d, d ^ i) for d in range(n_dp)])]
    select_n x0 -> x2, other arithmetic: none -> 3.28 us  [on_device(): jnp.where(at_end, own(0, 1, p), add(own(n_z - 2, far, p), passed[n_z - 3,...]
    convert_element_type x1 -> x0, other arithmetic: 2.63 us -> none  [on_device(): sum((gates[i] * outs[i].astype(F32) for i in range(n_ex))).astype(BF16)]
  transfers between devices with their start and end apart: 36 -> 32, of which waited for: 18 -> 18; matrix products, arithmetic and copies ran while one was open for 9% -> 10% of each run, Pallas kernels for 15% -> 14%
where the time goes in v2:
time: 169 us; the launch traced here: 167 us
  waiting for transfers between devices  74 us (44%)
  starting transfers between devices  41 us (24%)
  Pallas kernels  29.5 us (17%)
  other arithmetic  16.1 us (10%)
  local copies, waits for them, and re-layouts  5.12 us (3%)
    ppermute x10, waiting for transfers between devices, line_permute(): lax.ppermute(value, 'dp', [(CORES * a + c, CORES * b + c) for a, b in pai...  35.7 us
    ppermute x12, waiting for transfers between devices, swap(): return lax.ppermute(value, 'expert', [(d, d ^ i) for d in range(n_ex)])  32.9 us
    ppermute x10, starting transfers between devices, line_permute(): lax.ppermute(value, 'dp', [(CORES * a + c, CORES * b + c) for a, b in pai...  21.6 us
    convert_element_type x14, other arithmetic, add(): return sum((part.astype(F32) for part in parts)).astype(BF16)  12 us
    ppermute x12, starting transfers between devices, swap(): return lax.ppermute(value, 'expert', [(d, d ^ i) for d in range(n_ex)])  11.3 us
    pallas_call x2, Pallas kernels, hidden_units(): pl.pallas_call(functools.partial(units_kernel, len(pieces), slot, not bef...  8.37 us
    ppermute x7, starting transfers between devices, send_sequences(): lax.ppermute(pieces[i], 'dp', [(d, d ^ i) for d in range(n_dp)])  7.48 us
    pallas_call x1, Pallas kernels, outputs(): pl.pallas_call(functools.partial(outputs_kernel, layer_groups, grad_group...  6.12 us
  transfers between devices with their start and end apart: 32, of which 18 were waited for; matrix products, arithmetic and copies ran while one was open for 10% of the time, Pallas kernels for 14%

profile of v2, /device:TPU:12, one launch (start us, length us, event | category | flops | bytes accessed | tf_op | source)
XLA Modules:
  0.0 166.7 jit_solution(4317362973683811224)
XLA Ops:
  2.7 2.1 %pick.1 = (bf16[16,2176]{1,0:T(8,128)(2,1)S(1)}, bf16[16,2176]{1,0:T(8,128)(2,1)S(1)}, bf16[16,2176]{1,0:T(8,128)(2,1)S(1)}, bf16[16,2176]{1,0:T(8,128)(2,1)S(1)...) custom-call(s32[1,1,8]{2,1,0:T(1,128)} %dest_hbm.1, ...), custom_call_target="tpu_custom_call" | custom-call | tf_op jit(solution)/shard_map/pick/pallas_call | solution.py:91
  5.4 2.5 %collective-permute-start.4 = (bf16[16,2176]{1,0:T(8,128)(2,1)S(1)}, bf16[16,2176]{1,0:T(8,128)(2,1)S(1)}, u32[]{:S(2)}, u32[]{:S(2)}) collective-permute-start(bf16[16,2176]{1,0:T(8,128)(2,1)S(1)} %get-tuple-element.58), channel_id=1, source_target_pairs={{0,28},{4,24},{8,20},{12,16},{16,12},{20,8},{24,4},{28,0},{1,29},{... | collective-permute-start | bytes 208904 | tf_op jit(solution)/shard_map/ppermute | solution.py:151
  7.9 6.7 %collective-permute-done.refs_1_ = bf16[128,2048]{1,0:T(8,128)(2,1)S(1)} collective-permute-done((bf16[128,2048]{1,0:T(8,128)(2,1)}, bf16[128,2048]{1,0:T(8,128)(2,1)S(1)}, u32[]{:S(2)}, u32[]{:S(2)}) %collective-permute-start) | collective-permute-done | bytes 524320 | tf_op jit(solution)/shard_map/ppermute | solution.py:173
  19.6 2.0 %collective-permute-done.10.refs_6_ = bf16[16,2176]{1,0:T(8,128)(2,1)S(1)} collective-permute-done((bf16[16,2176]{1,0:T(8,128)(2,1)S(1)}, bf16[16,2176]{1,0:T(8,128)(2,1)S(1)}, u32[]{:S(2)}, u32[]{:S(2)}) %collective-permute-start.10) | collective-permute-done | bytes 69664 | tf_op jit(solution)/shard_map/ppermute | solution.py:151
  21.6 1.8 %collective-permute-start.9 = (bf16[16,2176]{1,0:T(8,128)(2,1)S(1)}, bf16[16,2176]{1,0:T(8,128)(2,1)S(1)}, u32[]{:S(2)}, u32[]{:S(2)}) collective-permute-start(bf16[16,2176]{1,0:T(8,128)(2,1)S(1)} %get-tuple-element.65), channel_id=1, source_target_pairs={{0,20},{4,16},{8,28},{12,24},{16,4},{20,0},{24,12},{28,8},{1,21},{... | collective-permute-start | bytes 208904 | tf_op jit(solution)/shard_map/ppermute | solution.py:151
  24.2 2.5 %collective-permute-done.9.refs_5_ = bf16[16,2176]{1,0:T(8,128)(2,1)S(1)} collective-permute-done((bf16[16,2176]{1,0:T(8,128)(2,1)S(1)}, bf16[16,2176]{1,0:T(8,128)(2,1)S(1)}, u32[]{:S(2)}, u32[]{:S(2)}) %collective-permute-start.9) | collective-permute-done | bytes 69664 | tf_op jit(solution)/shard_map/ppermute | solution.py:151
  26.9 1.7 %collective-permute-start.11 = (bf16[128,2176]{1,0:T(8,128)(2,1)S(1)}, bf16[128,2176]{1,0:T(8,128)(2,1)S(1)}, u32[]{:S(2)}, u32[]{:S(2)}) collective-permute-start(bf16[128,2176]{1,0:T(8,128)(2,1)S(1)} %assemble.1.refs_0_), channel_id=1, source_target_pairs={{0,1},{1,0},{2,3},{3,2},{4,5},{5,4},{6,7},{7,6},{8,9},{9,8},{10,11... | collective-permute-start | bytes 1671176 | tf_op jit(solution)/shard_map/ppermute | solution.py:173
  31.1 2.7 %hidden_grad.1 = (f32[512,768]{1,0:T(8,128)S(1)}, bf16[512,2048]{1,0:T(8,128)(2,1)S(1)}) custom-call(bf16[768,2048]{1,0:T(8,128)(2,1)S(1)} %bitcast.60, bf16[128,2048]{1,0:T(8,128)(2,1)S(1)} %copy-done.13, bf16[128,2048]{1,0:T(8,128)(2,1)S(1)} %collective-permute-done.refs_1_, bf16[128,2048]{1,0:T(8,128)(2,1)S(1)} %collective-permute-done.1.refs_2_, ...), custom_call_target="tpu_custom_call" | custom-call | flops 1610612736 | bytes 7340032 | tf_op jit(solution)/shard_map/hidden_grad/pallas_call | solution.py:232
  33.9 7.7 %collective-permute-done.11.refs_1_ = bf16[128,2176]{1,0:T(8,128)(2,1)S(1)} collective-permute-done((bf16[128,2176]{1,0:T(8,128)(2,1)S(1)}, bf16[128,2176]{1,0:T(8,128)(2,1)S(1)}, u32[]{:S(2)}, u32[]{:S(2)}) %collective-permute-start.11) | collective-permute-done | bytes 557088 | tf_op jit(solution)/shard_map/ppermute | solution.py:173
  41.6 2.0 %collective-permute-done.12.refs_2_ = bf16[128,2176]{1,0:T(8,128)(2,1)S(1)} collective-permute-done((bf16[128,2176]{1,0:T(8,128)(2,1)S(1)}, bf16[128,2176]{1,0:T(8,128)(2,1)S(1)}, u32[]{:S(2)}, u32[]{:S(2)}) %collective-permute-start.12) | collective-permute-done | bytes 557088 | tf_op jit(solution)/shard_map/ppermute | solution.py:173
  45.8 5.5 %hidden_units.2 = (bf16[512,768]{1,0:T(8,128)(2,1)S(1)}, bf16[512,768]{1,0:T(8,128)(2,1)S(1)}, bf16[512,768]{1,0:T(8,128)(2,1)S(1)}, bf16[768,512]{1,0:T(8,128)(...) custom-call(bf16[2048,768]{1,0:T(8,128)(2,1)S(1)} %bitcast.52, bf16[2048,768]{1,0:T(8,128)(2,1)S(1)} %bitcast.55, ...), custom_call_target="tpu_custom_call" | custom-call | flops 2415919104 | bytes 9437184 | tf_op jit(solution)/shard_map/hidden_units/pallas_call | solution.py:310
  53.8 2.9 %hidden_units.3 = (bf16[512,768]{1,0:T(8,128)(2,1)S(1)}, bf16[512,768]{1,0:T(8,128)(2,1)S(1)}, bf16[512,768]{1,0:T(8,128)(2,1)S(1)}, bf16[768,512]{1,0:T(8,128)(...) custom-call(bf16[2048,768]{1,0:T(8,128)(2,1)S(1)} %bitcast.53, ...), custom_call_target="tpu_custom_call", output_to_operand_aliasing={{0}: (3, {}), {1}: (4, {}), {2}: (5, {}), {3}: (6, {}), {4}... | custom-call | flops 805306368 | bytes 7340032 | tf_op jit(solution)/shard_map/hidden_units/pallas_call | solution.py:310
  56.7 2.5 %far_grads.1 = (bf16[2,256,768]{2,1,0:T(8,128)(2,1)}, bf16[2,256,768]{2,1,0:T(8,128)(2,1)}) custom-call(bf16[2048,512]{1,0:T(8,128)(2,1)S(1)} %get-tuple-element.85.x_ref, bf16[512,768]{1,0:T(8,128)(2,1)S(1)} %get-tuple-element.90.gate_ref, bf16[512,768]{1,0:T(8,128)(2,1)S(1)} %get-tuple-element.91.up_ref), custom_call_target="tpu_custom_call" | custom-call | flops 805306368 | bytes 4718592 | tf_op jit(solution)/shard_map/far_grads/pallas_call | solution.py:359
  59.2 3.5 %row_grad.1 = (bf16[4,96,2048]{2,1,0:T(8,128)(2,1)}, bf16[4,96,2048]{2,1,0:T(8,128)(2,1)}) custom-call(bf16[768,512]{1,0:T(8,128)(2,1)S(1)} %get-tuple-element.82.hid_ref, bf16[512,2048]{1,0:T(8,128)(2,1)S(1)} %get-tuple-element.83.dy_ref), custom_call_target="tpu_custom_call" | custom-call | flops 1610612736 | bytes 5242880 | tf_op jit(solution)/shard_map/row_grad/pallas_call | solution.py:415
  63.2 4.0 %rest_grads.1 = (bf16[3,2,256,768]{3,2,1,0:T(8,128)(2,1)}, bf16[3,2,256,768]{3,2,1,0:T(8,128)(2,1)}) custom-call(bf16[2048,512]{1,0:T(8,128)(2,1)S(1)} %get-tuple-element.85.x_ref, bf16[512,768]{1,0:T(8,128)(2,1)S(1)} %get-tuple-element.90.gate_ref, bf16[512,768]{1,0:T(8,128)(2,1)S(1)} %get-tuple-element.91.up_ref), custom_call_target="tpu_custom_call" | custom-call | flops 3221225472 | bytes 7864320 | tf_op jit(solution)/shard_map/rest_grads/pallas_call | solution.py:388
  69.7 20.3 %collective-permute-done.16 = bf16[2,256,768]{2,1,0:T(8,128)(2,1)} collective-permute-done((bf16[2,256,768]{2,1,0:T(8,128)(2,1)}, bf16[2,256,768]{2,1,0:T(8,128)(2,1)}, u32[]{:S(2)}, u32[]{:S(2)}) %collective-permute-start.16) | collective-permute-done | bytes 786464 | tf_op jit(solution)/shard_map/ppermute | solution.py:486
  90.0 1.7 %add_convert_fusion.1 = bf16[2,256,768]{2,1,0:T(8,128)(2,1)S(1)} fusion(bf16[2,256,768]{2,1,0:T(8,128)(2,1)} %collective-permute-done.16, bf16[2,256,768]{2,1,0:T(8,128)(2,1)} %add_convert_fusion.6), kind=kLoop, calls=%fused_computation.7 | loop fusion | flops 1572864 | bytes 2359296 | tf_op jit(solution)/shard_map/convert_element_type | solution.py:462
  91.8 2.1 %collective-permute-start.25 = (bf16[2,256,768]{2,1,0:T(8,128)(2,1)S(1)}, bf16[2,256,768]{2,1,0:T(8,128)(2,1)S(1)}, u32[]{:S(2)}, u32[]{:S(2)}) collective-permute-start(bf16[2,256,768]{2,1,0:T(8,128)(2,1)S(1)} %add_convert_fusion.1), channel_id=1, source_target_pairs={{8,16},{12,20},{16,8},{20,12},{9,17},{13,21},{17,9},{21,13},{10,18... | collective-permute-start | bytes 2359304 | tf_op jit(solution)/shard_map/ppermute | solution.py:486
  97.9 1.9 %copy-done.12 = bf16[1,768,2048]{2,1,0:T(8,128)(2,1)S(1)} copy-done((bf16[1,768,2048]{2,1,0:T(8,128)(2,1)S(1)}, bf16[1,768,2048]{2,1,0:T(8,128)(2,1)}, u32[]{:S(2)}) %copy-start.12) | copy-done | bytes 3145752
  99.8 6.1 %outputs.1 = (bf16[1,128,2048]{2,1,0:T(8,128)(2,1)S(1)}, bf16[1,128,2048]{2,1,0:T(8,128)(2,1)S(1)}, bf16[2,128,2048]{2,1,0:T(8,128)(2,1)S(1)}, bf16[1,128,2048]{...) custom-call(bf16[512,768]{1,0:T(8,128)(2,1)S(1)} %copy-done.8, ...), custom_call_target="tpu_custom_call" | custom-call | flops 4831838208 | bytes 13631488 | tf_op jit(solution)/shard_map/outputs/pallas_call | solution.py:449
  108.9 3.5 %collective-permute-done.25 = bf16[2,256,768]{2,1,0:T(8,128)(2,1)S(1)} collective-permute-done((bf16[2,256,768]{2,1,0:T(8,128)(2,1)S(1)}, bf16[2,256,768]{2,1,0:T(8,128)(2,1)S(1)}, u32[]{:S(2)}, u32[]{:S(2)}) %collective-permute-start.25) | collective-permute-done | bytes 786464 | tf_op jit(solution)/shard_map/ppermute | solution.py:486
  112.4 2.2 %collective-permute-start.26 = (bf16[96,2048]{1,0:T(8,128)(2,1)S(1)}, bf16[96,2048]{1,0:T(8,128)(2,1)S(1)}, u32[]{:S(2)}, u32[]{:S(2)}) collective-permute-start(bf16[96,2048]{1,0:T(8,128)(2,1)S(1)} %add_convert_fusion.14), channel_id=1, source_target_pairs={{8,16},{12,20},{16,8},{20,12},{9,17},{13,21},{17,9},{21,13},{10,18... | collective-permute-start | bytes 1179656 | tf_op jit(solution)/shard_map/ppermute | solution.py:486
  117.4 1.9 %fusion.13 = bf16[2,256,768]{2,1,0:T(8,128)(2,1)S(1)} fusion(bf16[2,256,768]{2,1,0:T(8,128)(2,1)S(1)} %collective-permute-done.25, pred[]{:T(512)S(6)} %eq.4, bf16[3,2,256,768]{3,2,1,0:T(8,128)(2,1)} %collective-permute-done.21, bf16[3,2,256,768]{3,2,1,0:T(8,128)(2,1)S(1)} %copy-done.14), kind=kLoop, calls=%fused_computation.28 | loop fusion | flops 5111808 | bytes 4718593 | tf_op jit(solution)/shard_map/jit(_where)/select_n | solution.py:557
  119.4 10.8 %collective-permute-done.19 = bf16[2,128,2048]{2,1,0:T(8,128)(2,1)S(1)} collective-permute-done((bf16[2,128,2048]{2,1,0:T(8,128)(2,1)S(1)}, bf16[2,128,2048]{2,1,0:T(8,128)(2,1)S(1)}, u32[]{:S(2)}, u32[]{:S(2)}) %collective-permute-start.19) | collective-permute-done | bytes 1048608 | tf_op jit(solution)/shard_map/ppermute | solution.py:173
  133.7 2.7 %collective-permute-start.31 = (bf16[96,2048]{1,0:T(8,128)(2,1)S(1)}, bf16[96,2048]{1,0:T(8,128)(2,1)S(1)}, u32[]{:S(2)}, u32[]{:S(2)}) collective-permute-start(bf16[96,2048]{1,0:T(8,128)(2,1)S(1)} %fusion.21), channel_id=1, source_target_pairs={{0,8},{4,12},{24,16},{28,20},{16,24},{20,28},{8,0},{12,4},{1,9},{5... | collective-permute-start | bytes 1179656 | tf_op jit(solution)/shard_map/ppermute | solution.py:486
  136.9 3.7 %collective-permute-start.27 = (bf16[2,256,768]{2,1,0:T(8,128)(2,1)S(1)}, bf16[2,256,768]{2,1,0:T(8,128)(2,1)S(1)}, u32[]{:S(2)}, u32[]{:S(2)}) collective-permute-start(bf16[2,256,768]{2,1,0:T(8,128)(2,1)S(1)} %add_convert_fusion.2), channel_id=1, source_target_pairs={{8,16},{12,20},{16,8},{20,12},{9,17},{13,21},{17,9},{21,13},{10,18... | collective-permute-start | bytes 2359304 | tf_op jit(solution)/shard_map/ppermute | solution.py:486
  140.6 1.9 %collective-permute-done.20 = bf16[128,2048]{1,0:T(8,128)(2,1)S(1)} collective-permute-done((bf16[128,2048]{1,0:T(8,128)(2,1)S(1)}, bf16[128,2048]{1,0:T(8,128)(2,1)S(1)}, u32[]{:S(2)}, u32[]{:S(2)}) %collective-permute-start.20) | collective-permute-done | bytes 524320 | tf_op jit(solution)/shard_map/ppermute | solution.py:173
  143.6 2.1 %collective-permute-start.28 = (bf16[2,256,768]{2,1,0:T(8,128)(2,1)S(1)}, bf16[2,256,768]{2,1,0:T(8,128)(2,1)S(1)}, u32[]{:S(2)}, u32[]{:S(2)}) collective-permute-start(bf16[2,256,768]{2,1,0:T(8,128)(2,1)S(1)} %fusion.13), channel_id=1, source_target_pairs={{0,8},{4,12},{24,16},{28,20},{16,24},{20,28},{8,0},{12,4},{1,9},{5... | collective-permute-start | bytes 2359304 | tf_op jit(solution)/shard_map/ppermute | solution.py:486
  146.7 8.1 %collective-permute-done.27 = bf16[2,256,768]{2,1,0:T(8,128)(2,1)S(1)} collective-permute-done((bf16[2,256,768]{2,1,0:T(8,128)(2,1)S(1)}, bf16[2,256,768]{2,1,0:T(8,128)(2,1)S(1)}, u32[]{:S(2)}, u32[]{:S(2)}) %collective-permute-start.27) | collective-permute-done | bytes 786464 | tf_op jit(solution)/shard_map/ppermute | solution.py:486
  154.8 3.5 %collective-permute-start.30 = (bf16[96,2048]{1,0:T(8,128)(2,1)S(1)}, bf16[96,2048]{1,0:T(8,128)(2,1)S(1)}, u32[]{:S(2)}, u32[]{:S(2)}) collective-permute-start(bf16[96,2048]{1,0:T(8,128)(2,1)S(1)} %add_convert_fusion.10), channel_id=1, source_target_pairs={{8,16},{12,20},{16,8},{20,12},{9,17},{13,21},{17,9},{21,13},{10,18... | collective-permute-start | bytes 1179656 | tf_op jit(solution)/shard_map/ppermute | solution.py:486
  158.3 2.0 %fusion.2 = bf16[2,256,768]{2,1,0:T(8,128)(2,1)S(1)} fusion(bf16[2,256,768]{2,1,0:T(8,128)(2,1)S(1)} %collective-permute-done.27, pred[]{:T(512)S(6)} %eq.10, pred[]{:T(512)S(6)} %eq.4, bf16[3,2,256,768]{3,2,1,0:T(8,128)(2,1)} %collective-permute-done.21, bf16[3,2,256,768]{3,2,1,0:T(8,128)(2,1)S(1)} %copy-done.14), kind=kLoop, calls=%fused_computation.4 | loop fusion | flops 6291456 | bytes 4718594 | tf_op jit(solution)/shard_map/convert_element_type | solution.py:462
  162.0 2.5 %collective-permute-done.30 = bf16[96,2048]{1,0:T(8,128)(2,1)S(1)} collective-permute-done((bf16[96,2048]{1,0:T(8,128)(2,1)S(1)}, bf16[96,2048]{1,0:T(8,128)(2,1)S(1)}, u32[]{:S(2)}, u32[]{:S(2)}) %collective-permute-start.30) | collective-permute-done | bytes 393248 | tf_op jit(solution)/shard_map/ppermute | solution.py:486
  (97 shorter events, 38.7 us)
Async XLA Ops:
  0.7 13.9 %collective-permute-start = (bf16[128,2048]{1,0:T(8,128)(2,1)}, bf16[128,2048]{1,0:T(8,128)(2,1)S(1)}, u32[]{:S(2)}, u32[]{:S(2)}) collective-permute-start(bf16[128,2048]{1,0:T(8,128)(2,1)} %refs_0_.1), channel_id=1, source_target_pairs={{0,1},{1,0},{2,3},{3,2},{4,5},{5,4},{6,7},{7,6},{8,9},{9,8},{10,11... | collective-permute-start | bytes 1572872 | tf_op jit(solution)/shard_map/ppermute | solution.py:173
  2.2 13.6 %collective-permute-start.1 = (bf16[128,2048]{1,0:T(8,128)(2,1)}, bf16[128,2048]{1,0:T(8,128)(2,1)S(1)}, u32[]{:S(2)}, u32[]{:S(2)}) collective-permute-start(bf16[128,2048]{1,0:T(8,128)(2,1)} %refs_0_.1), channel_id=1, source_target_pairs={{0,2},{1,3},{2,0},{3,1},{4,6},{5,7},{6,4},{7,5},{8,10},{9,11},{10,... | collective-permute-start | bytes 1572872 | tf_op jit(solution)/shard_map/ppermute | solution.py:173
  4.8 11.0 %collective-permute-start.2 = (bf16[16,2176]{1,0:T(8,128)(2,1)S(1)}, bf16[16,2176]{1,0:T(8,128)(2,1)S(1)}, u32[]{:S(2)}, u32[]{:S(2)}) collective-permute-start(bf16[16,2176]{1,0:T(8,128)(2,1)S(1)} %get-tuple-element.56), channel_id=1, source_target_pairs={{0,4},{4,0},{8,12},{12,8},{16,20},{20,16},{24,28},{28,24},{1,5},{5... | collective-permute-start | bytes 208904 | tf_op jit(solution)/shard_map/ppermute | solution.py:151
  4.9 10.9 %collective-permute-start.3 = (bf16[16,2176]{1,0:T(8,128)(2,1)S(1)}, bf16[16,2176]{1,0:T(8,128)(2,1)S(1)}, u32[]{:S(2)}, u32[]{:S(2)}) collective-permute-start(bf16[16,2176]{1,0:T(8,128)(2,1)S(1)} %get-tuple-element.57), channel_id=1, source_target_pairs={{0,8},{4,12},{8,0},{12,4},{16,24},{20,28},{24,16},{28,20},{1,9},{5... | collective-permute-start | bytes 208904 | tf_op jit(solution)/shard_map/ppermute | solution.py:151
  5.4 10.4 %collective-permute-start.4 = (bf16[16,2176]{1,0:T(8,128)(2,1)S(1)}, bf16[16,2176]{1,0:T(8,128)(2,1)S(1)}, u32[]{:S(2)}, u32[]{:S(2)}) collective-permute-start(bf16[16,2176]{1,0:T(8,128)(2,1)S(1)} %get-tuple-element.58), channel_id=1, source_target_pairs={{0,28},{4,24},{8,20},{12,16},{16,12},{20,8},{24,4},{28,0},{1,29},{... | collective-permute-start | bytes 208904 | tf_op jit(solution)/shard_map/ppermute | solution.py:151
  15.9 10.8 %collective-permute-start.5 = (bf16[64,2048]{1,0:T(8,128)(2,1)S(1)}, bf16[64,2048]{1,0:T(8,128)(2,1)S(1)}, u32[]{:S(2)}, u32[]{:S(2)}) collective-permute-start(bf16[64,2048]{1,0:T(8,128)(2,1)S(1)} %slice.96), channel_id=1, source_target_pairs={{0,2},{1,3},{2,0},{3,1},{4,6},{5,7},{6,4},{7,5},{8,10},{9,11},{10,... | collective-permute-start | bytes 786440 | tf_op jit(solution)/shard_map/ppermute | solution.py:173
  16.4 10.3 %collective-permute-start.6 = (bf16[64,2048]{1,0:T(8,128)(2,1)S(1)}, bf16[64,2048]{1,0:T(8,128)(2,1)S(1)}, u32[]{:S(2)}, u32[]{:S(2)}) collective-permute-start(bf16[64,2048]{1,0:T(8,128)(2,1)S(1)} %slice.97), channel_id=1, source_target_pairs={{0,1},{1,0},{2,3},{3,2},{4,5},{5,4},{6,7},{7,6},{8,9},{9,8},{10,11... | collective-permute-start | bytes 786440 | tf_op jit(solution)/shard_map/ppermute | solution.py:173
  17.0 4.7 %collective-permute-start.10 = (bf16[16,2176]{1,0:T(8,128)(2,1)S(1)}, bf16[16,2176]{1,0:T(8,128)(2,1)S(1)}, u32[]{:S(2)}, u32[]{:S(2)}) collective-permute-start(bf16[16,2176]{1,0:T(8,128)(2,1)S(1)} %get-tuple-element.66), channel_id=1, source_target_pairs={{0,24},{4,28},{8,16},{12,20},{16,8},{20,12},{24,0},{28,4},{1,25},{... | collective-permute-start | bytes 208904 | tf_op jit(solution)/shard_map/ppermute | solution.py:151
  18.5 4.8 %collective-permute-start.7 = (bf16[16,2176]{1,0:T(8,128)(2,1)S(1)}, bf16[16,2176]{1,0:T(8,128)(2,1)S(1)}, u32[]{:S(2)}, u32[]{:S(2)}) collective-permute-start(bf16[16,2176]{1,0:T(8,128)(2,1)S(1)} %get-tuple-element.63), channel_id=1, source_target_pairs={{0,12},{4,8},{8,4},{12,0},{16,28},{20,24},{24,20},{28,16},{1,13},{... | collective-permute-start | bytes 208904 | tf_op jit(solution)/shard_map/ppermute | solution.py:151
  18.5 5.7 %collective-permute-start.8 = (bf16[16,2176]{1,0:T(8,128)(2,1)S(1)}, bf16[16,2176]{1,0:T(8,128)(2,1)S(1)}, u32[]{:S(2)}, u32[]{:S(2)}) collective-permute-start(bf16[16,2176]{1,0:T(8,128)(2,1)S(1)} %get-tuple-element.64), channel_id=1, source_target_pairs={{0,16},{4,20},{8,24},{12,28},{16,0},{20,4},{24,8},{28,12},{1,17},{... | collective-permute-start | bytes 208904 | tf_op jit(solution)/shard_map/ppermute | solution.py:151
  21.6 5.1 %collective-permute-start.9 = (bf16[16,2176]{1,0:T(8,128)(2,1)S(1)}, bf16[16,2176]{1,0:T(8,128)(2,1)S(1)}, u32[]{:S(2)}, u32[]{:S(2)}) collective-permute-start(bf16[16,2176]{1,0:T(8,128)(2,1)S(1)} %get-tuple-element.65), channel_id=1, source_target_pairs={{0,20},{4,16},{8,28},{12,24},{16,4},{20,0},{24,12},{28,8},{1,21},{... | collective-permute-start | bytes 208904 | tf_op jit(solution)/shard_map/ppermute | solution.py:151
  26.9 14.7 %collective-permute-start.11 = (bf16[128,2176]{1,0:T(8,128)(2,1)S(1)}, bf16[128,2176]{1,0:T(8,128)(2,1)S(1)}, u32[]{:S(2)}, u32[]{:S(2)}) collective-permute-start(bf16[128,2176]{1,0:T(8,128)(2,1)S(1)} %assemble.1.refs_0_), channel_id=1, source_target_pairs={{0,1},{1,0},{2,3},{3,2},{4,5},{5,4},{6,7},{7,6},{8,9},{9,8},{10,11... | collective-permute-start | bytes 1671176 | tf_op jit(solution)/shard_map/ppermute | solution.py:173
  28.6 15.1 %collective-permute-start.12 = (bf16[128,2176]{1,0:T(8,128)(2,1)S(1)}, bf16[128,2176]{1,0:T(8,128)(2,1)S(1)}, u32[]{:S(2)}, u32[]{:S(2)}) collective-permute-start(bf16[128,2176]{1,0:T(8,128)(2,1)S(1)} %assemble.1.refs_0_), channel_id=1, source_target_pairs={{0,2},{1,3},{2,0},{3,1},{4,6},{5,7},{6,4},{7,5},{8,10},{9,11},{10,... | collective-permute-start | bytes 1671176 | tf_op jit(solution)/shard_map/ppermute | solution.py:173
  43.6 8.9 %collective-permute-start.13 = (bf16[64,2176]{1,0:T(8,128)(2,1)S(1)}, bf16[64,2176]{1,0:T(8,128)(2,1)S(1)}, u32[]{:S(2)}, u32[]{:S(2)}) collective-permute-start(bf16[64,2176]{1,0:T(8,128)(2,1)S(1)} %slice.98), channel_id=1, source_target_pairs={{0,2},{1,3},{2,0},{3,1},{4,6},{5,7},{6,4},{7,5},{8,10},{9,11},{10,... | collective-permute-start | bytes 835592 | tf_op jit(solution)/shard_map/ppermute | solution.py:173
  45.2 8.5 %collective-permute-start.14 = (bf16[64,2176]{1,0:T(8,128)(2,1)S(1)}, bf16[64,2176]{1,0:T(8,128)(2,1)S(1)}, u32[]{:S(2)}, u32[]{:S(2)}) collective-permute-start(bf16[64,2176]{1,0:T(8,128)(2,1)S(1)} %slice.99), channel_id=1, source_target_pairs={{0,1},{1,0},{2,3},{3,2},{4,5},{5,4},{6,7},{7,6},{8,9},{9,8},{10,11... | collective-permute-start | bytes 835592 | tf_op jit(solution)/shard_map/ppermute | solution.py:173
  59.2 8.1 %collective-permute-start.15 = (bf16[2,256,768]{2,1,0:T(8,128)(2,1)}, bf16[2,256,768]{2,1,0:T(8,128)(2,1)S(1)}, u32[]{:S(2)}, u32[]{:S(2)}) collective-permute-start(bf16[2,256,768]{2,1,0:T(8,128)(2,1)} %get-tuple-element.81), channel_id=1, source_target_pairs={{0,4},{4,0},{8,12},{12,8},{16,20},{20,16},{24,28},{28,24},{1,5},{5... | collective-permute-start | bytes 2359304 | tf_op jit(solution)/shard_map/ppermute | solution.py:504
  62.7 31.1 %collective-permute-start.23 = (bf16[4,96,2048]{2,1,0:T(8,128)(2,1)}, bf16[4,96,2048]{2,1,0:T(8,128)(2,1)}, u32[]{:S(2)}, u32[]{:S(2)}) collective-permute-start(bf16[4,96,2048]{2,1,0:T(8,128)(2,1)} %get-tuple-element.84), channel_id=1, source_target_pairs={{0,4},{4,0},{8,12},{12,8},{16,20},{20,16},{24,28},{28,24},{1,5},{5... | collective-permute-start | bytes 4718600 | tf_op jit(solution)/shard_map/ppermute | solution.py:504
  68.3 21.7 %collective-permute-start.16 = (bf16[2,256,768]{2,1,0:T(8,128)(2,1)}, bf16[2,256,768]{2,1,0:T(8,128)(2,1)}, u32[]{:S(2)}, u32[]{:S(2)}) collective-permute-start(bf16[2,256,768]{2,1,0:T(8,128)(2,1)} %add_convert_fusion.6), channel_id=1, source_target_pairs={{0,8},{4,12},{24,16},{28,20},{1,9},{5,13},{25,17},{29,21},{2,10},{... | collective-permute-start | bytes 2359304 | tf_op jit(solution)/shard_map/ppermute | solution.py:486
  69.6 45.0 %collective-permute-start.21 = (bf16[3,2,256,768]{3,2,1,0:T(8,128)(2,1)}, bf16[3,2,256,768]{3,2,1,0:T(8,128)(2,1)}, u32[]{:S(2)}, u32[]{:S(2)}) collective-permute-start(bf16[3,2,256,768]{3,2,1,0:T(8,128)(2,1)} %get-tuple-element.86), channel_id=1, source_target_pairs={{0,4},{4,0},{8,12},{12,8},{16,20},{20,16},{24,28},{28,24},{1,5},{5... | collective-permute-start | bytes 7077896 | tf_op jit(solution)/shard_map/ppermute | solution.py:504
  91.8 20.7 %collective-permute-start.25 = (bf16[2,256,768]{2,1,0:T(8,128)(2,1)S(1)}, bf16[2,256,768]{2,1,0:T(8,128)(2,1)S(1)}, u32[]{:S(2)}, u32[]{:S(2)}) collective-permute-start(bf16[2,256,768]{2,1,0:T(8,128)(2,1)S(1)} %add_convert_fusion.1), channel_id=1, source_target_pairs={{8,16},{12,20},{16,8},{20,12},{9,17},{13,21},{17,9},{21,13},{10,18... | collective-permute-start | bytes 2359304 | tf_op jit(solution)/shard_map/ppermute | solution.py:486
  95.4 12.1 %collective-permute-start.24 = (bf16[96,2048]{1,0:T(8,128)(2,1)S(1)}, bf16[96,2048]{1,0:T(8,128)(2,1)S(1)}, u32[]{:S(2)}, u32[]{:S(2)}) collective-permute-start(bf16[96,2048]{1,0:T(8,128)(2,1)S(1)} %get-tuple-element.108), channel_id=1, source_target_pairs={{0,8},{4,12},{24,16},{28,20},{1,9},{5,13},{25,17},{29,21},{2,10},{... | collective-permute-start | bytes 1179656 | tf_op jit(solution)/shard_map/ppermute | solution.py:486
  105.9 24.3 %collective-permute-start.19 = (bf16[2,128,2048]{2,1,0:T(8,128)(2,1)S(1)}, bf16[2,128,2048]{2,1,0:T(8,128)(2,1)S(1)}, u32[]{:S(2)}, u32[]{:S(2)}) collective-permute-start(bf16[2,128,2048]{2,1,0:T(8,128)(2,1)S(1)} %get-tuple-element.96), channel_id=1, source_target_pairs={{0,2},{1,3},{2,0},{3,1},{4,6},{5,7},{6,4},{7,5},{8,10},{9,11},{10,... | collective-permute-start | bytes 3145736 | tf_op jit(solution)/shard_map/ppermute | solution.py:173
  106.5 24.5 %collective-permute-start.17 = (bf16[2,128,2048]{2,1,0:T(8,128)(2,1)S(1)}, bf16[2,128,2048]{2,1,0:T(8,128)(2,1)S(1)}, u32[]{:S(2)}, u32[]{:S(2)}) collective-permute-start(bf16[2,128,2048]{2,1,0:T(8,128)(2,1)S(1)} %get-tuple-element.93), channel_id=1, source_target_pairs={{0,1},{1,0},{2,3},{3,2},{4,5},{5,4},{6,7},{7,6},{8,9},{9,8},{10,11... | collective-permute-start | bytes 3145736 | tf_op jit(solution)/shard_map/ppermute | solution.py:173
  107.5 11.7 %collective-permute-start.29 = (bf16[96,2048]{1,0:T(8,128)(2,1)S(1)}, bf16[96,2048]{1,0:T(8,128)(2,1)S(1)}, u32[]{:S(2)}, u32[]{:S(2)}) collective-permute-start(bf16[96,2048]{1,0:T(8,128)(2,1)S(1)} %get-tuple-element.104), channel_id=1, source_target_pairs={{0,8},{4,12},{24,16},{28,20},{1,9},{5,13},{25,17},{29,21},{2,10},{... | collective-permute-start | bytes 1179656 | tf_op jit(solution)/shard_map/ppermute | solution.py:486
  112.4 19.9 %collective-permute-start.26 = (bf16[96,2048]{1,0:T(8,128)(2,1)S(1)}, bf16[96,2048]{1,0:T(8,128)(2,1)S(1)}, u32[]{:S(2)}, u32[]{:S(2)}) collective-permute-start(bf16[96,2048]{1,0:T(8,128)(2,1)S(1)} %add_convert_fusion.14), channel_id=1, source_target_pairs={{8,16},{12,20},{16,8},{20,12},{9,17},{13,21},{17,9},{21,13},{10,18... | collective-permute-start | bytes 1179656 | tf_op jit(solution)/shard_map/ppermute | solution.py:486
  115.9 20.7 %collective-permute-start.22 = (bf16[2,256,768]{2,1,0:T(8,128)(2,1)S(1)}, bf16[2,256,768]{2,1,0:T(8,128)(2,1)S(1)}, u32[]{:S(2)}, u32[]{:S(2)}) collective-permute-start(bf16[2,256,768]{2,1,0:T(8,128)(2,1)S(1)} %fusion.12), channel_id=1, source_target_pairs={{0,8},{4,12},{24,16},{28,20},{1,9},{5,13},{25,17},{29,21},{2,10},{... | collective-permute-start | bytes 2359304 | tf_op jit(solution)/shard_map/ppermute | solution.py:486
  130.4 12.1 %collective-permute-start.20 = (bf16[128,2048]{1,0:T(8,128)(2,1)S(1)}, bf16[128,2048]{1,0:T(8,128)(2,1)S(1)}, u32[]{:S(2)}, u32[]{:S(2)}) collective-permute-start(bf16[128,2048]{1,0:T(8,128)(2,1)S(1)} %fusion.15), channel_id=1, source_target_pairs={{0,1},{1,0},{2,3},{3,2},{4,5},{5,4},{6,7},{7,6},{8,9},{9,8},{10,11... | collective-permute-start | bytes 1572872 | tf_op jit(solution)/shard_map/ppermute | solution.py:173
  131.1 14.6 %collective-permute-start.18 = (bf16[128,2048]{1,0:T(8,128)(2,1)S(1)}, bf16[128,2048]{1,0:T(8,128)(2,1)S(1)}, u32[]{:S(2)}, u32[]{:S(2)}) collective-permute-start(bf16[128,2048]{1,0:T(8,128)(2,1)S(1)} %fusion.14), channel_id=1, source_target_pairs={{0,2},{1,3},{2,0},{3,1},{4,6},{5,7},{6,4},{7,5},{8,10},{9,11},{10,... | collective-permute-start | bytes 1572872 | tf_op jit(solution)/shard_map/ppermute | solution.py:173
  133.7 32.1 %collective-permute-start.31 = (bf16[96,2048]{1,0:T(8,128)(2,1)S(1)}, bf16[96,2048]{1,0:T(8,128)(2,1)S(1)}, u32[]{:S(2)}, u32[]{:S(2)}) collective-permute-start(bf16[96,2048]{1,0:T(8,128)(2,1)S(1)} %fusion.21), channel_id=1, source_target_pairs={{0,8},{4,12},{24,16},{28,20},{16,24},{20,28},{8,0},{12,4},{1,9},{5... | collective-permute-start | bytes 1179656 | tf_op jit(solution)/shard_map/ppermute | solution.py:486
  136.9 17.9 %collective-permute-start.27 = (bf16[2,256,768]{2,1,0:T(8,128)(2,1)S(1)}, bf16[2,256,768]{2,1,0:T(8,128)(2,1)S(1)}, u32[]{:S(2)}, u32[]{:S(2)}) collective-permute-start(bf16[2,256,768]{2,1,0:T(8,128)(2,1)S(1)} %add_convert_fusion.2), channel_id=1, source_target_pairs={{8,16},{12,20},{16,8},{20,12},{9,17},{13,21},{17,9},{21,13},{10,18... | collective-permute-start | bytes 2359304 | tf_op jit(solution)/shard_map/ppermute | solution.py:486
  143.6 17.3 %collective-permute-start.28 = (bf16[2,256,768]{2,1,0:T(8,128)(2,1)S(1)}, bf16[2,256,768]{2,1,0:T(8,128)(2,1)S(1)}, u32[]{:S(2)}, u32[]{:S(2)}) collective-permute-start(bf16[2,256,768]{2,1,0:T(8,128)(2,1)S(1)} %fusion.13), channel_id=1, source_target_pairs={{0,8},{4,12},{24,16},{28,20},{16,24},{20,28},{8,0},{12,4},{1,9},{5... | collective-permute-start | bytes 2359304 | tf_op jit(solution)/shard_map/ppermute | solution.py:486
  154.8 9.7 %collective-permute-start.30 = (bf16[96,2048]{1,0:T(8,128)(2,1)S(1)}, bf16[96,2048]{1,0:T(8,128)(2,1)S(1)}, u32[]{:S(2)}, u32[]{:S(2)}) collective-permute-start(bf16[96,2048]{1,0:T(8,128)(2,1)S(1)} %add_convert_fusion.10), channel_id=1, source_target_pairs={{8,16},{12,20},{16,8},{20,12},{9,17},{13,21},{17,9},{21,13},{10,18... | collective-permute-start | bytes 1179656 | tf_op jit(solution)/shard_map/ppermute | solution.py:486
  (17 other events, 166.7 us)

commit v3 on v2

--- a/solution.py
+++ b/solution.py
@@ -13,8 +13,8 @@
 F32 = jnp.float32
 BF16 = jnp.bfloat16
 MIB = 1 << 20
+PIECES = 1
 BIG = 24
-EARLY = (1, 2, 7)
 
 
 def contract(left, right, left_dim, right_dim):
@@ -50,7 +50,7 @@
 
 
 def pick_kernel(n_dp, dest_hbm, len_hbm, adv_hbm, rows_hbm, *refs):
-    outs, (dest_ref, len_ref, adv_ref, sems, row_sems) = refs[:n_dp], refs[n_dp:]
+    outs, (dest_ref, len_ref, adv_ref, sems, row_sems) = refs[:-5], refs[-5:]
     small = [
         pltpu.make_async_copy(source, target, sems.at[i])
         for i, (source, target) in enumerate(((dest_hbm, dest_ref), (len_hbm, len_ref), (adv_hbm, adv_ref)))
@@ -63,7 +63,9 @@
     me = lax.axis_index("dp")
     small[0].wait()
     found, copies = [], []
-    for i, out in enumerate(outs):
+    for i in range(n_dp):
+        out = outs[i // CORES]
+        here = pl.ds(i % CORES * slot, slot)
         seq = jnp.int32(0)
         live = jnp.int32(0)
         for s in range(seqs):
@@ -71,17 +73,18 @@
             seq = jnp.where(hit, s, seq)
             live = jnp.where(hit, 1, live)
         found.append((seq, live))
-        copies.append(pltpu.make_async_copy(rows_hbm.at[seq], out.at[:, pl.ds(0, width)], row_sems.at[i]))
+        copies.append(pltpu.make_async_copy(rows_hbm.at[seq], out.at[here, pl.ds(0, width)], row_sems.at[i]))
         copies[-1].start()
     small[1].wait()
     small[2].wait()
     lengths = len_ref[0].astype(F32)
     advs = adv_ref[0].astype(F32)
-    for (seq, live), out in zip(found, outs):
+    for i, (seq, live) in enumerate(found):
         mine = (which == seq) & (live == 1)
         length = jnp.sum(jnp.where(mine, lengths, 0.0), axis=1, keepdims=True)
         adv = jnp.sum(jnp.where(mine, advs, 0.0), axis=1, keepdims=True)
-        out[:, width:] = jnp.where(lane == LENGTH, length, jnp.where(lane == ADV, adv, 0.0)).astype(BF16)
+        value = jnp.where(lane == LENGTH, length, jnp.where(lane == ADV, adv, 0.0)).astype(BF16)
+        outs[i // CORES][i % CORES * slot : (i % CORES + 1) * slot, width:] = value
     for copy in copies:
         copy.wait()
 
@@ -90,9 +93,9 @@
     seqs, slot, width = rows.shape
     return pl.pallas_call(
         functools.partial(pick_kernel, n_dp),
-        out_shape=[jax.ShapeDtypeStruct((slot, width + LANES), BF16)] * n_dp,
+        out_shape=[jax.ShapeDtypeStruct((CORES * slot, width + LANES), BF16)] * (n_dp // CORES),
         in_specs=[hbm()] * 4,
-        out_specs=[vmem()] * n_dp,
+        out_specs=[vmem()] * (n_dp // CORES),
         scratch_shapes=[
             pltpu.SMEM(dest.shape, jnp.int32),
             pltpu.VMEM(lengths.shape, lengths.dtype),
@@ -118,71 +121,113 @@
     return jnp.where(part == 0, high, jnp.where(part == 1, middle, low))
 
 
-def assemble_kernel(n_dp, ids_ref, gates_ref, *refs):
-    pieces, x_ref = refs[:n_dp], refs[-1]
-    slot, wide = pieces[0].shape
+def regroup_kernel(count, *refs):
+    pieces, (mine, other) = refs[:count], refs[-2:]
+    slot = pieces[0].shape[0] // CORES
+    for i, piece in enumerate(pieces):
+        mine[i * slot : (i + 1) * slot, :] = piece[:slot]
+        other[i * slot : (i + 1) * slot, :] = piece[slot:]
+
+
+def regroup(pieces, after):
+    rows, wide = pieces[0].shape
+    count = len(pieces)
+    out = jax.ShapeDtypeStruct((count * rows // CORES, wide), BF16)
+    return pl.pallas_call(
+        functools.partial(regroup_kernel, count),
+        out_shape=[out, out],
+        in_specs=[vmem()] * count + [hbm()] * len(after),
+        out_specs=[vmem()] * 2,
+        compiler_params=params(16),
+        name="regroup",
+    )(*pieces, *after)
+
+
+def assemble_kernel(slot, ids_ref, gates_ref, mine, other, *halves):
+    rows, wide = halves[0].shape
     width = wide - LANES
+    per_half = rows // slot
     me = lax.axis_index("dp")
-    for i, piece in enumerate(pieces):
-        at = pl.multiple_of((me ^ i) * slot, slot)
-        x_ref[pl.ds(at, slot), :] = piece[...]
     notes = gate_notes(ids_ref[...], gates_ref[...]).T
-    x_ref[:, width:] = (x_ref[:, width:].astype(F32) + notes).astype(BF16)
-
-
-def assemble(pieces, ids, gates, after):
-    slot, wide = pieces[0].shape
-    n_dp = len(pieces)
-    return pl.pallas_call(
-        functools.partial(assemble_kernel, n_dp),
-        out_shape=jax.ShapeDtypeStruct((slot * n_dp, wide), BF16),
-        in_specs=[vmem()] * (2 + n_dp) + [hbm()] * len(after),
-        out_specs=vmem(),
+    for i in range(CORES * per_half):
+        piece = (mine, other)[i % CORES][i // CORES * slot : (i // CORES + 1) * slot, :]
+        place = me ^ i
+        at = pl.multiple_of((place % per_half) * slot, slot)
+        for h, half in enumerate(halves):
+
+            @pl.when(place // per_half == h)
+            def _(piece=piece, half=half, at=at):
+                half[pl.ds(at, slot), :] = piece
+
+    for h, half in enumerate(halves):
+        own = notes[h * rows : (h + 1) * rows]
+        half[:, width:] = (half[:, width:].astype(F32) + own).astype(BF16)
+
+
+def assemble(mine, other, slot, ids, gates):
+    return pl.pallas_call(
+        functools.partial(assemble_kernel, slot),
+        out_shape=[jax.ShapeDtypeStruct(mine.shape, BF16)] * 2,
+        in_specs=[vmem()] * 4,
+        out_specs=[vmem()] * 2,
         compiler_params=params(16),
         name="assemble",
-    )(ids, gates, *pieces, *after)
-
-
-def send_sequences(gen_rows, gen_lengths, gen_adv, destination, n_dp):
+    )(ids, gates, mine, other)
+
+
+def send_sequences(gen_rows, gen_lengths, gen_adv, destination, n_dp, after):
     seq_dev = destination.shape[2]
     slot = gen_rows.shape[0] // seq_dev
-    pieces = pick(destination, gen_lengths, gen_adv, gen_rows.reshape(seq_dev, slot, gen_rows.shape[1]), n_dp)
-    return [pieces[0]] + [
-        lax.ppermute(pieces[i], "dp", [(d, d ^ i) for d in range(n_dp)]) for i in range(1, n_dp)
-    ]
-
-
-def place_sequences(got, seq_dev, ids, gates, after):
-    n_dp = len(got)
+    pieces = list(pick(destination, gen_lengths, gen_adv, gen_rows.reshape(seq_dev, slot, gen_rows.shape[1]), n_dp))
+    for i in range(1, len(pieces)):
+        pieces[i] = lax.ppermute(pieces[i], "dp", [(d, d ^ (CORES * i)) for d in range(n_dp)])
+    mine, other = regroup(pieces, after)
+    return mine, lax.ppermute(other, "dp", [(d, d ^ 1) for d in range(n_dp)])
+
+
+def place_sequences(mine, other, n_dp, seq_dev, ids, gates):
+    slot = CORES * mine.shape[0] // n_dp
     if n_dp == seq_dev:
-        return assemble(got, ids.T, gates.T, after)
-    slot, wide = got[0].shape
+        return assemble(mine, other, slot, ids.T, gates.T)
+    wide = mine.shape[1]
     width = wide - LANES
     g = lax.axis_index("dp")
-    stack = jnp.stack(got)[jnp.arange(n_dp, dtype=jnp.int32) ^ g]
+    stack = jnp.stack([mine.reshape(-1, slot, wide), other.reshape(-1, slot, wide)], axis=1)
+    stack = stack.reshape(n_dp, slot, wide)[jnp.arange(n_dp, dtype=jnp.int32) ^ g]
     arrived = stack[:, 0, width + LENGTH] > 0
     arrival = jnp.cumsum(arrived.astype(jnp.int32)) - 1
     chosen = arrived[None, :] & (arrival[None, :] == jnp.arange(seq_dev, dtype=jnp.int32)[:, None])
     from_peer = jnp.sum(jnp.where(chosen, jnp.arange(n_dp, dtype=jnp.int32)[None, :], 0), axis=1)
     x = stack[from_peer].reshape(seq_dev * slot, wide)
     notes = (x[:, width:].astype(F32) + gate_notes(ids.T, gates.T).T).astype(BF16)
-    return jnp.concatenate([x[:, :width], notes], axis=1)
+    x = jnp.concatenate([x[:, :width], notes], axis=1)
+    half = x.shape[0] // 2
+    return x[:half], x[half:]
 
 
 def swap(value, i, n_ex):
     return lax.ppermute(value, "expert", [(d, d ^ i) for d in range(n_ex)])
 
 
-def gather_rows(rows, n_ex, between=None):
+def gather_rows(rows, n_ex):
     if n_ex != 4:
         return [rows] + [swap(rows, i, n_ex) for i in range(1, n_ex)]
     half = rows.shape[0] // 2
     first = swap(rows, 1, n_ex)
     second = swap(rows, 2, n_ex)
-    low, high = first[:half], second[half:]
-    if between:
-        low, high, *_ = lax.optimization_barrier((low, high, *between))
-    return [rows, first, second, swap(low, 2, n_ex), swap(high, 1, n_ex)]
+    return [rows, first, second, swap(first[:half], 2, n_ex), swap(second[half:], 1, n_ex)]
+
+
+def gather_halves(low, high, n_ex, between):
+    if n_ex != 4:
+        pieces = [low, high]
+        for i in range(1, n_ex):
+            pieces += [swap(low, i, n_ex), swap(high, i, n_ex)]
+        return pieces
+    first_low, second_high = swap(low, 1, n_ex), swap(high, 2, n_ex)
+    first_high, second_low = swap(high, 1, n_ex), swap(low, 2, n_ex)
+    on_low, on_high, _ = lax.optimization_barrier((first_low, second_high, between))
+    return [low, high, first_low, first_high, second_low, second_high, swap(on_low, 2, n_ex), swap(on_high, 1, n_ex)]
 
 
 def with_last(pieces, size):
@@ -368,7 +413,7 @@
     )(turned_x, gate_grad, up_grad)
 
 
-def rest_grads_kernel(shard, x_ref, gate_ref, up_ref, other, mine):
+def rest_grads_kernel(shard, x_ref, gate_ref, up_ref, _, other, mine):
     count = other.shape[0]
     for k, out in enumerate((other, mine)):
         x = x_ref[pl.ds((k * (count + 1) + 1) * shard, count * shard), :]
@@ -378,7 +423,7 @@
                 out[b, p] = value[b * shard : (b + 1) * shard]
 
 
-def rest_grads(turned_x, gate_grad, up_grad, n_dp):
+def rest_grads(turned_x, gate_grad, up_grad, after, n_dp):
     rows, units = gate_grad.shape
     width = turned_x.shape[0]
     n_z, shard = n_dp // CORES, width // n_dp
@@ -388,13 +433,13 @@
     return pl.pallas_call(
         functools.partial(rest_grads_kernel, shard),
         grid=(units // tile,),
-        in_specs=[pl.BlockSpec((width, rows), lambda j: (0, 0)), columns, columns],
+        in_specs=[pl.BlockSpec((width, rows), lambda j: (0, 0)), columns, columns, hbm()],
         out_specs=[out, out],
         out_shape=[pltpu.HBM((n_z - 1, 2, shard, units), BF16)] * 2,
         compiler_params=params(room(rows, width)),
         cost_estimate=cost(4 * rows * units * width, 4 * units * width + 4 * rows * units),
         name="rest_grads",
-    )(turned_x, gate_grad, up_grad)
+    )(turned_x, gate_grad, up_grad, after)
 
 
 def row_grad_kernel(hid_ref, dy_ref, other, mine):
@@ -424,7 +469,7 @@
     )(turned_hid, dy)
 
 
-def outputs_kernel(layer_groups, grad_groups, hid_ref, gates_ref, gate_ref, up_ref, wd_ref, wg_ref, wu_ref, *outs):
+def outputs_kernel(layer_groups, grad_groups, hid_ref, gates_ref, gate_ref, up_ref, wd_ref, wg_ref, wu_ref, _, *outs):
     layer = jnp.dot(hid_ref[...], wd_ref[...], preferred_element_type=F32) * gates_ref[...]
     value = contract(gate_ref[...], wg_ref[...], 1, 1) + contract(up_ref[...], wu_ref[...], 1, 1)
     size = outs[0].shape[1]
@@ -437,7 +482,7 @@
                 out[n] = result[i * size : (i + 1) * size]
 
 
-def outputs(hid, gates, gate_grad, up_grad, w_down, w_gate, w_up, n_ex, layer_groups, grad_groups):
+def outputs(hid, gates, gate_grad, up_grad, w_down, w_gate, w_up, after, n_ex, layer_groups, grad_groups):
     rows, units = hid.shape
     width = w_down.shape[1]
     tile = 512
@@ -450,20 +495,20 @@
         functools.partial(outputs_kernel, layer_groups, grad_groups),
         grid=(width // tile,),
         out_shape=[jax.ShapeDtypeStruct((n, size, width), BF16) for n in counts],
-        in_specs=[whole, pl.BlockSpec((rows, 1), lambda j: (0, 0)), whole, whole, columns, weights, weights],
+        in_specs=[whole, pl.BlockSpec((rows, 1), lambda j: (0, 0)), whole, whole, columns, weights, weights, hbm()],
         out_specs=[pl.BlockSpec((n, size, tile), lambda j: (0, 0, j)) for n in counts],
         compiler_params=params(room(rows, width)),
         cost_estimate=cost(6 * rows * units * width, 6 * units * width + 4 * rows * width),
         name="outputs",
-    )(hid, gates, gate_grad, up_grad, w_down, w_gate, w_up)
+    )(hid, gates, gate_grad, up_grad, w_down, w_gate, w_up, after)
 
 
 def add(*parts):
     return sum(part.astype(F32) for part in parts).astype(BF16)
 
 
-def outputs_home(hid, gates, gate_grad, up_grad, w_down, w_gate, w_up, n_ex):
-    weights = (hid, gates, gate_grad, up_grad, w_down, w_gate, w_up, n_ex)
+def outputs_home(hid, gates, gate_grad, up_grad, w_down, w_gate, w_up, after, n_ex):
+    weights = (hid, gates, gate_grad, up_grad, w_down, w_gate, w_up, after, n_ex)
     if n_ex != 4:
         single = [[i] for i in range(n_ex)]
         parts = outputs(*weights, single, single)
@@ -471,18 +516,104 @@
         for i in range(n_ex):
             layer.append(swap(parts[i][0], i, n_ex) if i else parts[i][0])
             grad.append(swap(parts[n_ex + i][0], i, n_ex) if i else parts[n_ex + i][0])
-        return add(*layer), add(*grad)
+        return add(*layer), add(*grad), []
     layer0, layer2, layer13, grad0, grad1, grad23 = outputs(*weights, [[0], [2], [1, 3]], [[0], [1], [2, 3]])
     layer_got = swap(layer13, 1, n_ex)
     grad_got = swap(grad23, 2, n_ex)
     layer_last = swap(add(layer2[0], layer_got[1]), 2, n_ex)
     grad_last = swap(add(grad1[0], grad_got[1]), 1, n_ex)
-    return add(layer0[0], layer_got[0], layer_last), add(grad0[0], grad_got[0], grad_last)
-
-
-def line_permute(value, links, n_dp):
+    layer, grad = add(layer0[0], layer_got[0], layer_last), add(grad0[0], grad_got[0], grad_last)
+    return layer, grad, [layer_last, grad_last]
+
+
+def fold_kernel(gu_mine, gu_got, row_mine, row_got, *refs):
+    out = refs[-1]
+    step = pl.program_id(0)
+
+    def put(mine, got):
+        value = (mine.astype(F32) + got.astype(F32)).astype(BF16)
+        rows, columns = value.shape
+        for i in range(columns // LANES):
+            out[0, i * rows : (i + 1) * rows, :] = value[:, i * LANES : (i + 1) * LANES]
+
+    @pl.when(step < 2)
+    def _():
+        put(gu_mine[0, 0], gu_got[0, 0])
+
+    @pl.when(step == 2)
+    def _():
+        put(row_mine[0], row_got[0])
+
+
+def fold(gu_mine, gu_got, row_mine, row_got, gu_at, row_at, piece, pieces, after):
+    _, _, shard, units = gu_mine.shape
+    _, row_shard, width = row_mine.shape
+    per = shard * units // LANES // pieces
+    gu = pl.BlockSpec((1, 1, shard, units // pieces), lambda j: (gu_at, jnp.minimum(j, 1), 0, piece))
+    row = pl.BlockSpec((1, row_shard, width // pieces), lambda j: (row_at, 0, piece))
+    return pl.pallas_call(
+        fold_kernel,
+        grid=(3,),
+        in_specs=[gu, gu, row, row] + [hbm()] * len(after),
+        out_specs=pl.BlockSpec((1, per, LANES), lambda j: (j, 0, 0)),
+        out_shape=jax.ShapeDtypeStruct((3, per, LANES), BF16),
+        compiler_params=params(16),
+        cost_estimate=cost(6 * per * LANES, 18 * per * LANES),
+        name="fold",
+    )(gu_mine, gu_got, row_mine, row_got, *after)
+
+
+def pass_on_kernel(own, got, *refs):
+    refs[-1][...] = (own[...].astype(F32) + got[...].astype(F32)).astype(BF16)
+
+
+def pass_on(own, at, got, after):
+    block = pl.BlockSpec((1,) + got.shape[1:], lambda j: (j, 0, 0))
+    return pl.pallas_call(
+        pass_on_kernel,
+        grid=(got.shape[0],),
+        in_specs=[pl.BlockSpec((1,) + got.shape[1:], lambda j: (j, at, 0)), block] + [hbm()] * len(after),
+        out_specs=block,
+        out_shape=jax.ShapeDtypeStruct(got.shape, BF16),
+        compiler_params=params(16),
+        cost_estimate=cost(2 * got.size, 6 * got.size),
+        name="pass_on",
+    )(own, got, *after)
+
+
+def unfold_kernel(count, *refs):
+    parts, outs = refs[:count], refs[count:]
+    per = max(part.shape[1] for part in parts)
+    total = sum(part[0].astype(F32) for part in parts if part.shape[1] == per)
+    pieces = [part[0].astype(F32) for part in parts if part.shape[1] < per]
+    if pieces:
+        total = total + jnp.concatenate(pieces, axis=0)
+    total = total.astype(BF16)
+    for j, out in enumerate(outs):
+
+        @pl.when(pl.program_id(0) == j)
+        def _(out=out):
+            rows, columns = out.shape[1:]
+            for i in range(columns // LANES):
+                out[0, :, i * LANES : (i + 1) * LANES] = total[i * rows : (i + 1) * rows]
+
+
+def unfold(parts, shapes):
+    return pl.pallas_call(
+        functools.partial(unfold_kernel, len(parts)),
+        grid=(3,),
+        in_specs=[pl.BlockSpec((1,) + part.shape[1:], lambda j: (j, 0, 0)) for part in parts],
+        out_specs=[pl.BlockSpec(shape, lambda j: (0, 0, 0)) for shape in shapes],
+        out_shape=[jax.ShapeDtypeStruct(shape, BF16) for shape in shapes],
+        compiler_params=params(24),
+        cost_estimate=cost(4 * parts[0].size, 10 * parts[0].size),
+        name="unfold",
+    )(*parts)
+
+
+def line_permute(value, link, n_dp):
     n_z = n_dp // CORES
-    pairs = [pair for k in links for pair in ((k, k + 1), (n_z - 1 - k, n_z - 2 - k))]
+    pairs = [(link, link + 1), (n_z - 1 - link, n_z - 2 - link)]
     return lax.ppermute(value, "dp", [(CORES * a + c, CORES * b + c) for a, b in pairs for c in range(CORES)])
 
 
@@ -503,11 +634,11 @@
     def swap_core(value):
         return lax.ppermute(value, "dp", other_core)
 
-    got = send_sequences(gen_rows, gen_lengths, gen_adv, destination, n_dp)
-    cot_pieces = gather_rows(cotangent, n_ex, [got[i] for i in EARLY if i < n_dp])
-    x = place_sequences(got, destination.shape[2], expert_ids, gate_values, cot_pieces[3:5])
+    cot_pieces = gather_rows(cotangent, n_ex)
+    mine, other = send_sequences(gen_rows, gen_lengths, gen_adv, destination, n_dp, cot_pieces[1:3])
+    low, high = place_sequences(mine, other, n_dp, destination.shape[2], expert_ids, gate_values)
     hg, dy_all = hidden_grad(cot_pieces, weight_down)
-    x_pieces = gather_rows(x, n_ex, [hg])
+    x_pieces = gather_halves(low, high, n_ex, hg)
     early, late = with_last(x_pieces, size)
     before = hidden_units(early, weight_gate, weight_up, hg, slot, n_dp)
     gate_grad, up_grad, hid, turned_hs, turned_x, gates = hidden_units(
@@ -517,58 +648,44 @@
     far = n_z - 1
     rest = list(range(far - 1, -1, -1))
     far_other, far_mine = far_grads(turned_x, gate_grad, up_grad, n_dp)
+    far_got = swap_core(far_other)
     row_other, row_mine = row_grad(tie(turned_hs, far_other), dy_all, n_dp)
-    rest_other, rest_mine = rest_grads(tie(turned_x, row_other), gate_grad, up_grad, n_dp)
-    far_got, row_got, rest_got = swap_core(far_other), swap_core(row_other), swap_core(rest_other)
-    sums = [[None, None] for _ in range(n_z)]
-    sums[far][0] = add(tie(far_mine, rest_other), far_got)
+    row_got = swap_core(row_other)
+    rest_other, rest_mine = rest_grads(tie(turned_x, row_other), gate_grad, up_grad, far_got, n_dp)
+    rest_got = swap_core(rest_other)
+    far_mine, far_got = far_mine[None], far_got[None]
+
+    def pieces(k):
+        return PIECES if k == far else 1
+
+    sums = []
     for k in range(n_z):
-        sums[k][1] = add(row_mine[far - k], row_got[far - k])
-    for i, k in enumerate(rest):
-        sums[k][0] = add(rest_mine[i], rest_got[i])
-
-    passed = {}
-    ends = [[], []]
-    joined = n_z > 3
-    at_end = near == 0
-
-    def own(link, d, p):
-        return sums[d if link < n_z // 2 else far - d][p]
-
-    for link in range(n_z - 1 - joined):
-        issued = []
-        for d in range(far, link + (joined and link == 0), -1):
-            for p in range(2):
-                value = own(link, d, p)
-                if link > 0:
-                    value = add(value, passed[link - 1, d, p])
-                ahead = 2 if link == 0 else 1
-                if len(issued) >= ahead:
-                    value = tie(value, issued[-ahead])
-                got = line_permute(value, [link], n_dp)
-                issued.append(got)
-                passed[link, d, p] = got
+        gu = (far_mine, far_got) if k == far else (rest_mine, rest_got)
+        at = max(far - 1 - k, 0)
+        sums.append([fold(*gu, row_mine, row_got, at, far - k, p, pieces(k), []) for p in range(pieces(k))])
+    passed, ends = {}, []
+    for link in range(n_z - 1):
+        for d in range(far, link, -1):
+            for p in range(pieces(d)):
+                here = sums[d if link < n_z // 2 else far - d]
+                if link == 0:
+                    value = here[p]
+                else:
+                    own, at = (here[p], 0) if len(here) == pieces(d) else (here[0], p)
+                    value = pass_on(own, at, passed[link - 1, d, p], [])
+                passed[link, d, p] = line_permute(value, link, n_dp)
                 if d == link + 1:
-                    ends[p].append(got)
-        if link == 0:
-            firsts = issued
-    if joined:
-        for p in range(2):
-            value = jnp.where(at_end, own(0, 1, p), add(own(n_z - 2, far, p), passed[n_z - 3, far, p]))
-            got = line_permute(tie(value, firsts[-2]), [0, n_z - 2], n_dp)
-            firsts.append(got)
-            ends[p].append(got)
-    totals = []
-    for p in range(2):
-        mine = sum(jnp.where(near == k, sums[k][p].astype(F32), 0.0) for k in range((n_z + 1) // 2))
-        mine = lax.optimization_barrier(add(mine, *ends[p][:-1]))
-        totals.append(add(mine, ends[p][-1]))
-
-    hid, gate_grad, up_grad, _ = lax.optimization_barrier((hid, gate_grad, up_grad, firsts[0]))
-    layer_out, input_grad = outputs_home(
-        hid, gates, gate_grad, up_grad, weight_down, weight_gate, weight_up, n_ex
+                    ends.append(passed[link, d, p])
+    own = sums[0][0]
+    for k in range(1, (n_z + 1) // 2):
+        own = jnp.where(near == k, sums[k][0], own)
+    shapes = [(1, w_gate.shape[1] // n_dp, w_gate.shape[2])] * 2 + [(1, w_down.shape[1] // n_dp, w_down.shape[2])]
+    totals = unfold([own] + ends, shapes)
+
+    layer_out, input_grad, _ = outputs_home(
+        hid, gates, gate_grad, up_grad, weight_down, weight_gate, weight_up, far_got, n_ex
     )
-    return layer_out, input_grad, totals[0][0:1], totals[0][1:2], totals[1][None]
+    return layer_out, input_grad, *totals
 
 
 def solution(mesh):

time: 169 us -> 163 us (0.964); the launches traced: 167 us -> 162 us
  starting transfers between devices: 41 us -> 27.3 us
  Pallas kernels: 29.5 us -> 41.5 us
  other arithmetic: 16.1 us -> 6.39 us
  waiting for transfers between devices: 74 us -> 81.7 us
    ppermute x10 -> x6, waiting for transfers between devices: 35.7 us -> 59.2 us  [line_permute(): lax.ppermute(value, 'dp', [(CORES * a + c, CORES * b + c) for a, b in pai...]
    ppermute x12 -> x14, waiting for transfers between devices: 32.9 us -> 11 us  [swap(): return lax.ppermute(value, 'expert', [(d, d ^ i) for d in range(n_ex)])]
    pallas_call x1 -> x10, Pallas kernels: 0.15 us -> 11.8 us  [the longest x3 6.36 us: pass_on(): pl.pallas_call(pass_on_kernel, grid=(got.shape[0],), in_specs=[pl.BlockSp...]
    ppermute x10 -> x6, starting transfers between devices: 21.6 us -> 11.3 us  [line_permute(): lax.ppermute(value, 'dp', [(CORES * a + c, CORES * b + c) for a, b in pai...]
    ppermute x7 -> x4, waiting for transfers between devices: 5.3 us -> 11.5 us  [the longest x3 11.5 us: send_sequences(): lax.ppermute(pieces[i], 'dp', [(d, d ^ CORES * i) for d in range(n_dp)])]
    convert_element_type x14 -> x4, other arithmetic: 12 us -> 6.27 us  [add(): return sum((part.astype(F32) for part in parts)).astype(BF16)]
    ppermute x7 -> x4, starting transfers between devices: 7.48 us -> 3.62 us  [the longest x3 3.55 us: send_sequences(): lax.ppermute(pieces[i], 'dp', [(d, d ^ CORES * i) for d in range(n_dp)])]
    select_n x2 -> x1, other arithmetic: 3.28 us -> 0.12 us  [on_device(): own = jnp.where(near == k, sums[k][0], own)]
  transfers between devices with their start and end apart: 32 -> 27, of which waited for: 18 -> 12; matrix products, arithmetic and copies ran while one was open for 10% -> 4% of each run, Pallas kernels for 14% -> 21%
where the time goes in v3:
time: 163 us; the launch traced here: 162 us
  waiting for transfers between devices  81.7 us (50%)
  Pallas kernels  41.5 us (25%)
  starting transfers between devices  27.3 us (17%)
  other arithmetic  6.39 us (4%)
  local copies, waits for them, and re-layouts  4.55 us (3%)
    ppermute x6, waiting for transfers between devices, line_permute(): lax.ppermute(value, 'dp', [(CORES * a + c, CORES * b + c) for a, b in pai...  59.2 us
    ppermute x14, starting transfers between devices, swap(): return lax.ppermute(value, 'expert', [(d, d ^ i) for d in range(n_ex)])  11.9 us
    ppermute x3, waiting for transfers between devices, send_sequences(): lax.ppermute(pieces[i], 'dp', [(d, d ^ CORES * i) for d in range(n_dp)])  11.5 us
    ppermute x6, starting transfers between devices, line_permute(): lax.ppermute(value, 'dp', [(CORES * a + c, CORES * b + c) for a, b in pai...  11.3 us
    ppermute x14, waiting for transfers between devices, swap(): return lax.ppermute(value, 'expert', [(d, d ^ i) for d in range(n_ex)])  11 us
    pallas_call x2, Pallas kernels, hidden_units(): pl.pallas_call(functools.partial(units_kernel, len(pieces), slot, not bef...  8.46 us
    pallas_call x3, Pallas kernels, pass_on(): pl.pallas_call(pass_on_kernel, grid=(got.shape[0],), in_specs=[pl.BlockSp...  6.36 us
    convert_element_type x4, other arithmetic, add(): return sum((part.astype(F32) for part in parts)).astype(BF16)  6.27 us
  transfers between devices with their start and end apart: 27, of which 12 were waited for; matrix products, arithmetic and copies ran while one was open for 4% of the time, Pallas kernels for 21%

profile of v3, /device:TPU:12, one launch (start us, length us, event | category | flops | bytes accessed | tf_op | source)
XLA Modules:
  0.0 162.5 jit_solution(11968936554878142811)
XLA Ops:
  2.7 2.1 %pick.1 = (bf16[32,2176]{1,0:T(8,128)(2,1)S(1)}, bf16[32,2176]{1,0:T(8,128)(2,1)S(1)}, bf16[32,2176]{1,0:T(8,128)(2,1)S(1)}, bf16[32,2176]{1,0:T(8,128)(2,1)S(1)}) custom-call(s32[1,1,8]{2,1,0:T(1,128)} %dest_hbm.1, s32[1,1,8]{2,1,0:T(1,128)} %len_hbm.1, bf16[1,1,8]{2,1,0:T(2,128)(2,1)} %adv_hbm.1, bf16[8,16,2048]{2,1,0:T(8,128)(2,1)} %bitcast.33), custom_call_target="tpu_custom_call" | custom-call | tf_op jit(solution)/shard_map/pick/pallas_call | solution.py:94
  5.3 2.6 %collective-permute-start.5 = (bf16[32,2176]{1,0:T(8,128)(2,1)S(1)}, bf16[32,2176]{1,0:T(8,128)(2,1)S(1)}, u32[]{:S(2)}, u32[]{:S(2)}) collective-permute-start(bf16[32,2176]{1,0:T(8,128)(2,1)S(1)} %get-tuple-element.49), channel_id=1, source_target_pairs={{0,16},{4,20},{8,24},{12,28},{16,0},{20,4},{24,8},{28,12},{1,17},{... | collective-permute-start | bytes 417800 | tf_op jit(solution)/shard_map/ppermute | solution.py:183
  8.4 2.5 %collective-permute-done.4.refs_1_ = bf16[32,2176]{1,0:T(8,128)(2,1)S(1)} collective-permute-done((bf16[32,2176]{1,0:T(8,128)(2,1)S(1)}, bf16[32,2176]{1,0:T(8,128)(2,1)S(1)}, u32[]{:S(2)}, u32[]{:S(2)}) %collective-permute-start.4) | collective-permute-done | bytes 139296 | tf_op jit(solution)/shard_map/ppermute | solution.py:183
  10.9 6.6 %collective-permute-done.5.refs_2_ = bf16[32,2176]{1,0:T(8,128)(2,1)S(1)} collective-permute-done((bf16[32,2176]{1,0:T(8,128)(2,1)S(1)}, bf16[32,2176]{1,0:T(8,128)(2,1)S(1)}, u32[]{:S(2)}, u32[]{:S(2)}) %collective-permute-start.5) | collective-permute-done | bytes 139296 | tf_op jit(solution)/shard_map/ppermute | solution.py:183
  17.5 2.4 %collective-permute-done.6.refs_3_ = bf16[32,2176]{1,0:T(8,128)(2,1)S(1)} collective-permute-done((bf16[32,2176]{1,0:T(8,128)(2,1)S(1)}, bf16[32,2176]{1,0:T(8,128)(2,1)S(1)}, u32[]{:S(2)}, u32[]{:S(2)}) %collective-permute-start.6) | collective-permute-done | bytes 139296 | tf_op jit(solution)/shard_map/ppermute | solution.py:183
  20.1 1.6 collective-permute-start.2
  25.5 3.7 %collective-permute-done.2.refs_3_ = bf16[64,2048]{1,0:T(8,128)(2,1)S(1)} collective-permute-done((bf16[64,2048]{1,0:T(8,128)(2,1)S(1)}, bf16[64,2048]{1,0:T(8,128)(2,1)S(1)}, u32[]{:S(2)}, u32[]{:S(2)}) %collective-permute-start.2) | collective-permute-done | bytes 262176 | tf_op jit(solution)/shard_map/ppermute | solution.py:209
  32.0 2.7 %hidden_grad.1 = (f32[512,768]{1,0:T(8,128)S(1)}, bf16[512,2048]{1,0:T(8,128)(2,1)S(1)}) custom-call(bf16[768,2048]{1,0:T(8,128)(2,1)S(1)} %bitcast.31, bf16[128,2048]{1,0:T(8,128)(2,1)S(1)} %copy-done.15, bf16[128,2048]{1,0:T(8,128)(2,1)S(1)} %collective-permute-done.refs_1_.refs_4_, bf16[128,2048]{1,0:T(8,128)(2,1)S(1)} %collective-permute-done.1.refs_2_.refs_5_, ...), custom_call_target="tpu_custom_call" | custom-call | flops 1610612736 | bytes 7340032 | tf_op jit(solution)/shard_map/hidden_grad/pallas_call | solution.py:277
  34.7 2.2 %collective-permute-done.8.refs_2_ = bf16[64,2176]{1,0:T(8,128)(2,1)S(1)} collective-permute-done((bf16[64,2176]{1,0:T(8,128)(2,1)S(1)}, bf16[64,2176]{1,0:T(8,128)(2,1)S(1)}, u32[]{:S(2)}, u32[]{:S(2)}) %collective-permute-start.8) | collective-permute-done | bytes 278560 | tf_op jit(solution)/shard_map/ppermute | solution.py:209
  37.9 4.9 %collective-permute-done.9.refs_3_ = bf16[64,2176]{1,0:T(8,128)(2,1)S(1)} collective-permute-done((bf16[64,2176]{1,0:T(8,128)(2,1)S(1)}, bf16[64,2176]{1,0:T(8,128)(2,1)S(1)}, u32[]{:S(2)}, u32[]{:S(2)}) %collective-permute-start.9) | collective-permute-done | bytes 278560 | tf_op jit(solution)/shard_map/ppermute | solution.py:209
  42.9 5.6 %hidden_units.2 = (bf16[512,768]{1,0:T(8,128)(2,1)S(1)}, bf16[512,768]{1,0:T(8,128)(2,1)S(1)}, bf16[512,768]{1,0:T(8,128)(2,1)S(1)}, bf16[768,512]{1,0:T(8,128)(...) custom-call(bf16[2048,768]{1,0:T(8,128)(2,1)S(1)} %bitcast.20, bf16[2048,768]{1,0:T(8,128)(2,1)S(1)} %bitcast.23, ...), custom_call_target="tpu_custom_call" | custom-call | flops 2415919104 | bytes 9437184 | tf_op jit(solution)/shard_map/hidden_units/pallas_call | solution.py:355
  48.5 2.9 %hidden_units.3 = (bf16[512,768]{1,0:T(8,128)(2,1)S(1)}, bf16[512,768]{1,0:T(8,128)(2,1)S(1)}, bf16[512,768]{1,0:T(8,128)(2,1)S(1)}, bf16[768,512]{1,0:T(8,128)(...) custom-call(bf16[2048,768]{1,0:T(8,128)(2,1)S(1)} %bitcast.21, ...), custom_call_target="tpu_custom_call", output_to_operand_aliasing={{0}: (3, {}), {1}: (4, {}), {2}: (5, {}), {3}: (6, {}), {4}... | custom-call | flops 805306368 | bytes 7340032 | tf_op jit(solution)/shard_map/hidden_units/pallas_call | solution.py:355
  51.4 2.5 %far_grads.1 = (bf16[2,256,768]{2,1,0:T(8,128)(2,1)}, bf16[2,256,768]{2,1,0:T(8,128)(2,1)}) custom-call(bf16[2048,512]{1,0:T(8,128)(2,1)S(1)} %get-tuple-element.79.x_ref, bf16[512,768]{1,0:T(8,128)(2,1)S(1)} %get-tuple-element.65.gate_ref, bf16[512,768]{1,0:T(8,128)(2,1)S(1)} %get-tuple-element.66.up_ref), custom_call_target="tpu_custom_call" | custom-call | flops 805306368 | bytes 4718592 | tf_op jit(solution)/shard_map/far_grads/pallas_call | solution.py:404
  53.9 3.6 %row_grad.1 = (bf16[4,96,2048]{2,1,0:T(8,128)(2,1)}, bf16[4,96,2048]{2,1,0:T(8,128)(2,1)}) custom-call(bf16[768,512]{1,0:T(8,128)(2,1)S(1)} %get-tuple-element.76.hid_ref, bf16[512,2048]{1,0:T(8,128)(2,1)S(1)} %get-tuple-element.77.dy_ref), custom_call_target="tpu_custom_call" | custom-call | flops 1610612736 | bytes 5242880 | tf_op jit(solution)/shard_map/row_grad/pallas_call | solution.py:460
  58.0 4.1 %rest_grads.1 = (bf16[3,2,256,768]{3,2,1,0:T(8,128)(2,1)}, bf16[3,2,256,768]{3,2,1,0:T(8,128)(2,1)}) custom-call(bf16[2048,512]{1,0:T(8,128)(2,1)S(1)} %get-tuple-element.79.x_ref, bf16[512,768]{1,0:T(8,128)(2,1)S(1)} %get-tuple-element.65.gate_ref, bf16[512,768]{1,0:T(8,128)(2,1)S(1)} %get-tuple-element.66.up_ref, ...), custom_call_target="tpu_custom_call" | custom-call | flops 3221225472 | bytes 7864320 | tf_op jit(solution)/shard_map/rest_grads/pallas_call | solution.py:433
  63.8 6.1 %outputs.1 = (bf16[1,128,2048]{2,1,0:T(8,128)(2,1)S(1)}, bf16[1,128,2048]{2,1,0:T(8,128)(2,1)S(1)}, bf16[2,128,2048]{2,1,0:T(8,128)(2,1)S(1)}, bf16[1,128,2048]{...) custom-call(bf16[512,768]{1,0:T(8,128)(2,1)S(1)} %get-tuple-element.63.hid_ref, ...), custom_call_target="tpu_custom_call" | custom-call | flops 4831838208 | bytes 13631488 | tf_op jit(solution)/shard_map/outputs/pallas_call | solution.py:494
  71.0 21.7 %collective-permute-done.24.got = bf16[3,1536,128]{2,1,0:T(8,128)(2,1)S(1)} collective-permute-done((bf16[3,1536,128]{2,1,0:T(8,128)(2,1)S(1)}, bf16[3,1536,128]{2,1,0:T(8,128)(2,1)S(1)}, u32[]{:S(2)}, u32[]{:S(2)}) %collective-permute-start.24) | collective-permute-done | bytes 1179680 | tf_op jit(solution)/shard_map/ppermute | solution.py:617
  92.7 1.7 %pass_on.4 = bf16[3,1536,128]{2,1,0:T(8,128)(2,1)} custom-call(bf16[3,1536,128]{2,1,0:T(8,128)(2,1)S(1)} %fold.7.own, bf16[3,1536,128]{2,1,0:T(8,128)(2,1)S(1)} %collective-permute-done.24.got), custom_call_target="tpu_custom_call" | custom-call | flops 1179648 | bytes 3538944 | tf_op jit(solution)/shard_map/pass_on/pallas_call | solution.py:572
  94.4 3.5 %collective-permute-start.25 = (bf16[3,1536,128]{2,1,0:T(8,128)(2,1)}, bf16[3,1536,128]{2,1,0:T(8,128)(2,1)}, u32[]{:S(2)}, u32[]{:S(2)}) collective-permute-start(bf16[3,1536,128]{2,1,0:T(8,128)(2,1)} %pass_on.4), channel_id=1, source_target_pairs={{8,16},{12,20},{16,8},{20,12},{9,17},{13,21},{17,9},{21,13},{10,18... | collective-permute-start | bytes 3538952 | tf_op jit(solution)/shard_map/ppermute | solution.py:617
  97.9 1.9 %fold.6.own = bf16[3,1536,128]{2,1,0:T(8,128)(2,1)} custom-call(bf16[3,2,256,768]{3,2,1,0:T(8,128)(2,1)S(1)} %copy-done.1, bf16[3,2,256,768]{3,2,1,0:T(8,128)(2,1)S(1)} %collective-permute-done.19.gu_got, bf16[4,96,2048]{2,1,0:T(8,128)(2,1)S(1)} %copy-done, bf16[4,96,2048]{2,1,0:T(8,128)(2,1)S(1)} %collective-permute-done.20.row_got), custom_call_target="tpu_custom_call" | custom-call | flops 1179648 | bytes 3538944 | tf_op jit(solution)/shard_map/fold/pallas_call | solution.py:554
  104.4 1.7 %copy-done.2 = bf16[3,2,256,768]{3,2,1,0:T(8,128)(2,1)S(1)} copy-done((bf16[3,2,256,768]{3,2,1,0:T(8,128)(2,1)S(1)}, bf16[3,2,256,768]{3,2,1,0:T(8,128)(2,1)}, u32[]{:S(2)}) %copy-start.2) | copy-done | bytes 2359320
  106.1 1.7 %copy-done.4 = bf16[3,2,256,768]{3,2,1,0:T(8,128)(2,1)S(1)} copy-done((bf16[3,2,256,768]{3,2,1,0:T(8,128)(2,1)S(1)}, bf16[3,2,256,768]{3,2,1,0:T(8,128)(2,1)}, u32[]{:S(2)}) %copy-start.4) | copy-done | bytes 2359320
  109.7 14.5 %collective-permute-done.25.got = bf16[3,1536,128]{2,1,0:T(8,128)(2,1)} collective-permute-done((bf16[3,1536,128]{2,1,0:T(8,128)(2,1)}, bf16[3,1536,128]{2,1,0:T(8,128)(2,1)}, u32[]{:S(2)}, u32[]{:S(2)}) %collective-permute-start.25) | collective-permute-done | bytes 1179680 | tf_op jit(solution)/shard_map/ppermute | solution.py:617
  124.2 2.2 %pass_on.5 = bf16[3,1536,128]{2,1,0:T(8,128)(2,1)S(1)} custom-call(bf16[3,1536,128]{2,1,0:T(8,128)(2,1)S(1)} %fold.5.own, bf16[3,1536,128]{2,1,0:T(8,128)(2,1)} %collective-permute-done.25.got), custom_call_target="tpu_custom_call" | custom-call | flops 1179648 | bytes 3538944 | tf_op jit(solution)/shard_map/pass_on/pallas_call | solution.py:572
  127.9 3.0 %collective-permute-done.22.got = bf16[3,1536,128]{2,1,0:T(8,128)(2,1)} collective-permute-done((bf16[3,1536,128]{2,1,0:T(8,128)(2,1)}, bf16[3,1536,128]{2,1,0:T(8,128)(2,1)}, u32[]{:S(2)}, u32[]{:S(2)}) %collective-permute-start.22) | collective-permute-done | bytes 1179680 | tf_op jit(solution)/shard_map/ppermute | solution.py:617
  130.9 2.5 %pass_on.3 = bf16[3,1536,128]{2,1,0:T(8,128)(2,1)S(1)} custom-call(bf16[3,1536,128]{2,1,0:T(8,128)(2,1)} %fold.6.own, bf16[3,1536,128]{2,1,0:T(8,128)(2,1)} %collective-permute-done.22.got), custom_call_target="tpu_custom_call" | custom-call | flops 1179648 | bytes 3538944 | tf_op jit(solution)/shard_map/pass_on/pallas_call | solution.py:572
  133.4 2.5 %collective-permute-start.23 = (bf16[3,1536,128]{2,1,0:T(8,128)(2,1)S(1)}, bf16[3,1536,128]{2,1,0:T(8,128)(2,1)S(1)}, u32[]{:S(2)}, u32[]{:S(2)}) collective-permute-start(bf16[3,1536,128]{2,1,0:T(8,128)(2,1)S(1)} %pass_on.3), channel_id=1, source_target_pairs={{8,16},{12,20},{16,8},{20,12},{9,17},{13,21},{17,9},{21,13},{10,18... | collective-permute-start | bytes 3538952 | tf_op jit(solution)/shard_map/ppermute | solution.py:617
  136.0 2.1 %fusion.1 = bf16[128,2048]{1,0:T(8,128)(2,1)} fusion(bf16[128,2048]{1,0:T(8,128)(2,1)} %collective-permute-done.16, bf16[1,128,2048]{2,1,0:T(8,128)(2,1)S(1)} %copy-done.11, bf16[2,128,2048]{2,1,0:T(8,128)(2,1)S(1)} %copy-done.19), kind=kLoop, calls=%fused_computation.4 | loop fusion | flops 1572864 | bytes 2097152 | tf_op jit(solution)/shard_map/convert_element_type | solution.py:507
  138.1 2.1 %fusion = bf16[128,2048]{1,0:T(8,128)(2,1)} fusion(bf16[128,2048]{1,0:T(8,128)(2,1)} %collective-permute-done.18, bf16[1,128,2048]{2,1,0:T(8,128)(2,1)S(1)} %copy-done.9, bf16[2,128,2048]{2,1,0:T(8,128)(2,1)S(1)} %copy-done.17), kind=kLoop, calls=%fused_computation.2 | loop fusion | flops 1572864 | bytes 2097152 | tf_op jit(solution)/shard_map/convert_element_type | solution.py:507
  140.3 14.3 %collective-permute-done.21.refs_1_ = bf16[3,1536,128]{2,1,0:T(8,128)(2,1)S(1)} collective-permute-done((bf16[3,1536,128]{2,1,0:T(8,128)(2,1)S(1)}, bf16[3,1536,128]{2,1,0:T(8,128)(2,1)S(1)}, u32[]{:S(2)}, u32[]{:S(2)}) %collective-permute-start.21) | collective-permute-done | bytes 1179680 | tf_op jit(solution)/shard_map/ppermute | solution.py:617
  154.5 5.7 %collective-permute-done.23.refs_2_ = bf16[3,1536,128]{2,1,0:T(8,128)(2,1)S(1)} collective-permute-done((bf16[3,1536,128]{2,1,0:T(8,128)(2,1)S(1)}, bf16[3,1536,128]{2,1,0:T(8,128)(2,1)S(1)}, u32[]{:S(2)}, u32[]{:S(2)}) %collective-permute-start.23) | collective-permute-done | bytes 1179680 | tf_op jit(solution)/shard_map/ppermute | solution.py:617
  160.2 2.2 %unfold.1 = (bf16[1,256,768]{2,1,0:T(8,128)(2,1)}, bf16[1,256,768]{2,1,0:T(8,128)(2,1)}, bf16[1,96,2048]{2,1,0:T(8,128)(2,1)}) custom-call(bf16[3,1536,128]{2,1,0:T(8,128)(2,1)S(1)} %broadcast_select_fusion.refs_0_, bf16[3,1536,128]{2,1,0:T(8,128)(2,1)S(1)} %collective-permute-done.21.refs_1_, bf16[3,1536,128]{2,1,0:T(8,128)(2,1)S(1)} %collective-permute-done.23.refs_2_, ...), custom_call_target="tpu_custom_call" | custom-call | flops 2359296 | bytes 5898240 | tf_op jit(solution)/shard_map/unfold/pallas_call | solution.py:602
  (87 shorter events, 22.2 us)
Async XLA Ops:
  0.6 19.3 %collective-permute-start = (bf16[128,2048]{1,0:T(8,128)(2,1)}, bf16[128,2048]{1,0:T(8,128)(2,1)S(1)}, u32[]{:S(2)}, u32[]{:S(2)}) collective-permute-start(bf16[128,2048]{1,0:T(8,128)(2,1)} %refs_0_.1), channel_id=1, source_target_pairs={{0,1},{1,0},{2,3},{3,2},{4,5},{5,4},{6,7},{7,6},{8,9},{9,8},{10,11... | collective-permute-start | bytes 1572872 | tf_op jit(solution)/shard_map/ppermute | solution.py:209
  2.2 17.7 %collective-permute-start.1 = (bf16[128,2048]{1,0:T(8,128)(2,1)}, bf16[128,2048]{1,0:T(8,128)(2,1)S(1)}, u32[]{:S(2)}, u32[]{:S(2)}) collective-permute-start(bf16[128,2048]{1,0:T(8,128)(2,1)} %refs_0_.1), channel_id=1, source_target_pairs={{0,2},{1,3},{2,0},{3,1},{4,6},{5,7},{6,4},{7,5},{8,10},{9,11},{10,... | collective-permute-start | bytes 1572872 | tf_op jit(solution)/shard_map/ppermute | solution.py:209
  2.7 28.2 %copy-start.14 = (bf16[1,768,2048]{2,1,0:T(8,128)(2,1)S(1)}, bf16[1,768,2048]{2,1,0:T(8,128)(2,1)}, u32[]{:S(2)}) copy-start(bf16[1,768,2048]{2,1,0:T(8,128)(2,1)} %param.19) | copy-start | bytes 9437188
  4.8 6.1 %collective-permute-start.4 = (bf16[32,2176]{1,0:T(8,128)(2,1)S(1)}, bf16[32,2176]{1,0:T(8,128)(2,1)S(1)}, u32[]{:S(2)}, u32[]{:S(2)}) collective-permute-start(bf16[32,2176]{1,0:T(8,128)(2,1)S(1)} %get-tuple-element.48), channel_id=1, source_target_pairs={{0,8},{4,12},{8,0},{12,4},{16,24},{20,28},{24,16},{28,20},{1,9},{5... | collective-permute-start | bytes 417800 | tf_op jit(solution)/shard_map/ppermute | solution.py:183
  5.3 12.2 %collective-permute-start.5 = (bf16[32,2176]{1,0:T(8,128)(2,1)S(1)}, bf16[32,2176]{1,0:T(8,128)(2,1)S(1)}, u32[]{:S(2)}, u32[]{:S(2)}) collective-permute-start(bf16[32,2176]{1,0:T(8,128)(2,1)S(1)} %get-tuple-element.49), channel_id=1, source_target_pairs={{0,16},{4,20},{8,24},{12,28},{16,0},{20,4},{24,8},{28,12},{1,17},{... | collective-permute-start | bytes 417800 | tf_op jit(solution)/shard_map/ppermute | solution.py:183
  7.9 12.0 %collective-permute-start.6 = (bf16[32,2176]{1,0:T(8,128)(2,1)S(1)}, bf16[32,2176]{1,0:T(8,128)(2,1)S(1)}, u32[]{:S(2)}, u32[]{:S(2)}) collective-permute-start(bf16[32,2176]{1,0:T(8,128)(2,1)S(1)} %get-tuple-element.50), channel_id=1, source_target_pairs={{0,24},{4,28},{8,16},{12,20},{16,8},{20,12},{24,0},{28,4},{1,25},{... | collective-permute-start | bytes 417800 | tf_op jit(solution)/shard_map/ppermute | solution.py:183
  20.0 2.3 %collective-permute-start.7 = (bf16[64,2176]{1,0:T(8,128)(2,1)S(1)}, bf16[64,2176]{1,0:T(8,128)(2,1)S(1)}, u32[]{:S(2)}, u32[]{:S(2)}) collective-permute-start(bf16[64,2176]{1,0:T(8,128)(2,1)S(1)} %get-tuple-element.52), channel_id=1, source_target_pairs={{0,4},{4,0},{8,12},{12,8},{16,20},{20,16},{24,28},{28,24},{1,5},{5... | collective-permute-start | bytes 835592 | tf_op jit(solution)/shard_map/ppermute | solution.py:185
  20.1 9.2 %collective-permute-start.2 = (bf16[64,2048]{1,0:T(8,128)(2,1)S(1)}, bf16[64,2048]{1,0:T(8,128)(2,1)S(1)}, u32[]{:S(2)}, u32[]{:S(2)}) collective-permute-start(bf16[64,2048]{1,0:T(8,128)(2,1)S(1)} %slice.24), channel_id=1, source_target_pairs={{0,2},{1,3},{2,0},{3,1},{4,6},{5,7},{6,4},{7,5},{8,10},{9,11},{10,... | collective-permute-start | bytes 786440 | tf_op jit(solution)/shard_map/ppermute | solution.py:209
  21.7 9.2 %collective-permute-start.3 = (bf16[64,2048]{1,0:T(8,128)(2,1)S(1)}, bf16[64,2048]{1,0:T(8,128)(2,1)S(1)}, u32[]{:S(2)}, u32[]{:S(2)}) collective-permute-start(bf16[64,2048]{1,0:T(8,128)(2,1)S(1)} %slice.25), channel_id=1, source_target_pairs={{0,1},{1,0},{2,3},{3,2},{4,5},{5,4},{6,7},{7,6},{8,9},{9,8},{10,11... | collective-permute-start | bytes 786440 | tf_op jit(solution)/shard_map/ppermute | solution.py:209
  22.3 20.5 %copy-start.6 = (bf16[1,2048,768]{2,1,0:T(8,128)(2,1)S(1)}, bf16[1,2048,768]{2,1,0:T(8,128)(2,1)}, u32[]{:S(2)}) copy-start(bf16[1,2048,768]{2,1,0:T(8,128)(2,1)} %param.18) | copy-start | bytes 9437188
  22.6 14.3 %collective-permute-start.8 = (bf16[64,2176]{1,0:T(8,128)(2,1)S(1)}, bf16[64,2176]{1,0:T(8,128)(2,1)S(1)}, u32[]{:S(2)}, u32[]{:S(2)}) collective-permute-start(bf16[64,2176]{1,0:T(8,128)(2,1)S(1)} %get-tuple-element.53.refs_0_), channel_id=1, source_target_pairs={{0,1},{1,0},{2,3},{3,2},{4,5},{5,4},{6,7},{7,6},{8,9},{9,8},{10,11... | collective-permute-start | bytes 835592 | tf_op jit(solution)/shard_map/ppermute | solution.py:209
  24.2 12.7 %collective-permute-start.11 = (bf16[64,2176]{1,0:T(8,128)(2,1)S(1)}, bf16[64,2176]{1,0:T(8,128)(2,1)S(1)}, u32[]{:S(2)}, u32[]{:S(2)}) collective-permute-start(bf16[64,2176]{1,0:T(8,128)(2,1)S(1)} %get-tuple-element.54.refs_1_), channel_id=1, source_target_pairs={{0,2},{1,3},{2,0},{3,1},{4,6},{5,7},{6,4},{7,5},{8,10},{9,11},{10,... | collective-permute-start | bytes 835592 | tf_op jit(solution)/shard_map/ppermute | solution.py:209
  24.7 18.2 %collective-permute-start.9 = (bf16[64,2176]{1,0:T(8,128)(2,1)S(1)}, bf16[64,2176]{1,0:T(8,128)(2,1)S(1)}, u32[]{:S(2)}, u32[]{:S(2)}) collective-permute-start(bf16[64,2176]{1,0:T(8,128)(2,1)S(1)} %get-tuple-element.54.refs_1_), channel_id=1, source_target_pairs={{0,1},{1,0},{2,3},{3,2},{4,5},{5,4},{6,7},{7,6},{8,9},{9,8},{10,11... | collective-permute-start | bytes 835592 | tf_op jit(solution)/shard_map/ppermute | solution.py:209
  29.3 13.6 %collective-permute-start.10 = (bf16[64,2176]{1,0:T(8,128)(2,1)S(1)}, bf16[64,2176]{1,0:T(8,128)(2,1)S(1)}, u32[]{:S(2)}, u32[]{:S(2)}) collective-permute-start(bf16[64,2176]{1,0:T(8,128)(2,1)S(1)} %get-tuple-element.53.refs_0_), channel_id=1, source_target_pairs={{0,2},{1,3},{2,0},{3,1},{4,6},{5,7},{6,4},{7,5},{8,10},{9,11},{10,... | collective-permute-start | bytes 835592 | tf_op jit(solution)/shard_map/ppermute | solution.py:209
  36.9 11.5 %collective-permute-start.12 = (bf16[64,2176]{1,0:T(8,128)(2,1)S(1)}, bf16[64,2176]{1,0:T(8,128)(2,1)S(1)}, u32[]{:S(2)}, u32[]{:S(2)}) collective-permute-start(bf16[64,2176]{1,0:T(8,128)(2,1)S(1)} %collective-permute-done.8.refs_2_), channel_id=1, source_target_pairs={{0,2},{1,3},{2,0},{3,1},{4,6},{5,7},{6,4},{7,5},{8,10},{9,11},{10,... | collective-permute-start | bytes 835592 | tf_op jit(solution)/shard_map/ppermute | solution.py:209
  37.4 11.0 %collective-permute-start.13 = (bf16[64,2176]{1,0:T(8,128)(2,1)S(1)}, bf16[64,2176]{1,0:T(8,128)(2,1)S(1)}, u32[]{:S(2)}, u32[]{:S(2)}) collective-permute-start(bf16[64,2176]{1,0:T(8,128)(2,1)S(1)} %collective-permute-done.11.refs_5_), channel_id=1, source_target_pairs={{0,1},{1,0},{2,3},{3,2},{4,5},{5,4},{6,7},{7,6},{8,9},{9,8},{10,11... | collective-permute-start | bytes 835592 | tf_op jit(solution)/shard_map/ppermute | solution.py:209
  53.9 4.1 %collective-permute-start.14 = (bf16[2,256,768]{2,1,0:T(8,128)(2,1)}, bf16[2,256,768]{2,1,0:T(8,128)(2,1)S(1)}, u32[]{:S(2)}, u32[]{:S(2)}) collective-permute-start(bf16[2,256,768]{2,1,0:T(8,128)(2,1)} %get-tuple-element.68), channel_id=1, source_target_pairs={{0,4},{4,0},{8,12},{12,8},{16,20},{20,16},{24,28},{28,24},{1,5},{5... | collective-permute-start | bytes 2359304 | tf_op jit(solution)/shard_map/ppermute | solution.py:635
  57.5 4.6 %collective-permute-start.20 = (bf16[4,96,2048]{2,1,0:T(8,128)(2,1)}, bf16[4,96,2048]{2,1,0:T(8,128)(2,1)S(1)}, u32[]{:S(2)}, u32[]{:S(2)}) collective-permute-start(bf16[4,96,2048]{2,1,0:T(8,128)(2,1)} %get-tuple-element.78), channel_id=1, source_target_pairs={{0,4},{4,0},{8,12},{12,8},{16,20},{20,16},{24,28},{28,24},{1,5},{5... | collective-permute-start | bytes 4718600 | tf_op jit(solution)/shard_map/ppermute | solution.py:635
  62.1 35.8 %collective-permute-start.19 = (bf16[3,2,256,768]{3,2,1,0:T(8,128)(2,1)}, bf16[3,2,256,768]{3,2,1,0:T(8,128)(2,1)S(1)}, u32[]{:S(2)}, u32[]{:S(2)}) collective-permute-start(bf16[3,2,256,768]{3,2,1,0:T(8,128)(2,1)} %get-tuple-element.81), channel_id=1, source_target_pairs={{0,4},{4,0},{8,12},{12,8},{16,20},{20,16},{24,28},{28,24},{1,5},{5... | collective-permute-start | bytes 7077896 | tf_op jit(solution)/shard_map/ppermute | solution.py:635
  62.5 30.3 %collective-permute-start.24 = (bf16[3,1536,128]{2,1,0:T(8,128)(2,1)S(1)}, bf16[3,1536,128]{2,1,0:T(8,128)(2,1)S(1)}, u32[]{:S(2)}, u32[]{:S(2)}) collective-permute-start(bf16[3,1536,128]{2,1,0:T(8,128)(2,1)S(1)} %fold.7.own), channel_id=1, source_target_pairs={{0,8},{4,12},{24,16},{28,20},{1,9},{5,13},{25,17},{29,21},{2,10},{... | collective-permute-start | bytes 3538952 | tf_op jit(solution)/shard_map/ppermute | solution.py:617
  69.9 24.5 %copy-start.8 = (bf16[1,128,2048]{2,1,0:T(8,128)(2,1)}, bf16[1,128,2048]{2,1,0:T(8,128)(2,1)S(1)}, u32[]{:S(2)}) copy-start(bf16[1,128,2048]{2,1,0:T(8,128)(2,1)S(1)} %get-tuple-element.72) | copy-start | bytes 1572868
  69.9 24.5 %copy-start.10 = (bf16[1,128,2048]{2,1,0:T(8,128)(2,1)}, bf16[1,128,2048]{2,1,0:T(8,128)(2,1)S(1)}, u32[]{:S(2)}) copy-start(bf16[1,128,2048]{2,1,0:T(8,128)(2,1)S(1)} %get-tuple-element.69) | copy-start | bytes 1572868
  69.9 31.2 %collective-permute-start.15 = (bf16[2,128,2048]{2,1,0:T(8,128)(2,1)S(1)}, bf16[2,128,2048]{2,1,0:T(8,128)(2,1)S(1)}, u32[]{:S(2)}, u32[]{:S(2)}) collective-permute-start(bf16[2,128,2048]{2,1,0:T(8,128)(2,1)S(1)} %get-tuple-element.70), channel_id=1, source_target_pairs={{0,1},{1,0},{2,3},{3,2},{4,5},{5,4},{6,7},{7,6},{8,9},{9,8},{10,11... | collective-permute-start | bytes 3145736 | tf_op jit(solution)/shard_map/ppermute | solution.py:209
  70.5 27.4 %copy-start.1 = (bf16[3,2,256,768]{3,2,1,0:T(8,128)(2,1)S(1)}, bf16[3,2,256,768]{3,2,1,0:T(8,128)(2,1)}, u32[]{:S(2)}) copy-start(bf16[3,2,256,768]{3,2,1,0:T(8,128)(2,1)} %get-tuple-element.80.gu_mine) | copy-start | bytes 7077892
  70.5 32.2 %collective-permute-start.17 = (bf16[2,128,2048]{2,1,0:T(8,128)(2,1)S(1)}, bf16[2,128,2048]{2,1,0:T(8,128)(2,1)S(1)}, u32[]{:S(2)}, u32[]{:S(2)}) collective-permute-start(bf16[2,128,2048]{2,1,0:T(8,128)(2,1)S(1)} %get-tuple-element.73), channel_id=1, source_target_pairs={{0,2},{1,3},{2,0},{3,1},{4,6},{5,7},{6,4},{7,5},{8,10},{9,11},{10,... | collective-permute-start | bytes 3145736 | tf_op jit(solution)/shard_map/ppermute | solution.py:209
  94.4 29.8 %collective-permute-start.25 = (bf16[3,1536,128]{2,1,0:T(8,128)(2,1)}, bf16[3,1536,128]{2,1,0:T(8,128)(2,1)}, u32[]{:S(2)}, u32[]{:S(2)}) collective-permute-start(bf16[3,1536,128]{2,1,0:T(8,128)(2,1)} %pass_on.4), channel_id=1, source_target_pairs={{8,16},{12,20},{16,8},{20,12},{9,17},{13,21},{17,9},{21,13},{10,18... | collective-permute-start | bytes 3538952 | tf_op jit(solution)/shard_map/ppermute | solution.py:617
  99.8 31.1 %collective-permute-start.22 = (bf16[3,1536,128]{2,1,0:T(8,128)(2,1)}, bf16[3,1536,128]{2,1,0:T(8,128)(2,1)}, u32[]{:S(2)}, u32[]{:S(2)}) collective-permute-start(bf16[3,1536,128]{2,1,0:T(8,128)(2,1)} %fold.6.own), channel_id=1, source_target_pairs={{0,8},{4,12},{24,16},{28,20},{1,9},{5,13},{25,17},{29,21},{2,10},{... | collective-permute-start | bytes 3538952 | tf_op jit(solution)/shard_map/ppermute | solution.py:617
  102.2 33.7 %collective-permute-start.16 = (bf16[128,2048]{1,0:T(8,128)(2,1)}, bf16[128,2048]{1,0:T(8,128)(2,1)}, u32[]{:S(2)}, u32[]{:S(2)}) collective-permute-start(bf16[128,2048]{1,0:T(8,128)(2,1)} %fusion.2), channel_id=1, source_target_pairs={{0,2},{1,3},{2,0},{3,1},{4,6},{5,7},{6,4},{7,5},{8,10},{9,11},{10,... | collective-permute-start | bytes 1572872 | tf_op jit(solution)/shard_map/ppermute | solution.py:209
  103.8 34.2 %collective-permute-start.18 = (bf16[128,2048]{1,0:T(8,128)(2,1)}, bf16[128,2048]{1,0:T(8,128)(2,1)}, u32[]{:S(2)}, u32[]{:S(2)}) collective-permute-start(bf16[128,2048]{1,0:T(8,128)(2,1)} %fusion.3), channel_id=1, source_target_pairs={{0,1},{1,0},{2,3},{3,2},{4,5},{5,4},{6,7},{7,6},{8,9},{9,8},{10,11... | collective-permute-start | bytes 1572872 | tf_op jit(solution)/shard_map/ppermute | solution.py:209
  108.1 46.5 %collective-permute-start.21 = (bf16[3,1536,128]{2,1,0:T(8,128)(2,1)S(1)}, bf16[3,1536,128]{2,1,0:T(8,128)(2,1)S(1)}, u32[]{:S(2)}, u32[]{:S(2)}) collective-permute-start(bf16[3,1536,128]{2,1,0:T(8,128)(2,1)S(1)} %fold.4), channel_id=1, source_target_pairs={{0,8},{4,12},{24,16},{28,20},{1,9},{5,13},{25,17},{29,21},{2,10},{... | collective-permute-start | bytes 3538952 | tf_op jit(solution)/shard_map/ppermute | solution.py:617
  126.4 28.1 %collective-permute-start.26 = (bf16[3,1536,128]{2,1,0:T(8,128)(2,1)S(1)}, bf16[3,1536,128]{2,1,0:T(8,128)(2,1)S(1)}, u32[]{:S(2)}, u32[]{:S(2)}) collective-permute-start(bf16[3,1536,128]{2,1,0:T(8,128)(2,1)S(1)} %pass_on.5), channel_id=1, source_target_pairs={{16,24},{20,28},{8,0},{12,4},{17,25},{21,29},{9,1},{13,5},{18,26},... | collective-permute-start | bytes 3538952 | tf_op jit(solution)/shard_map/ppermute | solution.py:617
  133.4 26.8 %collective-permute-start.23 = (bf16[3,1536,128]{2,1,0:T(8,128)(2,1)S(1)}, bf16[3,1536,128]{2,1,0:T(8,128)(2,1)S(1)}, u32[]{:S(2)}, u32[]{:S(2)}) collective-permute-start(bf16[3,1536,128]{2,1,0:T(8,128)(2,1)S(1)} %pass_on.3), channel_id=1, source_target_pairs={{8,16},{12,20},{16,8},{20,12},{9,17},{13,21},{17,9},{21,13},{10,18... | collective-permute-start | bytes 3538952 | tf_op jit(solution)/shard_map/ppermute | solution.py:617
  (15 other events, 63.3 us)

commit v4 on v3

--- a/solution.py
+++ b/solution.py
@@ -567,27 +567,54 @@
     refs[-1][...] = (own[...].astype(F32) + got[...].astype(F32)).astype(BF16)
 
 
-def pass_on(own, at, got, after):
-    block = pl.BlockSpec((1,) + got.shape[1:], lambda j: (j, 0, 0))
+def pass_on(own, got, piece, pieces, whole, after):
+    per = whole // pieces
+
+    def part(array):
+        at = piece if array.shape[1] > per else 0
+        return pl.BlockSpec((1, per, LANES), lambda j: (j, at, 0))
+
     return pl.pallas_call(
         pass_on_kernel,
         grid=(got.shape[0],),
-        in_specs=[pl.BlockSpec((1,) + got.shape[1:], lambda j: (j, at, 0)), block] + [hbm()] * len(after),
-        out_specs=block,
-        out_shape=jax.ShapeDtypeStruct(got.shape, BF16),
+        in_specs=[part(own), part(got)] + [hbm()] * len(after),
+        out_specs=pl.BlockSpec((1, per, LANES), lambda j: (j, 0, 0)),
+        out_shape=jax.ShapeDtypeStruct((got.shape[0], per, LANES), BF16),
         compiler_params=params(16),
         cost_estimate=cost(2 * got.size, 6 * got.size),
         name="pass_on",
     )(own, got, *after)
 
 
-def unfold_kernel(count, *refs):
-    parts, outs = refs[:count], refs[count:]
-    per = max(part.shape[1] for part in parts)
-    total = sum(part[0].astype(F32) for part in parts if part.shape[1] == per)
-    pieces = [part[0].astype(F32) for part in parts if part.shape[1] < per]
-    if pieces:
-        total = total + jnp.concatenate(pieces, axis=0)
+def choose_kernel(place_ref, one, other, *refs):
+    refs[-1][...] = jnp.where(place_ref[0] > 0, one[...].astype(F32), other[...].astype(F32)).astype(BF16)
+
+
+def choose(place, one, other, after):
+    block = pl.BlockSpec((1,) + one.shape[1:], lambda j, place: (j, 0, 0))
+    return pl.pallas_call(
+        choose_kernel,
+        grid_spec=pltpu.PrefetchScalarGridSpec(
+            num_scalar_prefetch=1,
+            grid=(one.shape[0],),
+            in_specs=[block, block] + [hbm()] * len(after),
+            out_specs=block,
+        ),
+        out_shape=jax.ShapeDtypeStruct(one.shape, BF16),
+        compiler_params=params(16),
+        cost_estimate=cost(one.size, 6 * one.size),
+        name="choose",
+    )(place.reshape(1).astype(jnp.int32), one, other, *after)
+
+
+def unfold_kernel(counts, *refs):
+    parts, outs = refs[: sum(counts)], refs[sum(counts) :]
+    total, at = None, 0
+    for count in counts:
+        pieces = [part[0].astype(F32) for part in parts[at : at + count]]
+        value = pieces[0] if count == 1 else jnp.concatenate(pieces, axis=0)
+        total = value if total is None else total + value
+        at += count
     total = total.astype(BF16)
     for j, out in enumerate(outs):
 
@@ -598,9 +625,10 @@
                 out[0, :, i * LANES : (i + 1) * LANES] = total[i * rows : (i + 1) * rows]
 
 
-def unfold(parts, shapes):
-    return pl.pallas_call(
-        functools.partial(unfold_kernel, len(parts)),
+def unfold(groups, shapes):
+    parts = [part for group in groups for part in group]
+    return pl.pallas_call(
+        functools.partial(unfold_kernel, [len(group) for group in groups]),
         grid=(3,),
         in_specs=[pl.BlockSpec((1,) + part.shape[1:], lambda j: (j, 0, 0)) for part in parts],
         out_specs=[pl.BlockSpec(shape, lambda j: (0, 0, 0)) for shape in shapes],
@@ -611,9 +639,7 @@
     )(*parts)
 
 
-def line_permute(value, link, n_dp):
-    n_z = n_dp // CORES
-    pairs = [(link, link + 1), (n_z - 1 - link, n_z - 2 - link)]
+def chips_permute(value, pairs, n_dp):
     return lax.ppermute(value, "dp", [(CORES * a + c, CORES * b + c) for a, b in pairs for c in range(CORES)])
 
 
@@ -651,39 +677,47 @@
     far_got = swap_core(far_other)
     row_other, row_mine = row_grad(tie(turned_hs, far_other), dy_all, n_dp)
     row_got = swap_core(row_other)
-    rest_other, rest_mine = rest_grads(tie(turned_x, row_other), gate_grad, up_grad, far_got, n_dp)
+    whole = w_gate.shape[1] * w_gate.shape[2] // n_dp // LANES
+    far_sum = fold(far_mine[None], far_got[None], row_mine, row_got, 0, 0, 0, 1, [])
+    rest_other, rest_mine = rest_grads(turned_x, gate_grad, up_grad, far_got, n_dp)
     rest_got = swap_core(rest_other)
-    far_mine, far_got = far_mine[None], far_got[None]
-
-    def pieces(k):
-        return PIECES if k == far else 1
-
-    sums = []
-    for k in range(n_z):
-        gu = (far_mine, far_got) if k == far else (rest_mine, rest_got)
-        at = max(far - 1 - k, 0)
-        sums.append([fold(*gu, row_mine, row_got, at, far - k, p, pieces(k), []) for p in range(pieces(k))])
-    passed, ends = {}, []
-    for link in range(n_z - 1):
-        for d in range(far, link, -1):
-            for p in range(pieces(d)):
-                here = sums[d if link < n_z // 2 else far - d]
-                if link == 0:
-                    value = here[p]
-                else:
-                    own, at = (here[p], 0) if len(here) == pieces(d) else (here[0], p)
-                    value = pass_on(own, at, passed[link - 1, d, p], [])
-                passed[link, d, p] = line_permute(value, link, n_dp)
+
+    def block(k, *after):
+        return fold(rest_mine, rest_got, row_mine, row_got, far - 1 - k, far - k, 0, 1, after)
+
+    if n_z == 4:
+        outward, across = [(0, 1), (3, 2)], [(0, 1), (1, 0), (2, 3), (3, 2)]
+        three = chips_permute(far_sum, outward, n_dp)
+        sum_two = block(2)
+        two = chips_permute(sum_two, outward, n_dp)
+        sum_one, sum_none = block(1), block(0)
+        three_sum = pass_on(far_sum, three, 0, 1, whole, [sum_two])
+        three_on = chips_permute(three_sum, [(1, 3), (2, 0)], n_dp)
+        two_sum = pass_on(sum_two, two, 0, 1, whole, [three_on])
+        two_on = chips_permute(two_sum, [(1, 2), (2, 1)], n_dp)
+        last = chips_permute(choose(near, sum_none, sum_one, [two]), across, n_dp)
+        own = add(jnp.where(near > 0, sum_one, sum_none), three_on)
+        ends = [[last], [two_on]]
+    else:
+        sums = [block(k) for k in range(far)] + [far_sum]
+        passed, ends = {}, []
+        for link in range(far):
+            for d in range(far, link, -1):
+                value = sums[d if link < n_z // 2 else far - d]
+                if link > 0:
+                    value = pass_on(value, passed[link - 1, d], 0, 1, whole, [])
+                pairs = [(link, link + 1), (far - link, far - 1 - link)]
+                passed[link, d] = chips_permute(value, pairs, n_dp)
                 if d == link + 1:
-                    ends.append(passed[link, d, p])
-    own = sums[0][0]
-    for k in range(1, (n_z + 1) // 2):
-        own = jnp.where(near == k, sums[k][0], own)
+                    ends.append([passed[link, d]])
+        own = sums[0]
+        for k in range(1, (n_z + 1) // 2):
+            own = jnp.where(near == k, sums[k], own)
     shapes = [(1, w_gate.shape[1] // n_dp, w_gate.shape[2])] * 2 + [(1, w_down.shape[1] // n_dp, w_down.shape[2])]
-    totals = unfold([own] + ends, shapes)
+    totals = unfold([[own]] + ends, shapes)
 
     layer_out, input_grad, _ = outputs_home(
-        hid, gates, gate_grad, up_grad, weight_down, weight_gate, weight_up, far_got, n_ex
+        hid, gates, gate_grad, up_grad, weight_down, weight_gate, weight_up, far_sum, n_ex
     )
     return layer_out, input_grad, *totals
 

time: 163 us -> 155 us (0.951)
  waiting for transfers between devices: 81.7 us -> 77.3 us
  starting transfers between devices: 27.3 us -> 24.9 us
  Pallas kernels: 41.5 us -> 39.2 us
    ppermute x6 -> x5, waiting for transfers between devices: 59.2 us -> 54.7 us  [chips_permute(): lax.ppermute(value, 'dp', [(CORES * a + c, CORES * b + c) for a, b in pai...]
    ppermute x6 -> x5, starting transfers between devices: 11.3 us -> 8.9 us  [chips_permute(): lax.ppermute(value, 'dp', [(CORES * a + c, CORES * b + c) for a, b in pai...]
    pallas_call x4, Pallas kernels: 8.58 us -> 6.43 us  [the longest x2 4.17 us: pass_on(): pl.pallas_call(pass_on_kernel, grid=(got.shape[0],), in_specs=[part(own),...]
    convert_element_type x4 -> x5, other arithmetic: 6.27 us -> 7.97 us  [add(): return sum((part.astype(F32) for part in parts)).astype(BF16)]
  transfers between devices with their start and end apart: 27 -> 26, of which waited for: 12 -> 12; matrix products, arithmetic and copies ran while one was open for 4% -> 5% of each run, Pallas kernels for 21% -> 21%
where the time goes in v4:
time: 155 us
  waiting for transfers between devices  77.3 us (50%)
  Pallas kernels  39.2 us (25%)
  starting transfers between devices  24.9 us (16%)
  other arithmetic  7.97 us (5%)
  local copies, waits for them, and re-layouts  4.55 us (3%)
    ppermute x5, waiting for transfers between devices, chips_permute(): lax.ppermute(value, 'dp', [(CORES * a + c, CORES * b + c) for a, b in pai...  54.7 us
    ppermute x14, starting transfers between devices, swap(): return lax.ppermute(value, 'expert', [(d, d ^ i) for d in range(n_ex)])  11.9 us
    ppermute x3, waiting for transfers between devices, send_sequences(): lax.ppermute(pieces[i], 'dp', [(d, d ^ CORES * i) for d in range(n_dp)])  11.5 us
    ppermute x14, waiting for transfers between devices, swap(): return lax.ppermute(value, 'expert', [(d, d ^ i) for d in range(n_ex)])  11 us
    ppermute x5, starting transfers between devices, chips_permute(): lax.ppermute(value, 'dp', [(CORES * a + c, CORES * b + c) for a, b in pai...  8.9 us
    pallas_call x2, Pallas kernels, hidden_units(): pl.pallas_call(functools.partial(units_kernel, len(pieces), slot, not bef...  8.46 us
    convert_element_type x5, other arithmetic, add(): return sum((part.astype(F32) for part in parts)).astype(BF16)  7.97 us
    pallas_call x1, Pallas kernels, outputs(): pl.pallas_call(functools.partial(outputs_kernel, layer_groups, grad_group...  6.14 us
  transfers between devices with their start and end apart: 26, of which 12 were waited for; matrix products, arithmetic and copies ran while one was open for 5% of the time, Pallas kernels for 21%

profile of v4, /device:TPU:12, one launch (start us, length us, event | category | flops | bytes accessed | tf_op | source)
XLA Modules:
  0.0 154.9 jit_solution(6222250596957958686)
XLA Ops:
  2.7 2.1 %pick.1 = (bf16[32,2176]{1,0:T(8,128)(2,1)S(1)}, bf16[32,2176]{1,0:T(8,128)(2,1)S(1)}, bf16[32,2176]{1,0:T(8,128)(2,1)S(1)}, bf16[32,2176]{1,0:T(8,128)(2,1)S(1)}) custom-call(s32[1,1,8]{2,1,0:T(1,128)} %dest_hbm.1, s32[1,1,8]{2,1,0:T(1,128)} %len_hbm.1, bf16[1,1,8]{2,1,0:T(2,128)(2,1)} %adv_hbm.1, bf16[8,16,2048]{2,1,0:T(8,128)(2,1)} %bitcast.33), custom_call_target="tpu_custom_call" | custom-call | tf_op jit(solution)/shard_map/pick/pallas_call | solution.py:94
  5.3 2.6 %collective-permute-start.5 = (bf16[32,2176]{1,0:T(8,128)(2,1)S(1)}, bf16[32,2176]{1,0:T(8,128)(2,1)S(1)}, u32[]{:S(2)}, u32[]{:S(2)}) collective-permute-start(bf16[32,2176]{1,0:T(8,128)(2,1)S(1)} %get-tuple-element.48), channel_id=1, source_target_pairs={{0,16},{4,20},{8,24},{12,28},{16,0},{20,4},{24,8},{28,12},{1,17},{... | collective-permute-start | bytes 417800 | tf_op jit(solution)/shard_map/ppermute | solution.py:183
  8.4 2.5 %collective-permute-done.4.refs_1_ = bf16[32,2176]{1,0:T(8,128)(2,1)S(1)} collective-permute-done((bf16[32,2176]{1,0:T(8,128)(2,1)S(1)}, bf16[32,2176]{1,0:T(8,128)(2,1)S(1)}, u32[]{:S(2)}, u32[]{:S(2)}) %collective-permute-start.4) | collective-permute-done | bytes 139296 | tf_op jit(solution)/shard_map/ppermute | solution.py:183
  10.9 6.6 %collective-permute-done.5.refs_2_ = bf16[32,2176]{1,0:T(8,128)(2,1)S(1)} collective-permute-done((bf16[32,2176]{1,0:T(8,128)(2,1)S(1)}, bf16[32,2176]{1,0:T(8,128)(2,1)S(1)}, u32[]{:S(2)}, u32[]{:S(2)}) %collective-permute-start.5) | collective-permute-done | bytes 139296 | tf_op jit(solution)/shard_map/ppermute | solution.py:183
  17.5 2.4 %collective-permute-done.6.refs_3_ = bf16[32,2176]{1,0:T(8,128)(2,1)S(1)} collective-permute-done((bf16[32,2176]{1,0:T(8,128)(2,1)S(1)}, bf16[32,2176]{1,0:T(8,128)(2,1)S(1)}, u32[]{:S(2)}, u32[]{:S(2)}) %collective-permute-start.6) | collective-permute-done | bytes 139296 | tf_op jit(solution)/shard_map/ppermute | solution.py:183
  20.1 1.6 %collective-permute-start.2 = (bf16[64,2048]{1,0:T(8,128)(2,1)S(1)}, bf16[64,2048]{1,0:T(8,128)(2,1)S(1)}, u32[]{:S(2)}, u32[]{:S(2)}) collective-permute-start(bf16[64,2048]{1,0:T(8,128)(2,1)S(1)} %slice.24), channel_id=1, source_target_pairs={{0,2},{1,3},{2,0},{3,1},{4,6},{5,7},{6,4},{7,5},{8,10},{9,11},{10,... | collective-permute-start | bytes 786440 | tf_op jit(solution)/shard_map/ppermute | solution.py:209
  25.5 3.7 %collective-permute-done.2.refs_3_ = bf16[64,2048]{1,0:T(8,128)(2,1)S(1)} collective-permute-done((bf16[64,2048]{1,0:T(8,128)(2,1)S(1)}, bf16[64,2048]{1,0:T(8,128)(2,1)S(1)}, u32[]{:S(2)}, u32[]{:S(2)}) %collective-permute-start.2) | collective-permute-done | bytes 262176 | tf_op jit(solution)/shard_map/ppermute | solution.py:209
  32.0 2.7 %hidden_grad.1 = (f32[512,768]{1,0:T(8,128)S(1)}, bf16[512,2048]{1,0:T(8,128)(2,1)S(1)}) custom-call(bf16[768,2048]{1,0:T(8,128)(2,1)S(1)} %bitcast.31, bf16[128,2048]{1,0:T(8,128)(2,1)S(1)} %copy-done.15, bf16[128,2048]{1,0:T(8,128)(2,1)S(1)} %collective-permute-done.refs_1_.refs_4_, bf16[128,2048]{1,0:T(8,128)(2,1)S(1)} %collective-permute-done.1.refs_2_.refs_5_, ...), custom_call_target="tpu_custom_call" | custom-call | flops 1610612736 | bytes 7340032 | tf_op jit(solution)/shard_map/hidden_grad/pallas_call | solution.py:277
  34.7 2.2 %collective-permute-done.8.refs_2_ = bf16[64,2176]{1,0:T(8,128)(2,1)S(1)} collective-permute-done((bf16[64,2176]{1,0:T(8,128)(2,1)S(1)}, bf16[64,2176]{1,0:T(8,128)(2,1)S(1)}, u32[]{:S(2)}, u32[]{:S(2)}) %collective-permute-start.8) | collective-permute-done | bytes 278560 | tf_op jit(solution)/shard_map/ppermute | solution.py:209
  37.9 4.9 %collective-permute-done.9.refs_3_ = bf16[64,2176]{1,0:T(8,128)(2,1)S(1)} collective-permute-done((bf16[64,2176]{1,0:T(8,128)(2,1)S(1)}, bf16[64,2176]{1,0:T(8,128)(2,1)S(1)}, u32[]{:S(2)}, u32[]{:S(2)}) %collective-permute-start.9) | collective-permute-done | bytes 278560 | tf_op jit(solution)/shard_map/ppermute | solution.py:209
  42.9 5.6 %hidden_units.2 = (bf16[512,768]{1,0:T(8,128)(2,1)S(1)}, bf16[512,768]{1,0:T(8,128)(2,1)S(1)}, bf16[512,768]{1,0:T(8,128)(2,1)S(1)}, bf16[768,512]{1,0:T(8,128)(...) custom-call(bf16[2048,768]{1,0:T(8,128)(2,1)S(1)} %bitcast.21, bf16[2048,768]{1,0:T(8,128)(2,1)S(1)} %bitcast.24, ...), custom_call_target="tpu_custom_call" | custom-call | flops 2415919104 | bytes 9437184 | tf_op jit(solution)/shard_map/hidden_units/pallas_call | solution.py:355
  48.5 2.9 %hidden_units.3 = (bf16[512,768]{1,0:T(8,128)(2,1)S(1)}, bf16[512,768]{1,0:T(8,128)(2,1)S(1)}, bf16[512,768]{1,0:T(8,128)(2,1)S(1)}, bf16[768,512]{1,0:T(8,128)(...) custom-call(bf16[2048,768]{1,0:T(8,128)(2,1)S(1)} %bitcast.22, ...), custom_call_target="tpu_custom_call", output_to_operand_aliasing={{0}: (3, {}), {1}: (4, {}), {2}: (5, {}), {3}: (6, {}), {4}... | custom-call | flops 805306368 | bytes 7340032 | tf_op jit(solution)/shard_map/hidden_units/pallas_call | solution.py:355
  51.4 2.6 %far_grads.1 = (bf16[2,256,768]{2,1,0:T(8,128)(2,1)}, bf16[2,256,768]{2,1,0:T(8,128)(2,1)}) custom-call(bf16[2048,512]{1,0:T(8,128)(2,1)S(1)} %get-tuple-element.66.x_ref, bf16[512,768]{1,0:T(8,128)(2,1)S(1)} %get-tuple-element.64.gate_ref, bf16[512,768]{1,0:T(8,128)(2,1)S(1)} %get-tuple-element.65.up_ref), custom_call_target="tpu_custom_call" | custom-call | flops 805306368 | bytes 4718592 | tf_op jit(solution)/shard_map/far_grads/pallas_call | solution.py:404
  53.9 3.5 %row_grad.1 = (bf16[4,96,2048]{2,1,0:T(8,128)(2,1)}, bf16[4,96,2048]{2,1,0:T(8,128)(2,1)}) custom-call(bf16[768,512]{1,0:T(8,128)(2,1)S(1)} %get-tuple-element.70.hid_ref, bf16[512,2048]{1,0:T(8,128)(2,1)S(1)} %get-tuple-element.71.dy_ref), custom_call_target="tpu_custom_call" | custom-call | flops 1610612736 | bytes 5242880 | tf_op jit(solution)/shard_map/row_grad/pallas_call | solution.py:460
  58.0 4.0 %rest_grads.1 = (bf16[3,2,256,768]{3,2,1,0:T(8,128)(2,1)}, bf16[3,2,256,768]{3,2,1,0:T(8,128)(2,1)}) custom-call(bf16[2048,512]{1,0:T(8,128)(2,1)S(1)} %get-tuple-element.66.x_ref, bf16[512,768]{1,0:T(8,128)(2,1)S(1)} %get-tuple-element.64.gate_ref, bf16[512,768]{1,0:T(8,128)(2,1)S(1)} %get-tuple-element.65.up_ref, ...), custom_call_target="tpu_custom_call" | custom-call | flops 3221225472 | bytes 7864320 | tf_op jit(solution)/shard_map/rest_grads/pallas_call | solution.py:433
  63.7 6.1 %outputs.1 = (bf16[1,128,2048]{2,1,0:T(8,128)(2,1)S(1)}, bf16[1,128,2048]{2,1,0:T(8,128)(2,1)S(1)}, bf16[2,128,2048]{2,1,0:T(8,128)(2,1)S(1)}, bf16[1,128,2048]{...) custom-call(bf16[512,768]{1,0:T(8,128)(2,1)S(1)} %get-tuple-element.62.hid_ref, ...), custom_call_target="tpu_custom_call" | custom-call | flops 4831838208 | bytes 13631488 | tf_op jit(solution)/shard_map/outputs/pallas_call | solution.py:494
  71.0 1.9 %fold.7.refs_0_.own = bf16[3,1536,128]{2,1,0:T(8,128)(2,1)} custom-call(bf16[3,2,256,768]{3,2,1,0:T(8,128)(2,1)S(1)} %copy-done.1, bf16[3,2,256,768]{3,2,1,0:T(8,128)(2,1)S(1)} %collective-permute-done.20.gu_got, bf16[4,96,2048]{2,1,0:T(8,128)(2,1)S(1)} %copy-done, bf16[4,96,2048]{2,1,0:T(8,128)(2,1)S(1)} %collective-permute-done.15.row_got), custom_call_target="tpu_custom_call" | custom-call | flops 1179648 | bytes 3538944 | tf_op jit(solution)/shard_map/fold/pallas_call | solution.py:554
  74.2 18.9 %collective-permute-done.21.got = bf16[3,1536,128]{2,1,0:T(8,128)(2,1)S(1)} collective-permute-done((bf16[3,1536,128]{2,1,0:T(8,128)(2,1)S(1)}, bf16[3,1536,128]{2,1,0:T(8,128)(2,1)S(1)}, u32[]{:S(2)}, u32[]{:S(2)}) %collective-permute-start.21) | collective-permute-done | bytes 1179680 | tf_op jit(solution)/shard_map/ppermute | solution.py:643
  93.1 1.7 %pass_on.2 = bf16[3,1536,128]{2,1,0:T(8,128)(2,1)} custom-call(bf16[3,1536,128]{2,1,0:T(8,128)(2,1)S(1)} %fold.4._.own, bf16[3,1536,128]{2,1,0:T(8,128)(2,1)S(1)} %collective-permute-done.21.got, bf16[3,1536,128]{2,1,0:T(8,128)(2,1)} %fold.7.refs_0_.own), custom_call_target="tpu_custom_call" | custom-call | flops 1179648 | bytes 3538944 | tf_op jit(solution)/shard_map/pass_on/pallas_call | solution.py:577
  94.8 3.5 %collective-permute-start.22 = (bf16[3,1536,128]{2,1,0:T(8,128)(2,1)}, bf16[3,1536,128]{2,1,0:T(8,128)(2,1)}, u32[]{:S(2)}, u32[]{:S(2)}) collective-permute-start(bf16[3,1536,128]{2,1,0:T(8,128)(2,1)} %pass_on.2), channel_id=1, source_target_pairs={{8,24},{12,28},{16,0},{20,4},{9,25},{13,29},{17,1},{21,5},{10,26},... | collective-permute-start | bytes 3538952 | tf_op jit(solution)/shard_map/ppermute | solution.py:643
  101.5 1.7 %copy-done.2 = bf16[3,2,256,768]{3,2,1,0:T(8,128)(2,1)S(1)} copy-done((bf16[3,2,256,768]{3,2,1,0:T(8,128)(2,1)S(1)}, bf16[3,2,256,768]{3,2,1,0:T(8,128)(2,1)}, u32[]{:S(2)}) %copy-start.2) | copy-done | bytes 2359320
  103.2 1.7 %copy-done.4 = bf16[3,2,256,768]{3,2,1,0:T(8,128)(2,1)S(1)} copy-done((bf16[3,2,256,768]{3,2,1,0:T(8,128)(2,1)S(1)}, bf16[3,2,256,768]{3,2,1,0:T(8,128)(2,1)}, u32[]{:S(2)}) %copy-start.4) | copy-done | bytes 2359320
  105.6 12.5 %collective-permute-done.23.refs_0_.got = bf16[3,1536,128]{2,1,0:T(8,128)(2,1)} collective-permute-done((bf16[3,1536,128]{2,1,0:T(8,128)(2,1)}, bf16[3,1536,128]{2,1,0:T(8,128)(2,1)}, u32[]{:S(2)}, u32[]{:S(2)}) %collective-permute-start.23) | collective-permute-done | bytes 1179680 | tf_op jit(solution)/shard_map/ppermute | solution.py:643
  118.5 3.8 %collective-permute-done.22.refs_0_ = bf16[3,1536,128]{2,1,0:T(8,128)(2,1)} collective-permute-done((bf16[3,1536,128]{2,1,0:T(8,128)(2,1)}, bf16[3,1536,128]{2,1,0:T(8,128)(2,1)}, u32[]{:S(2)}, u32[]{:S(2)}) %collective-permute-start.22) | collective-permute-done | bytes 1179680 | tf_op jit(solution)/shard_map/ppermute | solution.py:643
  122.3 2.5 %pass_on.3 = bf16[3,1536,128]{2,1,0:T(8,128)(2,1)S(1)} custom-call(bf16[3,1536,128]{2,1,0:T(8,128)(2,1)} %fold.7.refs_0_.own, bf16[3,1536,128]{2,1,0:T(8,128)(2,1)} %collective-permute-done.23.refs_0_.got, bf16[3,1536,128]{2,1,0:T(8,128)(2,1)} %collective-permute-done.22.refs_0_), custom_call_target="tpu_custom_call" | custom-call | flops 1179648 | bytes 3538944 | tf_op jit(solution)/shard_map/pass_on/pallas_call | solution.py:577
  124.8 2.7 %collective-permute-start.25 = (bf16[3,1536,128]{2,1,0:T(8,128)(2,1)S(1)}, bf16[3,1536,128]{2,1,0:T(8,128)(2,1)S(1)}, u32[]{:S(2)}, u32[]{:S(2)}) collective-permute-start(bf16[3,1536,128]{2,1,0:T(8,128)(2,1)S(1)} %pass_on.3), channel_id=1, source_target_pairs={{8,16},{12,20},{16,8},{20,12},{9,17},{13,21},{17,9},{21,13},{10,18... | collective-permute-start | bytes 3538952 | tf_op jit(solution)/shard_map/ppermute | solution.py:643
  127.5 2.1 %fusion.1 = bf16[128,2048]{1,0:T(8,128)(2,1)} fusion(bf16[128,2048]{1,0:T(8,128)(2,1)} %collective-permute-done.17, bf16[1,128,2048]{2,1,0:T(8,128)(2,1)S(1)} %copy-done.11, bf16[2,128,2048]{2,1,0:T(8,128)(2,1)S(1)} %copy-done.19), kind=kLoop, calls=%fused_computation.4 | loop fusion | flops 1572864 | bytes 2097152 | tf_op jit(solution)/shard_map/convert_element_type | solution.py:507
  129.6 2.1 %fusion = bf16[128,2048]{1,0:T(8,128)(2,1)} fusion(bf16[128,2048]{1,0:T(8,128)(2,1)} %collective-permute-done.19, bf16[1,128,2048]{2,1,0:T(8,128)(2,1)S(1)} %copy-done.9, bf16[2,128,2048]{2,1,0:T(8,128)(2,1)S(1)} %copy-done.17), kind=kLoop, calls=%fused_computation.2 | loop fusion | flops 1572864 | bytes 2097152 | tf_op jit(solution)/shard_map/convert_element_type | solution.py:507
  131.7 1.7 %add_convert_fusion.refs_0_ = bf16[3,1536,128]{2,1,0:T(8,128)(2,1)S(1)} fusion(bf16[3,1536,128]{2,1,0:T(8,128)(2,1)} %collective-permute-done.22.refs_0_, bf16[3,1536,128]{2,1,0:T(8,128)(2,1)S(1)} %fold.5.other, bf16[3,1536,128]{2,1,0:T(8,128)(2,1)S(1)} %fold.6.one, pred[]{:T(512)S(6)} %gt.3), kind=kLoop, calls=%fused_computation | loop fusion | flops 2949120 | bytes 4718593 | tf_op jit(solution)/shard_map/convert_element_type | solution.py:507
  133.4 14.1 %collective-permute-done.24.refs_1_ = bf16[3,1536,128]{2,1,0:T(8,128)(2,1)S(1)} collective-permute-done((bf16[3,1536,128]{2,1,0:T(8,128)(2,1)S(1)}, bf16[3,1536,128]{2,1,0:T(8,128)(2,1)S(1)}, u32[]{:S(2)}, u32[]{:S(2)}) %collective-permute-start.24) | collective-permute-done | bytes 1179680 | tf_op jit(solution)/shard_map/ppermute | solution.py:643
  147.5 5.5 %collective-permute-done.25.refs_2_ = bf16[3,1536,128]{2,1,0:T(8,128)(2,1)S(1)} collective-permute-done((bf16[3,1536,128]{2,1,0:T(8,128)(2,1)S(1)}, bf16[3,1536,128]{2,1,0:T(8,128)(2,1)S(1)}, u32[]{:S(2)}, u32[]{:S(2)}) %collective-permute-start.25) | collective-permute-done | bytes 1179680 | tf_op jit(solution)/shard_map/ppermute | solution.py:643
  153.0 1.9 %unfold.1 = (bf16[1,256,768]{2,1,0:T(8,128)(2,1)}, bf16[1,256,768]{2,1,0:T(8,128)(2,1)}, bf16[1,96,2048]{2,1,0:T(8,128)(2,1)}) custom-call(bf16[3,1536,128]{2,1,0:T(8,128)(2,1)S(1)} %add_convert_fusion.refs_0_, bf16[3,1536,128]{2,1,0:T(8,128)(2,1)S(1)} %collective-permute-done.24.refs_1_, bf16[3,1536,128]{2,1,0:T(8,128)(2,1)S(1)} %collective-permute-done.25.refs_2_), custom_call_target="tpu_custom_call" | custom-call | flops 2359296 | bytes 5898240 | tf_op jit(solution)/shard_map/unfold/pallas_call | solution.py:630
  (85 shorter events, 19.6 us)
Async XLA Ops:
  0.6 19.3 %collective-permute-start = (bf16[128,2048]{1,0:T(8,128)(2,1)}, bf16[128,2048]{1,0:T(8,128)(2,1)S(1)}, u32[]{:S(2)}, u32[]{:S(2)}) collective-permute-start(bf16[128,2048]{1,0:T(8,128)(2,1)} %refs_0_.1), channel_id=1, source_target_pairs={{0,1},{1,0},{2,3},{3,2},{4,5},{5,4},{6,7},{7,6},{8,9},{9,8},{10,11... | collective-permute-start | bytes 1572872 | tf_op jit(solution)/shard_map/ppermute | solution.py:209
  2.2 17.7 %collective-permute-start.1 = (bf16[128,2048]{1,0:T(8,128)(2,1)}, bf16[128,2048]{1,0:T(8,128)(2,1)S(1)}, u32[]{:S(2)}, u32[]{:S(2)}) collective-permute-start(bf16[128,2048]{1,0:T(8,128)(2,1)} %refs_0_.1), channel_id=1, source_target_pairs={{0,2},{1,3},{2,0},{3,1},{4,6},{5,7},{6,4},{7,5},{8,10},{9,11},{10,... | collective-permute-start | bytes 1572872 | tf_op jit(solution)/shard_map/ppermute | solution.py:209
  2.7 28.2 %copy-start.14 = (bf16[1,768,2048]{2,1,0:T(8,128)(2,1)S(1)}, bf16[1,768,2048]{2,1,0:T(8,128)(2,1)}, u32[]{:S(2)}) copy-start(bf16[1,768,2048]{2,1,0:T(8,128)(2,1)} %param.19) | copy-start | bytes 9437188
  4.8 6.1 %collective-permute-start.4 = (bf16[32,2176]{1,0:T(8,128)(2,1)S(1)}, bf16[32,2176]{1,0:T(8,128)(2,1)S(1)}, u32[]{:S(2)}, u32[]{:S(2)}) collective-permute-start(bf16[32,2176]{1,0:T(8,128)(2,1)S(1)} %get-tuple-element.47), channel_id=1, source_target_pairs={{0,8},{4,12},{8,0},{12,4},{16,24},{20,28},{24,16},{28,20},{1,9},{5... | collective-permute-start | bytes 417800 | tf_op jit(solution)/shard_map/ppermute | solution.py:183
  5.3 12.2 %collective-permute-start.5 = (bf16[32,2176]{1,0:T(8,128)(2,1)S(1)}, bf16[32,2176]{1,0:T(8,128)(2,1)S(1)}, u32[]{:S(2)}, u32[]{:S(2)}) collective-permute-start(bf16[32,2176]{1,0:T(8,128)(2,1)S(1)} %get-tuple-element.48), channel_id=1, source_target_pairs={{0,16},{4,20},{8,24},{12,28},{16,0},{20,4},{24,8},{28,12},{1,17},{... | collective-permute-start | bytes 417800 | tf_op jit(solution)/shard_map/ppermute | solution.py:183
  7.9 12.0 %collective-permute-start.6 = (bf16[32,2176]{1,0:T(8,128)(2,1)S(1)}, bf16[32,2176]{1,0:T(8,128)(2,1)S(1)}, u32[]{:S(2)}, u32[]{:S(2)}) collective-permute-start(bf16[32,2176]{1,0:T(8,128)(2,1)S(1)} %get-tuple-element.49), channel_id=1, source_target_pairs={{0,24},{4,28},{8,16},{12,20},{16,8},{20,12},{24,0},{28,4},{1,25},{... | collective-permute-start | bytes 417800 | tf_op jit(solution)/shard_map/ppermute | solution.py:183
  20.0 2.3 %collective-permute-start.7 = (bf16[64,2176]{1,0:T(8,128)(2,1)S(1)}, bf16[64,2176]{1,0:T(8,128)(2,1)S(1)}, u32[]{:S(2)}, u32[]{:S(2)}) collective-permute-start(bf16[64,2176]{1,0:T(8,128)(2,1)S(1)} %get-tuple-element.51), channel_id=1, source_target_pairs={{0,4},{4,0},{8,12},{12,8},{16,20},{20,16},{24,28},{28,24},{1,5},{5... | collective-permute-start | bytes 835592 | tf_op jit(solution)/shard_map/ppermute | solution.py:185
  20.1 9.2 %collective-permute-start.2 = (bf16[64,2048]{1,0:T(8,128)(2,1)S(1)}, bf16[64,2048]{1,0:T(8,128)(2,1)S(1)}, u32[]{:S(2)}, u32[]{:S(2)}) collective-permute-start(bf16[64,2048]{1,0:T(8,128)(2,1)S(1)} %slice.24), channel_id=1, source_target_pairs={{0,2},{1,3},{2,0},{3,1},{4,6},{5,7},{6,4},{7,5},{8,10},{9,11},{10,... | collective-permute-start | bytes 786440 | tf_op jit(solution)/shard_map/ppermute | solution.py:209
  21.7 9.2 %collective-permute-start.3 = (bf16[64,2048]{1,0:T(8,128)(2,1)S(1)}, bf16[64,2048]{1,0:T(8,128)(2,1)S(1)}, u32[]{:S(2)}, u32[]{:S(2)}) collective-permute-start(bf16[64,2048]{1,0:T(8,128)(2,1)S(1)} %slice.25), channel_id=1, source_target_pairs={{0,1},{1,0},{2,3},{3,2},{4,5},{5,4},{6,7},{7,6},{8,9},{9,8},{10,11... | collective-permute-start | bytes 786440 | tf_op jit(solution)/shard_map/ppermute | solution.py:209
  22.3 20.5 %copy-start.6 = (bf16[1,2048,768]{2,1,0:T(8,128)(2,1)S(1)}, bf16[1,2048,768]{2,1,0:T(8,128)(2,1)}, u32[]{:S(2)}) copy-start(bf16[1,2048,768]{2,1,0:T(8,128)(2,1)} %param.18) | copy-start | bytes 9437188
  22.6 14.3 %collective-permute-start.8 = (bf16[64,2176]{1,0:T(8,128)(2,1)S(1)}, bf16[64,2176]{1,0:T(8,128)(2,1)S(1)}, u32[]{:S(2)}, u32[]{:S(2)}) collective-permute-start(bf16[64,2176]{1,0:T(8,128)(2,1)S(1)} %get-tuple-element.52.refs_0_), channel_id=1, source_target_pairs={{0,1},{1,0},{2,3},{3,2},{4,5},{5,4},{6,7},{7,6},{8,9},{9,8},{10,11... | collective-permute-start | bytes 835592 | tf_op jit(solution)/shard_map/ppermute | solution.py:209
  24.2 12.7 %collective-permute-start.11 = (bf16[64,2176]{1,0:T(8,128)(2,1)S(1)}, bf16[64,2176]{1,0:T(8,128)(2,1)S(1)}, u32[]{:S(2)}, u32[]{:S(2)}) collective-permute-start(bf16[64,2176]{1,0:T(8,128)(2,1)S(1)} %get-tuple-element.53.refs_1_), channel_id=1, source_target_pairs={{0,2},{1,3},{2,0},{3,1},{4,6},{5,7},{6,4},{7,5},{8,10},{9,11},{10,... | collective-permute-start | bytes 835592 | tf_op jit(solution)/shard_map/ppermute | solution.py:209
  24.7 18.2 %collective-permute-start.9 = (bf16[64,2176]{1,0:T(8,128)(2,1)S(1)}, bf16[64,2176]{1,0:T(8,128)(2,1)S(1)}, u32[]{:S(2)}, u32[]{:S(2)}) collective-permute-start(bf16[64,2176]{1,0:T(8,128)(2,1)S(1)} %get-tuple-element.53.refs_1_), channel_id=1, source_target_pairs={{0,1},{1,0},{2,3},{3,2},{4,5},{5,4},{6,7},{7,6},{8,9},{9,8},{10,11... | collective-permute-start | bytes 835592 | tf_op jit(solution)/shard_map/ppermute | solution.py:209
  29.3 13.6 %collective-permute-start.10 = (bf16[64,2176]{1,0:T(8,128)(2,1)S(1)}, bf16[64,2176]{1,0:T(8,128)(2,1)S(1)}, u32[]{:S(2)}, u32[]{:S(2)}) collective-permute-start(bf16[64,2176]{1,0:T(8,128)(2,1)S(1)} %get-tuple-element.52.refs_0_), channel_id=1, source_target_pairs={{0,2},{1,3},{2,0},{3,1},{4,6},{5,7},{6,4},{7,5},{8,10},{9,11},{10,... | collective-permute-start | bytes 835592 | tf_op jit(solution)/shard_map/ppermute | solution.py:209
  32.0 10.9 %copy-start.5 = (bf16[1,2048,768]{2,1,0:T(8,128)(2,1)S(1)}, bf16[1,2048,768]{2,1,0:T(8,128)(2,1)}, u32[]{:S(2)}) copy-start(bf16[1,2048,768]{2,1,0:T(8,128)(2,1)} %param.17) | copy-start | bytes 9437188
  36.9 11.5 %collective-permute-start.12 = (bf16[64,2176]{1,0:T(8,128)(2,1)S(1)}, bf16[64,2176]{1,0:T(8,128)(2,1)S(1)}, u32[]{:S(2)}, u32[]{:S(2)}) collective-permute-start(bf16[64,2176]{1,0:T(8,128)(2,1)S(1)} %collective-permute-done.8.refs_2_), channel_id=1, source_target_pairs={{0,2},{1,3},{2,0},{3,1},{4,6},{5,7},{6,4},{7,5},{8,10},{9,11},{10,... | collective-permute-start | bytes 835592 | tf_op jit(solution)/shard_map/ppermute | solution.py:209
  37.4 11.0 %collective-permute-start.13 = (bf16[64,2176]{1,0:T(8,128)(2,1)S(1)}, bf16[64,2176]{1,0:T(8,128)(2,1)S(1)}, u32[]{:S(2)}, u32[]{:S(2)}) collective-permute-start(bf16[64,2176]{1,0:T(8,128)(2,1)S(1)} %collective-permute-done.11.refs_5_), channel_id=1, source_target_pairs={{0,1},{1,0},{2,3},{3,2},{4,5},{5,4},{6,7},{7,6},{8,9},{9,8},{10,11... | collective-permute-start | bytes 835592 | tf_op jit(solution)/shard_map/ppermute | solution.py:209
  53.9 4.1 %collective-permute-start.14 = (bf16[2,256,768]{2,1,0:T(8,128)(2,1)}, bf16[2,256,768]{2,1,0:T(8,128)(2,1)S(1)}, u32[]{:S(2)}, u32[]{:S(2)}) collective-permute-start(bf16[2,256,768]{2,1,0:T(8,128)(2,1)} %get-tuple-element.68), channel_id=1, source_target_pairs={{0,4},{4,0},{8,12},{12,8},{16,20},{20,16},{24,28},{28,24},{1,5},{5... | collective-permute-start | bytes 2359304 | tf_op jit(solution)/shard_map/ppermute | solution.py:661
  57.5 4.6 %collective-permute-start.15 = (bf16[4,96,2048]{2,1,0:T(8,128)(2,1)}, bf16[4,96,2048]{2,1,0:T(8,128)(2,1)S(1)}, u32[]{:S(2)}, u32[]{:S(2)}) collective-permute-start(bf16[4,96,2048]{2,1,0:T(8,128)(2,1)} %get-tuple-element.73), channel_id=1, source_target_pairs={{0,4},{4,0},{8,12},{12,8},{16,20},{20,16},{24,28},{28,24},{1,5},{5... | collective-permute-start | bytes 4718600 | tf_op jit(solution)/shard_map/ppermute | solution.py:661
  62.0 9.0 %collective-permute-start.20 = (bf16[3,2,256,768]{3,2,1,0:T(8,128)(2,1)}, bf16[3,2,256,768]{3,2,1,0:T(8,128)(2,1)S(1)}, u32[]{:S(2)}, u32[]{:S(2)}) collective-permute-start(bf16[3,2,256,768]{3,2,1,0:T(8,128)(2,1)} %get-tuple-element.81), channel_id=1, source_target_pairs={{0,4},{4,0},{8,12},{12,8},{16,20},{20,16},{24,28},{28,24},{1,5},{5... | collective-permute-start | bytes 7077896 | tf_op jit(solution)/shard_map/ppermute | solution.py:661
  62.4 30.7 %collective-permute-start.21 = (bf16[3,1536,128]{2,1,0:T(8,128)(2,1)S(1)}, bf16[3,1536,128]{2,1,0:T(8,128)(2,1)S(1)}, u32[]{:S(2)}, u32[]{:S(2)}) collective-permute-start(bf16[3,1536,128]{2,1,0:T(8,128)(2,1)S(1)} %fold.4._.own), channel_id=1, source_target_pairs={{0,8},{4,12},{24,16},{28,20},{1,9},{5,13},{25,17},{29,21},{2,10},{... | collective-permute-start | bytes 3538952 | tf_op jit(solution)/shard_map/ppermute | solution.py:643
  63.7 7.3 %copy-start.1 = (bf16[3,2,256,768]{3,2,1,0:T(8,128)(2,1)S(1)}, bf16[3,2,256,768]{3,2,1,0:T(8,128)(2,1)}, u32[]{:S(2)}) copy-start(bf16[3,2,256,768]{3,2,1,0:T(8,128)(2,1)} %get-tuple-element.80.gu_mine) | copy-start | bytes 7077892
  69.9 28.4 %collective-permute-start.16 = (bf16[2,128,2048]{2,1,0:T(8,128)(2,1)S(1)}, bf16[2,128,2048]{2,1,0:T(8,128)(2,1)S(1)}, u32[]{:S(2)}, u32[]{:S(2)}) collective-permute-start(bf16[2,128,2048]{2,1,0:T(8,128)(2,1)S(1)} %get-tuple-element.75), channel_id=1, source_target_pairs={{0,1},{1,0},{2,3},{3,2},{4,5},{5,4},{6,7},{7,6},{8,9},{9,8},{10,11... | collective-permute-start | bytes 3145736 | tf_op jit(solution)/shard_map/ppermute | solution.py:209
  70.5 29.3 %collective-permute-start.18 = (bf16[2,128,2048]{2,1,0:T(8,128)(2,1)S(1)}, bf16[2,128,2048]{2,1,0:T(8,128)(2,1)S(1)}, u32[]{:S(2)}, u32[]{:S(2)}) collective-permute-start(bf16[2,128,2048]{2,1,0:T(8,128)(2,1)S(1)} %get-tuple-element.78), channel_id=1, source_target_pairs={{0,2},{1,3},{2,0},{3,1},{4,6},{5,7},{6,4},{7,5},{8,10},{9,11},{10,... | collective-permute-start | bytes 3145736 | tf_op jit(solution)/shard_map/ppermute | solution.py:209
  72.9 45.2 %collective-permute-start.23 = (bf16[3,1536,128]{2,1,0:T(8,128)(2,1)}, bf16[3,1536,128]{2,1,0:T(8,128)(2,1)}, u32[]{:S(2)}, u32[]{:S(2)}) collective-permute-start(bf16[3,1536,128]{2,1,0:T(8,128)(2,1)} %fold.7.refs_0_.own), channel_id=1, source_target_pairs={{0,8},{4,12},{24,16},{28,20},{1,9},{5,13},{25,17},{29,21},{2,10},{... | collective-permute-start | bytes 3538952 | tf_op jit(solution)/shard_map/ppermute | solution.py:643
  94.8 27.5 %collective-permute-start.22 = (bf16[3,1536,128]{2,1,0:T(8,128)(2,1)}, bf16[3,1536,128]{2,1,0:T(8,128)(2,1)}, u32[]{:S(2)}, u32[]{:S(2)}) collective-permute-start(bf16[3,1536,128]{2,1,0:T(8,128)(2,1)} %pass_on.2), channel_id=1, source_target_pairs={{8,24},{12,28},{16,0},{20,4},{9,25},{13,29},{17,1},{21,5},{10,26},... | collective-permute-start | bytes 3538952 | tf_op jit(solution)/shard_map/ppermute | solution.py:643
  99.4 28.2 %collective-permute-start.17 = (bf16[128,2048]{1,0:T(8,128)(2,1)}, bf16[128,2048]{1,0:T(8,128)(2,1)}, u32[]{:S(2)}, u32[]{:S(2)}) collective-permute-start(bf16[128,2048]{1,0:T(8,128)(2,1)} %fusion.2), channel_id=1, source_target_pairs={{0,2},{1,3},{2,0},{3,1},{4,6},{5,7},{6,4},{7,5},{8,10},{9,11},{10,... | collective-permute-start | bytes 1572872 | tf_op jit(solution)/shard_map/ppermute | solution.py:209
  101.0 28.6 %collective-permute-start.19 = (bf16[128,2048]{1,0:T(8,128)(2,1)}, bf16[128,2048]{1,0:T(8,128)(2,1)}, u32[]{:S(2)}, u32[]{:S(2)}) collective-permute-start(bf16[128,2048]{1,0:T(8,128)(2,1)} %fusion.3), channel_id=1, source_target_pairs={{0,1},{1,0},{2,3},{3,2},{4,5},{5,4},{6,7},{7,6},{8,9},{9,8},{10,11... | collective-permute-start | bytes 1572872 | tf_op jit(solution)/shard_map/ppermute | solution.py:209
  118.4 9.1 %copy-start.11 = (bf16[1,128,2048]{2,1,0:T(8,128)(2,1)S(1)}, bf16[1,128,2048]{2,1,0:T(8,128)(2,1)}, u32[]{:S(2)}) copy-start(bf16[1,128,2048]{2,1,0:T(8,128)(2,1)} %copy-done.10) | copy-start | bytes 1572868
  118.4 9.1 %copy-start.19 = (bf16[2,128,2048]{2,1,0:T(8,128)(2,1)S(1)}, bf16[2,128,2048]{2,1,0:T(8,128)(2,1)}, u32[]{:S(2)}) copy-start(bf16[2,128,2048]{2,1,0:T(8,128)(2,1)} %copy-done.18) | copy-start | bytes 3145732
  118.4 29.1 %collective-permute-start.24 = (bf16[3,1536,128]{2,1,0:T(8,128)(2,1)S(1)}, bf16[3,1536,128]{2,1,0:T(8,128)(2,1)S(1)}, u32[]{:S(2)}, u32[]{:S(2)}) collective-permute-start(bf16[3,1536,128]{2,1,0:T(8,128)(2,1)S(1)} %choose.1), channel_id=1, source_target_pairs={{0,8},{4,12},{8,0},{12,4},{16,24},{20,28},{24,16},{28,20},{1,9},{5... | collective-permute-start | bytes 3538952 | tf_op jit(solution)/shard_map/ppermute | solution.py:643
  124.8 28.2 %collective-permute-start.25 = (bf16[3,1536,128]{2,1,0:T(8,128)(2,1)S(1)}, bf16[3,1536,128]{2,1,0:T(8,128)(2,1)S(1)}, u32[]{:S(2)}, u32[]{:S(2)}) collective-permute-start(bf16[3,1536,128]{2,1,0:T(8,128)(2,1)S(1)} %pass_on.3), channel_id=1, source_target_pairs={{8,16},{12,20},{16,8},{20,12},{9,17},{13,21},{17,9},{21,13},{10,18... | collective-permute-start | bytes 3538952 | tf_op jit(solution)/shard_map/ppermute | solution.py:643
  (14 other events, 39.7 us)

commit v5 on v4

--- a/solution.py
+++ b/solution.py
@@ -175,14 +175,13 @@
     )(ids, gates, mine, other)
 
 
-def send_sequences(gen_rows, gen_lengths, gen_adv, destination, n_dp, after):
+def send_sequences(gen_rows, gen_lengths, gen_adv, destination, n_dp):
     seq_dev = destination.shape[2]
     slot = gen_rows.shape[0] // seq_dev
     pieces = list(pick(destination, gen_lengths, gen_adv, gen_rows.reshape(seq_dev, slot, gen_rows.shape[1]), n_dp))
     for i in range(1, len(pieces)):
         pieces[i] = lax.ppermute(pieces[i], "dp", [(d, d ^ (CORES * i)) for d in range(n_dp)])
-    mine, other = regroup(pieces, after)
-    return mine, lax.ppermute(other, "dp", [(d, d ^ 1) for d in range(n_dp)])
+    return pieces
 
 
 def place_sequences(mine, other, n_dp, seq_dev, ids, gates):
@@ -567,7 +566,7 @@
     refs[-1][...] = (own[...].astype(F32) + got[...].astype(F32)).astype(BF16)
 
 
-def pass_on(own, got, piece, pieces, whole, after):
+def pass_on(own, got, piece, pieces, whole, after, weight=1):
     per = whole // pieces
 
     def part(array):
@@ -581,7 +580,7 @@
         out_specs=pl.BlockSpec((1, per, LANES), lambda j: (j, 0, 0)),
         out_shape=jax.ShapeDtypeStruct((got.shape[0], per, LANES), BF16),
         compiler_params=params(16),
-        cost_estimate=cost(2 * got.size, 6 * got.size),
+        cost_estimate=cost(2 * weight * got.size, 6 * weight * got.size),
         name="pass_on",
     )(own, got, *after)
 
@@ -660,8 +659,10 @@
     def swap_core(value):
         return lax.ppermute(value, "dp", other_core)
 
-    cot_pieces = gather_rows(cotangent, n_ex)
-    mine, other = send_sequences(gen_rows, gen_lengths, gen_adv, destination, n_dp, cot_pieces[1:3])
+    pieces = send_sequences(gen_rows, gen_lengths, gen_adv, destination, n_dp)
+    cot_pieces = gather_rows(tie(cotangent, pieces[0]), n_ex)
+    mine, other = regroup(pieces, cot_pieces[1:3])
+    other = swap_core(other)
     low, high = place_sequences(mine, other, n_dp, destination.shape[2], expert_ids, gate_values)
     hg, dy_all = hidden_grad(cot_pieces, weight_down)
     x_pieces = gather_halves(low, high, n_ex, hg)
@@ -693,8 +694,8 @@
         sum_one, sum_none = block(1), block(0)
         three_sum = pass_on(far_sum, three, 0, 1, whole, [sum_two])
         three_on = chips_permute(three_sum, [(1, 3), (2, 0)], n_dp)
-        two_sum = pass_on(sum_two, two, 0, 1, whole, [three_on])
-        two_on = chips_permute(two_sum, [(1, 2), (2, 1)], n_dp)
+        two_sum = pass_on(sum_two, two, 0, 1, whole, [])
+        two_on = chips_permute(tie(two_sum, three_on), [(1, 2), (2, 1)], n_dp)
         last = chips_permute(choose(near, sum_none, sum_one, [two]), across, n_dp)
         own = add(jnp.where(near > 0, sum_one, sum_none), three_on)
         ends = [[last], [two_on]]

time: 155 us -> 153 us (0.987)
  waiting for transfers between devices: 77.3 us -> 74.9 us
    ppermute x5, waiting for transfers between devices: 54.7 us -> 52.3 us  [chips_permute(): lax.ppermute(value, 'dp', [(CORES * a + c, CORES * b + c) for a, b in pai...]
  transfers between devices with their start and end apart: 26 -> 26, of which waited for: 12 -> 12; matrix products, arithmetic and copies ran while one was open for 5% -> 5% of each run, Pallas kernels for 21% -> 20%
where the time goes in v5:
time: 153 us
  waiting for transfers between devices  74.9 us (49%)
  Pallas kernels  39.4 us (26%)
  starting transfers between devices  24.8 us (16%)
  other arithmetic  7.97 us (5%)
  local copies, waits for them, and re-layouts  4.55 us (3%)
    ppermute x5, waiting for transfers between devices, chips_permute(): lax.ppermute(value, 'dp', [(CORES * a + c, CORES * b + c) for a, b in pai...  52.3 us
    ppermute x14, starting transfers between devices, swap(): return lax.ppermute(value, 'expert', [(d, d ^ i) for d in range(n_ex)])  11.9 us
    ppermute x3, waiting for transfers between devices, send_sequences(): lax.ppermute(pieces[i], 'dp', [(d, d ^ CORES * i) for d in range(n_dp)])  11.5 us
    ppermute x14, waiting for transfers between devices, swap(): return lax.ppermute(value, 'expert', [(d, d ^ i) for d in range(n_ex)])  11 us
    ppermute x5, starting transfers between devices, chips_permute(): lax.ppermute(value, 'dp', [(CORES * a + c, CORES * b + c) for a, b in pai...  8.85 us
    pallas_call x2, Pallas kernels, hidden_units(): pl.pallas_call(functools.partial(units_kernel, len(pieces), slot, not bef...  8.46 us
    convert_element_type x5, other arithmetic, add(): return sum((part.astype(F32) for part in parts)).astype(BF16)  7.97 us
    pallas_call x1, Pallas kernels, outputs(): pl.pallas_call(functools.partial(outputs_kernel, layer_groups, grad_group...  6.14 us
  transfers between devices with their start and end apart: 26, of which 12 were waited for; matrix products, arithmetic and copies ran while one was open for 5% of the time, Pallas kernels for 20%

profile of v5, /device:TPU:12, one launch (start us, length us, event | category | flops | bytes accessed | tf_op | source)
XLA Modules:
  0.0 152.6 jit_solution(3247788422973374916)
XLA Ops:
  0.6 2.1 %pick.1 = (bf16[32,2176]{1,0:T(8,128)(2,1)S(1)}, bf16[32,2176]{1,0:T(8,128)(2,1)S(1)}, bf16[32,2176]{1,0:T(8,128)(2,1)S(1)}, bf16[32,2176]{1,0:T(8,128)(2,1)S(1)}) custom-call(s32[1,1,8]{2,1,0:T(1,128)} %dest_hbm.1, s32[1,1,8]{2,1,0:T(1,128)} %len_hbm.1, bf16[1,1,8]{2,1,0:T(2,128)(2,1)} %adv_hbm.1, bf16[8,16,2048]{2,1,0:T(8,128)(2,1)} %bitcast.33), custom_call_target="tpu_custom_call" | custom-call | tf_op jit(solution)/shard_map/pick/pallas_call | solution.py:94
  2.8 1.6 %collective-permute-start = (bf16[128,2048]{1,0:T(8,128)(2,1)}, bf16[128,2048]{1,0:T(8,128)(2,1)S(1)}, u32[]{:S(2)}, u32[]{:S(2)}) collective-permute-start(bf16[128,2048]{1,0:T(8,128)(2,1)} %refs_0_), channel_id=1, source_target_pairs={{0,1},{1,0},{2,3},{3,2},{4,5},{5,4},{6,7},{7,6},{8,9},{9,8},{10,11... | collective-permute-start | bytes 1572872 | tf_op jit(solution)/shard_map/ppermute | solution.py:208
  5.3 2.6 %collective-permute-start.5 = (bf16[32,2176]{1,0:T(8,128)(2,1)S(1)}, bf16[32,2176]{1,0:T(8,128)(2,1)S(1)}, u32[]{:S(2)}, u32[]{:S(2)}) collective-permute-start(bf16[32,2176]{1,0:T(8,128)(2,1)S(1)} %get-tuple-element.51), channel_id=1, source_target_pairs={{0,16},{4,20},{8,24},{12,28},{16,0},{20,4},{24,8},{28,12},{1,17},{... | collective-permute-start | bytes 417800 | tf_op jit(solution)/shard_map/ppermute | solution.py:183
  8.3 2.5 %collective-permute-done.4.refs_1_ = bf16[32,2176]{1,0:T(8,128)(2,1)S(1)} collective-permute-done((bf16[32,2176]{1,0:T(8,128)(2,1)S(1)}, bf16[32,2176]{1,0:T(8,128)(2,1)S(1)}, u32[]{:S(2)}, u32[]{:S(2)}) %collective-permute-start.4) | collective-permute-done | bytes 139296 | tf_op jit(solution)/shard_map/ppermute | solution.py:183
  10.8 6.6 %collective-permute-done.5.refs_2_ = bf16[32,2176]{1,0:T(8,128)(2,1)S(1)} collective-permute-done((bf16[32,2176]{1,0:T(8,128)(2,1)S(1)}, bf16[32,2176]{1,0:T(8,128)(2,1)S(1)}, u32[]{:S(2)}, u32[]{:S(2)}) %collective-permute-start.5) | collective-permute-done | bytes 139296 | tf_op jit(solution)/shard_map/ppermute | solution.py:183
  17.5 2.4 %collective-permute-done.6.refs_3_ = bf16[32,2176]{1,0:T(8,128)(2,1)S(1)} collective-permute-done((bf16[32,2176]{1,0:T(8,128)(2,1)S(1)}, bf16[32,2176]{1,0:T(8,128)(2,1)S(1)}, u32[]{:S(2)}, u32[]{:S(2)}) %collective-permute-start.6) | collective-permute-done | bytes 139296 | tf_op jit(solution)/shard_map/ppermute | solution.py:183
  20.0 1.6 %collective-permute-start.2 = (bf16[64,2048]{1,0:T(8,128)(2,1)S(1)}, bf16[64,2048]{1,0:T(8,128)(2,1)S(1)}, u32[]{:S(2)}, u32[]{:S(2)}) collective-permute-start(bf16[64,2048]{1,0:T(8,128)(2,1)S(1)} %slice.24), channel_id=1, source_target_pairs={{0,2},{1,3},{2,0},{3,1},{4,6},{5,7},{6,4},{7,5},{8,10},{9,11},{10,... | collective-permute-start | bytes 786440 | tf_op jit(solution)/shard_map/ppermute | solution.py:208
  25.4 3.7 %collective-permute-done.2.refs_3_ = bf16[64,2048]{1,0:T(8,128)(2,1)S(1)} collective-permute-done((bf16[64,2048]{1,0:T(8,128)(2,1)S(1)}, bf16[64,2048]{1,0:T(8,128)(2,1)S(1)}, u32[]{:S(2)}, u32[]{:S(2)}) %collective-permute-start.2) | collective-permute-done | bytes 262176 | tf_op jit(solution)/shard_map/ppermute | solution.py:208
  31.9 2.7 %hidden_grad.1 = (f32[512,768]{1,0:T(8,128)S(1)}, bf16[512,2048]{1,0:T(8,128)(2,1)S(1)}) custom-call(bf16[768,2048]{1,0:T(8,128)(2,1)S(1)} %bitcast.31, bf16[128,2048]{1,0:T(8,128)(2,1)S(1)} %copy-done.15, bf16[128,2048]{1,0:T(8,128)(2,1)S(1)} %collective-permute-done.refs_1_.refs_4_, bf16[128,2048]{1,0:T(8,128)(2,1)S(1)} %collective-permute-done.1.refs_2_.refs_5_, ...), custom_call_target="tpu_custom_call" | custom-call | flops 1610612736 | bytes 7340032 | tf_op jit(solution)/shard_map/hidden_grad/pallas_call | solution.py:276
  34.6 2.2 %collective-permute-done.8.refs_2_ = bf16[64,2176]{1,0:T(8,128)(2,1)S(1)} collective-permute-done((bf16[64,2176]{1,0:T(8,128)(2,1)S(1)}, bf16[64,2176]{1,0:T(8,128)(2,1)S(1)}, u32[]{:S(2)}, u32[]{:S(2)}) %collective-permute-start.8) | collective-permute-done | bytes 278560 | tf_op jit(solution)/shard_map/ppermute | solution.py:208
  37.9 4.9 %collective-permute-done.9.refs_3_ = bf16[64,2176]{1,0:T(8,128)(2,1)S(1)} collective-permute-done((bf16[64,2176]{1,0:T(8,128)(2,1)S(1)}, bf16[64,2176]{1,0:T(8,128)(2,1)S(1)}, u32[]{:S(2)}, u32[]{:S(2)}) %collective-permute-start.9) | collective-permute-done | bytes 278560 | tf_op jit(solution)/shard_map/ppermute | solution.py:208
  42.8 5.6 %hidden_units.2 = (bf16[512,768]{1,0:T(8,128)(2,1)S(1)}, bf16[512,768]{1,0:T(8,128)(2,1)S(1)}, bf16[512,768]{1,0:T(8,128)(2,1)S(1)}, bf16[768,512]{1,0:T(8,128)(...) custom-call(bf16[2048,768]{1,0:T(8,128)(2,1)S(1)} %bitcast.21, bf16[2048,768]{1,0:T(8,128)(2,1)S(1)} %bitcast.24, ...), custom_call_target="tpu_custom_call" | custom-call | flops 2415919104 | bytes 9437184 | tf_op jit(solution)/shard_map/hidden_units/pallas_call | solution.py:354
  48.4 2.9 %hidden_units.3 = (bf16[512,768]{1,0:T(8,128)(2,1)S(1)}, bf16[512,768]{1,0:T(8,128)(2,1)S(1)}, bf16[512,768]{1,0:T(8,128)(2,1)S(1)}, bf16[768,512]{1,0:T(8,128)(...) custom-call(bf16[2048,768]{1,0:T(8,128)(2,1)S(1)} %bitcast.22, ...), custom_call_target="tpu_custom_call", output_to_operand_aliasing={{0}: (3, {}), {1}: (4, {}), {2}: (5, {}), {3}: (6, {}), {4}... | custom-call | flops 805306368 | bytes 7340032 | tf_op jit(solution)/shard_map/hidden_units/pallas_call | solution.py:354
  51.3 2.6 %far_grads.1 = (bf16[2,256,768]{2,1,0:T(8,128)(2,1)}, bf16[2,256,768]{2,1,0:T(8,128)(2,1)}) custom-call(bf16[2048,512]{1,0:T(8,128)(2,1)S(1)} %get-tuple-element.69.x_ref, bf16[512,768]{1,0:T(8,128)(2,1)S(1)} %get-tuple-element.67.gate_ref, bf16[512,768]{1,0:T(8,128)(2,1)S(1)} %get-tuple-element.68.up_ref), custom_call_target="tpu_custom_call" | custom-call | flops 805306368 | bytes 4718592 | tf_op jit(solution)/shard_map/far_grads/pallas_call | solution.py:403
  53.9 3.5 %row_grad.1 = (bf16[4,96,2048]{2,1,0:T(8,128)(2,1)}, bf16[4,96,2048]{2,1,0:T(8,128)(2,1)}) custom-call(bf16[768,512]{1,0:T(8,128)(2,1)S(1)} %get-tuple-element.73.hid_ref, bf16[512,2048]{1,0:T(8,128)(2,1)S(1)} %get-tuple-element.74.dy_ref), custom_call_target="tpu_custom_call" | custom-call | flops 1610612736 | bytes 5242880 | tf_op jit(solution)/shard_map/row_grad/pallas_call | solution.py:459
  57.9 4.0 %rest_grads.1 = (bf16[3,2,256,768]{3,2,1,0:T(8,128)(2,1)}, bf16[3,2,256,768]{3,2,1,0:T(8,128)(2,1)}) custom-call(bf16[2048,512]{1,0:T(8,128)(2,1)S(1)} %get-tuple-element.69.x_ref, bf16[512,768]{1,0:T(8,128)(2,1)S(1)} %get-tuple-element.67.gate_ref, bf16[512,768]{1,0:T(8,128)(2,1)S(1)} %get-tuple-element.68.up_ref, ...), custom_call_target="tpu_custom_call" | custom-call | flops 3221225472 | bytes 7864320 | tf_op jit(solution)/shard_map/rest_grads/pallas_call | solution.py:432
  63.7 6.1 %outputs.1 = (bf16[1,128,2048]{2,1,0:T(8,128)(2,1)S(1)}, bf16[1,128,2048]{2,1,0:T(8,128)(2,1)S(1)}, bf16[2,128,2048]{2,1,0:T(8,128)(2,1)S(1)}, bf16[1,128,2048]{...) custom-call(bf16[512,768]{1,0:T(8,128)(2,1)S(1)} %get-tuple-element.65.hid_ref, ...), custom_call_target="tpu_custom_call" | custom-call | flops 4831838208 | bytes 13631488 | tf_op jit(solution)/shard_map/outputs/pallas_call | solution.py:493
  71.0 1.9 %fold.7.refs_0_.own = bf16[3,1536,128]{2,1,0:T(8,128)(2,1)} custom-call(bf16[3,2,256,768]{3,2,1,0:T(8,128)(2,1)S(1)} %copy-done.1, bf16[3,2,256,768]{3,2,1,0:T(8,128)(2,1)S(1)} %collective-permute-done.20.gu_got, bf16[4,96,2048]{2,1,0:T(8,128)(2,1)S(1)} %copy-done, bf16[4,96,2048]{2,1,0:T(8,128)(2,1)S(1)} %collective-permute-done.15.row_got), custom_call_target="tpu_custom_call" | custom-call | flops 1179648 | bytes 3538944 | tf_op jit(solution)/shard_map/fold/pallas_call | solution.py:553
  74.1 18.9 %collective-permute-done.21.got = bf16[3,1536,128]{2,1,0:T(8,128)(2,1)S(1)} collective-permute-done((bf16[3,1536,128]{2,1,0:T(8,128)(2,1)S(1)}, bf16[3,1536,128]{2,1,0:T(8,128)(2,1)S(1)}, u32[]{:S(2)}, u32[]{:S(2)}) %collective-permute-start.21) | collective-permute-done | bytes 1179680 | tf_op jit(solution)/shard_map/ppermute | solution.py:642
  93.0 1.7 %pass_on.2 = bf16[3,1536,128]{2,1,0:T(8,128)(2,1)} custom-call(bf16[3,1536,128]{2,1,0:T(8,128)(2,1)S(1)} %fold.4._.own, bf16[3,1536,128]{2,1,0:T(8,128)(2,1)S(1)} %collective-permute-done.21.got, bf16[3,1536,128]{2,1,0:T(8,128)(2,1)} %fold.7.refs_0_.own), custom_call_target="tpu_custom_call" | custom-call | flops 1179648 | bytes 3538944 | tf_op jit(solution)/shard_map/pass_on/pallas_call | solution.py:576
  94.8 3.5 %collective-permute-start.22 = (bf16[3,1536,128]{2,1,0:T(8,128)(2,1)}, bf16[3,1536,128]{2,1,0:T(8,128)(2,1)}, u32[]{:S(2)}, u32[]{:S(2)}) collective-permute-start(bf16[3,1536,128]{2,1,0:T(8,128)(2,1)} %pass_on.2), channel_id=1, source_target_pairs={{8,24},{12,28},{16,0},{20,4},{9,25},{13,29},{17,1},{21,5},{10,26},... | collective-permute-start | bytes 3538952 | tf_op jit(solution)/shard_map/ppermute | solution.py:642
  101.5 1.7 %copy-done.2 = bf16[3,2,256,768]{3,2,1,0:T(8,128)(2,1)S(1)} copy-done((bf16[3,2,256,768]{3,2,1,0:T(8,128)(2,1)S(1)}, bf16[3,2,256,768]{3,2,1,0:T(8,128)(2,1)}, u32[]{:S(2)}) %copy-start.2) | copy-done | bytes 2359320
  103.1 1.7 %copy-done.4 = bf16[3,2,256,768]{3,2,1,0:T(8,128)(2,1)S(1)} copy-done((bf16[3,2,256,768]{3,2,1,0:T(8,128)(2,1)S(1)}, bf16[3,2,256,768]{3,2,1,0:T(8,128)(2,1)}, u32[]{:S(2)}) %copy-start.4) | copy-done | bytes 2359320
  105.5 12.5 %collective-permute-done.23.refs_0_.got = bf16[3,1536,128]{2,1,0:T(8,128)(2,1)} collective-permute-done((bf16[3,1536,128]{2,1,0:T(8,128)(2,1)}, bf16[3,1536,128]{2,1,0:T(8,128)(2,1)}, u32[]{:S(2)}, u32[]{:S(2)}) %collective-permute-start.23) | collective-permute-done | bytes 1179680 | tf_op jit(solution)/shard_map/ppermute | solution.py:642
  118.4 2.6 %pass_on.3 = bf16[3,1536,128]{2,1,0:T(8,128)(2,1)S(1)} custom-call(bf16[3,1536,128]{2,1,0:T(8,128)(2,1)} %fold.7.refs_0_.own, bf16[3,1536,128]{2,1,0:T(8,128)(2,1)} %collective-permute-done.23.refs_0_.got), custom_call_target="tpu_custom_call" | custom-call | flops 1179648 | bytes 3538944 | tf_op jit(solution)/shard_map/pass_on/pallas_call | solution.py:576
  122.2 2.7 %collective-permute-start.25 = (bf16[3,1536,128]{2,1,0:T(8,128)(2,1)S(1)}, bf16[3,1536,128]{2,1,0:T(8,128)(2,1)S(1)}, u32[]{:S(2)}, u32[]{:S(2)}) collective-permute-start(bf16[3,1536,128]{2,1,0:T(8,128)(2,1)S(1)} %pass_on.3), channel_id=1, source_target_pairs={{8,16},{12,20},{16,8},{20,12},{9,17},{13,21},{17,9},{21,13},{10,18... | collective-permute-start | bytes 3538952 | tf_op jit(solution)/shard_map/ppermute | solution.py:642
  125.0 2.1 %fusion.1 = bf16[128,2048]{1,0:T(8,128)(2,1)} fusion(bf16[128,2048]{1,0:T(8,128)(2,1)} %collective-permute-done.17, bf16[1,128,2048]{2,1,0:T(8,128)(2,1)S(1)} %copy-done.11, bf16[2,128,2048]{2,1,0:T(8,128)(2,1)S(1)} %copy-done.19), kind=kLoop, calls=%fused_computation.4 | loop fusion | flops 1572864 | bytes 2097152 | tf_op jit(solution)/shard_map/convert_element_type | solution.py:506
  127.1 2.1 %fusion = bf16[128,2048]{1,0:T(8,128)(2,1)} fusion(bf16[128,2048]{1,0:T(8,128)(2,1)} %collective-permute-done.19, bf16[1,128,2048]{2,1,0:T(8,128)(2,1)S(1)} %copy-done.9, bf16[2,128,2048]{2,1,0:T(8,128)(2,1)S(1)} %copy-done.17), kind=kLoop, calls=%fused_computation.2 | loop fusion | flops 1572864 | bytes 2097152 | tf_op jit(solution)/shard_map/convert_element_type | solution.py:506
  129.2 1.7 %add_convert_fusion.refs_0_ = bf16[3,1536,128]{2,1,0:T(8,128)(2,1)S(1)} fusion(bf16[3,1536,128]{2,1,0:T(8,128)(2,1)} %collective-permute-done.22, bf16[3,1536,128]{2,1,0:T(8,128)(2,1)S(1)} %fold.5.other, bf16[3,1536,128]{2,1,0:T(8,128)(2,1)S(1)} %fold.6.one, pred[]{:T(512)S(6)} %gt.3), kind=kLoop, calls=%fused_computation | loop fusion | flops 2949120 | bytes 4718593 | tf_op jit(solution)/shard_map/convert_element_type | solution.py:506
  130.9 16.6 %collective-permute-done.24.refs_1_ = bf16[3,1536,128]{2,1,0:T(8,128)(2,1)S(1)} collective-permute-done((bf16[3,1536,128]{2,1,0:T(8,128)(2,1)S(1)}, bf16[3,1536,128]{2,1,0:T(8,128)(2,1)S(1)}, u32[]{:S(2)}, u32[]{:S(2)}) %collective-permute-start.24) | collective-permute-done | bytes 1179680 | tf_op jit(solution)/shard_map/ppermute | solution.py:642
  147.5 3.1 %collective-permute-done.25.refs_2_ = bf16[3,1536,128]{2,1,0:T(8,128)(2,1)S(1)} collective-permute-done((bf16[3,1536,128]{2,1,0:T(8,128)(2,1)S(1)}, bf16[3,1536,128]{2,1,0:T(8,128)(2,1)S(1)}, u32[]{:S(2)}, u32[]{:S(2)}) %collective-permute-start.25) | collective-permute-done | bytes 1179680 | tf_op jit(solution)/shard_map/ppermute | solution.py:642
  150.6 1.9 %unfold.1 = (bf16[1,256,768]{2,1,0:T(8,128)(2,1)}, bf16[1,256,768]{2,1,0:T(8,128)(2,1)}, bf16[1,96,2048]{2,1,0:T(8,128)(2,1)}) custom-call(bf16[3,1536,128]{2,1,0:T(8,128)(2,1)S(1)} %add_convert_fusion.refs_0_, bf16[3,1536,128]{2,1,0:T(8,128)(2,1)S(1)} %collective-permute-done.24.refs_1_, bf16[3,1536,128]{2,1,0:T(8,128)(2,1)S(1)} %collective-permute-done.25.refs_2_), custom_call_target="tpu_custom_call" | custom-call | flops 2359296 | bytes 5898240 | tf_op jit(solution)/shard_map/unfold/pallas_call | solution.py:629
  (85 shorter events, 19.2 us)
Async XLA Ops:
  0.6 30.2 %copy-start.14 = (bf16[1,768,2048]{2,1,0:T(8,128)(2,1)S(1)}, bf16[1,768,2048]{2,1,0:T(8,128)(2,1)}, u32[]{:S(2)}) copy-start(bf16[1,768,2048]{2,1,0:T(8,128)(2,1)} %param.19) | copy-start | bytes 9437188
  2.8 17.1 %collective-permute-start = (bf16[128,2048]{1,0:T(8,128)(2,1)}, bf16[128,2048]{1,0:T(8,128)(2,1)S(1)}, u32[]{:S(2)}, u32[]{:S(2)}) collective-permute-start(bf16[128,2048]{1,0:T(8,128)(2,1)} %refs_0_), channel_id=1, source_target_pairs={{0,1},{1,0},{2,3},{3,2},{4,5},{5,4},{6,7},{7,6},{8,9},{9,8},{10,11... | collective-permute-start | bytes 1572872 | tf_op jit(solution)/shard_map/ppermute | solution.py:208
  4.3 15.5 %collective-permute-start.1 = (bf16[128,2048]{1,0:T(8,128)(2,1)}, bf16[128,2048]{1,0:T(8,128)(2,1)S(1)}, u32[]{:S(2)}, u32[]{:S(2)}) collective-permute-start(bf16[128,2048]{1,0:T(8,128)(2,1)} %refs_0_), channel_id=1, source_target_pairs={{0,2},{1,3},{2,0},{3,1},{4,6},{5,7},{6,4},{7,5},{8,10},{9,11},{10,... | collective-permute-start | bytes 1572872 | tf_op jit(solution)/shard_map/ppermute | solution.py:208
  4.8 6.0 %collective-permute-start.4 = (bf16[32,2176]{1,0:T(8,128)(2,1)S(1)}, bf16[32,2176]{1,0:T(8,128)(2,1)S(1)}, u32[]{:S(2)}, u32[]{:S(2)}) collective-permute-start(bf16[32,2176]{1,0:T(8,128)(2,1)S(1)} %get-tuple-element.50), channel_id=1, source_target_pairs={{0,8},{4,12},{8,0},{12,4},{16,24},{20,28},{24,16},{28,20},{1,9},{5... | collective-permute-start | bytes 417800 | tf_op jit(solution)/shard_map/ppermute | solution.py:183
  5.3 12.2 %collective-permute-start.5 = (bf16[32,2176]{1,0:T(8,128)(2,1)S(1)}, bf16[32,2176]{1,0:T(8,128)(2,1)S(1)}, u32[]{:S(2)}, u32[]{:S(2)}) collective-permute-start(bf16[32,2176]{1,0:T(8,128)(2,1)S(1)} %get-tuple-element.51), channel_id=1, source_target_pairs={{0,16},{4,20},{8,24},{12,28},{16,0},{20,4},{24,8},{28,12},{1,17},{... | collective-permute-start | bytes 417800 | tf_op jit(solution)/shard_map/ppermute | solution.py:183
  7.9 14.4 %copy-start.12 = (s32[128,2]{0,1:T(2,128)S(1)}, s32[128,2]{0,1:T(2,128)}, u32[]{:S(2)}) copy-start(s32[128,2]{0,1:T(2,128)} %param.14) | copy-start | bytes 3076
  7.9 14.4 %copy-start.13 = (f32[128,2]{0,1:T(2,128)S(1)}, f32[128,2]{0,1:T(2,128)}, u32[]{:S(2)}) copy-start(f32[128,2]{0,1:T(2,128)} %param.15) | copy-start | bytes 3076
  7.9 12.0 %collective-permute-start.6 = (bf16[32,2176]{1,0:T(8,128)(2,1)S(1)}, bf16[32,2176]{1,0:T(8,128)(2,1)S(1)}, u32[]{:S(2)}, u32[]{:S(2)}) collective-permute-start(bf16[32,2176]{1,0:T(8,128)(2,1)S(1)} %get-tuple-element.52), channel_id=1, source_target_pairs={{0,24},{4,28},{8,16},{12,20},{16,8},{20,12},{24,0},{28,4},{1,25},{... | collective-permute-start | bytes 417800 | tf_op jit(solution)/shard_map/ppermute | solution.py:183
  19.9 2.3 %collective-permute-start.7 = (bf16[64,2176]{1,0:T(8,128)(2,1)S(1)}, bf16[64,2176]{1,0:T(8,128)(2,1)S(1)}, u32[]{:S(2)}, u32[]{:S(2)}) collective-permute-start(bf16[64,2176]{1,0:T(8,128)(2,1)S(1)} %get-tuple-element.54), channel_id=1, source_target_pairs={{0,4},{4,0},{8,12},{12,8},{16,20},{20,16},{24,28},{28,24},{1,5},{5... | collective-permute-start | bytes 835592 | tf_op jit(solution)/shard_map/ppermute | solution.py:660
  20.0 9.2 %collective-permute-start.2 = (bf16[64,2048]{1,0:T(8,128)(2,1)S(1)}, bf16[64,2048]{1,0:T(8,128)(2,1)S(1)}, u32[]{:S(2)}, u32[]{:S(2)}) collective-permute-start(bf16[64,2048]{1,0:T(8,128)(2,1)S(1)} %slice.24), channel_id=1, source_target_pairs={{0,2},{1,3},{2,0},{3,1},{4,6},{5,7},{6,4},{7,5},{8,10},{9,11},{10,... | collective-permute-start | bytes 786440 | tf_op jit(solution)/shard_map/ppermute | solution.py:208
  21.6 9.2 %collective-permute-start.3 = (bf16[64,2048]{1,0:T(8,128)(2,1)S(1)}, bf16[64,2048]{1,0:T(8,128)(2,1)S(1)}, u32[]{:S(2)}, u32[]{:S(2)}) collective-permute-start(bf16[64,2048]{1,0:T(8,128)(2,1)S(1)} %slice.25), channel_id=1, source_target_pairs={{0,1},{1,0},{2,3},{3,2},{4,5},{5,4},{6,7},{7,6},{8,9},{9,8},{10,11... | collective-permute-start | bytes 786440 | tf_op jit(solution)/shard_map/ppermute | solution.py:208
  22.2 20.5 %copy-start.6 = (bf16[1,2048,768]{2,1,0:T(8,128)(2,1)S(1)}, bf16[1,2048,768]{2,1,0:T(8,128)(2,1)}, u32[]{:S(2)}) copy-start(bf16[1,2048,768]{2,1,0:T(8,128)(2,1)} %param.18) | copy-start | bytes 9437188
  22.5 14.3 %collective-permute-start.8 = (bf16[64,2176]{1,0:T(8,128)(2,1)S(1)}, bf16[64,2176]{1,0:T(8,128)(2,1)S(1)}, u32[]{:S(2)}, u32[]{:S(2)}) collective-permute-start(bf16[64,2176]{1,0:T(8,128)(2,1)S(1)} %get-tuple-element.55.refs_0_), channel_id=1, source_target_pairs={{0,1},{1,0},{2,3},{3,2},{4,5},{5,4},{6,7},{7,6},{8,9},{9,8},{10,11... | collective-permute-start | bytes 835592 | tf_op jit(solution)/shard_map/ppermute | solution.py:208
  24.1 12.7 %collective-permute-start.11 = (bf16[64,2176]{1,0:T(8,128)(2,1)S(1)}, bf16[64,2176]{1,0:T(8,128)(2,1)S(1)}, u32[]{:S(2)}, u32[]{:S(2)}) collective-permute-start(bf16[64,2176]{1,0:T(8,128)(2,1)S(1)} %get-tuple-element.56.refs_1_), channel_id=1, source_target_pairs={{0,2},{1,3},{2,0},{3,1},{4,6},{5,7},{6,4},{7,5},{8,10},{9,11},{10,... | collective-permute-start | bytes 835592 | tf_op jit(solution)/shard_map/ppermute | solution.py:208
  24.6 18.2 %collective-permute-start.9 = (bf16[64,2176]{1,0:T(8,128)(2,1)S(1)}, bf16[64,2176]{1,0:T(8,128)(2,1)S(1)}, u32[]{:S(2)}, u32[]{:S(2)}) collective-permute-start(bf16[64,2176]{1,0:T(8,128)(2,1)S(1)} %get-tuple-element.56.refs_1_), channel_id=1, source_target_pairs={{0,1},{1,0},{2,3},{3,2},{4,5},{5,4},{6,7},{7,6},{8,9},{9,8},{10,11... | collective-permute-start | bytes 835592 | tf_op jit(solution)/shard_map/ppermute | solution.py:208
  29.2 13.6 %collective-permute-start.10 = (bf16[64,2176]{1,0:T(8,128)(2,1)S(1)}, bf16[64,2176]{1,0:T(8,128)(2,1)S(1)}, u32[]{:S(2)}, u32[]{:S(2)}) collective-permute-start(bf16[64,2176]{1,0:T(8,128)(2,1)S(1)} %get-tuple-element.55.refs_0_), channel_id=1, source_target_pairs={{0,2},{1,3},{2,0},{3,1},{4,6},{5,7},{6,4},{7,5},{8,10},{9,11},{10,... | collective-permute-start | bytes 835592 | tf_op jit(solution)/shard_map/ppermute | solution.py:208
  31.9 10.9 %copy-start.5 = (bf16[1,2048,768]{2,1,0:T(8,128)(2,1)S(1)}, bf16[1,2048,768]{2,1,0:T(8,128)(2,1)}, u32[]{:S(2)}) copy-start(bf16[1,2048,768]{2,1,0:T(8,128)(2,1)} %param.17) | copy-start | bytes 9437188
  36.8 11.5 %collective-permute-start.12 = (bf16[64,2176]{1,0:T(8,128)(2,1)S(1)}, bf16[64,2176]{1,0:T(8,128)(2,1)S(1)}, u32[]{:S(2)}, u32[]{:S(2)}) collective-permute-start(bf16[64,2176]{1,0:T(8,128)(2,1)S(1)} %collective-permute-done.8.refs_2_), channel_id=1, source_target_pairs={{0,2},{1,3},{2,0},{3,1},{4,6},{5,7},{6,4},{7,5},{8,10},{9,11},{10,... | collective-permute-start | bytes 835592 | tf_op jit(solution)/shard_map/ppermute | solution.py:208
  37.3 11.0 %collective-permute-start.13 = (bf16[64,2176]{1,0:T(8,128)(2,1)S(1)}, bf16[64,2176]{1,0:T(8,128)(2,1)S(1)}, u32[]{:S(2)}, u32[]{:S(2)}) collective-permute-start(bf16[64,2176]{1,0:T(8,128)(2,1)S(1)} %collective-permute-done.11.refs_5_), channel_id=1, source_target_pairs={{0,1},{1,0},{2,3},{3,2},{4,5},{5,4},{6,7},{7,6},{8,9},{9,8},{10,11... | collective-permute-start | bytes 835592 | tf_op jit(solution)/shard_map/ppermute | solution.py:208
  53.9 4.1 %collective-permute-start.14 = (bf16[2,256,768]{2,1,0:T(8,128)(2,1)}, bf16[2,256,768]{2,1,0:T(8,128)(2,1)S(1)}, u32[]{:S(2)}, u32[]{:S(2)}) collective-permute-start(bf16[2,256,768]{2,1,0:T(8,128)(2,1)} %get-tuple-element.71), channel_id=1, source_target_pairs={{0,4},{4,0},{8,12},{12,8},{16,20},{20,16},{24,28},{28,24},{1,5},{5... | collective-permute-start | bytes 2359304 | tf_op jit(solution)/shard_map/ppermute | solution.py:660
  57.4 4.6 %collective-permute-start.15 = (bf16[4,96,2048]{2,1,0:T(8,128)(2,1)}, bf16[4,96,2048]{2,1,0:T(8,128)(2,1)S(1)}, u32[]{:S(2)}, u32[]{:S(2)}) collective-permute-start(bf16[4,96,2048]{2,1,0:T(8,128)(2,1)} %get-tuple-element.76), channel_id=1, source_target_pairs={{0,4},{4,0},{8,12},{12,8},{16,20},{20,16},{24,28},{28,24},{1,5},{5... | collective-permute-start | bytes 4718600 | tf_op jit(solution)/shard_map/ppermute | solution.py:660
  62.0 9.0 %collective-permute-start.20 = (bf16[3,2,256,768]{3,2,1,0:T(8,128)(2,1)}, bf16[3,2,256,768]{3,2,1,0:T(8,128)(2,1)S(1)}, u32[]{:S(2)}, u32[]{:S(2)}) collective-permute-start(bf16[3,2,256,768]{3,2,1,0:T(8,128)(2,1)} %get-tuple-element.84), channel_id=1, source_target_pairs={{0,4},{4,0},{8,12},{12,8},{16,20},{20,16},{24,28},{28,24},{1,5},{5... | collective-permute-start | bytes 7077896 | tf_op jit(solution)/shard_map/ppermute | solution.py:660
  62.4 30.7 %collective-permute-start.21 = (bf16[3,1536,128]{2,1,0:T(8,128)(2,1)S(1)}, bf16[3,1536,128]{2,1,0:T(8,128)(2,1)S(1)}, u32[]{:S(2)}, u32[]{:S(2)}) collective-permute-start(bf16[3,1536,128]{2,1,0:T(8,128)(2,1)S(1)} %fold.4._.own), channel_id=1, source_target_pairs={{0,8},{4,12},{24,16},{28,20},{1,9},{5,13},{25,17},{29,21},{2,10},{... | collective-permute-start | bytes 3538952 | tf_op jit(solution)/shard_map/ppermute | solution.py:642
  63.7 7.3 %copy-start.1 = (bf16[3,2,256,768]{3,2,1,0:T(8,128)(2,1)S(1)}, bf16[3,2,256,768]{3,2,1,0:T(8,128)(2,1)}, u32[]{:S(2)}) copy-start(bf16[3,2,256,768]{3,2,1,0:T(8,128)(2,1)} %get-tuple-element.83.gu_mine) | copy-start | bytes 7077892
  69.8 28.4 %collective-permute-start.16 = (bf16[2,128,2048]{2,1,0:T(8,128)(2,1)S(1)}, bf16[2,128,2048]{2,1,0:T(8,128)(2,1)S(1)}, u32[]{:S(2)}, u32[]{:S(2)}) collective-permute-start(bf16[2,128,2048]{2,1,0:T(8,128)(2,1)S(1)} %get-tuple-element.78), channel_id=1, source_target_pairs={{0,1},{1,0},{2,3},{3,2},{4,5},{5,4},{6,7},{7,6},{8,9},{9,8},{10,11... | collective-permute-start | bytes 3145736 | tf_op jit(solution)/shard_map/ppermute | solution.py:208
  70.4 29.4 %collective-permute-start.18 = (bf16[2,128,2048]{2,1,0:T(8,128)(2,1)S(1)}, bf16[2,128,2048]{2,1,0:T(8,128)(2,1)S(1)}, u32[]{:S(2)}, u32[]{:S(2)}) collective-permute-start(bf16[2,128,2048]{2,1,0:T(8,128)(2,1)S(1)} %get-tuple-element.81), channel_id=1, source_target_pairs={{0,2},{1,3},{2,0},{3,1},{4,6},{5,7},{6,4},{7,5},{8,10},{9,11},{10,... | collective-permute-start | bytes 3145736 | tf_op jit(solution)/shard_map/ppermute | solution.py:208
  72.8 45.2 %collective-permute-start.23 = (bf16[3,1536,128]{2,1,0:T(8,128)(2,1)}, bf16[3,1536,128]{2,1,0:T(8,128)(2,1)}, u32[]{:S(2)}, u32[]{:S(2)}) collective-permute-start(bf16[3,1536,128]{2,1,0:T(8,128)(2,1)} %fold.7.refs_0_.own), channel_id=1, source_target_pairs={{0,8},{4,12},{24,16},{28,20},{1,9},{5,13},{25,17},{29,21},{2,10},{... | collective-permute-start | bytes 3538952 | tf_op jit(solution)/shard_map/ppermute | solution.py:642
  94.8 27.5 %collective-permute-start.22 = (bf16[3,1536,128]{2,1,0:T(8,128)(2,1)}, bf16[3,1536,128]{2,1,0:T(8,128)(2,1)}, u32[]{:S(2)}, u32[]{:S(2)}) collective-permute-start(bf16[3,1536,128]{2,1,0:T(8,128)(2,1)} %pass_on.2), channel_id=1, source_target_pairs={{8,24},{12,28},{16,0},{20,4},{9,25},{13,29},{17,1},{21,5},{10,26},... | collective-permute-start | bytes 3538952 | tf_op jit(solution)/shard_map/ppermute | solution.py:642
  99.3 25.7 %collective-permute-start.17 = (bf16[128,2048]{1,0:T(8,128)(2,1)}, bf16[128,2048]{1,0:T(8,128)(2,1)}, u32[]{:S(2)}, u32[]{:S(2)}) collective-permute-start(bf16[128,2048]{1,0:T(8,128)(2,1)} %fusion.2), channel_id=1, source_target_pairs={{0,2},{1,3},{2,0},{3,1},{4,6},{5,7},{6,4},{7,5},{8,10},{9,11},{10,... | collective-permute-start | bytes 1572872 | tf_op jit(solution)/shard_map/ppermute | solution.py:208
  101.0 26.1 %collective-permute-start.19 = (bf16[128,2048]{1,0:T(8,128)(2,1)}, bf16[128,2048]{1,0:T(8,128)(2,1)}, u32[]{:S(2)}, u32[]{:S(2)}) collective-permute-start(bf16[128,2048]{1,0:T(8,128)(2,1)} %fusion.3), channel_id=1, source_target_pairs={{0,1},{1,0},{2,3},{3,2},{4,5},{5,4},{6,7},{7,6},{8,9},{9,8},{10,11... | collective-permute-start | bytes 1572872 | tf_op jit(solution)/shard_map/ppermute | solution.py:208
  118.3 29.2 %collective-permute-start.24 = (bf16[3,1536,128]{2,1,0:T(8,128)(2,1)S(1)}, bf16[3,1536,128]{2,1,0:T(8,128)(2,1)S(1)}, u32[]{:S(2)}, u32[]{:S(2)}) collective-permute-start(bf16[3,1536,128]{2,1,0:T(8,128)(2,1)S(1)} %choose.1), channel_id=1, source_target_pairs={{0,8},{4,12},{8,0},{12,4},{16,24},{20,28},{24,16},{28,20},{1,9},{5... | collective-permute-start | bytes 3538952 | tf_op jit(solution)/shard_map/ppermute | solution.py:642
  122.2 28.4 %collective-permute-start.25 = (bf16[3,1536,128]{2,1,0:T(8,128)(2,1)S(1)}, bf16[3,1536,128]{2,1,0:T(8,128)(2,1)S(1)}, u32[]{:S(2)}, u32[]{:S(2)}) collective-permute-start(bf16[3,1536,128]{2,1,0:T(8,128)(2,1)S(1)} %pass_on.3), channel_id=1, source_target_pairs={{8,16},{12,20},{16,8},{20,12},{9,17},{13,21},{17,9},{21,13},{10,18... | collective-permute-start | bytes 3538952 | tf_op jit(solution)/shard_map/ppermute | solution.py:642
  (14 other events, 50.6 us)

commit v6 on v5

--- a/solution.py
+++ b/solution.py
@@ -323,8 +323,9 @@
             turned_x[pl.ds(at, strip), :] = whole[:, i * strip : (i + 1) * strip].T
 
     x = whole[:, :width]
-    gate = jnp.dot(x, wg_ref[...], preferred_element_type=F32)
-    up = jnp.dot(x, wu_ref[...], preferred_element_type=F32)
+    here = pl.ds(pl.multiple_of(step * gate_out.shape[1], LANES), gate_out.shape[1])
+    gate = jnp.dot(x, wg_ref[:, here], preferred_element_type=F32)
+    up = jnp.dot(x, wu_ref[:, here], preferred_element_type=F32)
     gs = gs_ref[...]
     sig = jax.nn.sigmoid(gate)
     act = gate * sig
@@ -349,7 +350,7 @@
     tile = 256
     at = 0 if before is None else total // rows - 1
     columns = pl.BlockSpec((rows, tile), lambda j: (at, j))
-    weights = pl.BlockSpec((width, tile), lambda j: (0, j))
+    weights = vmem()
     before = before or []
     return pl.pallas_call(
         functools.partial(units_kernel, len(pieces), slot, not before, n_dp),

time: 153 us -> 153 us (level)
  transfers between devices with their start and end apart: 26 -> 26, of which waited for: 12 -> 13; matrix products, arithmetic and copies ran while one was open for 5% -> 5% of each run, Pallas kernels for 20% -> 19%
where the time goes in v6:
time: 153 us; the launch traced here: 152 us
  waiting for transfers between devices  75 us (49%)
  Pallas kernels  38.5 us (25%)
  starting transfers between devices  24.8 us (16%)
  other arithmetic  7.97 us (5%)
  local copies, waits for them, and re-layouts  4.55 us (3%)
    ppermute x5, waiting for transfers between devices, chips_permute(): lax.ppermute(value, 'dp', [(CORES * a + c, CORES * b + c) for a, b in pai...  52.3 us
    ppermute x14, starting transfers between devices, swap(): return lax.ppermute(value, 'expert', [(d, d ^ i) for d in range(n_ex)])  11.8 us
    ppermute x3, waiting for transfers between devices, send_sequences(): lax.ppermute(pieces[i], 'dp', [(d, d ^ CORES * i) for d in range(n_dp)])  11.5 us
    ppermute x14, waiting for transfers between devices, swap(): return lax.ppermute(value, 'expert', [(d, d ^ i) for d in range(n_ex)])  11.1 us
    ppermute x5, starting transfers between devices, chips_permute(): lax.ppermute(value, 'dp', [(CORES * a + c, CORES * b + c) for a, b in pai...  8.87 us
    convert_element_type x5, other arithmetic, add(): return sum((part.astype(F32) for part in parts)).astype(BF16)  7.97 us
    pallas_call x2, Pallas kernels, hidden_units(): pl.pallas_call(functools.partial(units_kernel, len(pieces), slot, not bef...  7.63 us
    pallas_call x1, Pallas kernels, outputs(): pl.pallas_call(functools.partial(outputs_kernel, layer_groups, grad_group...  6.14 us
  transfers between devices with their start and end apart: 26, of which 13 were waited for; matrix products, arithmetic and copies ran while one was open for 5% of the time, Pallas kernels for 19%

profile of v6, /device:TPU:12, one launch (start us, length us, event | category | flops | bytes accessed | tf_op | source)
XLA Modules:
  0.0 151.8 jit_solution(3471865433555132876)
XLA Ops:
  0.6 2.1 %pick.1 = (bf16[32,2176]{1,0:T(8,128)(2,1)S(1)}, bf16[32,2176]{1,0:T(8,128)(2,1)S(1)}, bf16[32,2176]{1,0:T(8,128)(2,1)S(1)}, bf16[32,2176]{1,0:T(8,128)(2,1)S(1)}) custom-call(s32[1,1,8]{2,1,0:T(1,128)} %dest_hbm.1, s32[1,1,8]{2,1,0:T(1,128)} %len_hbm.1, bf16[1,1,8]{2,1,0:T(2,128)(2,1)} %adv_hbm.1, bf16[8,16,2048]{2,1,0:T(8,128)(2,1)} %bitcast.33), custom_call_target="tpu_custom_call" | custom-call | tf_op jit(solution)/shard_map/pick/pallas_call | solution.py:94
  2.8 1.6 %collective-permute-start = (bf16[128,2048]{1,0:T(8,128)(2,1)}, bf16[128,2048]{1,0:T(8,128)(2,1)S(1)}, u32[]{:S(2)}, u32[]{:S(2)}) collective-permute-start(bf16[128,2048]{1,0:T(8,128)(2,1)} %refs_0_), channel_id=1, source_target_pairs={{0,1},{1,0},{2,3},{3,2},{4,5},{5,4},{6,7},{7,6},{8,9},{9,8},{10,11... | collective-permute-start | bytes 1572872 | tf_op jit(solution)/shard_map/ppermute | solution.py:208
  5.3 2.6 %collective-permute-start.5 = (bf16[32,2176]{1,0:T(8,128)(2,1)S(1)}, bf16[32,2176]{1,0:T(8,128)(2,1)S(1)}, u32[]{:S(2)}, u32[]{:S(2)}) collective-permute-start(bf16[32,2176]{1,0:T(8,128)(2,1)S(1)} %get-tuple-element.51), channel_id=1, source_target_pairs={{0,16},{4,20},{8,24},{12,28},{16,0},{20,4},{24,8},{28,12},{1,17},{... | collective-permute-start | bytes 417800 | tf_op jit(solution)/shard_map/ppermute | solution.py:183
  8.3 2.5 %collective-permute-done.4.refs_1_ = bf16[32,2176]{1,0:T(8,128)(2,1)S(1)} collective-permute-done((bf16[32,2176]{1,0:T(8,128)(2,1)S(1)}, bf16[32,2176]{1,0:T(8,128)(2,1)S(1)}, u32[]{:S(2)}, u32[]{:S(2)}) %collective-permute-start.4) | collective-permute-done | bytes 139296 | tf_op jit(solution)/shard_map/ppermute | solution.py:183
  10.8 6.6 %collective-permute-done.5.refs_2_ = bf16[32,2176]{1,0:T(8,128)(2,1)S(1)} collective-permute-done((bf16[32,2176]{1,0:T(8,128)(2,1)S(1)}, bf16[32,2176]{1,0:T(8,128)(2,1)S(1)}, u32[]{:S(2)}, u32[]{:S(2)}) %collective-permute-start.5) | collective-permute-done | bytes 139296 | tf_op jit(solution)/shard_map/ppermute | solution.py:183
  17.5 2.4 %collective-permute-done.6.refs_3_ = bf16[32,2176]{1,0:T(8,128)(2,1)S(1)} collective-permute-done((bf16[32,2176]{1,0:T(8,128)(2,1)S(1)}, bf16[32,2176]{1,0:T(8,128)(2,1)S(1)}, u32[]{:S(2)}, u32[]{:S(2)}) %collective-permute-start.6) | collective-permute-done | bytes 139296 | tf_op jit(solution)/shard_map/ppermute | solution.py:183
  20.0 1.6 %collective-permute-start.2 = (bf16[64,2048]{1,0:T(8,128)(2,1)S(1)}, bf16[64,2048]{1,0:T(8,128)(2,1)S(1)}, u32[]{:S(2)}, u32[]{:S(2)}) collective-permute-start(bf16[64,2048]{1,0:T(8,128)(2,1)S(1)} %slice.24), channel_id=1, source_target_pairs={{0,2},{1,3},{2,0},{3,1},{4,6},{5,7},{6,4},{7,5},{8,10},{9,11},{10,... | collective-permute-start | bytes 786440 | tf_op jit(solution)/shard_map/ppermute | solution.py:208
  25.4 3.7 %collective-permute-done.2.refs_3_ = bf16[64,2048]{1,0:T(8,128)(2,1)S(1)} collective-permute-done((bf16[64,2048]{1,0:T(8,128)(2,1)S(1)}, bf16[64,2048]{1,0:T(8,128)(2,1)S(1)}, u32[]{:S(2)}, u32[]{:S(2)}) %collective-permute-start.2) | collective-permute-done | bytes 262176 | tf_op jit(solution)/shard_map/ppermute | solution.py:208
  31.9 2.7 %hidden_grad.1 = (f32[512,768]{1,0:T(8,128)S(1)}, bf16[512,2048]{1,0:T(8,128)(2,1)S(1)}) custom-call(bf16[768,2048]{1,0:T(8,128)(2,1)S(1)} %bitcast.31, bf16[128,2048]{1,0:T(8,128)(2,1)S(1)} %copy-done.15, bf16[128,2048]{1,0:T(8,128)(2,1)S(1)} %collective-permute-done.refs_1_.refs_4_, bf16[128,2048]{1,0:T(8,128)(2,1)S(1)} %collective-permute-done.1.refs_2_.refs_5_, ...), custom_call_target="tpu_custom_call" | custom-call | flops 1610612736 | bytes 7340032 | tf_op jit(solution)/shard_map/hidden_grad/pallas_call | solution.py:276
  34.6 2.2 %collective-permute-done.8.refs_2_ = bf16[64,2176]{1,0:T(8,128)(2,1)S(1)} collective-permute-done((bf16[64,2176]{1,0:T(8,128)(2,1)S(1)}, bf16[64,2176]{1,0:T(8,128)(2,1)S(1)}, u32[]{:S(2)}, u32[]{:S(2)}) %collective-permute-start.8) | collective-permute-done | bytes 278560 | tf_op jit(solution)/shard_map/ppermute | solution.py:208
  37.9 4.9 %collective-permute-done.9.refs_3_ = bf16[64,2176]{1,0:T(8,128)(2,1)S(1)} collective-permute-done((bf16[64,2176]{1,0:T(8,128)(2,1)S(1)}, bf16[64,2176]{1,0:T(8,128)(2,1)S(1)}, u32[]{:S(2)}, u32[]{:S(2)}) %collective-permute-start.9) | collective-permute-done | bytes 278560 | tf_op jit(solution)/shard_map/ppermute | solution.py:208
  42.8 5.1 %hidden_units.2 = (bf16[512,768]{1,0:T(8,128)(2,1)S(1)}, bf16[512,768]{1,0:T(8,128)(2,1)S(1)}, bf16[512,768]{1,0:T(8,128)(2,1)S(1)}, bf16[768,512]{1,0:T(8,128)(...) custom-call(bf16[2048,768]{1,0:T(8,128)(2,1)S(1)} %bitcast.21, bf16[2048,768]{1,0:T(8,128)(2,1)S(1)} %bitcast.24, ...), custom_call_target="tpu_custom_call" | custom-call | flops 2415919104 | bytes 9437184 | tf_op jit(solution)/shard_map/hidden_units/pallas_call | solution.py:355
  48.0 2.5 %hidden_units.3 = (bf16[512,768]{1,0:T(8,128)(2,1)S(1)}, bf16[512,768]{1,0:T(8,128)(2,1)S(1)}, bf16[512,768]{1,0:T(8,128)(2,1)S(1)}, bf16[768,512]{1,0:T(8,128)(...) custom-call(bf16[2048,768]{1,0:T(8,128)(2,1)S(1)} %bitcast.22, ...), custom_call_target="tpu_custom_call", output_to_operand_aliasing={{0}: (3, {}), {1}: (4, {}), {2}: (5, {}), {3}: (6, {}), {4}... | custom-call | flops 805306368 | bytes 7340032 | tf_op jit(solution)/shard_map/hidden_units/pallas_call | solution.py:355
  50.5 2.6 %far_grads.1 = (bf16[2,256,768]{2,1,0:T(8,128)(2,1)}, bf16[2,256,768]{2,1,0:T(8,128)(2,1)}) custom-call(bf16[2048,512]{1,0:T(8,128)(2,1)S(1)} %get-tuple-element.69.x_ref, bf16[512,768]{1,0:T(8,128)(2,1)S(1)} %get-tuple-element.67.gate_ref, bf16[512,768]{1,0:T(8,128)(2,1)S(1)} %get-tuple-element.68.up_ref), custom_call_target="tpu_custom_call" | custom-call | flops 805306368 | bytes 4718592 | tf_op jit(solution)/shard_map/far_grads/pallas_call | solution.py:404
  53.1 3.5 %row_grad.1 = (bf16[4,96,2048]{2,1,0:T(8,128)(2,1)}, bf16[4,96,2048]{2,1,0:T(8,128)(2,1)}) custom-call(bf16[768,512]{1,0:T(8,128)(2,1)S(1)} %get-tuple-element.73.hid_ref, bf16[512,2048]{1,0:T(8,128)(2,1)S(1)} %get-tuple-element.74.dy_ref), custom_call_target="tpu_custom_call" | custom-call | flops 1610612736 | bytes 5242880 | tf_op jit(solution)/shard_map/row_grad/pallas_call | solution.py:460
  57.2 4.0 %rest_grads.1 = (bf16[3,2,256,768]{3,2,1,0:T(8,128)(2,1)}, bf16[3,2,256,768]{3,2,1,0:T(8,128)(2,1)}) custom-call(bf16[2048,512]{1,0:T(8,128)(2,1)S(1)} %get-tuple-element.69.x_ref, bf16[512,768]{1,0:T(8,128)(2,1)S(1)} %get-tuple-element.67.gate_ref, bf16[512,768]{1,0:T(8,128)(2,1)S(1)} %get-tuple-element.68.up_ref, ...), custom_call_target="tpu_custom_call" | custom-call | flops 3221225472 | bytes 7864320 | tf_op jit(solution)/shard_map/rest_grads/pallas_call | solution.py:433
  62.9 6.1 %outputs.1 = (bf16[1,128,2048]{2,1,0:T(8,128)(2,1)S(1)}, bf16[1,128,2048]{2,1,0:T(8,128)(2,1)S(1)}, bf16[2,128,2048]{2,1,0:T(8,128)(2,1)S(1)}, bf16[1,128,2048]{...) custom-call(bf16[512,768]{1,0:T(8,128)(2,1)S(1)} %get-tuple-element.65.hid_ref, ...), custom_call_target="tpu_custom_call" | custom-call | flops 4831838208 | bytes 13631488 | tf_op jit(solution)/shard_map/outputs/pallas_call | solution.py:494
  70.2 1.9 %fold.7.refs_0_.own = bf16[3,1536,128]{2,1,0:T(8,128)(2,1)} custom-call(bf16[3,2,256,768]{3,2,1,0:T(8,128)(2,1)S(1)} %copy-done.1, bf16[3,2,256,768]{3,2,1,0:T(8,128)(2,1)S(1)} %collective-permute-done.20.gu_got, bf16[4,96,2048]{2,1,0:T(8,128)(2,1)S(1)} %copy-done, bf16[4,96,2048]{2,1,0:T(8,128)(2,1)S(1)} %collective-permute-done.15.row_got), custom_call_target="tpu_custom_call" | custom-call | flops 1179648 | bytes 3538944 | tf_op jit(solution)/shard_map/fold/pallas_call | solution.py:554
  73.4 18.9 %collective-permute-done.21.got = bf16[3,1536,128]{2,1,0:T(8,128)(2,1)S(1)} collective-permute-done((bf16[3,1536,128]{2,1,0:T(8,128)(2,1)S(1)}, bf16[3,1536,128]{2,1,0:T(8,128)(2,1)S(1)}, u32[]{:S(2)}, u32[]{:S(2)}) %collective-permute-start.21) | collective-permute-done | bytes 1179680 | tf_op jit(solution)/shard_map/ppermute | solution.py:643
  92.3 1.7 %pass_on.2 = bf16[3,1536,128]{2,1,0:T(8,128)(2,1)} custom-call(bf16[3,1536,128]{2,1,0:T(8,128)(2,1)S(1)} %fold.4._.own, bf16[3,1536,128]{2,1,0:T(8,128)(2,1)S(1)} %collective-permute-done.21.got, bf16[3,1536,128]{2,1,0:T(8,128)(2,1)} %fold.7.refs_0_.own), custom_call_target="tpu_custom_call" | custom-call | flops 1179648 | bytes 3538944 | tf_op jit(solution)/shard_map/pass_on/pallas_call | solution.py:577
  94.0 3.5 %collective-permute-start.22 = (bf16[3,1536,128]{2,1,0:T(8,128)(2,1)}, bf16[3,1536,128]{2,1,0:T(8,128)(2,1)}, u32[]{:S(2)}, u32[]{:S(2)}) collective-permute-start(bf16[3,1536,128]{2,1,0:T(8,128)(2,1)} %pass_on.2), channel_id=1, source_target_pairs={{8,24},{12,28},{16,0},{20,4},{9,25},{13,29},{17,1},{21,5},{10,26},... | collective-permute-start | bytes 3538952 | tf_op jit(solution)/shard_map/ppermute | solution.py:643
  100.7 1.7 %copy-done.2 = bf16[3,2,256,768]{3,2,1,0:T(8,128)(2,1)S(1)} copy-done((bf16[3,2,256,768]{3,2,1,0:T(8,128)(2,1)S(1)}, bf16[3,2,256,768]{3,2,1,0:T(8,128)(2,1)}, u32[]{:S(2)}) %copy-start.2) | copy-done | bytes 2359320
  102.4 1.7 %copy-done.4 = bf16[3,2,256,768]{3,2,1,0:T(8,128)(2,1)S(1)} copy-done((bf16[3,2,256,768]{3,2,1,0:T(8,128)(2,1)S(1)}, bf16[3,2,256,768]{3,2,1,0:T(8,128)(2,1)}, u32[]{:S(2)}) %copy-start.4) | copy-done | bytes 2359320
  104.8 12.5 %collective-permute-done.23.refs_0_.got = bf16[3,1536,128]{2,1,0:T(8,128)(2,1)} collective-permute-done((bf16[3,1536,128]{2,1,0:T(8,128)(2,1)}, bf16[3,1536,128]{2,1,0:T(8,128)(2,1)}, u32[]{:S(2)}, u32[]{:S(2)}) %collective-permute-start.23) | collective-permute-done | bytes 1179680 | tf_op jit(solution)/shard_map/ppermute | solution.py:643
  117.7 2.6 %pass_on.3 = bf16[3,1536,128]{2,1,0:T(8,128)(2,1)S(1)} custom-call(bf16[3,1536,128]{2,1,0:T(8,128)(2,1)} %fold.7.refs_0_.own, bf16[3,1536,128]{2,1,0:T(8,128)(2,1)} %collective-permute-done.23.refs_0_.got), custom_call_target="tpu_custom_call" | custom-call | flops 1179648 | bytes 3538944 | tf_op jit(solution)/shard_map/pass_on/pallas_call | solution.py:577
  121.5 2.7 %collective-permute-start.25 = (bf16[3,1536,128]{2,1,0:T(8,128)(2,1)S(1)}, bf16[3,1536,128]{2,1,0:T(8,128)(2,1)S(1)}, u32[]{:S(2)}, u32[]{:S(2)}) collective-permute-start(bf16[3,1536,128]{2,1,0:T(8,128)(2,1)S(1)} %pass_on.3), channel_id=1, source_target_pairs={{8,16},{12,20},{16,8},{20,12},{9,17},{13,21},{17,9},{21,13},{10,18... | collective-permute-start | bytes 3538952 | tf_op jit(solution)/shard_map/ppermute | solution.py:643
  124.2 2.1 %fusion.1 = bf16[128,2048]{1,0:T(8,128)(2,1)} fusion(bf16[128,2048]{1,0:T(8,128)(2,1)} %collective-permute-done.17, bf16[1,128,2048]{2,1,0:T(8,128)(2,1)S(1)} %copy-done.11, bf16[2,128,2048]{2,1,0:T(8,128)(2,1)S(1)} %copy-done.19), kind=kLoop, calls=%fused_computation.4 | loop fusion | flops 1572864 | bytes 2097152 | tf_op jit(solution)/shard_map/convert_element_type | solution.py:507
  126.3 2.1 %fusion = bf16[128,2048]{1,0:T(8,128)(2,1)} fusion(bf16[128,2048]{1,0:T(8,128)(2,1)} %collective-permute-done.19, bf16[1,128,2048]{2,1,0:T(8,128)(2,1)S(1)} %copy-done.9, bf16[2,128,2048]{2,1,0:T(8,128)(2,1)S(1)} %copy-done.17), kind=kLoop, calls=%fused_computation.2 | loop fusion | flops 1572864 | bytes 2097152 | tf_op jit(solution)/shard_map/convert_element_type | solution.py:507
  128.4 1.7 %add_convert_fusion.refs_0_ = bf16[3,1536,128]{2,1,0:T(8,128)(2,1)S(1)} fusion(bf16[3,1536,128]{2,1,0:T(8,128)(2,1)} %collective-permute-done.22, bf16[3,1536,128]{2,1,0:T(8,128)(2,1)S(1)} %fold.5.other, bf16[3,1536,128]{2,1,0:T(8,128)(2,1)S(1)} %fold.6.one, pred[]{:T(512)S(6)} %gt.3), kind=kLoop, calls=%fused_computation | loop fusion | flops 2949120 | bytes 4718593 | tf_op jit(solution)/shard_map/convert_element_type | solution.py:507
  130.1 16.6 %collective-permute-done.24.refs_1_ = bf16[3,1536,128]{2,1,0:T(8,128)(2,1)S(1)} collective-permute-done((bf16[3,1536,128]{2,1,0:T(8,128)(2,1)S(1)}, bf16[3,1536,128]{2,1,0:T(8,128)(2,1)S(1)}, u32[]{:S(2)}, u32[]{:S(2)}) %collective-permute-start.24) | collective-permute-done | bytes 1179680 | tf_op jit(solution)/shard_map/ppermute | solution.py:643
  146.7 3.1 %collective-permute-done.25.refs_2_ = bf16[3,1536,128]{2,1,0:T(8,128)(2,1)S(1)} collective-permute-done((bf16[3,1536,128]{2,1,0:T(8,128)(2,1)S(1)}, bf16[3,1536,128]{2,1,0:T(8,128)(2,1)S(1)}, u32[]{:S(2)}, u32[]{:S(2)}) %collective-permute-start.25) | collective-permute-done | bytes 1179680 | tf_op jit(solution)/shard_map/ppermute | solution.py:643
  149.9 1.9 %unfold.1 = (bf16[1,256,768]{2,1,0:T(8,128)(2,1)}, bf16[1,256,768]{2,1,0:T(8,128)(2,1)}, bf16[1,96,2048]{2,1,0:T(8,128)(2,1)}) custom-call(bf16[3,1536,128]{2,1,0:T(8,128)(2,1)S(1)} %add_convert_fusion.refs_0_, bf16[3,1536,128]{2,1,0:T(8,128)(2,1)S(1)} %collective-permute-done.24.refs_1_, bf16[3,1536,128]{2,1,0:T(8,128)(2,1)S(1)} %collective-permute-done.25.refs_2_), custom_call_target="tpu_custom_call" | custom-call | flops 2359296 | bytes 5898240 | tf_op jit(solution)/shard_map/unfold/pallas_call | solution.py:630
  (85 shorter events, 19.3 us)
Async XLA Ops:
  0.6 30.2 %copy-start.14 = (bf16[1,768,2048]{2,1,0:T(8,128)(2,1)S(1)}, bf16[1,768,2048]{2,1,0:T(8,128)(2,1)}, u32[]{:S(2)}) copy-start(bf16[1,768,2048]{2,1,0:T(8,128)(2,1)} %param.19) | copy-start | bytes 9437188
  2.8 17.1 %collective-permute-start = (bf16[128,2048]{1,0:T(8,128)(2,1)}, bf16[128,2048]{1,0:T(8,128)(2,1)S(1)}, u32[]{:S(2)}, u32[]{:S(2)}) collective-permute-start(bf16[128,2048]{1,0:T(8,128)(2,1)} %refs_0_), channel_id=1, source_target_pairs={{0,1},{1,0},{2,3},{3,2},{4,5},{5,4},{6,7},{7,6},{8,9},{9,8},{10,11... | collective-permute-start | bytes 1572872 | tf_op jit(solution)/shard_map/ppermute | solution.py:208
  4.3 15.5 %collective-permute-start.1 = (bf16[128,2048]{1,0:T(8,128)(2,1)}, bf16[128,2048]{1,0:T(8,128)(2,1)S(1)}, u32[]{:S(2)}, u32[]{:S(2)}) collective-permute-start(bf16[128,2048]{1,0:T(8,128)(2,1)} %refs_0_), channel_id=1, source_target_pairs={{0,2},{1,3},{2,0},{3,1},{4,6},{5,7},{6,4},{7,5},{8,10},{9,11},{10,... | collective-permute-start | bytes 1572872 | tf_op jit(solution)/shard_map/ppermute | solution.py:208
  4.8 6.0 %collective-permute-start.4 = (bf16[32,2176]{1,0:T(8,128)(2,1)S(1)}, bf16[32,2176]{1,0:T(8,128)(2,1)S(1)}, u32[]{:S(2)}, u32[]{:S(2)}) collective-permute-start(bf16[32,2176]{1,0:T(8,128)(2,1)S(1)} %get-tuple-element.50), channel_id=1, source_target_pairs={{0,8},{4,12},{8,0},{12,4},{16,24},{20,28},{24,16},{28,20},{1,9},{5... | collective-permute-start | bytes 417800 | tf_op jit(solution)/shard_map/ppermute | solution.py:183
  5.3 12.2 %collective-permute-start.5 = (bf16[32,2176]{1,0:T(8,128)(2,1)S(1)}, bf16[32,2176]{1,0:T(8,128)(2,1)S(1)}, u32[]{:S(2)}, u32[]{:S(2)}) collective-permute-start(bf16[32,2176]{1,0:T(8,128)(2,1)S(1)} %get-tuple-element.51), channel_id=1, source_target_pairs={{0,16},{4,20},{8,24},{12,28},{16,0},{20,4},{24,8},{28,12},{1,17},{... | collective-permute-start | bytes 417800 | tf_op jit(solution)/shard_map/ppermute | solution.py:183
  7.9 14.4 %copy-start.12 = (s32[128,2]{0,1:T(2,128)S(1)}, s32[128,2]{0,1:T(2,128)}, u32[]{:S(2)}) copy-start(s32[128,2]{0,1:T(2,128)} %param.14) | copy-start | bytes 3076
  7.9 14.4 %copy-start.13 = (f32[128,2]{0,1:T(2,128)S(1)}, f32[128,2]{0,1:T(2,128)}, u32[]{:S(2)}) copy-start(f32[128,2]{0,1:T(2,128)} %param.15) | copy-start | bytes 3076
  7.9 12.0 %collective-permute-start.6 = (bf16[32,2176]{1,0:T(8,128)(2,1)S(1)}, bf16[32,2176]{1,0:T(8,128)(2,1)S(1)}, u32[]{:S(2)}, u32[]{:S(2)}) collective-permute-start(bf16[32,2176]{1,0:T(8,128)(2,1)S(1)} %get-tuple-element.52), channel_id=1, source_target_pairs={{0,24},{4,28},{8,16},{12,20},{16,8},{20,12},{24,0},{28,4},{1,25},{... | collective-permute-start | bytes 417800 | tf_op jit(solution)/shard_map/ppermute | solution.py:183
  19.9 2.3 %collective-permute-start.7 = (bf16[64,2176]{1,0:T(8,128)(2,1)S(1)}, bf16[64,2176]{1,0:T(8,128)(2,1)S(1)}, u32[]{:S(2)}, u32[]{:S(2)}) collective-permute-start(bf16[64,2176]{1,0:T(8,128)(2,1)S(1)} %get-tuple-element.54), channel_id=1, source_target_pairs={{0,4},{4,0},{8,12},{12,8},{16,20},{20,16},{24,28},{28,24},{1,5},{5... | collective-permute-start | bytes 835592 | tf_op jit(solution)/shard_map/ppermute | solution.py:661
  20.0 9.2 %collective-permute-start.2 = (bf16[64,2048]{1,0:T(8,128)(2,1)S(1)}, bf16[64,2048]{1,0:T(8,128)(2,1)S(1)}, u32[]{:S(2)}, u32[]{:S(2)}) collective-permute-start(bf16[64,2048]{1,0:T(8,128)(2,1)S(1)} %slice.24), channel_id=1, source_target_pairs={{0,2},{1,3},{2,0},{3,1},{4,6},{5,7},{6,4},{7,5},{8,10},{9,11},{10,... | collective-permute-start | bytes 786440 | tf_op jit(solution)/shard_map/ppermute | solution.py:208
  21.6 9.2 %collective-permute-start.3 = (bf16[64,2048]{1,0:T(8,128)(2,1)S(1)}, bf16[64,2048]{1,0:T(8,128)(2,1)S(1)}, u32[]{:S(2)}, u32[]{:S(2)}) collective-permute-start(bf16[64,2048]{1,0:T(8,128)(2,1)S(1)} %slice.25), channel_id=1, source_target_pairs={{0,1},{1,0},{2,3},{3,2},{4,5},{5,4},{6,7},{7,6},{8,9},{9,8},{10,11... | collective-permute-start | bytes 786440 | tf_op jit(solution)/shard_map/ppermute | solution.py:208
  22.2 20.5 %copy-start.6 = (bf16[1,2048,768]{2,1,0:T(8,128)(2,1)S(1)}, bf16[1,2048,768]{2,1,0:T(8,128)(2,1)}, u32[]{:S(2)}) copy-start(bf16[1,2048,768]{2,1,0:T(8,128)(2,1)} %param.18) | copy-start | bytes 9437188
  22.5 14.3 %collective-permute-start.8 = (bf16[64,2176]{1,0:T(8,128)(2,1)S(1)}, bf16[64,2176]{1,0:T(8,128)(2,1)S(1)}, u32[]{:S(2)}, u32[]{:S(2)}) collective-permute-start(bf16[64,2176]{1,0:T(8,128)(2,1)S(1)} %get-tuple-element.55.refs_0_), channel_id=1, source_target_pairs={{0,1},{1,0},{2,3},{3,2},{4,5},{5,4},{6,7},{7,6},{8,9},{9,8},{10,11... | collective-permute-start | bytes 835592 | tf_op jit(solution)/shard_map/ppermute | solution.py:208
  24.1 12.7 %collective-permute-start.11 = (bf16[64,2176]{1,0:T(8,128)(2,1)S(1)}, bf16[64,2176]{1,0:T(8,128)(2,1)S(1)}, u32[]{:S(2)}, u32[]{:S(2)}) collective-permute-start(bf16[64,2176]{1,0:T(8,128)(2,1)S(1)} %get-tuple-element.56.refs_1_), channel_id=1, source_target_pairs={{0,2},{1,3},{2,0},{3,1},{4,6},{5,7},{6,4},{7,5},{8,10},{9,11},{10,... | collective-permute-start | bytes 835592 | tf_op jit(solution)/shard_map/ppermute | solution.py:208
  24.6 18.2 %collective-permute-start.9 = (bf16[64,2176]{1,0:T(8,128)(2,1)S(1)}, bf16[64,2176]{1,0:T(8,128)(2,1)S(1)}, u32[]{:S(2)}, u32[]{:S(2)}) collective-permute-start(bf16[64,2176]{1,0:T(8,128)(2,1)S(1)} %get-tuple-element.56.refs_1_), channel_id=1, source_target_pairs={{0,1},{1,0},{2,3},{3,2},{4,5},{5,4},{6,7},{7,6},{8,9},{9,8},{10,11... | collective-permute-start | bytes 835592 | tf_op jit(solution)/shard_map/ppermute | solution.py:208
  29.2 13.6 %collective-permute-start.10 = (bf16[64,2176]{1,0:T(8,128)(2,1)S(1)}, bf16[64,2176]{1,0:T(8,128)(2,1)S(1)}, u32[]{:S(2)}, u32[]{:S(2)}) collective-permute-start(bf16[64,2176]{1,0:T(8,128)(2,1)S(1)} %get-tuple-element.55.refs_0_), channel_id=1, source_target_pairs={{0,2},{1,3},{2,0},{3,1},{4,6},{5,7},{6,4},{7,5},{8,10},{9,11},{10,... | collective-permute-start | bytes 835592 | tf_op jit(solution)/shard_map/ppermute | solution.py:208
  31.9 10.9 %copy-start.5 = (bf16[1,2048,768]{2,1,0:T(8,128)(2,1)S(1)}, bf16[1,2048,768]{2,1,0:T(8,128)(2,1)}, u32[]{:S(2)}) copy-start(bf16[1,2048,768]{2,1,0:T(8,128)(2,1)} %param.17) | copy-start | bytes 9437188
  36.8 11.1 %collective-permute-start.12 = (bf16[64,2176]{1,0:T(8,128)(2,1)S(1)}, bf16[64,2176]{1,0:T(8,128)(2,1)S(1)}, u32[]{:S(2)}, u32[]{:S(2)}) collective-permute-start(bf16[64,2176]{1,0:T(8,128)(2,1)S(1)} %collective-permute-done.8.refs_2_), channel_id=1, source_target_pairs={{0,2},{1,3},{2,0},{3,1},{4,6},{5,7},{6,4},{7,5},{8,10},{9,11},{10,... | collective-permute-start | bytes 835592 | tf_op jit(solution)/shard_map/ppermute | solution.py:208
  37.3 10.7 %collective-permute-start.13 = (bf16[64,2176]{1,0:T(8,128)(2,1)S(1)}, bf16[64,2176]{1,0:T(8,128)(2,1)S(1)}, u32[]{:S(2)}, u32[]{:S(2)}) collective-permute-start(bf16[64,2176]{1,0:T(8,128)(2,1)S(1)} %collective-permute-done.11.refs_5_), channel_id=1, source_target_pairs={{0,1},{1,0},{2,3},{3,2},{4,5},{5,4},{6,7},{7,6},{8,9},{9,8},{10,11... | collective-permute-start | bytes 835592 | tf_op jit(solution)/shard_map/ppermute | solution.py:208
  53.1 4.1 %collective-permute-start.14 = (bf16[2,256,768]{2,1,0:T(8,128)(2,1)}, bf16[2,256,768]{2,1,0:T(8,128)(2,1)S(1)}, u32[]{:S(2)}, u32[]{:S(2)}) collective-permute-start(bf16[2,256,768]{2,1,0:T(8,128)(2,1)} %get-tuple-element.71), channel_id=1, source_target_pairs={{0,4},{4,0},{8,12},{12,8},{16,20},{20,16},{24,28},{28,24},{1,5},{5... | collective-permute-start | bytes 2359304 | tf_op jit(solution)/shard_map/ppermute | solution.py:661
  56.6 4.6 %collective-permute-start.15 = (bf16[4,96,2048]{2,1,0:T(8,128)(2,1)}, bf16[4,96,2048]{2,1,0:T(8,128)(2,1)S(1)}, u32[]{:S(2)}, u32[]{:S(2)}) collective-permute-start(bf16[4,96,2048]{2,1,0:T(8,128)(2,1)} %get-tuple-element.76), channel_id=1, source_target_pairs={{0,4},{4,0},{8,12},{12,8},{16,20},{20,16},{24,28},{28,24},{1,5},{5... | collective-permute-start | bytes 4718600 | tf_op jit(solution)/shard_map/ppermute | solution.py:661
  61.2 9.0 %collective-permute-start.20 = (bf16[3,2,256,768]{3,2,1,0:T(8,128)(2,1)}, bf16[3,2,256,768]{3,2,1,0:T(8,128)(2,1)S(1)}, u32[]{:S(2)}, u32[]{:S(2)}) collective-permute-start(bf16[3,2,256,768]{3,2,1,0:T(8,128)(2,1)} %get-tuple-element.84), channel_id=1, source_target_pairs={{0,4},{4,0},{8,12},{12,8},{16,20},{20,16},{24,28},{28,24},{1,5},{5... | collective-permute-start | bytes 7077896 | tf_op jit(solution)/shard_map/ppermute | solution.py:661
  61.6 30.7 %collective-permute-start.21 = (bf16[3,1536,128]{2,1,0:T(8,128)(2,1)S(1)}, bf16[3,1536,128]{2,1,0:T(8,128)(2,1)S(1)}, u32[]{:S(2)}, u32[]{:S(2)}) collective-permute-start(bf16[3,1536,128]{2,1,0:T(8,128)(2,1)S(1)} %fold.4._.own), channel_id=1, source_target_pairs={{0,8},{4,12},{24,16},{28,20},{1,9},{5,13},{25,17},{29,21},{2,10},{... | collective-permute-start | bytes 3538952 | tf_op jit(solution)/shard_map/ppermute | solution.py:643
  62.9 7.3 %copy-start.1 = (bf16[3,2,256,768]{3,2,1,0:T(8,128)(2,1)S(1)}, bf16[3,2,256,768]{3,2,1,0:T(8,128)(2,1)}, u32[]{:S(2)}) copy-start(bf16[3,2,256,768]{3,2,1,0:T(8,128)(2,1)} %get-tuple-element.83.gu_mine) | copy-start | bytes 7077892
  69.1 28.4 %collective-permute-start.16 = (bf16[2,128,2048]{2,1,0:T(8,128)(2,1)S(1)}, bf16[2,128,2048]{2,1,0:T(8,128)(2,1)S(1)}, u32[]{:S(2)}, u32[]{:S(2)}) collective-permute-start(bf16[2,128,2048]{2,1,0:T(8,128)(2,1)S(1)} %get-tuple-element.78), channel_id=1, source_target_pairs={{0,1},{1,0},{2,3},{3,2},{4,5},{5,4},{6,7},{7,6},{8,9},{9,8},{10,11... | collective-permute-start | bytes 3145736 | tf_op jit(solution)/shard_map/ppermute | solution.py:208
  69.7 29.4 %collective-permute-start.18 = (bf16[2,128,2048]{2,1,0:T(8,128)(2,1)S(1)}, bf16[2,128,2048]{2,1,0:T(8,128)(2,1)S(1)}, u32[]{:S(2)}, u32[]{:S(2)}) collective-permute-start(bf16[2,128,2048]{2,1,0:T(8,128)(2,1)S(1)} %get-tuple-element.81), channel_id=1, source_target_pairs={{0,2},{1,3},{2,0},{3,1},{4,6},{5,7},{6,4},{7,5},{8,10},{9,11},{10,... | collective-permute-start | bytes 3145736 | tf_op jit(solution)/shard_map/ppermute | solution.py:208
  72.1 45.2 %collective-permute-start.23 = (bf16[3,1536,128]{2,1,0:T(8,128)(2,1)}, bf16[3,1536,128]{2,1,0:T(8,128)(2,1)}, u32[]{:S(2)}, u32[]{:S(2)}) collective-permute-start(bf16[3,1536,128]{2,1,0:T(8,128)(2,1)} %fold.7.refs_0_.own), channel_id=1, source_target_pairs={{0,8},{4,12},{24,16},{28,20},{1,9},{5,13},{25,17},{29,21},{2,10},{... | collective-permute-start | bytes 3538952 | tf_op jit(solution)/shard_map/ppermute | solution.py:643
  94.0 27.5 %collective-permute-start.22 = (bf16[3,1536,128]{2,1,0:T(8,128)(2,1)}, bf16[3,1536,128]{2,1,0:T(8,128)(2,1)}, u32[]{:S(2)}, u32[]{:S(2)}) collective-permute-start(bf16[3,1536,128]{2,1,0:T(8,128)(2,1)} %pass_on.2), channel_id=1, source_target_pairs={{8,24},{12,28},{16,0},{20,4},{9,25},{13,29},{17,1},{21,5},{10,26},... | collective-permute-start | bytes 3538952 | tf_op jit(solution)/shard_map/ppermute | solution.py:643
  98.6 25.6 %collective-permute-start.17 = (bf16[128,2048]{1,0:T(8,128)(2,1)}, bf16[128,2048]{1,0:T(8,128)(2,1)}, u32[]{:S(2)}, u32[]{:S(2)}) collective-permute-start(bf16[128,2048]{1,0:T(8,128)(2,1)} %fusion.2), channel_id=1, source_target_pairs={{0,2},{1,3},{2,0},{3,1},{4,6},{5,7},{6,4},{7,5},{8,10},{9,11},{10,... | collective-permute-start | bytes 1572872 | tf_op jit(solution)/shard_map/ppermute | solution.py:208
  100.2 26.1 %collective-permute-start.19 = (bf16[128,2048]{1,0:T(8,128)(2,1)}, bf16[128,2048]{1,0:T(8,128)(2,1)}, u32[]{:S(2)}, u32[]{:S(2)}) collective-permute-start(bf16[128,2048]{1,0:T(8,128)(2,1)} %fusion.3), channel_id=1, source_target_pairs={{0,1},{1,0},{2,3},{3,2},{4,5},{5,4},{6,7},{7,6},{8,9},{9,8},{10,11... | collective-permute-start | bytes 1572872 | tf_op jit(solution)/shard_map/ppermute | solution.py:208
  117.6 29.1 %collective-permute-start.24 = (bf16[3,1536,128]{2,1,0:T(8,128)(2,1)S(1)}, bf16[3,1536,128]{2,1,0:T(8,128)(2,1)S(1)}, u32[]{:S(2)}, u32[]{:S(2)}) collective-permute-start(bf16[3,1536,128]{2,1,0:T(8,128)(2,1)S(1)} %choose.1), channel_id=1, source_target_pairs={{0,8},{4,12},{8,0},{12,4},{16,24},{20,28},{24,16},{28,20},{1,9},{5... | collective-permute-start | bytes 3538952 | tf_op jit(solution)/shard_map/ppermute | solution.py:643
  121.5 28.4 %collective-permute-start.25 = (bf16[3,1536,128]{2,1,0:T(8,128)(2,1)S(1)}, bf16[3,1536,128]{2,1,0:T(8,128)(2,1)S(1)}, u32[]{:S(2)}, u32[]{:S(2)}) collective-permute-start(bf16[3,1536,128]{2,1,0:T(8,128)(2,1)S(1)} %pass_on.3), channel_id=1, source_target_pairs={{8,16},{12,20},{16,8},{20,12},{9,17},{13,21},{17,9},{21,13},{10,18... | collective-permute-start | bytes 3538952 | tf_op jit(solution)/shard_map/ppermute | solution.py:643
  (14 other events, 50.6 us)

commit v7 on v6

--- a/solution.py
+++ b/solution.py
@@ -568,18 +568,18 @@
 
 
 def pass_on(own, got, piece, pieces, whole, after, weight=1):
-    per = whole // pieces
+    per, count = whole // pieces, got.shape[0]
 
     def part(array):
         at = piece if array.shape[1] > per else 0
-        return pl.BlockSpec((1, per, LANES), lambda j: (j, at, 0))
+        return pl.BlockSpec((count, per, LANES), lambda j: (0, at, 0))
 
     return pl.pallas_call(
         pass_on_kernel,
-        grid=(got.shape[0],),
+        grid=(1,),
         in_specs=[part(own), part(got)] + [hbm()] * len(after),
-        out_specs=pl.BlockSpec((1, per, LANES), lambda j: (j, 0, 0)),
-        out_shape=jax.ShapeDtypeStruct((got.shape[0], per, LANES), BF16),
+        out_specs=pl.BlockSpec((count, per, LANES), lambda j: (0, 0, 0)),
+        out_shape=jax.ShapeDtypeStruct((count, per, LANES), BF16),
         compiler_params=params(16),
         cost_estimate=cost(2 * weight * got.size, 6 * weight * got.size),
         name="pass_on",
@@ -609,28 +609,25 @@
 
 def unfold_kernel(counts, *refs):
     parts, outs = refs[: sum(counts)], refs[sum(counts) :]
-    total, at = None, 0
-    for count in counts:
-        pieces = [part[0].astype(F32) for part in parts[at : at + count]]
-        value = pieces[0] if count == 1 else jnp.concatenate(pieces, axis=0)
-        total = value if total is None else total + value
-        at += count
-    total = total.astype(BF16)
     for j, out in enumerate(outs):
-
-        @pl.when(pl.program_id(0) == j)
-        def _(out=out):
-            rows, columns = out.shape[1:]
-            for i in range(columns // LANES):
-                out[0, :, i * LANES : (i + 1) * LANES] = total[i * rows : (i + 1) * rows]
+        total, at = None, 0
+        for count in counts:
+            pieces = [part[j].astype(F32) for part in parts[at : at + count]]
+            value = pieces[0] if count == 1 else jnp.concatenate(pieces, axis=0)
+            total = value if total is None else total + value
+            at += count
+        total = total.astype(BF16)
+        rows, columns = out.shape[1:]
+        for i in range(columns // LANES):
+            out[0, :, i * LANES : (i + 1) * LANES] = total[i * rows : (i + 1) * rows]
 
 
 def unfold(groups, shapes):
     parts = [part for group in groups for part in group]
     return pl.pallas_call(
         functools.partial(unfold_kernel, [len(group) for group in groups]),
-        grid=(3,),
-        in_specs=[pl.BlockSpec((1,) + part.shape[1:], lambda j: (j, 0, 0)) for part in parts],
+        grid=(1,),
+        in_specs=[pl.BlockSpec(part.shape, lambda j: (0, 0, 0)) for part in parts],
         out_specs=[pl.BlockSpec(shape, lambda j: (0, 0, 0)) for shape in shapes],
         out_shape=[jax.ShapeDtypeStruct(shape, BF16) for shape in shapes],
         compiler_params=params(24),

time: 153 us -> 152 us (level)
  no operation moved by 1% of the time
where the time goes in v7:
time: 152 us; the launch traced here: 151 us
  waiting for transfers between devices  75.5 us (50%)
  Pallas kernels  37 us (24%)
  starting transfers between devices  24.7 us (16%)
  other arithmetic  7.97 us (5%)
  local copies, waits for them, and re-layouts  4.55 us (3%)
    ppermute x5, waiting for transfers between devices, chips_permute(): lax.ppermute(value, 'dp', [(CORES * a + c, CORES * b + c) for a, b in pai...  52.9 us
    ppermute x14, starting transfers between devices, swap(): return lax.ppermute(value, 'expert', [(d, d ^ i) for d in range(n_ex)])  11.8 us
    ppermute x3, waiting for transfers between devices, send_sequences(): lax.ppermute(pieces[i], 'dp', [(d, d ^ CORES * i) for d in range(n_dp)])  11.5 us
    ppermute x14, waiting for transfers between devices, swap(): return lax.ppermute(value, 'expert', [(d, d ^ i) for d in range(n_ex)])  11.1 us
    ppermute x5, starting transfers between devices, chips_permute(): lax.ppermute(value, 'dp', [(CORES * a + c, CORES * b + c) for a, b in pai...  8.74 us
    convert_element_type x5, other arithmetic, add(): return sum((part.astype(F32) for part in parts)).astype(BF16)  7.97 us
    pallas_call x2, Pallas kernels, hidden_units(): pl.pallas_call(functools.partial(units_kernel, len(pieces), slot, not bef...  7.63 us
    pallas_call x1, Pallas kernels, outputs(): pl.pallas_call(functools.partial(outputs_kernel, layer_groups, grad_group...  6.14 us
  transfers between devices with their start and end apart: 26, of which 13 were waited for; matrix products, arithmetic and copies ran while one was open for 5% of the time, Pallas kernels for 19%

profile of v7, /device:TPU:12, one launch (start us, length us, event | category | flops | bytes accessed | tf_op | source)
XLA Modules:
  0.0 150.7 jit_solution(11172300025967382988)
XLA Ops:
  0.6 2.1 %pick.1 = (bf16[32,2176]{1,0:T(8,128)(2,1)S(1)}, bf16[32,2176]{1,0:T(8,128)(2,1)S(1)}, bf16[32,2176]{1,0:T(8,128)(2,1)S(1)}, bf16[32,2176]{1,0:T(8,128)(2,1)S(1)}) custom-call(s32[1,1,8]{2,1,0:T(1,128)} %dest_hbm.1, s32[1,1,8]{2,1,0:T(1,128)} %len_hbm.1, bf16[1,1,8]{2,1,0:T(2,128)(2,1)} %adv_hbm.1, bf16[8,16,2048]{2,1,0:T(8,128)(2,1)} %bitcast.33), custom_call_target="tpu_custom_call" | custom-call | tf_op jit(solution)/shard_map/pick/pallas_call | solution.py:94
  2.8 1.6 %collective-permute-start = (bf16[128,2048]{1,0:T(8,128)(2,1)}, bf16[128,2048]{1,0:T(8,128)(2,1)S(1)}, u32[]{:S(2)}, u32[]{:S(2)}) collective-permute-start(bf16[128,2048]{1,0:T(8,128)(2,1)} %refs_0_), channel_id=1, source_target_pairs={{0,1},{1,0},{2,3},{3,2},{4,5},{5,4},{6,7},{7,6},{8,9},{9,8},{10,11... | collective-permute-start | bytes 1572872 | tf_op jit(solution)/shard_map/ppermute | solution.py:208
  5.3 2.6 %collective-permute-start.5 = (bf16[32,2176]{1,0:T(8,128)(2,1)S(1)}, bf16[32,2176]{1,0:T(8,128)(2,1)S(1)}, u32[]{:S(2)}, u32[]{:S(2)}) collective-permute-start(bf16[32,2176]{1,0:T(8,128)(2,1)S(1)} %get-tuple-element.51), channel_id=1, source_target_pairs={{0,16},{4,20},{8,24},{12,28},{16,0},{20,4},{24,8},{28,12},{1,17},{... | collective-permute-start | bytes 417800 | tf_op jit(solution)/shard_map/ppermute | solution.py:183
  8.3 2.5 %collective-permute-done.4.refs_1_ = bf16[32,2176]{1,0:T(8,128)(2,1)S(1)} collective-permute-done((bf16[32,2176]{1,0:T(8,128)(2,1)S(1)}, bf16[32,2176]{1,0:T(8,128)(2,1)S(1)}, u32[]{:S(2)}, u32[]{:S(2)}) %collective-permute-start.4) | collective-permute-done | bytes 139296 | tf_op jit(solution)/shard_map/ppermute | solution.py:183
  10.8 6.6 %collective-permute-done.5.refs_2_ = bf16[32,2176]{1,0:T(8,128)(2,1)S(1)} collective-permute-done((bf16[32,2176]{1,0:T(8,128)(2,1)S(1)}, bf16[32,2176]{1,0:T(8,128)(2,1)S(1)}, u32[]{:S(2)}, u32[]{:S(2)}) %collective-permute-start.5) | collective-permute-done | bytes 139296 | tf_op jit(solution)/shard_map/ppermute | solution.py:183
  17.5 2.4 %collective-permute-done.6.refs_3_ = bf16[32,2176]{1,0:T(8,128)(2,1)S(1)} collective-permute-done((bf16[32,2176]{1,0:T(8,128)(2,1)S(1)}, bf16[32,2176]{1,0:T(8,128)(2,1)S(1)}, u32[]{:S(2)}, u32[]{:S(2)}) %collective-permute-start.6) | collective-permute-done | bytes 139296 | tf_op jit(solution)/shard_map/ppermute | solution.py:183
  20.0 1.6 %collective-permute-start.2 = (bf16[64,2048]{1,0:T(8,128)(2,1)S(1)}, bf16[64,2048]{1,0:T(8,128)(2,1)S(1)}, u32[]{:S(2)}, u32[]{:S(2)}) collective-permute-start(bf16[64,2048]{1,0:T(8,128)(2,1)S(1)} %slice.24), channel_id=1, source_target_pairs={{0,2},{1,3},{2,0},{3,1},{4,6},{5,7},{6,4},{7,5},{8,10},{9,11},{10,... | collective-permute-start | bytes 786440 | tf_op jit(solution)/shard_map/ppermute | solution.py:208
  22.5 1.6 %collective-permute-start.8 = (bf16[64,2176]{1,0:T(8,128)(2,1)S(1)}, bf16[64,2176]{1,0:T(8,128)(2,1)S(1)}, u32[]{:S(2)}, u32[]{:S(2)}) collective-permute-start(bf16[64,2176]{1,0:T(8,128)(2,1)S(1)} %get-tuple-element.55.refs_0_), channel_id=1, source_target_pairs={{0,1},{1,0},{2,3},{3,2},{4,5},{5,4},{6,7},{7,6},{8,9},{9,8},{10,11... | collective-permute-start | bytes 835592 | tf_op jit(solution)/shard_map/ppermute | solution.py:208
  25.4 3.7 %collective-permute-done.2.refs_3_ = bf16[64,2048]{1,0:T(8,128)(2,1)S(1)} collective-permute-done((bf16[64,2048]{1,0:T(8,128)(2,1)S(1)}, bf16[64,2048]{1,0:T(8,128)(2,1)S(1)}, u32[]{:S(2)}, u32[]{:S(2)}) %collective-permute-start.2) | collective-permute-done | bytes 262176 | tf_op jit(solution)/shard_map/ppermute | solution.py:208
  29.2 1.5 %collective-permute-start.10 = (bf16[64,2176]{1,0:T(8,128)(2,1)S(1)}, bf16[64,2176]{1,0:T(8,128)(2,1)S(1)}, u32[]{:S(2)}, u32[]{:S(2)}) collective-permute-start(bf16[64,2176]{1,0:T(8,128)(2,1)S(1)} %get-tuple-element.55.refs_0_), channel_id=1, source_target_pairs={{0,2},{1,3},{2,0},{3,1},{4,6},{5,7},{6,4},{7,5},{8,10},{9,11},{10,... | collective-permute-start | bytes 835592 | tf_op jit(solution)/shard_map/ppermute | solution.py:208
  31.9 2.7 %hidden_grad.1 = (f32[512,768]{1,0:T(8,128)S(1)}, bf16[512,2048]{1,0:T(8,128)(2,1)S(1)}) custom-call(bf16[768,2048]{1,0:T(8,128)(2,1)S(1)} %bitcast.31, bf16[128,2048]{1,0:T(8,128)(2,1)S(1)} %copy-done.15, bf16[128,2048]{1,0:T(8,128)(2,1)S(1)} %collective-permute-done.refs_1_.refs_4_, bf16[128,2048]{1,0:T(8,128)(2,1)S(1)} %collective-permute-done.1.refs_2_.refs_5_, ...), custom_call_target="tpu_custom_call" | custom-call | flops 1610612736 | bytes 7340032 | tf_op jit(solution)/shard_map/hidden_grad/pallas_call | solution.py:276
  34.6 2.2 %collective-permute-done.8.refs_2_ = bf16[64,2176]{1,0:T(8,128)(2,1)S(1)} collective-permute-done((bf16[64,2176]{1,0:T(8,128)(2,1)S(1)}, bf16[64,2176]{1,0:T(8,128)(2,1)S(1)}, u32[]{:S(2)}, u32[]{:S(2)}) %collective-permute-start.8) | collective-permute-done | bytes 278560 | tf_op jit(solution)/shard_map/ppermute | solution.py:208
  37.9 4.9 %collective-permute-done.9.refs_3_ = bf16[64,2176]{1,0:T(8,128)(2,1)S(1)} collective-permute-done((bf16[64,2176]{1,0:T(8,128)(2,1)S(1)}, bf16[64,2176]{1,0:T(8,128)(2,1)S(1)}, u32[]{:S(2)}, u32[]{:S(2)}) %collective-permute-start.9) | collective-permute-done | bytes 278560 | tf_op jit(solution)/shard_map/ppermute | solution.py:208
  42.8 5.1 %hidden_units.2 = (bf16[512,768]{1,0:T(8,128)(2,1)S(1)}, bf16[512,768]{1,0:T(8,128)(2,1)S(1)}, bf16[512,768]{1,0:T(8,128)(2,1)S(1)}, bf16[768,512]{1,0:T(8,128)(...) custom-call(bf16[2048,768]{1,0:T(8,128)(2,1)S(1)} %bitcast.21, bf16[2048,768]{1,0:T(8,128)(2,1)S(1)} %bitcast.24, ...), custom_call_target="tpu_custom_call" | custom-call | flops 2415919104 | bytes 9437184 | tf_op jit(solution)/shard_map/hidden_units/pallas_call | solution.py:355
  48.0 2.5 %hidden_units.3 = (bf16[512,768]{1,0:T(8,128)(2,1)S(1)}, bf16[512,768]{1,0:T(8,128)(2,1)S(1)}, bf16[512,768]{1,0:T(8,128)(2,1)S(1)}, bf16[768,512]{1,0:T(8,128)(...) custom-call(bf16[2048,768]{1,0:T(8,128)(2,1)S(1)} %bitcast.22, ...), custom_call_target="tpu_custom_call", output_to_operand_aliasing={{0}: (3, {}), {1}: (4, {}), {2}: (5, {}), {3}: (6, {}), {4}... | custom-call | flops 805306368 | bytes 7340032 | tf_op jit(solution)/shard_map/hidden_units/pallas_call | solution.py:355
  50.5 2.6 %far_grads.1 = (bf16[2,256,768]{2,1,0:T(8,128)(2,1)}, bf16[2,256,768]{2,1,0:T(8,128)(2,1)}) custom-call(bf16[2048,512]{1,0:T(8,128)(2,1)S(1)} %get-tuple-element.69.x_ref, bf16[512,768]{1,0:T(8,128)(2,1)S(1)} %get-tuple-element.67.gate_ref, bf16[512,768]{1,0:T(8,128)(2,1)S(1)} %get-tuple-element.68.up_ref), custom_call_target="tpu_custom_call" | custom-call | flops 805306368 | bytes 4718592 | tf_op jit(solution)/shard_map/far_grads/pallas_call | solution.py:404
  53.1 3.5 %row_grad.1 = (bf16[4,96,2048]{2,1,0:T(8,128)(2,1)}, bf16[4,96,2048]{2,1,0:T(8,128)(2,1)}) custom-call(bf16[768,512]{1,0:T(8,128)(2,1)S(1)} %get-tuple-element.73.hid_ref, bf16[512,2048]{1,0:T(8,128)(2,1)S(1)} %get-tuple-element.74.dy_ref), custom_call_target="tpu_custom_call" | custom-call | flops 1610612736 | bytes 5242880 | tf_op jit(solution)/shard_map/row_grad/pallas_call | solution.py:460
  57.2 4.0 %rest_grads.1 = (bf16[3,2,256,768]{3,2,1,0:T(8,128)(2,1)}, bf16[3,2,256,768]{3,2,1,0:T(8,128)(2,1)}) custom-call(bf16[2048,512]{1,0:T(8,128)(2,1)S(1)} %get-tuple-element.69.x_ref, bf16[512,768]{1,0:T(8,128)(2,1)S(1)} %get-tuple-element.67.gate_ref, bf16[512,768]{1,0:T(8,128)(2,1)S(1)} %get-tuple-element.68.up_ref, ...), custom_call_target="tpu_custom_call" | custom-call | flops 3221225472 | bytes 7864320 | tf_op jit(solution)/shard_map/rest_grads/pallas_call | solution.py:433
  62.9 6.1 %outputs.1 = (bf16[1,128,2048]{2,1,0:T(8,128)(2,1)S(1)}, bf16[1,128,2048]{2,1,0:T(8,128)(2,1)S(1)}, bf16[2,128,2048]{2,1,0:T(8,128)(2,1)S(1)}, bf16[1,128,2048]{...) custom-call(bf16[512,768]{1,0:T(8,128)(2,1)S(1)} %get-tuple-element.65.hid_ref, ...), custom_call_target="tpu_custom_call" | custom-call | flops 4831838208 | bytes 13631488 | tf_op jit(solution)/shard_map/outputs/pallas_call | solution.py:494
  70.2 1.9 %fold.7.refs_0_.own = bf16[3,1536,128]{2,1,0:T(8,128)(2,1)} custom-call(bf16[3,2,256,768]{3,2,1,0:T(8,128)(2,1)S(1)} %copy-done.1, bf16[3,2,256,768]{3,2,1,0:T(8,128)(2,1)S(1)} %collective-permute-done.20.gu_got, bf16[4,96,2048]{2,1,0:T(8,128)(2,1)S(1)} %copy-done, bf16[4,96,2048]{2,1,0:T(8,128)(2,1)S(1)} %collective-permute-done.15.row_got), custom_call_target="tpu_custom_call" | custom-call | flops 1179648 | bytes 3538944 | tf_op jit(solution)/shard_map/fold/pallas_call | solution.py:554
  73.4 18.9 %collective-permute-done.21.got = bf16[3,1536,128]{2,1,0:T(8,128)(2,1)S(1)} collective-permute-done((bf16[3,1536,128]{2,1,0:T(8,128)(2,1)S(1)}, bf16[3,1536,128]{2,1,0:T(8,128)(2,1)S(1)}, u32[]{:S(2)}, u32[]{:S(2)}) %collective-permute-start.21) | collective-permute-done | bytes 1179680 | tf_op jit(solution)/shard_map/ppermute | solution.py:640
  93.7 3.5 %collective-permute-start.22 = (bf16[3,1536,128]{2,1,0:T(8,128)(2,1)}, bf16[3,1536,128]{2,1,0:T(8,128)(2,1)}, u32[]{:S(2)}, u32[]{:S(2)}) collective-permute-start(bf16[3,1536,128]{2,1,0:T(8,128)(2,1)} %pass_on.2), channel_id=1, source_target_pairs={{8,24},{12,28},{16,0},{20,4},{9,25},{13,29},{17,1},{21,5},{10,26},... | collective-permute-start | bytes 3538952 | tf_op jit(solution)/shard_map/ppermute | solution.py:640
  100.4 1.7 %copy-done.2 = bf16[3,2,256,768]{3,2,1,0:T(8,128)(2,1)S(1)} copy-done((bf16[3,2,256,768]{3,2,1,0:T(8,128)(2,1)S(1)}, bf16[3,2,256,768]{3,2,1,0:T(8,128)(2,1)}, u32[]{:S(2)}) %copy-start.2) | copy-done | bytes 2359320
  102.0 1.7 %copy-done.4 = bf16[3,2,256,768]{3,2,1,0:T(8,128)(2,1)S(1)} copy-done((bf16[3,2,256,768]{3,2,1,0:T(8,128)(2,1)S(1)}, bf16[3,2,256,768]{3,2,1,0:T(8,128)(2,1)}, u32[]{:S(2)}) %copy-start.4) | copy-done | bytes 2359320
  104.4 12.9 %collective-permute-done.23.refs_0_.got = bf16[3,1536,128]{2,1,0:T(8,128)(2,1)} collective-permute-done((bf16[3,1536,128]{2,1,0:T(8,128)(2,1)}, bf16[3,1536,128]{2,1,0:T(8,128)(2,1)}, u32[]{:S(2)}, u32[]{:S(2)}) %collective-permute-start.23) | collective-permute-done | bytes 1179680 | tf_op jit(solution)/shard_map/ppermute | solution.py:640
  117.7 2.0 %pass_on.3 = bf16[3,1536,128]{2,1,0:T(8,128)(2,1)S(1)} custom-call(bf16[3,1536,128]{2,1,0:T(8,128)(2,1)} %fold.7.refs_0_.own, bf16[3,1536,128]{2,1,0:T(8,128)(2,1)} %collective-permute-done.23.refs_0_.got), custom_call_target="tpu_custom_call" | custom-call | flops 1179648 | bytes 3538944 | tf_op jit(solution)/shard_map/pass_on/pallas_call | solution.py:577
  121.1 2.6 %collective-permute-start.25 = (bf16[3,1536,128]{2,1,0:T(8,128)(2,1)S(1)}, bf16[3,1536,128]{2,1,0:T(8,128)(2,1)S(1)}, u32[]{:S(2)}, u32[]{:S(2)}) collective-permute-start(bf16[3,1536,128]{2,1,0:T(8,128)(2,1)S(1)} %pass_on.3), channel_id=1, source_target_pairs={{8,16},{12,20},{16,8},{20,12},{9,17},{13,21},{17,9},{21,13},{10,18... | collective-permute-start | bytes 3538952 | tf_op jit(solution)/shard_map/ppermute | solution.py:640
  123.7 2.1 %fusion.1 = bf16[128,2048]{1,0:T(8,128)(2,1)} fusion(bf16[128,2048]{1,0:T(8,128)(2,1)} %collective-permute-done.17, bf16[1,128,2048]{2,1,0:T(8,128)(2,1)S(1)} %copy-done.11, bf16[2,128,2048]{2,1,0:T(8,128)(2,1)S(1)} %copy-done.19), kind=kLoop, calls=%fused_computation.4 | loop fusion | flops 1572864 | bytes 2097152 | tf_op jit(solution)/shard_map/convert_element_type | solution.py:507
  125.8 2.1 %fusion = bf16[128,2048]{1,0:T(8,128)(2,1)} fusion(bf16[128,2048]{1,0:T(8,128)(2,1)} %collective-permute-done.19, bf16[1,128,2048]{2,1,0:T(8,128)(2,1)S(1)} %copy-done.9, bf16[2,128,2048]{2,1,0:T(8,128)(2,1)S(1)} %copy-done.17), kind=kLoop, calls=%fused_computation.2 | loop fusion | flops 1572864 | bytes 2097152 | tf_op jit(solution)/shard_map/convert_element_type | solution.py:507
  127.9 1.7 %add_convert_fusion.refs_0_ = bf16[3,1536,128]{2,1,0:T(8,128)(2,1)S(1)} fusion(bf16[3,1536,128]{2,1,0:T(8,128)(2,1)} %collective-permute-done.22, bf16[3,1536,128]{2,1,0:T(8,128)(2,1)S(1)} %fold.5.other, bf16[3,1536,128]{2,1,0:T(8,128)(2,1)S(1)} %fold.6.one, pred[]{:T(512)S(6)} %gt.3), kind=kLoop, calls=%fused_computation | loop fusion | flops 2949120 | bytes 4718593 | tf_op jit(solution)/shard_map/convert_element_type | solution.py:507
  129.6 16.7 %collective-permute-done.24.refs_1_ = bf16[3,1536,128]{2,1,0:T(8,128)(2,1)S(1)} collective-permute-done((bf16[3,1536,128]{2,1,0:T(8,128)(2,1)S(1)}, bf16[3,1536,128]{2,1,0:T(8,128)(2,1)S(1)}, u32[]{:S(2)}, u32[]{:S(2)}) %collective-permute-start.24) | collective-permute-done | bytes 1179680 | tf_op jit(solution)/shard_map/ppermute | solution.py:640
  146.4 2.9 %collective-permute-done.25.refs_2_ = bf16[3,1536,128]{2,1,0:T(8,128)(2,1)S(1)} collective-permute-done((bf16[3,1536,128]{2,1,0:T(8,128)(2,1)S(1)}, bf16[3,1536,128]{2,1,0:T(8,128)(2,1)S(1)}, u32[]{:S(2)}, u32[]{:S(2)}) %collective-permute-start.25) | collective-permute-done | bytes 1179680 | tf_op jit(solution)/shard_map/ppermute | solution.py:640
  (85 shorter events, 19.2 us)
Async XLA Ops:
  0.6 30.2 %copy-start.14 = (bf16[1,768,2048]{2,1,0:T(8,128)(2,1)S(1)}, bf16[1,768,2048]{2,1,0:T(8,128)(2,1)}, u32[]{:S(2)}) copy-start(bf16[1,768,2048]{2,1,0:T(8,128)(2,1)} %param.19) | copy-start | bytes 9437188
  2.8 17.1 %collective-permute-start = (bf16[128,2048]{1,0:T(8,128)(2,1)}, bf16[128,2048]{1,0:T(8,128)(2,1)S(1)}, u32[]{:S(2)}, u32[]{:S(2)}) collective-permute-start(bf16[128,2048]{1,0:T(8,128)(2,1)} %refs_0_), channel_id=1, source_target_pairs={{0,1},{1,0},{2,3},{3,2},{4,5},{5,4},{6,7},{7,6},{8,9},{9,8},{10,11... | collective-permute-start | bytes 1572872 | tf_op jit(solution)/shard_map/ppermute | solution.py:208
  4.3 15.5 %collective-permute-start.1 = (bf16[128,2048]{1,0:T(8,128)(2,1)}, bf16[128,2048]{1,0:T(8,128)(2,1)S(1)}, u32[]{:S(2)}, u32[]{:S(2)}) collective-permute-start(bf16[128,2048]{1,0:T(8,128)(2,1)} %refs_0_), channel_id=1, source_target_pairs={{0,2},{1,3},{2,0},{3,1},{4,6},{5,7},{6,4},{7,5},{8,10},{9,11},{10,... | collective-permute-start | bytes 1572872 | tf_op jit(solution)/shard_map/ppermute | solution.py:208
  4.8 6.0 %collective-permute-start.4 = (bf16[32,2176]{1,0:T(8,128)(2,1)S(1)}, bf16[32,2176]{1,0:T(8,128)(2,1)S(1)}, u32[]{:S(2)}, u32[]{:S(2)}) collective-permute-start(bf16[32,2176]{1,0:T(8,128)(2,1)S(1)} %get-tuple-element.50), channel_id=1, source_target_pairs={{0,8},{4,12},{8,0},{12,4},{16,24},{20,28},{24,16},{28,20},{1,9},{5... | collective-permute-start | bytes 417800 | tf_op jit(solution)/shard_map/ppermute | solution.py:183
  5.3 12.2 %collective-permute-start.5 = (bf16[32,2176]{1,0:T(8,128)(2,1)S(1)}, bf16[32,2176]{1,0:T(8,128)(2,1)S(1)}, u32[]{:S(2)}, u32[]{:S(2)}) collective-permute-start(bf16[32,2176]{1,0:T(8,128)(2,1)S(1)} %get-tuple-element.51), channel_id=1, source_target_pairs={{0,16},{4,20},{8,24},{12,28},{16,0},{20,4},{24,8},{28,12},{1,17},{... | collective-permute-start | bytes 417800 | tf_op jit(solution)/shard_map/ppermute | solution.py:183
  7.9 14.4 %copy-start.12 = (s32[128,2]{0,1:T(2,128)S(1)}, s32[128,2]{0,1:T(2,128)}, u32[]{:S(2)}) copy-start(s32[128,2]{0,1:T(2,128)} %param.14) | copy-start | bytes 3076
  7.9 14.4 %copy-start.13 = (f32[128,2]{0,1:T(2,128)S(1)}, f32[128,2]{0,1:T(2,128)}, u32[]{:S(2)}) copy-start(f32[128,2]{0,1:T(2,128)} %param.15) | copy-start | bytes 3076
  7.9 12.0 %collective-permute-start.6 = (bf16[32,2176]{1,0:T(8,128)(2,1)S(1)}, bf16[32,2176]{1,0:T(8,128)(2,1)S(1)}, u32[]{:S(2)}, u32[]{:S(2)}) collective-permute-start(bf16[32,2176]{1,0:T(8,128)(2,1)S(1)} %get-tuple-element.52), channel_id=1, source_target_pairs={{0,24},{4,28},{8,16},{12,20},{16,8},{20,12},{24,0},{28,4},{1,25},{... | collective-permute-start | bytes 417800 | tf_op jit(solution)/shard_map/ppermute | solution.py:183
  19.9 2.3 %collective-permute-start.7 = (bf16[64,2176]{1,0:T(8,128)(2,1)S(1)}, bf16[64,2176]{1,0:T(8,128)(2,1)S(1)}, u32[]{:S(2)}, u32[]{:S(2)}) collective-permute-start(bf16[64,2176]{1,0:T(8,128)(2,1)S(1)} %get-tuple-element.54), channel_id=1, source_target_pairs={{0,4},{4,0},{8,12},{12,8},{16,20},{20,16},{24,28},{28,24},{1,5},{5... | collective-permute-start | bytes 835592 | tf_op jit(solution)/shard_map/ppermute | solution.py:658
  20.0 9.2 %collective-permute-start.2 = (bf16[64,2048]{1,0:T(8,128)(2,1)S(1)}, bf16[64,2048]{1,0:T(8,128)(2,1)S(1)}, u32[]{:S(2)}, u32[]{:S(2)}) collective-permute-start(bf16[64,2048]{1,0:T(8,128)(2,1)S(1)} %slice.24), channel_id=1, source_target_pairs={{0,2},{1,3},{2,0},{3,1},{4,6},{5,7},{6,4},{7,5},{8,10},{9,11},{10,... | collective-permute-start | bytes 786440 | tf_op jit(solution)/shard_map/ppermute | solution.py:208
  21.6 9.2 %collective-permute-start.3 = (bf16[64,2048]{1,0:T(8,128)(2,1)S(1)}, bf16[64,2048]{1,0:T(8,128)(2,1)S(1)}, u32[]{:S(2)}, u32[]{:S(2)}) collective-permute-start(bf16[64,2048]{1,0:T(8,128)(2,1)S(1)} %slice.25), channel_id=1, source_target_pairs={{0,1},{1,0},{2,3},{3,2},{4,5},{5,4},{6,7},{7,6},{8,9},{9,8},{10,11... | collective-permute-start | bytes 786440 | tf_op jit(solution)/shard_map/ppermute | solution.py:208
  22.2 20.5 %copy-start.6 = (bf16[1,2048,768]{2,1,0:T(8,128)(2,1)S(1)}, bf16[1,2048,768]{2,1,0:T(8,128)(2,1)}, u32[]{:S(2)}) copy-start(bf16[1,2048,768]{2,1,0:T(8,128)(2,1)} %param.18) | copy-start | bytes 9437188
  22.5 14.3 %collective-permute-start.8 = (bf16[64,2176]{1,0:T(8,128)(2,1)S(1)}, bf16[64,2176]{1,0:T(8,128)(2,1)S(1)}, u32[]{:S(2)}, u32[]{:S(2)}) collective-permute-start(bf16[64,2176]{1,0:T(8,128)(2,1)S(1)} %get-tuple-element.55.refs_0_), channel_id=1, source_target_pairs={{0,1},{1,0},{2,3},{3,2},{4,5},{5,4},{6,7},{7,6},{8,9},{9,8},{10,11... | collective-permute-start | bytes 835592 | tf_op jit(solution)/shard_map/ppermute | solution.py:208
  24.1 12.7 %collective-permute-start.11 = (bf16[64,2176]{1,0:T(8,128)(2,1)S(1)}, bf16[64,2176]{1,0:T(8,128)(2,1)S(1)}, u32[]{:S(2)}, u32[]{:S(2)}) collective-permute-start(bf16[64,2176]{1,0:T(8,128)(2,1)S(1)} %get-tuple-element.56.refs_1_), channel_id=1, source_target_pairs={{0,2},{1,3},{2,0},{3,1},{4,6},{5,7},{6,4},{7,5},{8,10},{9,11},{10,... | collective-permute-start | bytes 835592 | tf_op jit(solution)/shard_map/ppermute | solution.py:208
  24.6 18.2 %collective-permute-start.9 = (bf16[64,2176]{1,0:T(8,128)(2,1)S(1)}, bf16[64,2176]{1,0:T(8,128)(2,1)S(1)}, u32[]{:S(2)}, u32[]{:S(2)}) collective-permute-start(bf16[64,2176]{1,0:T(8,128)(2,1)S(1)} %get-tuple-element.56.refs_1_), channel_id=1, source_target_pairs={{0,1},{1,0},{2,3},{3,2},{4,5},{5,4},{6,7},{7,6},{8,9},{9,8},{10,11... | collective-permute-start | bytes 835592 | tf_op jit(solution)/shard_map/ppermute | solution.py:208
  29.2 13.6 %collective-permute-start.10 = (bf16[64,2176]{1,0:T(8,128)(2,1)S(1)}, bf16[64,2176]{1,0:T(8,128)(2,1)S(1)}, u32[]{:S(2)}, u32[]{:S(2)}) collective-permute-start(bf16[64,2176]{1,0:T(8,128)(2,1)S(1)} %get-tuple-element.55.refs_0_), channel_id=1, source_target_pairs={{0,2},{1,3},{2,0},{3,1},{4,6},{5,7},{6,4},{7,5},{8,10},{9,11},{10,... | collective-permute-start | bytes 835592 | tf_op jit(solution)/shard_map/ppermute | solution.py:208
  31.9 10.9 %copy-start.5 = (bf16[1,2048,768]{2,1,0:T(8,128)(2,1)S(1)}, bf16[1,2048,768]{2,1,0:T(8,128)(2,1)}, u32[]{:S(2)}) copy-start(bf16[1,2048,768]{2,1,0:T(8,128)(2,1)} %param.17) | copy-start | bytes 9437188
  36.8 11.1 %collective-permute-start.12 = (bf16[64,2176]{1,0:T(8,128)(2,1)S(1)}, bf16[64,2176]{1,0:T(8,128)(2,1)S(1)}, u32[]{:S(2)}, u32[]{:S(2)}) collective-permute-start(bf16[64,2176]{1,0:T(8,128)(2,1)S(1)} %collective-permute-done.8.refs_2_), channel_id=1, source_target_pairs={{0,2},{1,3},{2,0},{3,1},{4,6},{5,7},{6,4},{7,5},{8,10},{9,11},{10,... | collective-permute-start | bytes 835592 | tf_op jit(solution)/shard_map/ppermute | solution.py:208
  37.3 10.7 %collective-permute-start.13 = (bf16[64,2176]{1,0:T(8,128)(2,1)S(1)}, bf16[64,2176]{1,0:T(8,128)(2,1)S(1)}, u32[]{:S(2)}, u32[]{:S(2)}) collective-permute-start(bf16[64,2176]{1,0:T(8,128)(2,1)S(1)} %collective-permute-done.11.refs_5_), channel_id=1, source_target_pairs={{0,1},{1,0},{2,3},{3,2},{4,5},{5,4},{6,7},{7,6},{8,9},{9,8},{10,11... | collective-permute-start | bytes 835592 | tf_op jit(solution)/shard_map/ppermute | solution.py:208
  53.1 4.1 %collective-permute-start.14 = (bf16[2,256,768]{2,1,0:T(8,128)(2,1)}, bf16[2,256,768]{2,1,0:T(8,128)(2,1)S(1)}, u32[]{:S(2)}, u32[]{:S(2)}) collective-permute-start(bf16[2,256,768]{2,1,0:T(8,128)(2,1)} %get-tuple-element.71), channel_id=1, source_target_pairs={{0,4},{4,0},{8,12},{12,8},{16,20},{20,16},{24,28},{28,24},{1,5},{5... | collective-permute-start | bytes 2359304 | tf_op jit(solution)/shard_map/ppermute | solution.py:658
  56.6 4.6 %collective-permute-start.15 = (bf16[4,96,2048]{2,1,0:T(8,128)(2,1)}, bf16[4,96,2048]{2,1,0:T(8,128)(2,1)S(1)}, u32[]{:S(2)}, u32[]{:S(2)}) collective-permute-start(bf16[4,96,2048]{2,1,0:T(8,128)(2,1)} %get-tuple-element.76), channel_id=1, source_target_pairs={{0,4},{4,0},{8,12},{12,8},{16,20},{20,16},{24,28},{28,24},{1,5},{5... | collective-permute-start | bytes 4718600 | tf_op jit(solution)/shard_map/ppermute | solution.py:658
  61.2 9.0 %collective-permute-start.20 = (bf16[3,2,256,768]{3,2,1,0:T(8,128)(2,1)}, bf16[3,2,256,768]{3,2,1,0:T(8,128)(2,1)S(1)}, u32[]{:S(2)}, u32[]{:S(2)}) collective-permute-start(bf16[3,2,256,768]{3,2,1,0:T(8,128)(2,1)} %get-tuple-element.84), channel_id=1, source_target_pairs={{0,4},{4,0},{8,12},{12,8},{16,20},{20,16},{24,28},{28,24},{1,5},{5... | collective-permute-start | bytes 7077896 | tf_op jit(solution)/shard_map/ppermute | solution.py:658
  61.6 30.7 %collective-permute-start.21 = (bf16[3,1536,128]{2,1,0:T(8,128)(2,1)S(1)}, bf16[3,1536,128]{2,1,0:T(8,128)(2,1)S(1)}, u32[]{:S(2)}, u32[]{:S(2)}) collective-permute-start(bf16[3,1536,128]{2,1,0:T(8,128)(2,1)S(1)} %fold.4._.own), channel_id=1, source_target_pairs={{0,8},{4,12},{24,16},{28,20},{1,9},{5,13},{25,17},{29,21},{2,10},{... | collective-permute-start | bytes 3538952 | tf_op jit(solution)/shard_map/ppermute | solution.py:640
  62.9 7.3 %copy-start.1 = (bf16[3,2,256,768]{3,2,1,0:T(8,128)(2,1)S(1)}, bf16[3,2,256,768]{3,2,1,0:T(8,128)(2,1)}, u32[]{:S(2)}) copy-start(bf16[3,2,256,768]{3,2,1,0:T(8,128)(2,1)} %get-tuple-element.83.gu_mine) | copy-start | bytes 7077892
  69.1 28.1 %collective-permute-start.16 = (bf16[2,128,2048]{2,1,0:T(8,128)(2,1)S(1)}, bf16[2,128,2048]{2,1,0:T(8,128)(2,1)S(1)}, u32[]{:S(2)}, u32[]{:S(2)}) collective-permute-start(bf16[2,128,2048]{2,1,0:T(8,128)(2,1)S(1)} %get-tuple-element.78), channel_id=1, source_target_pairs={{0,1},{1,0},{2,3},{3,2},{4,5},{5,4},{6,7},{7,6},{8,9},{9,8},{10,11... | collective-permute-start | bytes 3145736 | tf_op jit(solution)/shard_map/ppermute | solution.py:208
  69.7 29.0 %collective-permute-start.18 = (bf16[2,128,2048]{2,1,0:T(8,128)(2,1)S(1)}, bf16[2,128,2048]{2,1,0:T(8,128)(2,1)S(1)}, u32[]{:S(2)}, u32[]{:S(2)}) collective-permute-start(bf16[2,128,2048]{2,1,0:T(8,128)(2,1)S(1)} %get-tuple-element.81), channel_id=1, source_target_pairs={{0,2},{1,3},{2,0},{3,1},{4,6},{5,7},{6,4},{7,5},{8,10},{9,11},{10,... | collective-permute-start | bytes 3145736 | tf_op jit(solution)/shard_map/ppermute | solution.py:208
  72.1 45.2 %collective-permute-start.23 = (bf16[3,1536,128]{2,1,0:T(8,128)(2,1)}, bf16[3,1536,128]{2,1,0:T(8,128)(2,1)}, u32[]{:S(2)}, u32[]{:S(2)}) collective-permute-start(bf16[3,1536,128]{2,1,0:T(8,128)(2,1)} %fold.7.refs_0_.own), channel_id=1, source_target_pairs={{0,8},{4,12},{24,16},{28,20},{1,9},{5,13},{25,17},{29,21},{2,10},{... | collective-permute-start | bytes 3538952 | tf_op jit(solution)/shard_map/ppermute | solution.py:640
  93.7 27.5 %collective-permute-start.22 = (bf16[3,1536,128]{2,1,0:T(8,128)(2,1)}, bf16[3,1536,128]{2,1,0:T(8,128)(2,1)}, u32[]{:S(2)}, u32[]{:S(2)}) collective-permute-start(bf16[3,1536,128]{2,1,0:T(8,128)(2,1)} %pass_on.2), channel_id=1, source_target_pairs={{8,24},{12,28},{16,0},{20,4},{9,25},{13,29},{17,1},{21,5},{10,26},... | collective-permute-start | bytes 3538952 | tf_op jit(solution)/shard_map/ppermute | solution.py:640
  98.2 25.5 %collective-permute-start.17 = (bf16[128,2048]{1,0:T(8,128)(2,1)}, bf16[128,2048]{1,0:T(8,128)(2,1)}, u32[]{:S(2)}, u32[]{:S(2)}) collective-permute-start(bf16[128,2048]{1,0:T(8,128)(2,1)} %fusion.2), channel_id=1, source_target_pairs={{0,2},{1,3},{2,0},{3,1},{4,6},{5,7},{6,4},{7,5},{8,10},{9,11},{10,... | collective-permute-start | bytes 1572872 | tf_op jit(solution)/shard_map/ppermute | solution.py:208
  99.8 26.0 %collective-permute-start.19 = (bf16[128,2048]{1,0:T(8,128)(2,1)}, bf16[128,2048]{1,0:T(8,128)(2,1)}, u32[]{:S(2)}, u32[]{:S(2)}) collective-permute-start(bf16[128,2048]{1,0:T(8,128)(2,1)} %fusion.3), channel_id=1, source_target_pairs={{0,1},{1,0},{2,3},{3,2},{4,5},{5,4},{6,7},{7,6},{8,9},{9,8},{10,11... | collective-permute-start | bytes 1572872 | tf_op jit(solution)/shard_map/ppermute | solution.py:208
  117.6 28.8 %collective-permute-start.24 = (bf16[3,1536,128]{2,1,0:T(8,128)(2,1)S(1)}, bf16[3,1536,128]{2,1,0:T(8,128)(2,1)S(1)}, u32[]{:S(2)}, u32[]{:S(2)}) collective-permute-start(bf16[3,1536,128]{2,1,0:T(8,128)(2,1)S(1)} %choose.1), channel_id=1, source_target_pairs={{0,8},{4,12},{8,0},{12,4},{16,24},{20,28},{24,16},{28,20},{1,9},{5... | collective-permute-start | bytes 3538952 | tf_op jit(solution)/shard_map/ppermute | solution.py:640
  121.1 28.2 %collective-permute-start.25 = (bf16[3,1536,128]{2,1,0:T(8,128)(2,1)S(1)}, bf16[3,1536,128]{2,1,0:T(8,128)(2,1)S(1)}, u32[]{:S(2)}, u32[]{:S(2)}) collective-permute-start(bf16[3,1536,128]{2,1,0:T(8,128)(2,1)S(1)} %pass_on.3), channel_id=1, source_target_pairs={{8,16},{12,20},{16,8},{20,12},{9,17},{13,21},{17,9},{21,13},{10,18... | collective-permute-start | bytes 3538952 | tf_op jit(solution)/shard_map/ppermute | solution.py:640
  (14 other events, 49.8 us)

commit v8 on v7

--- a/solution.py
+++ b/solution.py
@@ -455,7 +455,7 @@
     units, rows = turned_hid.shape
     width = dy.shape[1]
     n_z, shard = n_dp // CORES, units // n_dp
-    tile = 512
+    tile = 1024
     block = pl.BlockSpec((n_z, shard, tile), lambda j: (0, 0, j))
     return pl.pallas_call(
         row_grad_kernel,
@@ -463,7 +463,7 @@
         in_specs=[pl.BlockSpec((units, rows), lambda j: (0, 0)), pl.BlockSpec((rows, tile), lambda j: (0, j))],
         out_specs=[block, block],
         out_shape=[pltpu.HBM((n_z, shard, width), BF16)] * 2,
-        compiler_params=params(BIG),
+        compiler_params=params(room(rows, width)),
         cost_estimate=cost(2 * rows * units * width, 2 * units * width + 2 * rows * width),
         name="row_grad",
     )(turned_hid, dy)

time: 152 us -> 151 us (level)
  no operation moved by 1% of the time
where the time goes in v8:
time: 151 us; the launch traced here: 150 us
  waiting for transfers between devices  75.5 us (50%)
  Pallas kernels  36.8 us (24%)
  starting transfers between devices  24.7 us (16%)
  other arithmetic  7.97 us (5%)
  local copies, waits for them, and re-layouts  4.55 us (3%)
    ppermute x5, waiting for transfers between devices, chips_permute(): lax.ppermute(value, 'dp', [(CORES * a + c, CORES * b + c) for a, b in pai...  52.9 us
    ppermute x14, starting transfers between devices, swap(): return lax.ppermute(value, 'expert', [(d, d ^ i) for d in range(n_ex)])  11.9 us
    ppermute x3, waiting for transfers between devices, send_sequences(): lax.ppermute(pieces[i], 'dp', [(d, d ^ CORES * i) for d in range(n_dp)])  11.5 us
    ppermute x14, waiting for transfers between devices, swap(): return lax.ppermute(value, 'expert', [(d, d ^ i) for d in range(n_ex)])  11.1 us
    ppermute x5, starting transfers between devices, chips_permute(): lax.ppermute(value, 'dp', [(CORES * a + c, CORES * b + c) for a, b in pai...  8.75 us
    convert_element_type x5, other arithmetic, add(): return sum((part.astype(F32) for part in parts)).astype(BF16)  7.97 us
    pallas_call x2, Pallas kernels, hidden_units(): pl.pallas_call(functools.partial(units_kernel, len(pieces), slot, not bef...  7.63 us
    pallas_call x1, Pallas kernels, outputs(): pl.pallas_call(functools.partial(outputs_kernel, layer_groups, grad_group...  6.14 us
  transfers between devices with their start and end apart: 26, of which 13 were waited for; matrix products, arithmetic and copies ran while one was open for 5% of the time, Pallas kernels for 19%

profile of v8, /device:TPU:12, one launch (start us, length us, event | category | flops | bytes accessed | tf_op | source)
XLA Modules:
  0.0 150.5 jit_solution(12291020017962521893)
XLA Ops:
  0.6 2.1 %pick.1 = (bf16[32,2176]{1,0:T(8,128)(2,1)S(1)}, bf16[32,2176]{1,0:T(8,128)(2,1)S(1)}, bf16[32,2176]{1,0:T(8,128)(2,1)S(1)}, bf16[32,2176]{1,0:T(8,128)(2,1)S(1)}) custom-call(s32[1,1,8]{2,1,0:T(1,128)} %dest_hbm.1, s32[1,1,8]{2,1,0:T(1,128)} %len_hbm.1, bf16[1,1,8]{2,1,0:T(2,128)(2,1)} %adv_hbm.1, bf16[8,16,2048]{2,1,0:T(8,128)(2,1)} %bitcast.33), custom_call_target="tpu_custom_call" | custom-call | tf_op jit(solution)/shard_map/pick/pallas_call | solution.py:94
  2.8 1.6 %collective-permute-start = (bf16[128,2048]{1,0:T(8,128)(2,1)}, bf16[128,2048]{1,0:T(8,128)(2,1)S(1)}, u32[]{:S(2)}, u32[]{:S(2)}) collective-permute-start(bf16[128,2048]{1,0:T(8,128)(2,1)} %refs_0_), channel_id=1, source_target_pairs={{0,1},{1,0},{2,3},{3,2},{4,5},{5,4},{6,7},{7,6},{8,9},{9,8},{10,11... | collective-permute-start | bytes 1572872 | tf_op jit(solution)/shard_map/ppermute | solution.py:208
  5.3 2.6 %collective-permute-start.5 = (bf16[32,2176]{1,0:T(8,128)(2,1)S(1)}, bf16[32,2176]{1,0:T(8,128)(2,1)S(1)}, u32[]{:S(2)}, u32[]{:S(2)}) collective-permute-start(bf16[32,2176]{1,0:T(8,128)(2,1)S(1)} %get-tuple-element.51), channel_id=1, source_target_pairs={{0,16},{4,20},{8,24},{12,28},{16,0},{20,4},{24,8},{28,12},{1,17},{... | collective-permute-start | bytes 417800 | tf_op jit(solution)/shard_map/ppermute | solution.py:183
  8.3 2.5 %collective-permute-done.4.refs_1_ = bf16[32,2176]{1,0:T(8,128)(2,1)S(1)} collective-permute-done((bf16[32,2176]{1,0:T(8,128)(2,1)S(1)}, bf16[32,2176]{1,0:T(8,128)(2,1)S(1)}, u32[]{:S(2)}, u32[]{:S(2)}) %collective-permute-start.4) | collective-permute-done | bytes 139296 | tf_op jit(solution)/shard_map/ppermute | solution.py:183
  10.8 6.6 %collective-permute-done.5.refs_2_ = bf16[32,2176]{1,0:T(8,128)(2,1)S(1)} collective-permute-done((bf16[32,2176]{1,0:T(8,128)(2,1)S(1)}, bf16[32,2176]{1,0:T(8,128)(2,1)S(1)}, u32[]{:S(2)}, u32[]{:S(2)}) %collective-permute-start.5) | collective-permute-done | bytes 139296 | tf_op jit(solution)/shard_map/ppermute | solution.py:183
  17.5 2.4 %collective-permute-done.6.refs_3_ = bf16[32,2176]{1,0:T(8,128)(2,1)S(1)} collective-permute-done((bf16[32,2176]{1,0:T(8,128)(2,1)S(1)}, bf16[32,2176]{1,0:T(8,128)(2,1)S(1)}, u32[]{:S(2)}, u32[]{:S(2)}) %collective-permute-start.6) | collective-permute-done | bytes 139296 | tf_op jit(solution)/shard_map/ppermute | solution.py:183
  20.0 1.6 %collective-permute-start.2 = (bf16[64,2048]{1,0:T(8,128)(2,1)S(1)}, bf16[64,2048]{1,0:T(8,128)(2,1)S(1)}, u32[]{:S(2)}, u32[]{:S(2)}) collective-permute-start(bf16[64,2048]{1,0:T(8,128)(2,1)S(1)} %slice.24), channel_id=1, source_target_pairs={{0,2},{1,3},{2,0},{3,1},{4,6},{5,7},{6,4},{7,5},{8,10},{9,11},{10,... | collective-permute-start | bytes 786440 | tf_op jit(solution)/shard_map/ppermute | solution.py:208
  22.5 1.6 %collective-permute-start.8 = (bf16[64,2176]{1,0:T(8,128)(2,1)S(1)}, bf16[64,2176]{1,0:T(8,128)(2,1)S(1)}, u32[]{:S(2)}, u32[]{:S(2)}) collective-permute-start(bf16[64,2176]{1,0:T(8,128)(2,1)S(1)} %get-tuple-element.55.refs_0_), channel_id=1, source_target_pairs={{0,1},{1,0},{2,3},{3,2},{4,5},{5,4},{6,7},{7,6},{8,9},{9,8},{10,11... | collective-permute-start | bytes 835592 | tf_op jit(solution)/shard_map/ppermute | solution.py:208
  25.4 3.7 %collective-permute-done.2.refs_3_ = bf16[64,2048]{1,0:T(8,128)(2,1)S(1)} collective-permute-done((bf16[64,2048]{1,0:T(8,128)(2,1)S(1)}, bf16[64,2048]{1,0:T(8,128)(2,1)S(1)}, u32[]{:S(2)}, u32[]{:S(2)}) %collective-permute-start.2) | collective-permute-done | bytes 262176 | tf_op jit(solution)/shard_map/ppermute | solution.py:208
  29.2 1.5 %collective-permute-start.10 = (bf16[64,2176]{1,0:T(8,128)(2,1)S(1)}, bf16[64,2176]{1,0:T(8,128)(2,1)S(1)}, u32[]{:S(2)}, u32[]{:S(2)}) collective-permute-start(bf16[64,2176]{1,0:T(8,128)(2,1)S(1)} %get-tuple-element.55.refs_0_), channel_id=1, source_target_pairs={{0,2},{1,3},{2,0},{3,1},{4,6},{5,7},{6,4},{7,5},{8,10},{9,11},{10,... | collective-permute-start | bytes 835592 | tf_op jit(solution)/shard_map/ppermute | solution.py:208
  31.9 2.7 %hidden_grad.1 = (f32[512,768]{1,0:T(8,128)S(1)}, bf16[512,2048]{1,0:T(8,128)(2,1)S(1)}) custom-call(bf16[768,2048]{1,0:T(8,128)(2,1)S(1)} %bitcast.31, bf16[128,2048]{1,0:T(8,128)(2,1)S(1)} %copy-done.15, bf16[128,2048]{1,0:T(8,128)(2,1)S(1)} %collective-permute-done.refs_1_.refs_4_, bf16[128,2048]{1,0:T(8,128)(2,1)S(1)} %collective-permute-done.1.refs_2_.refs_5_, ...), custom_call_target="tpu_custom_call" | custom-call | flops 1610612736 | bytes 7340032 | tf_op jit(solution)/shard_map/hidden_grad/pallas_call | solution.py:276
  34.6 2.2 %collective-permute-done.8.refs_2_ = bf16[64,2176]{1,0:T(8,128)(2,1)S(1)} collective-permute-done((bf16[64,2176]{1,0:T(8,128)(2,1)S(1)}, bf16[64,2176]{1,0:T(8,128)(2,1)S(1)}, u32[]{:S(2)}, u32[]{:S(2)}) %collective-permute-start.8) | collective-permute-done | bytes 278560 | tf_op jit(solution)/shard_map/ppermute | solution.py:208
  37.9 4.9 %collective-permute-done.9.refs_3_ = bf16[64,2176]{1,0:T(8,128)(2,1)S(1)} collective-permute-done((bf16[64,2176]{1,0:T(8,128)(2,1)S(1)}, bf16[64,2176]{1,0:T(8,128)(2,1)S(1)}, u32[]{:S(2)}, u32[]{:S(2)}) %collective-permute-start.9) | collective-permute-done | bytes 278560 | tf_op jit(solution)/shard_map/ppermute | solution.py:208
  42.8 5.1 %hidden_units.2 = (bf16[512,768]{1,0:T(8,128)(2,1)S(1)}, bf16[512,768]{1,0:T(8,128)(2,1)S(1)}, bf16[512,768]{1,0:T(8,128)(2,1)S(1)}, bf16[768,512]{1,0:T(8,128)(...) custom-call(bf16[2048,768]{1,0:T(8,128)(2,1)S(1)} %bitcast.21, bf16[2048,768]{1,0:T(8,128)(2,1)S(1)} %bitcast.24, ...), custom_call_target="tpu_custom_call" | custom-call | flops 2415919104 | bytes 9437184 | tf_op jit(solution)/shard_map/hidden_units/pallas_call | solution.py:355
  48.0 2.5 %hidden_units.3 = (bf16[512,768]{1,0:T(8,128)(2,1)S(1)}, bf16[512,768]{1,0:T(8,128)(2,1)S(1)}, bf16[512,768]{1,0:T(8,128)(2,1)S(1)}, bf16[768,512]{1,0:T(8,128)(...) custom-call(bf16[2048,768]{1,0:T(8,128)(2,1)S(1)} %bitcast.22, ...), custom_call_target="tpu_custom_call", output_to_operand_aliasing={{0}: (3, {}), {1}: (4, {}), {2}: (5, {}), {3}: (6, {}), {4}... | custom-call | flops 805306368 | bytes 7340032 | tf_op jit(solution)/shard_map/hidden_units/pallas_call | solution.py:355
  50.5 2.6 %far_grads.1 = (bf16[2,256,768]{2,1,0:T(8,128)(2,1)}, bf16[2,256,768]{2,1,0:T(8,128)(2,1)}) custom-call(bf16[2048,512]{1,0:T(8,128)(2,1)S(1)} %get-tuple-element.69.x_ref, bf16[512,768]{1,0:T(8,128)(2,1)S(1)} %get-tuple-element.67.gate_ref, bf16[512,768]{1,0:T(8,128)(2,1)S(1)} %get-tuple-element.68.up_ref), custom_call_target="tpu_custom_call" | custom-call | flops 805306368 | bytes 4718592 | tf_op jit(solution)/shard_map/far_grads/pallas_call | solution.py:404
  53.1 3.3 %row_grad.1 = (bf16[4,96,2048]{2,1,0:T(8,128)(2,1)}, bf16[4,96,2048]{2,1,0:T(8,128)(2,1)}) custom-call(bf16[768,512]{1,0:T(8,128)(2,1)S(1)} %get-tuple-element.73.hid_ref, bf16[512,2048]{1,0:T(8,128)(2,1)S(1)} %get-tuple-element.74.dy_ref), custom_call_target="tpu_custom_call" | custom-call | flops 1610612736 | bytes 5242880 | tf_op jit(solution)/shard_map/row_grad/pallas_call | solution.py:460
  56.9 4.0 %rest_grads.1 = (bf16[3,2,256,768]{3,2,1,0:T(8,128)(2,1)}, bf16[3,2,256,768]{3,2,1,0:T(8,128)(2,1)}) custom-call(bf16[2048,512]{1,0:T(8,128)(2,1)S(1)} %get-tuple-element.69.x_ref, bf16[512,768]{1,0:T(8,128)(2,1)S(1)} %get-tuple-element.67.gate_ref, bf16[512,768]{1,0:T(8,128)(2,1)S(1)} %get-tuple-element.68.up_ref, ...), custom_call_target="tpu_custom_call" | custom-call | flops 3221225472 | bytes 7864320 | tf_op jit(solution)/shard_map/rest_grads/pallas_call | solution.py:433
  62.6 6.1 %outputs.1 = (bf16[1,128,2048]{2,1,0:T(8,128)(2,1)S(1)}, bf16[1,128,2048]{2,1,0:T(8,128)(2,1)S(1)}, bf16[2,128,2048]{2,1,0:T(8,128)(2,1)S(1)}, bf16[1,128,2048]{...) custom-call(bf16[512,768]{1,0:T(8,128)(2,1)S(1)} %get-tuple-element.65.hid_ref, ...), custom_call_target="tpu_custom_call" | custom-call | flops 4831838208 | bytes 13631488 | tf_op jit(solution)/shard_map/outputs/pallas_call | solution.py:494
  69.9 1.9 %fold.7.refs_0_.own = bf16[3,1536,128]{2,1,0:T(8,128)(2,1)} custom-call(bf16[3,2,256,768]{3,2,1,0:T(8,128)(2,1)S(1)} %copy-done.1, bf16[3,2,256,768]{3,2,1,0:T(8,128)(2,1)S(1)} %collective-permute-done.20.gu_got, bf16[4,96,2048]{2,1,0:T(8,128)(2,1)S(1)} %copy-done, bf16[4,96,2048]{2,1,0:T(8,128)(2,1)S(1)} %collective-permute-done.15.row_got), custom_call_target="tpu_custom_call" | custom-call | flops 1179648 | bytes 3538944 | tf_op jit(solution)/shard_map/fold/pallas_call | solution.py:554
  73.1 18.9 %collective-permute-done.21.got = bf16[3,1536,128]{2,1,0:T(8,128)(2,1)S(1)} collective-permute-done((bf16[3,1536,128]{2,1,0:T(8,128)(2,1)S(1)}, bf16[3,1536,128]{2,1,0:T(8,128)(2,1)S(1)}, u32[]{:S(2)}, u32[]{:S(2)}) %collective-permute-start.21) | collective-permute-done | bytes 1179680 | tf_op jit(solution)/shard_map/ppermute | solution.py:640
  93.4 3.5 %collective-permute-start.22 = (bf16[3,1536,128]{2,1,0:T(8,128)(2,1)}, bf16[3,1536,128]{2,1,0:T(8,128)(2,1)}, u32[]{:S(2)}, u32[]{:S(2)}) collective-permute-start(bf16[3,1536,128]{2,1,0:T(8,128)(2,1)} %pass_on.2), channel_id=1, source_target_pairs={{8,24},{12,28},{16,0},{20,4},{9,25},{13,29},{17,1},{21,5},{10,26},... | collective-permute-start | bytes 3538952 | tf_op jit(solution)/shard_map/ppermute | solution.py:640
  100.1 1.7 %copy-done.2 = bf16[3,2,256,768]{3,2,1,0:T(8,128)(2,1)S(1)} copy-done((bf16[3,2,256,768]{3,2,1,0:T(8,128)(2,1)S(1)}, bf16[3,2,256,768]{3,2,1,0:T(8,128)(2,1)}, u32[]{:S(2)}) %copy-start.2) | copy-done | bytes 2359320
  101.8 1.7 %copy-done.4 = bf16[3,2,256,768]{3,2,1,0:T(8,128)(2,1)S(1)} copy-done((bf16[3,2,256,768]{3,2,1,0:T(8,128)(2,1)S(1)}, bf16[3,2,256,768]{3,2,1,0:T(8,128)(2,1)}, u32[]{:S(2)}) %copy-start.4) | copy-done | bytes 2359320
  104.1 12.8 %collective-permute-done.23.refs_0_.got = bf16[3,1536,128]{2,1,0:T(8,128)(2,1)} collective-permute-done((bf16[3,1536,128]{2,1,0:T(8,128)(2,1)}, bf16[3,1536,128]{2,1,0:T(8,128)(2,1)}, u32[]{:S(2)}, u32[]{:S(2)}) %collective-permute-start.23) | collective-permute-done | bytes 1179680 | tf_op jit(solution)/shard_map/ppermute | solution.py:640
  117.4 2.0 %pass_on.3 = bf16[3,1536,128]{2,1,0:T(8,128)(2,1)S(1)} custom-call(bf16[3,1536,128]{2,1,0:T(8,128)(2,1)} %fold.7.refs_0_.own, bf16[3,1536,128]{2,1,0:T(8,128)(2,1)} %collective-permute-done.23.refs_0_.got), custom_call_target="tpu_custom_call" | custom-call | flops 1179648 | bytes 3538944 | tf_op jit(solution)/shard_map/pass_on/pallas_call | solution.py:577
  120.9 2.6 %collective-permute-start.25 = (bf16[3,1536,128]{2,1,0:T(8,128)(2,1)S(1)}, bf16[3,1536,128]{2,1,0:T(8,128)(2,1)S(1)}, u32[]{:S(2)}, u32[]{:S(2)}) collective-permute-start(bf16[3,1536,128]{2,1,0:T(8,128)(2,1)S(1)} %pass_on.3), channel_id=1, source_target_pairs={{8,16},{12,20},{16,8},{20,12},{9,17},{13,21},{17,9},{21,13},{10,18... | collective-permute-start | bytes 3538952 | tf_op jit(solution)/shard_map/ppermute | solution.py:640
  123.5 2.1 %fusion.1 = bf16[128,2048]{1,0:T(8,128)(2,1)} fusion(bf16[128,2048]{1,0:T(8,128)(2,1)} %collective-permute-done.17, bf16[1,128,2048]{2,1,0:T(8,128)(2,1)S(1)} %copy-done.11, bf16[2,128,2048]{2,1,0:T(8,128)(2,1)S(1)} %copy-done.19), kind=kLoop, calls=%fused_computation.4 | loop fusion | flops 1572864 | bytes 2097152 | tf_op jit(solution)/shard_map/convert_element_type | solution.py:507
  125.6 2.1 %fusion = bf16[128,2048]{1,0:T(8,128)(2,1)} fusion(bf16[128,2048]{1,0:T(8,128)(2,1)} %collective-permute-done.19, bf16[1,128,2048]{2,1,0:T(8,128)(2,1)S(1)} %copy-done.9, bf16[2,128,2048]{2,1,0:T(8,128)(2,1)S(1)} %copy-done.17), kind=kLoop, calls=%fused_computation.2 | loop fusion | flops 1572864 | bytes 2097152 | tf_op jit(solution)/shard_map/convert_element_type | solution.py:507
  127.7 1.7 %add_convert_fusion.refs_0_ = bf16[3,1536,128]{2,1,0:T(8,128)(2,1)S(1)} fusion(bf16[3,1536,128]{2,1,0:T(8,128)(2,1)} %collective-permute-done.22, bf16[3,1536,128]{2,1,0:T(8,128)(2,1)S(1)} %fold.5.other, bf16[3,1536,128]{2,1,0:T(8,128)(2,1)S(1)} %fold.6.one, pred[]{:T(512)S(6)} %gt.3), kind=kLoop, calls=%fused_computation | loop fusion | flops 2949120 | bytes 4718593 | tf_op jit(solution)/shard_map/convert_element_type | solution.py:507
  129.4 16.7 %collective-permute-done.24.refs_1_ = bf16[3,1536,128]{2,1,0:T(8,128)(2,1)S(1)} collective-permute-done((bf16[3,1536,128]{2,1,0:T(8,128)(2,1)S(1)}, bf16[3,1536,128]{2,1,0:T(8,128)(2,1)S(1)}, u32[]{:S(2)}, u32[]{:S(2)}) %collective-permute-start.24) | collective-permute-done | bytes 1179680 | tf_op jit(solution)/shard_map/ppermute | solution.py:640
  146.1 3.0 %collective-permute-done.25.refs_2_ = bf16[3,1536,128]{2,1,0:T(8,128)(2,1)S(1)} collective-permute-done((bf16[3,1536,128]{2,1,0:T(8,128)(2,1)S(1)}, bf16[3,1536,128]{2,1,0:T(8,128)(2,1)S(1)}, u32[]{:S(2)}, u32[]{:S(2)}) %collective-permute-start.25) | collective-permute-done | bytes 1179680 | tf_op jit(solution)/shard_map/ppermute | solution.py:640
  (85 shorter events, 19.2 us)
Async XLA Ops:
  0.6 30.2 %copy-start.14 = (bf16[1,768,2048]{2,1,0:T(8,128)(2,1)S(1)}, bf16[1,768,2048]{2,1,0:T(8,128)(2,1)}, u32[]{:S(2)}) copy-start(bf16[1,768,2048]{2,1,0:T(8,128)(2,1)} %param.19) | copy-start | bytes 9437188
  2.8 17.1 %collective-permute-start = (bf16[128,2048]{1,0:T(8,128)(2,1)}, bf16[128,2048]{1,0:T(8,128)(2,1)S(1)}, u32[]{:S(2)}, u32[]{:S(2)}) collective-permute-start(bf16[128,2048]{1,0:T(8,128)(2,1)} %refs_0_), channel_id=1, source_target_pairs={{0,1},{1,0},{2,3},{3,2},{4,5},{5,4},{6,7},{7,6},{8,9},{9,8},{10,11... | collective-permute-start | bytes 1572872 | tf_op jit(solution)/shard_map/ppermute | solution.py:208
  4.3 15.5 %collective-permute-start.1 = (bf16[128,2048]{1,0:T(8,128)(2,1)}, bf16[128,2048]{1,0:T(8,128)(2,1)S(1)}, u32[]{:S(2)}, u32[]{:S(2)}) collective-permute-start(bf16[128,2048]{1,0:T(8,128)(2,1)} %refs_0_), channel_id=1, source_target_pairs={{0,2},{1,3},{2,0},{3,1},{4,6},{5,7},{6,4},{7,5},{8,10},{9,11},{10,... | collective-permute-start | bytes 1572872 | tf_op jit(solution)/shard_map/ppermute | solution.py:208
  4.8 6.0 %collective-permute-start.4 = (bf16[32,2176]{1,0:T(8,128)(2,1)S(1)}, bf16[32,2176]{1,0:T(8,128)(2,1)S(1)}, u32[]{:S(2)}, u32[]{:S(2)}) collective-permute-start(bf16[32,2176]{1,0:T(8,128)(2,1)S(1)} %get-tuple-element.50), channel_id=1, source_target_pairs={{0,8},{4,12},{8,0},{12,4},{16,24},{20,28},{24,16},{28,20},{1,9},{5... | collective-permute-start | bytes 417800 | tf_op jit(solution)/shard_map/ppermute | solution.py:183
  5.3 12.2 %collective-permute-start.5 = (bf16[32,2176]{1,0:T(8,128)(2,1)S(1)}, bf16[32,2176]{1,0:T(8,128)(2,1)S(1)}, u32[]{:S(2)}, u32[]{:S(2)}) collective-permute-start(bf16[32,2176]{1,0:T(8,128)(2,1)S(1)} %get-tuple-element.51), channel_id=1, source_target_pairs={{0,16},{4,20},{8,24},{12,28},{16,0},{20,4},{24,8},{28,12},{1,17},{... | collective-permute-start | bytes 417800 | tf_op jit(solution)/shard_map/ppermute | solution.py:183
  7.9 14.4 %copy-start.12 = (s32[128,2]{0,1:T(2,128)S(1)}, s32[128,2]{0,1:T(2,128)}, u32[]{:S(2)}) copy-start(s32[128,2]{0,1:T(2,128)} %param.14) | copy-start | bytes 3076
  7.9 14.4 %copy-start.13 = (f32[128,2]{0,1:T(2,128)S(1)}, f32[128,2]{0,1:T(2,128)}, u32[]{:S(2)}) copy-start(f32[128,2]{0,1:T(2,128)} %param.15) | copy-start | bytes 3076
  7.9 12.0 %collective-permute-start.6 = (bf16[32,2176]{1,0:T(8,128)(2,1)S(1)}, bf16[32,2176]{1,0:T(8,128)(2,1)S(1)}, u32[]{:S(2)}, u32[]{:S(2)}) collective-permute-start(bf16[32,2176]{1,0:T(8,128)(2,1)S(1)} %get-tuple-element.52), channel_id=1, source_target_pairs={{0,24},{4,28},{8,16},{12,20},{16,8},{20,12},{24,0},{28,4},{1,25},{... | collective-permute-start | bytes 417800 | tf_op jit(solution)/shard_map/ppermute | solution.py:183
  19.9 2.3 %collective-permute-start.7 = (bf16[64,2176]{1,0:T(8,128)(2,1)S(1)}, bf16[64,2176]{1,0:T(8,128)(2,1)S(1)}, u32[]{:S(2)}, u32[]{:S(2)}) collective-permute-start(bf16[64,2176]{1,0:T(8,128)(2,1)S(1)} %get-tuple-element.54), channel_id=1, source_target_pairs={{0,4},{4,0},{8,12},{12,8},{16,20},{20,16},{24,28},{28,24},{1,5},{5... | collective-permute-start | bytes 835592 | tf_op jit(solution)/shard_map/ppermute | solution.py:658
  20.0 9.2 %collective-permute-start.2 = (bf16[64,2048]{1,0:T(8,128)(2,1)S(1)}, bf16[64,2048]{1,0:T(8,128)(2,1)S(1)}, u32[]{:S(2)}, u32[]{:S(2)}) collective-permute-start(bf16[64,2048]{1,0:T(8,128)(2,1)S(1)} %slice.24), channel_id=1, source_target_pairs={{0,2},{1,3},{2,0},{3,1},{4,6},{5,7},{6,4},{7,5},{8,10},{9,11},{10,... | collective-permute-start | bytes 786440 | tf_op jit(solution)/shard_map/ppermute | solution.py:208
  21.6 9.2 %collective-permute-start.3 = (bf16[64,2048]{1,0:T(8,128)(2,1)S(1)}, bf16[64,2048]{1,0:T(8,128)(2,1)S(1)}, u32[]{:S(2)}, u32[]{:S(2)}) collective-permute-start(bf16[64,2048]{1,0:T(8,128)(2,1)S(1)} %slice.25), channel_id=1, source_target_pairs={{0,1},{1,0},{2,3},{3,2},{4,5},{5,4},{6,7},{7,6},{8,9},{9,8},{10,11... | collective-permute-start | bytes 786440 | tf_op jit(solution)/shard_map/ppermute | solution.py:208
  22.2 20.5 %copy-start.6 = (bf16[1,2048,768]{2,1,0:T(8,128)(2,1)S(1)}, bf16[1,2048,768]{2,1,0:T(8,128)(2,1)}, u32[]{:S(2)}) copy-start(bf16[1,2048,768]{2,1,0:T(8,128)(2,1)} %param.18) | copy-start | bytes 9437188
  22.5 14.3 %collective-permute-start.8 = (bf16[64,2176]{1,0:T(8,128)(2,1)S(1)}, bf16[64,2176]{1,0:T(8,128)(2,1)S(1)}, u32[]{:S(2)}, u32[]{:S(2)}) collective-permute-start(bf16[64,2176]{1,0:T(8,128)(2,1)S(1)} %get-tuple-element.55.refs_0_), channel_id=1, source_target_pairs={{0,1},{1,0},{2,3},{3,2},{4,5},{5,4},{6,7},{7,6},{8,9},{9,8},{10,11... | collective-permute-start | bytes 835592 | tf_op jit(solution)/shard_map/ppermute | solution.py:208
  24.1 12.7 %collective-permute-start.11 = (bf16[64,2176]{1,0:T(8,128)(2,1)S(1)}, bf16[64,2176]{1,0:T(8,128)(2,1)S(1)}, u32[]{:S(2)}, u32[]{:S(2)}) collective-permute-start(bf16[64,2176]{1,0:T(8,128)(2,1)S(1)} %get-tuple-element.56.refs_1_), channel_id=1, source_target_pairs={{0,2},{1,3},{2,0},{3,1},{4,6},{5,7},{6,4},{7,5},{8,10},{9,11},{10,... | collective-permute-start | bytes 835592 | tf_op jit(solution)/shard_map/ppermute | solution.py:208
  24.6 18.2 %collective-permute-start.9 = (bf16[64,2176]{1,0:T(8,128)(2,1)S(1)}, bf16[64,2176]{1,0:T(8,128)(2,1)S(1)}, u32[]{:S(2)}, u32[]{:S(2)}) collective-permute-start(bf16[64,2176]{1,0:T(8,128)(2,1)S(1)} %get-tuple-element.56.refs_1_), channel_id=1, source_target_pairs={{0,1},{1,0},{2,3},{3,2},{4,5},{5,4},{6,7},{7,6},{8,9},{9,8},{10,11... | collective-permute-start | bytes 835592 | tf_op jit(solution)/shard_map/ppermute | solution.py:208
  29.2 13.6 %collective-permute-start.10 = (bf16[64,2176]{1,0:T(8,128)(2,1)S(1)}, bf16[64,2176]{1,0:T(8,128)(2,1)S(1)}, u32[]{:S(2)}, u32[]{:S(2)}) collective-permute-start(bf16[64,2176]{1,0:T(8,128)(2,1)S(1)} %get-tuple-element.55.refs_0_), channel_id=1, source_target_pairs={{0,2},{1,3},{2,0},{3,1},{4,6},{5,7},{6,4},{7,5},{8,10},{9,11},{10,... | collective-permute-start | bytes 835592 | tf_op jit(solution)/shard_map/ppermute | solution.py:208
  31.9 10.9 %copy-start.5 = (bf16[1,2048,768]{2,1,0:T(8,128)(2,1)S(1)}, bf16[1,2048,768]{2,1,0:T(8,128)(2,1)}, u32[]{:S(2)}) copy-start(bf16[1,2048,768]{2,1,0:T(8,128)(2,1)} %param.17) | copy-start | bytes 9437188
  36.8 11.1 %collective-permute-start.12 = (bf16[64,2176]{1,0:T(8,128)(2,1)S(1)}, bf16[64,2176]{1,0:T(8,128)(2,1)S(1)}, u32[]{:S(2)}, u32[]{:S(2)}) collective-permute-start(bf16[64,2176]{1,0:T(8,128)(2,1)S(1)} %collective-permute-done.8.refs_2_), channel_id=1, source_target_pairs={{0,2},{1,3},{2,0},{3,1},{4,6},{5,7},{6,4},{7,5},{8,10},{9,11},{10,... | collective-permute-start | bytes 835592 | tf_op jit(solution)/shard_map/ppermute | solution.py:208
  37.3 10.7 %collective-permute-start.13 = (bf16[64,2176]{1,0:T(8,128)(2,1)S(1)}, bf16[64,2176]{1,0:T(8,128)(2,1)S(1)}, u32[]{:S(2)}, u32[]{:S(2)}) collective-permute-start(bf16[64,2176]{1,0:T(8,128)(2,1)S(1)} %collective-permute-done.11.refs_5_), channel_id=1, source_target_pairs={{0,1},{1,0},{2,3},{3,2},{4,5},{5,4},{6,7},{7,6},{8,9},{9,8},{10,11... | collective-permute-start | bytes 835592 | tf_op jit(solution)/shard_map/ppermute | solution.py:208
  53.1 3.8 %collective-permute-start.14 = (bf16[2,256,768]{2,1,0:T(8,128)(2,1)}, bf16[2,256,768]{2,1,0:T(8,128)(2,1)S(1)}, u32[]{:S(2)}, u32[]{:S(2)}) collective-permute-start(bf16[2,256,768]{2,1,0:T(8,128)(2,1)} %get-tuple-element.71), channel_id=1, source_target_pairs={{0,4},{4,0},{8,12},{12,8},{16,20},{20,16},{24,28},{28,24},{1,5},{5... | collective-permute-start | bytes 2359304 | tf_op jit(solution)/shard_map/ppermute | solution.py:658
  56.4 4.6 %collective-permute-start.15 = (bf16[4,96,2048]{2,1,0:T(8,128)(2,1)}, bf16[4,96,2048]{2,1,0:T(8,128)(2,1)S(1)}, u32[]{:S(2)}, u32[]{:S(2)}) collective-permute-start(bf16[4,96,2048]{2,1,0:T(8,128)(2,1)} %get-tuple-element.76), channel_id=1, source_target_pairs={{0,4},{4,0},{8,12},{12,8},{16,20},{20,16},{24,28},{28,24},{1,5},{5... | collective-permute-start | bytes 4718600 | tf_op jit(solution)/shard_map/ppermute | solution.py:658
  60.9 9.0 %collective-permute-start.20 = (bf16[3,2,256,768]{3,2,1,0:T(8,128)(2,1)}, bf16[3,2,256,768]{3,2,1,0:T(8,128)(2,1)S(1)}, u32[]{:S(2)}, u32[]{:S(2)}) collective-permute-start(bf16[3,2,256,768]{3,2,1,0:T(8,128)(2,1)} %get-tuple-element.84), channel_id=1, source_target_pairs={{0,4},{4,0},{8,12},{12,8},{16,20},{20,16},{24,28},{28,24},{1,5},{5... | collective-permute-start | bytes 7077896 | tf_op jit(solution)/shard_map/ppermute | solution.py:658
  61.3 30.7 %collective-permute-start.21 = (bf16[3,1536,128]{2,1,0:T(8,128)(2,1)S(1)}, bf16[3,1536,128]{2,1,0:T(8,128)(2,1)S(1)}, u32[]{:S(2)}, u32[]{:S(2)}) collective-permute-start(bf16[3,1536,128]{2,1,0:T(8,128)(2,1)S(1)} %fold.4._.own), channel_id=1, source_target_pairs={{0,8},{4,12},{24,16},{28,20},{1,9},{5,13},{25,17},{29,21},{2,10},{... | collective-permute-start | bytes 3538952 | tf_op jit(solution)/shard_map/ppermute | solution.py:640
  62.6 7.3 %copy-start.1 = (bf16[3,2,256,768]{3,2,1,0:T(8,128)(2,1)S(1)}, bf16[3,2,256,768]{3,2,1,0:T(8,128)(2,1)}, u32[]{:S(2)}) copy-start(bf16[3,2,256,768]{3,2,1,0:T(8,128)(2,1)} %get-tuple-element.83.gu_mine) | copy-start | bytes 7077892
  68.8 28.1 %collective-permute-start.16 = (bf16[2,128,2048]{2,1,0:T(8,128)(2,1)S(1)}, bf16[2,128,2048]{2,1,0:T(8,128)(2,1)S(1)}, u32[]{:S(2)}, u32[]{:S(2)}) collective-permute-start(bf16[2,128,2048]{2,1,0:T(8,128)(2,1)S(1)} %get-tuple-element.78), channel_id=1, source_target_pairs={{0,1},{1,0},{2,3},{3,2},{4,5},{5,4},{6,7},{7,6},{8,9},{9,8},{10,11... | collective-permute-start | bytes 3145736 | tf_op jit(solution)/shard_map/ppermute | solution.py:208
  69.4 29.0 %collective-permute-start.18 = (bf16[2,128,2048]{2,1,0:T(8,128)(2,1)S(1)}, bf16[2,128,2048]{2,1,0:T(8,128)(2,1)S(1)}, u32[]{:S(2)}, u32[]{:S(2)}) collective-permute-start(bf16[2,128,2048]{2,1,0:T(8,128)(2,1)S(1)} %get-tuple-element.81), channel_id=1, source_target_pairs={{0,2},{1,3},{2,0},{3,1},{4,6},{5,7},{6,4},{7,5},{8,10},{9,11},{10,... | collective-permute-start | bytes 3145736 | tf_op jit(solution)/shard_map/ppermute | solution.py:208
  71.8 45.2 %collective-permute-start.23 = (bf16[3,1536,128]{2,1,0:T(8,128)(2,1)}, bf16[3,1536,128]{2,1,0:T(8,128)(2,1)}, u32[]{:S(2)}, u32[]{:S(2)}) collective-permute-start(bf16[3,1536,128]{2,1,0:T(8,128)(2,1)} %fold.7.refs_0_.own), channel_id=1, source_target_pairs={{0,8},{4,12},{24,16},{28,20},{1,9},{5,13},{25,17},{29,21},{2,10},{... | collective-permute-start | bytes 3538952 | tf_op jit(solution)/shard_map/ppermute | solution.py:640
  93.4 27.5 %collective-permute-start.22 = (bf16[3,1536,128]{2,1,0:T(8,128)(2,1)}, bf16[3,1536,128]{2,1,0:T(8,128)(2,1)}, u32[]{:S(2)}, u32[]{:S(2)}) collective-permute-start(bf16[3,1536,128]{2,1,0:T(8,128)(2,1)} %pass_on.2), channel_id=1, source_target_pairs={{8,24},{12,28},{16,0},{20,4},{9,25},{13,29},{17,1},{21,5},{10,26},... | collective-permute-start | bytes 3538952 | tf_op jit(solution)/shard_map/ppermute | solution.py:640
  97.9 25.5 %collective-permute-start.17 = (bf16[128,2048]{1,0:T(8,128)(2,1)}, bf16[128,2048]{1,0:T(8,128)(2,1)}, u32[]{:S(2)}, u32[]{:S(2)}) collective-permute-start(bf16[128,2048]{1,0:T(8,128)(2,1)} %fusion.2), channel_id=1, source_target_pairs={{0,2},{1,3},{2,0},{3,1},{4,6},{5,7},{6,4},{7,5},{8,10},{9,11},{10,... | collective-permute-start | bytes 1572872 | tf_op jit(solution)/shard_map/ppermute | solution.py:208
  99.6 26.0 %collective-permute-start.19 = (bf16[128,2048]{1,0:T(8,128)(2,1)}, bf16[128,2048]{1,0:T(8,128)(2,1)}, u32[]{:S(2)}, u32[]{:S(2)}) collective-permute-start(bf16[128,2048]{1,0:T(8,128)(2,1)} %fusion.3), channel_id=1, source_target_pairs={{0,1},{1,0},{2,3},{3,2},{4,5},{5,4},{6,7},{7,6},{8,9},{9,8},{10,11... | collective-permute-start | bytes 1572872 | tf_op jit(solution)/shard_map/ppermute | solution.py:208
  117.3 28.8 %collective-permute-start.24 = (bf16[3,1536,128]{2,1,0:T(8,128)(2,1)S(1)}, bf16[3,1536,128]{2,1,0:T(8,128)(2,1)S(1)}, u32[]{:S(2)}, u32[]{:S(2)}) collective-permute-start(bf16[3,1536,128]{2,1,0:T(8,128)(2,1)S(1)} %choose.1), channel_id=1, source_target_pairs={{0,8},{4,12},{8,0},{12,4},{16,24},{20,28},{24,16},{28,20},{1,9},{5... | collective-permute-start | bytes 3538952 | tf_op jit(solution)/shard_map/ppermute | solution.py:640
  120.9 28.2 %collective-permute-start.25 = (bf16[3,1536,128]{2,1,0:T(8,128)(2,1)S(1)}, bf16[3,1536,128]{2,1,0:T(8,128)(2,1)S(1)}, u32[]{:S(2)}, u32[]{:S(2)}) collective-permute-start(bf16[3,1536,128]{2,1,0:T(8,128)(2,1)S(1)} %pass_on.3), channel_id=1, source_target_pairs={{8,16},{12,20},{16,8},{20,12},{9,17},{13,21},{17,9},{21,13},{10,18... | collective-permute-start | bytes 3538952 | tf_op jit(solution)/shard_map/ppermute | solution.py:640
  (14 other events, 49.9 us)
